TPU v7x, 32 devices: a whole 2x2x4 slice. The times are simulated.
32 devices in a mesh: rows: 8 (over y, x, core), seq: 4 (over z).
Axes of the slice: x: 2, y: 2, z: 4, core: 2. Of those that a mesh axis runs over, the one named last changes fastest.
Arguments:
- block_input: bfloat16 [24, 512, 512], P('rows', 'seq'), may hold values from -6 to 6
- cotangent: bfloat16 [24, 512, 512], P('rows', 'seq'), may hold values from -6 to 6
- gain_attn: float32 [512], replicated, may hold values from 0.5 to 1.5
- w_query: bfloat16 [512, 512], replicated, may hold values from -0.0625 to 0.0625
- w_key: bfloat16 [512, 512], replicated, may hold values from -0.25 to 0.25
- w_value: bfloat16 [512, 512], replicated, may hold values from -0.25 to 0.25
- w_out: bfloat16 [512, 512], replicated, may hold values from -1 to 1
- gain_mlp: float32 [512], replicated, may hold values from 0.5 to 1.5
- w_inner: bfloat16 [512, 2048], replicated, may hold values from -0.25 to 0.25
- outer_weight: bfloat16 [2048, 512], replicated, may hold values from -0.125 to 0.125
- bias_table: float32 [32, 8], replicated, may hold values from -6 to 6
- lengths: int32 [24, 4], P('rows'), may hold values from 1 to 385, 512 in all within a row
- observed: int32 [24, 512], P('rows', 'seq'), may hold values 0 or 1
Outputs:
- block_output: bfloat16 [24, 512, 512], P('rows', 'seq')
- input_grad: bfloat16 [24, 512, 512], P('rows', 'seq')
- grad_gain_attn: float32 [512], replicated
- grad_query: float32 [512, 512], replicated
- grad_key: float32 [512, 512], replicated
- grad_value: float32 [512, 512], replicated
- grad_out: float32 [512, 512], replicated
- grad_gain_mlp: float32 [512], replicated
- grad_inner: float32 [512, 2048], replicated
- grad_outer: float32 [2048, 512], replicated
- grad_table: float32 [32, 8], replicated
Inputs may be any that keep to these rules, and one draw needn't show every extreme that they name: The 4 lengths of a row sum to 512; the largest of each row is 385.
All inputs are finite; a program needn't handle non-finite values. No bound on the sum of `observed` on one device may be relied on, other than what follows from the above.
Results may differ from a plain program's by a relative error of at most 0.014.
Values may be sent and summed in bfloat16 or wider, within the bound.
No kernel may reach another device: no remote copies, remote signals or barrier semaphores. Data moves between devices by JAX's collectives and lax.ppermute only.
A program may use at most 128 MiB of HBM per device.

v0:
```python
import jax
import jax.numpy as jnp
from jax import lax
from jax.sharding import PartitionSpec as P

D = 512
H = 8
HD = 64
BUCKETS = 32
PACKED_LENGTH = 512


EPSILON = 1e-06
BUCKET_EDGES = (12, 16, 23, 32, 46, 64, 91)
EXACT_MATMUL = lax.Precision.HIGHEST


def bucket_of(relative):
    distance = jnp.abs(relative)
    beyond = jnp.full(distance.shape, 8, jnp.int32)
    for edge_value in BUCKET_EDGES:
        beyond = beyond + (distance >= edge_value).astype(jnp.int32)
    near = jnp.where(distance < 8, distance, beyond)
    return jnp.where(relative > 0, 16, 0).astype(jnp.int32) + near


def segment_ids(lengths, total_len):
    segment_ends = jnp.cumsum(lengths, -1)
    places = jnp.arange(total_len, dtype=jnp.int32)
    return jnp.sum((segment_ends[..., None, :] <= places[:, None]).astype(jnp.int32), -1)


def rms_inverse(values):
    return lax.rsqrt(jnp.mean(values * values, -1, keepdims=True) + EPSILON)


def norm_back(values, inv_rms, gain, grad_normed):
    grad_gain = jnp.sum(grad_normed * values * inv_rms, axis=(0, 1))
    scaled = grad_normed * gain
    grad_values = inv_rms * scaled - values * inv_rms**3 * jnp.mean(
        scaled * values, -1, keepdims=True
    )
    return (grad_values, grad_gain)


def flat_dot(left_side, right_side):
    result = jnp.dot(
        left_side.reshape(-1, left_side.shape[-1]), right_side, preferred_element_type=jnp.float32
    )
    return result.reshape(left_side.shape[:-1] + (right_side.shape[1],))


def dot_back(left_side, right_side):
    result = lax.dot_general(
        left_side.reshape(-1, left_side.shape[-1]),
        right_side,
        (((1,), (1,)), ((), ())),
        preferred_element_type=jnp.float32,
    )
    return result.reshape(left_side.shape[:-1] + (right_side.shape[0],))


def weight_grad(left_side, right_side):
    return lax.dot_general(
        left_side.reshape(-1, left_side.shape[-1]),
        right_side.reshape(-1, right_side.shape[-1]),
        (((0,), (0,)), ((), ())),
        preferred_element_type=jnp.float32,
    )


def scores_block(
    query_heads,
    key_block,
    mask_block,
    seg_query,
    seg_key,
    place_query,
    place_key,
    bucket_bias_lookup,
):
    row_count, key_count = (key_block.shape[0], key_block.shape[1])
    key_heads = key_block.reshape(row_count, key_count, H, HD)
    raw_scores = jnp.einsum(
        "rqhe,rkhe->rhqk", query_heads, key_heads, preferred_element_type=jnp.float32
    )
    buckets = bucket_of(place_key[None, :] - place_query[:, None])
    bucket_indicator = (
        buckets[None] == jnp.arange(BUCKETS, dtype=jnp.int32)[:, None, None]
    ).astype(jnp.float32)
    relative_position_bias = jnp.einsum(
        "tag,ty->yag", bucket_indicator, bucket_bias_lookup, precision=EXACT_MATMUL
    )
    allowed = (seg_query[:, :, None] == seg_key[:, None, :]) & (
        (mask_block[:, None, :] == 1) | (place_query[:, None] == place_key[None, :])[None]
    )
    scores = jnp.where(allowed[:, None], raw_scores + relative_position_bias[None], -1000000000.0)
    return (scores, bucket_indicator)


def body(
    block_input,
    cotangent,
    gain_attn,
    w_query,
    w_key,
    w_value,
    w_out,
    gain_mlp,
    w_inner,
    outer_weight,
    bias_table,
    lengths,
    observed,
):
    row_count, tokens_here = (block_input.shape[0], block_input.shape[1])
    first_place = lax.axis_index("seq") * tokens_here
    place_query = first_place + jnp.arange(tokens_here, dtype=jnp.int32)
    segments = segment_ids(lengths, PACKED_LENGTH)
    seg_query = lax.dynamic_slice_in_dim(segments, first_place, tokens_here, 1)
    block_f = block_input.astype(jnp.float32)
    inv_attn = rms_inverse(block_f)
    normed = (block_f * inv_attn * gain_attn).astype(jnp.bfloat16)
    queries = flat_dot(normed, w_query).astype(jnp.bfloat16)
    keys_local = flat_dot(normed, w_key).astype(jnp.bfloat16)
    value_rows_local = flat_dot(normed, w_value).astype(jnp.bfloat16)
    keys_all, values_all, mask_all = (
        lax.all_gather(keys_local, "seq", axis=1, tiled=True),
        lax.all_gather(value_rows_local, "seq", axis=1, tiled=True),
        lax.all_gather(observed, "seq", axis=1, tiled=True),
    )
    query_heads = queries.reshape(row_count, tokens_here, H, HD)
    scores, bucket_indicator = scores_block(
        query_heads,
        keys_all,
        mask_all,
        seg_query,
        segments,
        place_query,
        jnp.arange(PACKED_LENGTH, dtype=jnp.int32),
        bias_table,
    )
    row_top = jnp.max(scores, -1, keepdims=True)
    exponent = jnp.exp(scores - row_top)
    row_total = jnp.sum(exponent, -1, keepdims=True)
    weights_soft = exponent / row_total
    log_total = row_top[..., 0] + jnp.log(row_total[..., 0])
    combined_head_outputs = jnp.einsum(
        "rhqk,rkhe->rqhe",
        weights_soft.astype(jnp.bfloat16),
        values_all.reshape(row_count, PACKED_LENGTH, H, HD),
        preferred_element_type=jnp.float32,
    )
    attended = combined_head_outputs.reshape(row_count, tokens_here, D).astype(jnp.bfloat16)
    middle = block_f + flat_dot(attended, w_out)
    inv_mlp = rms_inverse(middle)
    normed_mlp = (middle * inv_mlp * gain_mlp).astype(jnp.bfloat16)
    inner_pre = flat_dot(normed_mlp, w_inner)
    active_f, gelu_pull = jax.vjp(
        lambda pre_value: jax.nn.gelu(pre_value, approximate=True), inner_pre
    )
    active = active_f.astype(jnp.bfloat16)
    block_output = (middle + flat_dot(active, outer_weight)).astype(jnp.bfloat16)
    grad_outer = weight_grad(active, cotangent)
    grad_inner_act = gelu_pull(dot_back(cotangent, outer_weight))[0].astype(jnp.bfloat16)
    grad_inner = weight_grad(normed_mlp, grad_inner_act)
    grad_normed_mlp = dot_back(grad_inner_act, w_inner)
    grad_middle, grad_gain_mlp = norm_back(middle, inv_mlp, gain_mlp, grad_normed_mlp)
    grad_middle = grad_middle + cotangent.astype(jnp.float32)
    grad_branch = grad_middle.astype(jnp.bfloat16)
    grad_out = weight_grad(attended, grad_branch)
    grad_attended = dot_back(grad_branch, w_out).astype(jnp.bfloat16)
    grad_heads = grad_attended.reshape(row_count, tokens_here, H, HD)
    row_delta = jnp.transpose(
        jnp.sum(grad_heads.astype(jnp.float32) * combined_head_outputs, -1), (0, 2, 1)
    )
    key_block = lax.all_gather(keys_local, "seq", axis=1, tiled=True)
    value_block = lax.all_gather(value_rows_local, "seq", axis=1, tiled=True)
    mask_block = lax.all_gather(observed, "seq", axis=1, tiled=True)
    key_count = key_block.shape[1]
    place_key = jnp.arange(key_count, dtype=jnp.int32)
    scores_now, onehot_now = scores_block(
        query_heads, key_block, mask_block, seg_query, segments, place_query, place_key, bias_table
    )
    probs_now = jnp.exp(scores_now - log_total[..., None])
    key_heads = key_block.reshape(row_count, key_count, H, HD)
    value_heads = value_block.reshape(row_count, key_count, H, HD)
    grad_probs = jnp.einsum(
        "rqhe,rkhe->rhqk", grad_heads, value_heads, preferred_element_type=jnp.float32
    )
    grad_scores = (probs_now * (grad_probs - row_delta[..., None])).astype(jnp.bfloat16)
    grad_queries = jnp.einsum(
        "rhqk,rkhe->rqhe", grad_scores, key_heads, preferred_element_type=jnp.float32
    ).reshape(row_count, tokens_here, D)
    key_part = jnp.einsum(
        "rhqk,rqhe->rkhe", grad_scores, query_heads, preferred_element_type=jnp.float32
    ).reshape(row_count, key_count, D)
    value_part = jnp.einsum(
        "rhqk,rqhe->rkhe",
        probs_now.astype(jnp.bfloat16),
        grad_heads,
        preferred_element_type=jnp.float32,
    ).reshape(row_count, key_count, D)
    grad_keys = key_part
    grad_values = value_part
    grad_table = jnp.einsum(
        "jgzl,vzl->vg",
        grad_scores,
        onehot_now.astype(jnp.bfloat16),
        preferred_element_type=jnp.float32,
    )
    running = (grad_queries, grad_keys, grad_values, grad_table)
    key_sums, value_sums = (
        lax.psum_scatter(
            running[1].astype(jnp.bfloat16), "seq", scatter_dimension=1, tiled=True
        ).astype(jnp.float32),
        lax.psum_scatter(
            running[2].astype(jnp.bfloat16), "seq", scatter_dimension=1, tiled=True
        ).astype(jnp.float32),
    )
    grad_table = running[3]
    grad_queries = running[0].astype(jnp.bfloat16)
    grad_keys = key_sums.astype(jnp.bfloat16)
    grad_values = value_sums.astype(jnp.bfloat16)
    grad_query = weight_grad(normed, grad_queries)
    grad_key = weight_grad(normed, grad_keys)
    grad_value = weight_grad(normed, grad_values)
    grad_normed = (
        dot_back(grad_queries, w_query)
        + dot_back(grad_keys, w_key)
        + dot_back(grad_values, w_value)
    )
    grad_block, grad_gain_attn = norm_back(block_f, inv_attn, gain_attn, grad_normed)
    input_grad = (grad_middle + grad_block).astype(jnp.bfloat16)
    summed = lax.psum(
        (
            grad_gain_attn,
            grad_query,
            grad_key,
            grad_value,
            grad_out,
            grad_gain_mlp,
            grad_inner,
            grad_outer,
            grad_table,
        ),
        ("rows", "seq"),
    )
    return (
        block_output,
        input_grad,
        summed[0],
        summed[1],
        summed[2],
        summed[3],
        summed[4],
        summed[5],
        summed[6],
        summed[7],
        summed[8],
    )


def solution(mesh):
    placed = (
        P("rows", "seq", None),
        P("rows", "seq", None),
        P(),
        P(),
        P(),
        P(),
        P(),
        P(),
        P(),
        P(),
        P(),
        P("rows", None),
        P("rows", "seq"),
    )
    return jax.shard_map(
        body,
        mesh=mesh,
        in_specs=placed,
        out_specs=(
            P("rows", "seq", None),
            P("rows", "seq", None),
            P(),
            P(),
            P(),
            P(),
            P(),
            P(),
            P(),
            P(),
            P(),
        ),
        check_vma=False,
    )
```

profile of v0, /device:TPU:1, one launch (start us, length us, event | category | flops | bytes accessed | tf_op | source)
XLA Modules:
  0.0 455.2 jit_solution(524171049359151808)
XLA Ops:
  7.2 1.3 fusion.36
  8.5 2.4 convolution_convert_fusion.3
  11.1 2.4 convolution_convert_fusion.5
  13.5 0.3 fusion.55
  13.8 1.2 iota_compare_fusion
  15.0 37.3 %copy.83 = pred[32,128,512]{2,0,1:T(32,128)(4,1)S(1)} copy(pred[32,128,512]{1,0,2:T(32,128)(4,1)S(1)} %iota_compare_fusion) | data formatting | bytes 4194304 | tf_op jit(solution)/shard_map/eq | solution.py:89
  52.3 2.2 convolution_bitcast_fusion.2
  54.6 2.5 copy.84
  57.1 0.2 reduce_window_sum.11
  57.3 0.2 copy.80
  57.5 0.4 convolution_convert_fusion.4
  57.9 0.2 copy.81
  58.2 11.1 %all_gather.13 = s32[3,512]{1,0:T(4,128)S(1)} all-gather(s32[3,128]{1,0:T(4,128)S(1)} %copy-done.38), channel_id=1, replica_groups=mesh['rows'=8,'seq'=4] {'seq'}, dimensions={1}, use_global_device_ids=true | all-gather | bytes 7680 | tf_op jit(solution)/shard_map/all_gather | solution.py:130
  69.4 0.2 or_and_fusion
  69.7 2.6 copy.82
  72.4 3.6 fusion.3
  76.0 1.9 fusion
  77.8 0.8 copy-done.2
  78.6 9.8 %all-gather.3.cloned.1.call-done = bf16[3,512,512]{2,1,0:T(8,128)(2,1)} async-done(((bf16[3,128,512]{2,1,0:T(8,128)(2,1)}), bf16[3,512,512]{2,1,0:T(8,128)(2,1)}) %all-gather.3.cloned.1.call-update) | async-done | bytes 1572880 | tf_op jit(solution)/shard_map/all_gather | solution.py:129
  88.4 2.6 copy.79
  91.0 6.9 %fusion.76 = (bf16[3,128,8,64]{1,3,2,0:T(8,128)(2,1)S(1)}, f32[3,128,8,64]{1,3,2,0:T(8,128)}) fusion(bf16[3,512,8,64]{1,3,2,0:T(8,128)(2,1)} %bitcast.106, f32[3,8,128,512]{3,2,1,0:T(8,128)} %copy-done.2, f32[3,8,128]{2,1,0:T(8,128)S(1)} %fusion, f32[3,8,128]{2,1,0:T(8,128)S(1)} %get-tuple-element.28, f32[8,128,512]{2,1,0:T(8,128)} %copy.84, ...), kind=kOutput, calls=%fused_computation.117 | convolution fusion | flops 209387520 | bytes 11362304 | tf_op jit(solution)/shard_map/rhqk,rkhe->rqhe/dot_general | solution.py:148
  97.9 0.5 multiply_reduce_fusion.3
  98.5 1.0 fusion.23
  99.5 0.7 copy-done.40
  100.2 2.9 fusion.10
  103.1 1.3 multiply_reduce_fusion
  104.4 0.3 convert_add_fusion.1
  104.7 0.9 copy-done.8
  105.6 1.2 convolution_convert_fusion.2
  106.8 1.9 copy.86
  108.7 1.3 multiply_reduce_fusion.1
  110.1 7.3 %convert_reduce_fusion = (bf16[8,128,512]{2,1,0:T(8,128)(2,1)}, bf16[3,8,128,512]{3,2,1,0:T(8,128)(2,1)S(1)}) fusion(f32[3,8,128]{2,1,0:T(8,128)S(1)} %bitcast.115, bf16[3,128,8,64]{1,3,2,0:T(8,128)(2,1)} %bitcast.104, bf16[3,512,8,64]{1,3,2,0:T(8,128)(2,1)} %bitcast.107, f32[3,8,128]{2,1,0:T(8,128)S(1)} %log_add_fusion, f32[3,8,128,512]{3,2,1,0:T(8,128)} %copy-done.2, ...), kind=kOutput, calls=%fused_computation.2 | convolution fusion | flops 213385216 | bytes 14770176 | tf_op jit(solution)/shard_map/rqhe,rkhe->rhqk/dot_general | solution.py:188
  117.4 2.1 convolution_convert_fusion
  119.4 0.1 copy-done.5
  119.5 2.6 copy.88
  122.3 5.9 %fusion.25 = bf16[3,8,64,512]{3,2,1,0:T(8,128)(2,1)} fusion(bf16[3,128,8,64]{1,3,2,0:T(8,128)(2,1)} %bitcast.105, f32[3,8,128,512]{3,2,1,0:T(8,128)} %copy-done.2, f32[3,8,128]{2,1,0:T(8,128)S(1)} %log_add_fusion, f32[8,128,512]{2,1,0:T(8,128)S(1)} %copy-done.4, pred[3,128,512]{2,1,0:T(8,128)(4,1)S(1)} %or_and_fusion), kind=kOutput, calls=%fused_computation.43 | convolution fusion | flops 208404480 | bytes 10563584 | tf_op jit(solution)/shard_map/rhqk,rqhe->rkhe/dot_general | solution.py:198
  128.2 2.7 copy.89
  130.9 0.3 all-reduce.4.cloned.1.call-start
  131.3 3.2 convolution_convert_fusion.1
  134.4 1.6 convolution_bitcast_fusion.6
  136.0 1.4 convolution_bitcast_fusion.3
  137.5 3.4 convolution_bitcast_fusion.1
  140.9 3.5 convolution_bitcast_fusion
  144.4 12.1 %reduce-scatter.3.cloned.1.call-done = bf16[3,128,512]{2,1,0:T(8,128)(2,1)} async-done(((bf16[3,512,512]{2,1,0:T(8,128)(2,1)}), bf16[3,128,512]{2,1,0:T(8,128)(2,1)}) %reduce-scatter.3.cloned.1.call-update) | async-done | bytes 393232 | tf_op jit(solution)/shard_map/reduce_scatter | solution.py:214
  156.5 2.5 convolution_bitcast_fusion.5
  159.0 33.9 %reduce-scatter.5.cloned.1.call-done = bf16[3,128,512]{2,1,0:T(8,128)(2,1)} async-done(((bf16[3,512,512]{2,1,0:T(8,128)(2,1)}), bf16[3,128,512]{2,1,0:T(8,128)(2,1)}) %reduce-scatter.5.cloned.1.call-update) | async-done | bytes 393232 | tf_op jit(solution)/shard_map/reduce_scatter | solution.py:217
  192.9 2.5 convolution_bitcast_fusion.4
  195.5 1.2 copy-done.18
  196.7 1.5 copy.96
  198.2 2.6 fusion.35
  200.7 1.5 fusion.50
  202.3 1.9 fusion.32
  204.2 0.4 convolution_add_fusion.1
  204.6 0.6 fusion.45
  205.2 41.4 %all-reduce = (f32[512]{0:T(512)}, f32[512]{0:T(512)}, f32[32,8]{0,1:T(8,128)}) all-reduce(f32[512]{0:T(512)S(1)} %get-tuple-element.13, f32[512]{0:T(512)S(1)} %get-tuple-element.11, f32[32,8]{0,1:T(8,128)S(1)} %fusion.35), channel_id=1, replica_groups=mesh['rows'=8,'seq'=4] {'rows','seq'}, use_global_device_ids=true, to_apply=%region_12.13 | all-reduce | flops 1280 | bytes 10240 | tf_op jit(solution)/shard_map/psum | solution.py:235
  246.6 1.0 fusion.42
  247.6 188.6 %all-reduce.4.cloned.1.call-done = (f32[512,512]{1,0:T(8,128)}, f32[512,512]{1,0:T(8,128)}, f32[512,512]{1,0:T(8,128)}, f32[512,512]{1,0:T(8,128)}, f32[512,2048]{1,0:T(8,128)}, /*index=5*/f32[2048,512]{1,0:T(8,128)}) async-done(((f32[512,512]{1,0:T(8,128)}, f32[512,512]{1,0:T(8,128)}, f32[512,512]{1,0:T(8,128)}, f32[512,512]{1,0:T(8,128)}, f32[512,2048]{1,0:T(8,128)}, /*index=5*/f32[2048,512]{1,0:T(8,128)}), ...) | async-done | bytes 12582928 | tf_op jit(solution)/shard_map/psum | solution.py:235
  436.2 2.4 copy.113
  438.6 2.4 copy.114
  441.0 1.0 copy.115
  442.0 1.0 copy.116
  443.0 2.1 copy.117
  445.1 1.6 copy-done.16
  446.7 2.0 copy.118
  (98 shorter events, 0.7 us)
Async XLA Ops:
  7.2 91.2 %copy-start = (bf16[512,2048]{1,0:T(8,128)(2,1)S(1)}, bf16[512,2048]{1,0:T(8,128)(2,1)}, u32[]{:S(2)}) copy-start(bf16[512,2048]{1,0:T(8,128)(2,1)} %param.21) | copy-start | bytes 6291460
  7.2 62.5 %all-gather.5.cloned.1.call-start = ((), (), s32[]{:S(2)}) async-start(), calls=%async_computation.3 | async-start | bytes 1966080 | tf_op jit(solution)/shard_map/all_gather | solution.py:128
  11.0 77.4 %all-gather.3.cloned.1.call-start = ((), (), s32[]{:S(2)}) async-start(), calls=%async_computation.2 | async-start | bytes 1966080 | tf_op jit(solution)/shard_map/all_gather | solution.py:129
  13.4 143.1 %reduce-scatter.3.cloned.1.call-start = ((), (), s32[]{:S(2)}) async-start(), calls=%async_computation.4 | async-start | bytes 1966080 | tf_op jit(solution)/shard_map/reduce_scatter | solution.py:214
  13.8 38.5 %copy-start.26 = (s32[128,512]{0,1:T(8,128)}, s32[128,512]{0,1:T(8,128)S(1)}, u32[]{:S(2)}) copy-start(s32[128,512]{0,1:T(8,128)S(1)} %fusion.55) | copy-start | bytes 786436
  13.8 38.5 %copy-start.37 = (f32[32,8]{0,1:T(8,128)S(1)}, f32[32,8]{0,1:T(8,128)}, u32[]{:S(2)}) copy-start(f32[32,8]{0,1:T(8,128)} %param.23) | copy-start | bytes 3076
  54.5 2.6 copy-start.39
  54.5 3.0 copy-start.6
  54.5 3.0 copy-start.31
  54.5 3.0 copy-start.36
  54.5 3.6 copy-start.38
  58.2 17.8 %copy-start.14 = (bf16[3,128,512]{1,2,0:T(8,128)(2,1)}, bf16[3,128,512]{1,2,0:T(8,128)(2,1)S(1)}, u32[]{:S(2)}) copy-start(bf16[3,128,512]{1,2,0:T(8,128)(2,1)S(1)} %copy.81) | copy-start | bytes 1179652
  72.3 3.6 copy-start.3
  75.9 2.7 copy-start.2
  91.0 6.9 %copy-start.19 = (bf16[512,512]{1,0:T(8,128)(2,1)S(1)}, bf16[512,512]{1,0:T(8,128)(2,1)}, u32[]{:S(2)}) copy-start(bf16[512,512]{1,0:T(8,128)(2,1)} %param.19) | copy-start | bytes 1572868
  91.0 7.4 %copy-start.35 = (f32[512]{0:T(512)S(1)}, f32[512]{0:T(512)}, u32[]{:S(2)}) copy-start(f32[512]{0:T(512)} %param.20) | copy-start | bytes 6148
  97.9 1.6 copy-start.23
  98.4 1.1 copy-start.33
  98.4 1.7 copy-start.40
  100.2 3.0 copy-start.11
  103.1 1.6 copy-start.21
  104.4 5.6 %copy-start.4 = (f32[8,128,512]{2,1,0:T(8,128)S(1)}, f32[8,128,512]{2,1,0:T(8,128)}, u32[]{:S(2)}) copy-start(f32[8,128,512]{2,1,0:T(8,128)} %copy.84) | copy-start | bytes 6291460
  104.7 0.9 copy-start.8
  110.0 7.3 %copy-start.15 = (bf16[3,128,512]{1,2,0:T(8,128)(2,1)S(1)}, bf16[3,128,512]{1,2,0:T(8,128)(2,1)}, u32[]{:S(2)}) copy-start(bf16[3,128,512]{1,2,0:T(8,128)(2,1)} %copy-done.14) | copy-start | bytes 1179652
  117.4 2.2 copy-start.5
  122.2 70.7 %reduce-scatter.5.cloned.1.call-start = ((), (), s32[]{:S(2)}) async-start(), calls=%async_computation.5 | async-start | bytes 1966080 | tf_op jit(solution)/shard_map/reduce_scatter | solution.py:217
  128.2 3.0 copy-start.7
  130.9 305.3 %all-reduce.4.cloned.1.call-start = ((), (), s32[]{:S(2)}) async-start(), calls=%async_computation.6 | async-start | bytes 25165824 | tf_op jit(solution)/shard_map/psum | solution.py:235
  131.2 4.8 %copy-start.9 = (f32[3,128,512]{2,1,0:T(8,128)S(1)}, f32[3,128,512]{2,1,0:T(8,128)}, u32[]{:S(2)}) copy-start(f32[3,128,512]{2,1,0:T(8,128)} %copy-done.8) | copy-start | bytes 2359300
  131.3 4.8 %copy-start.24 = (bf16[3,128,8,64]{1,3,2,0:T(8,128)(2,1)S(1)}, bf16[3,128,8,64]{1,3,2,0:T(8,128)(2,1)}, u32[]{:S(2)}) copy-start(bf16[3,128,8,64]{1,3,2,0:T(8,128)(2,1)} %copy-done.23) | copy-start | bytes 1179652
  134.4 3.0 copy-start.22
  137.5 3.4 copy-start.12
  137.5 3.4 copy-start.34
  195.5 1.2 copy-start.18
  195.5 2.7 copy-start.27
  198.2 4.0 copy-start.13
  198.2 4.0 copy-start.41
  202.2 1.9 copy-start.20
  202.2 1.9 copy-start.30
  202.2 2.3 copy-start.25
  202.2 2.3 copy-start.32
  204.1 42.4 %copy-start.10 = (f32[3,128,512]{2,1,0:T(8,128)S(1)}, f32[3,128,512]{2,1,0:T(8,128)}, u32[]{:S(2)}) copy-start(f32[3,128,512]{2,1,0:T(8,128)} %copy-done.8) | copy-start | bytes 2359300
  436.2 4.8 %copy-start.29 = (f32[512,512]{1,0:T(8,128)S(1)}, f32[512,512]{1,0:T(8,128)}, u32[]{:S(2)}) copy-start(f32[512,512]{1,0:T(8,128)} %get-tuple-element.43) | copy-start | bytes 3145732
  436.2 5.8 %copy-start.28 = (f32[512,512]{1,0:T(8,128)S(1)}, f32[512,512]{1,0:T(8,128)}, u32[]{:S(2)}) copy-start(f32[512,512]{1,0:T(8,128)} %get-tuple-element.44) | copy-start | bytes 3145732
  438.6 4.4 copy-start.17
  443.0 3.7 copy-start.16
  443.0 5.7 %copy-start.1 = (bf16[512,2048]{1,0:T(8,128)(2,1)S(1)}, bf16[512,2048]{1,0:T(8,128)(2,1)}, u32[]{:S(2)}) copy-start(bf16[512,2048]{1,0:T(8,128)(2,1)} %param.21) | copy-start | bytes 6291460
Sparse Core Ops, SparseCore 0:
  11.1 39.0 all-gather.4
  52.3 36.0 all-gather.2
  122.3 34.1 reduce-scatter.2
  158.7 34.2 reduce-scatter.4
  200.4 235.7 all-reduce.3
where the time goes:
time: 457 us; the launch traced here: 455 us
  waiting for transfers between devices  245 us (54%)
  local copies, waits for them, and re-layouts  70.4 us (15%)
  matrix products  65.1 us (14%)
  blocking collectives  52.5 us (11%)
  between operations  14.3 us (3%)
  other arithmetic  7.84 us (2%)
    psum x1, waiting for transfers between devices, body(): lax.psum((grad_gain_attn, grad_query, grad_key, grad_value, grad_out, gra...  189 us
    psum x1, blocking collectives, body(): lax.psum((grad_gain_attn, grad_query, grad_key, grad_value, grad_out, gra...  41.4 us
    eq x1, local copies, waits for them, and re-layouts, scores_block(): buckets[None] == jnp.arange(BUCKETS, dtype=jnp.int32)[:, None, None]  37.3 us
    reduce_scatter x1, waiting for transfers between devices, body(): lax.psum_scatter(running[2].astype(jnp.bfloat16), 'seq', scatter_dimensio...  33.9 us
    unnamed x90, local copies, waits for them, and re-layouts  16.3 us
    dot_general x6, matrix products, weight_grad(): lax.dot_general(left_side.reshape(-1, left_side.shape[-1]), right_side.re...  15 us
    reduce_scatter x1, waiting for transfers between devices, body(): lax.psum_scatter(running[1].astype(jnp.bfloat16), 'seq', scatter_dimensio...  12.1 us
    all_gather x1, blocking collectives, body(): lax.all_gather(observed, 'seq', axis=1, tiled=True)  11.1 us
  transfers between devices with their start and end apart: 5, of which 4 were waited for; matrix products, arithmetic and copies ran while one was open for 20% of the time, Pallas kernels for 0%

commit v1 on v0

v1 whole, which is shorter than its diff:
```python
import functools

import jax
import jax.numpy as jnp
from jax import lax
from jax.experimental import pallas as pl
from jax.experimental.pallas import tpu as pltpu
from jax.sharding import PartitionSpec as P

D = 512
FF = 2048
H = 8
HD = 64
PAIRS = H // 2
BUCKETS = 32
PACKED_LENGTH = 512
EPSILON = 1e-06
BUCKET_EDGES = (12, 16, 23, 32, 46, 64, 91)
SPAN = 2 * PACKED_LENGTH
CHUNKS = 32
HALF = CHUNKS // 2
OUTER_ROWS = FF // CHUNKS
SMALL_ROWS = D // CHUNKS
FF_TILE = 512
MASKED = -1000000000.0
VMEM_LIMIT = 30 * 1024 * 1024
F32 = jnp.float32
BF16 = jnp.bfloat16


def dot(left, right, contract=(1, 0), precision=None):
    return lax.dot_general(
        left,
        right,
        (((contract[0],), (contract[1],)), ((), ())),
        preferred_element_type=F32,
        precision=precision,
    )


def xor_pairs(size, bit):
    return [(i, i ^ bit) for i in range(size)]


def bucket_of(relative):
    distance = jnp.abs(relative)
    beyond = jnp.full(distance.shape, 8, jnp.int32)
    for edge_value in BUCKET_EDGES:
        beyond = beyond + (distance >= edge_value).astype(jnp.int32)
    near = jnp.where(distance < 8, distance, beyond)
    return jnp.where(relative > 0, 16, 0).astype(jnp.int32) + near


def bucket_rows(shape, bucket_axis):
    place_axis = 1 - bucket_axis
    relative = lax.broadcasted_iota(jnp.int32, shape, place_axis) - PACKED_LENGTH
    return (bucket_of(relative) == lax.broadcasted_iota(jnp.int32, shape, bucket_axis)).astype(F32)


def split_heads(pair):
    lane = lax.broadcasted_iota(jnp.int32, pair.shape, 1)
    zero = jnp.zeros_like(pair)
    return jnp.concatenate(
        [jnp.where(lane < HD, pair, zero), jnp.where(lane >= HD, pair, zero)], axis=0
    )


def join_heads(stacked):
    half = stacked.shape[0] // 2
    lane = lax.broadcasted_iota(jnp.int32, (half, stacked.shape[1]), 1)
    return jnp.where(lane < HD, stacked[:half], stacked[half:])


def bias_kernel(place_ref, table_ref, bias_ref, line_ref, *, here, seq):
    line_ref[...] = dot(
        table_ref[...], bucket_rows((BUCKETS, SPAN), 0), (0, 0), lax.Precision.HIGHEST
    )
    me = place_ref[0]
    for block in range(seq):
        offset = ((me ^ block) - me) * here + PACKED_LENGTH - here
        window = line_ref[:, pl.ds(pl.multiple_of(offset, 128), 2 * here)]
        for head in range(H):
            spread = jnp.broadcast_to(window[head : head + 1], (here, 2 * here))
            skewed = pltpu.roll(spread, here, 1, stride=1, stride_axis=0)
            row = (head % 2) * here
            bias_ref[head // 2, row : row + here, block * here : (block + 1) * here] = skewed[
                :, :here
            ]


def attention_kernel(
    place_ref,
    lengths_ref,
    x0_ref,
    x1_ref,
    x2_ref,
    x3_ref,
    seen_ref,
    gain_ref,
    wq_ref,
    wk_ref,
    wv_ref,
    w_out_ref,
    gain_mlp_ref,
    bias_ref,
    *refs,
    row,
    here,
    seq,
):
    (
        normed_mlp_ref,
        attended_ref,
        middle_ref,
        mixed_ref,
        normed_ref,
        q_ref,
        k_ref,
        v_ref,
        p_ref,
    ) = refs[-9:]
    me = place_ref[0]
    own_x = x0_ref[0].astype(F32)
    x = jnp.concatenate(
        [own_x] + [ref[...].astype(F32) for ref in (x1_ref, x2_ref, x3_ref)], axis=0
    )
    inv = lax.rsqrt(jnp.mean(x * x, -1, keepdims=True) + EPSILON)
    normed = (x * inv * gain_ref[...]).astype(BF16)
    normed_ref[0] = normed
    q = dot(normed[:here], wq_ref[...]).astype(BF16)
    k = dot(normed, wk_ref[...]).astype(BF16)
    v = dot(normed, wv_ref[...]).astype(BF16)
    q_ref[0] = q
    k_ref[0] = k
    v_ref[0] = v
    ends = [lengths_ref[row, 0]]
    for part in range(1, lengths_ref.shape[1]):
        ends.append(ends[-1] + lengths_ref[row, part])

    def segment(place):
        total = jnp.zeros(place.shape, jnp.int32)
        for end in ends:
            total = total + (end <= place).astype(jnp.int32)
        return total

    query_place = me * here + lax.broadcasted_iota(jnp.int32, (here, 1), 0)
    lane = lax.broadcasted_iota(jnp.int32, (1, here), 1)
    key_place = jnp.concatenate([(me ^ block) * here + lane for block in range(seq)], axis=1)
    seen = jnp.concatenate([seen_ref[0, block : block + 1] for block in range(seq)], axis=1)
    key_segment = jnp.where(seen == 1, segment(key_place), -1)
    allowed = (segment(query_place) == key_segment) | (query_place == key_place)
    allowed = jnp.concatenate([allowed.astype(jnp.int32)] * 2, axis=0) == 1
    attended = []
    for pair in range(PAIRS):
        lanes = slice(pair * 2 * HD, (pair + 1) * 2 * HD)
        scores = dot(split_heads(q[:, lanes]), k[:, lanes], (1, 1)) + bias_ref[pair]
        scores = jnp.where(allowed, scores, MASKED)
        exponent = jnp.exp(scores - jnp.max(scores, -1, keepdims=True))
        share = 1.0 / jnp.sum(exponent, -1, keepdims=True)
        probs = (exponent * share).astype(BF16)
        p_ref[0, pair] = probs
        mixed = join_heads(dot(probs, v[:, lanes]))
        mixed_ref[0, :, lanes] = mixed
        attended.append(mixed.astype(BF16))
    attended = jnp.concatenate(attended, axis=1)
    attended_ref[0] = attended
    middle = own_x + dot(attended, w_out_ref[...])
    middle_ref[0] = middle
    inv = lax.rsqrt(jnp.mean(middle * middle, -1, keepdims=True) + EPSILON)
    normed_mlp_ref[...] = (middle * inv * gain_mlp_ref[...]).astype(BF16)


def gelu_both(u):
    scale = 0.7978845608028654
    square = u * u
    t = jnp.tanh(u * (scale + (scale * 0.044715) * square))
    half_up = 0.5 + 0.5 * t
    slope = half_up + (0.5 * u) * (1.0 - t * t) * (scale + (3.0 * 0.044715 * scale) * square)
    return u * half_up, slope


def mlp_kernel(half_ref, nm_ref, g_ref, w_inner_ref, w_outer_ref, *refs, deal, prior):
    if deal:
        label_ref = half_ref
        old_nm = refs[:prior]
        old_active = refs[prior : 2 * prior]
        old_grad = refs[2 * prior : 3 * prior]
        old_g = refs[3 * prior]
        total_in, back_in = refs[3 * prior + 1 : 3 * prior + 3]
        total_ref, back_ref, parts_ref = refs[-3:]
    else:
        total_ref, back_ref, active_ref, grad_ref = refs[-4:]
    step = pl.program_id(0)
    normed = nm_ref[...]
    g = g_ref[0]
    w_inner = w_inner_ref[...]
    w_outer = w_outer_ref[...]
    active_f, slope = gelu_both(dot(normed, w_inner))
    active = active_f.astype(BF16)
    grad_act = (dot(g, w_outer, (1, 1)) * slope).astype(BF16)

    @pl.when(step == 0)
    def _():
        if deal:
            total_ref[...] = total_in[...]
            back_ref[...] = back_in[...]
        else:
            total_ref[...] = jnp.zeros_like(total_ref)
            back_ref[...] = jnp.zeros_like(back_ref)

    total_ref[0] += dot(active, w_outer)
    back_ref[0] += dot(grad_act, w_inner, (1, 1))
    if not deal:
        active_ref[...] = active
        grad_ref[...] = grad_act
        return
    all_active = jnp.concatenate([ref[...] for ref in old_active] + [active], axis=0)
    all_grad = jnp.concatenate([ref[...] for ref in old_grad] + [grad_act], axis=0)
    all_normed = jnp.concatenate([ref[...] for ref in old_nm] + [normed], axis=0)
    all_g = jnp.concatenate([old_g[i] for i in range(prior)] + [g], axis=0)
    outer = dot(all_active, all_g, (0, 0)).astype(BF16)
    inner = dot(all_grad, all_normed, (0, 0)).astype(BF16)
    label = label_ref[1]
    for part in range(FF_TILE // OUTER_ROWS):
        slot = (step * (FF_TILE // OUTER_ROWS) + part) ^ label
        rows = slice(part * OUTER_ROWS, (part + 1) * OUTER_ROWS)
        parts_ref[slot, :OUTER_ROWS] = outer[rows]
        parts_ref[slot, OUTER_ROWS:] = inner[rows]


def back_kernel(
    place_ref,
    code_ref,
    g_ref,
    total_ref,
    back_ref,
    middle_ref,
    attended_ref,
    mixed_ref,
    normed_ref,
    q_ref,
    k_ref,
    v_ref,
    p_ref,
    gain_mlp_ref,
    w_out_ref,
    wq_ref,
    wk_ref,
    wv_ref,
    pin_ref,
    block_output_ref,
    grad_middle_ref,
    dx_keep_ref,
    dx_send_ref,
    keep_ref,
    send_ref,
    table_ref,
    gain_grad_ref,
    gain_mlp_grad_ref,
    table_sum_ref,
    line_ref,
    go_ref,
    gq_ref,
    gk_ref,
    gv_ref,
    stage_ref,
    *,
    here,
    seq,
):
    step = pl.program_id(0)

    @pl.when(step == 0)
    def _():
        for ref in (table_sum_ref, go_ref, gq_ref, gk_ref, gv_ref, gain_mlp_grad_ref):
            ref[...] = jnp.zeros_like(ref)

    middle = middle_ref[0]
    back = back_ref[0]
    block_output_ref[0] = (middle + total_ref[0]).astype(BF16)
    inv = lax.rsqrt(jnp.mean(middle * middle, -1, keepdims=True) + EPSILON)
    gain_mlp_grad_ref[...] += jnp.sum(back * middle * inv, axis=0, keepdims=True)
    scaled = back * gain_mlp_ref[...]
    grad_middle = (
        g_ref[0].astype(F32)
        + inv * scaled
        - middle * (inv * inv * inv) * jnp.mean(scaled * middle, -1, keepdims=True)
    )
    grad_middle_ref[0] = grad_middle
    branch = grad_middle.astype(BF16)
    ga = dot(branch, w_out_ref[...], (1, 1)).astype(BF16)
    go_ref[...] += dot(attended_ref[0], branch, (0, 0))
    q = q_ref[0]
    k = k_ref[0]
    v = v_ref[0]
    normed = normed_ref[0]
    dq, dkt, dvt = [], [], []
    for pair in range(PAIRS):
        lanes = slice(pair * 2 * HD, (pair + 1) * 2 * HD)
        ga_split = split_heads(ga[:, lanes])
        q_split = split_heads(q[:, lanes])
        mixed = mixed_ref[0, :, lanes]
        probs = p_ref[0, pair]
        delta = jnp.sum(
            ga_split.astype(F32) * jnp.concatenate([mixed, mixed], axis=0), -1, keepdims=True
        )
        grad_probs = dot(ga_split, v[:, lanes], (1, 1))
        grad_scores_f = probs.astype(F32) * (grad_probs - delta)
        table_sum_ref[pair] += grad_scores_f
        grad_scores = grad_scores_f.astype(BF16)
        dq.append(join_heads(dot(grad_scores, k[:, lanes])).astype(BF16))
        dkt.append(dot(q_split, grad_scores, (0, 0)).astype(BF16))
        dvt.append(dot(ga_split, probs, (0, 0)).astype(BF16))
    dq = jnp.concatenate(dq, axis=1)
    dkt = jnp.concatenate(dkt, axis=0)
    dvt = jnp.concatenate(dvt, axis=0)
    dxt = dot(wk_ref[...], dkt) + dot(wv_ref[...], dvt)
    own = dxt[:, :here] + dot(wq_ref[...], dq, (1, 1))
    dx_keep_ref[0, 0] = own.astype(BF16)
    for block in range(1, seq):
        target = dx_send_ref if block % 2 else dx_keep_ref
        target[block // 2, 0] = dxt[:, block * here : (block + 1) * here].astype(BF16)
    gq_ref[...] += dot(normed[:here], dq, (0, 0))
    gk_ref[...] += dot(dkt, normed)
    gv_ref[...] += dot(dvt, normed)

    @pl.when(step == pl.num_programs(0) - 1)
    def _():
        me = place_ref[0]
        line_ref[...] = jnp.zeros_like(line_ref)
        for block in range(seq):
            offset = ((me ^ block) - me) * here + PACKED_LENGTH - here
            window = pl.ds(pl.multiple_of(offset, 128), 2 * here)
            for head in range(H):
                row = (head % 2) * here
                tile = table_sum_ref[
                    head // 2, row : row + here, block * here : (block + 1) * here
                ]
                total = jnp.zeros((8, 2 * here), F32)
                empty = jnp.zeros((8, here), F32)
                for group in range(here // 8):
                    wide = jnp.concatenate([tile[group * 8 : group * 8 + 8], empty], axis=1)
                    total = total + pltpu.roll(wide, here - 8 * group, 1)
                line_ref[head * 8 : head * 8 + 8, window] += total
        lines = line_ref[...]
        sub = lax.broadcasted_iota(jnp.int32, lines.shape, 0)
        for bit in (1, 2, 4):
            lines = jnp.where((sub & bit) != 0, pltpu.roll(lines, SPAN - bit, 1), lines)
        by_head = jnp.concatenate(
            [jnp.sum(lines[h * 8 : h * 8 + 8], axis=0, keepdims=True) for h in range(H)], axis=0
        )
        table_ref[...] = dot(
            by_head, bucket_rows((SPAN, 128), 1), (1, 0), lax.Precision.HIGHEST
        )
        gk = gk_ref[...].T
        gv = gv_ref[...].T
        gq = gq_ref[...]
        gain = (
            wq_ref[...].astype(F32) * gq
            + wk_ref[...].astype(F32) * gk
            + wv_ref[...].astype(F32) * gv
        )
        gain_grad_ref[...] = dot(
            jnp.ones((8, D), F32), gain, (1, 1), lax.Precision.HIGHEST
        )
        core, label, other = code_ref[0], code_ref[1], code_ref[2]
        for index, grad in enumerate((go_ref[...], gq, gk, gv)):
            stage_ref[...] = grad
            rows = slice(index * SMALL_ROWS, (index + 1) * SMALL_ROWS)
            for slot in range(HALF):
                for target, chunk in (
                    (keep_ref, core * HALF + (slot ^ label)),
                    (send_ref, (1 - core) * HALF + (slot ^ other)),
                ):
                    first = pl.multiple_of(chunk * SMALL_ROWS, SMALL_ROWS)
                    target[slot, rows] = stage_ref[pl.ds(first, SMALL_ROWS), :].astype(BF16)


def pick(code_ref, low_ref, high_ref, chunk, use):
    core, label, other = code_ref[0], code_ref[1], code_ref[2]

    @pl.when(core == chunk[0])
    def _():
        use(low_ref, chunk[1] ^ label)

    @pl.when(core != chunk[0])
    def _():
        use(high_ref, chunk[1] ^ other)


def finish_mlp_kernel(code_ref, low_ref, high_ref, outer_ref, inner_ref, stage_ref):
    step = pl.program_id(0)
    per_step = FF_TILE // OUTER_ROWS
    for part in range(per_step):
        chunk = step * per_step + part
        rows = slice(part * OUTER_ROWS, (part + 1) * OUTER_ROWS)

        def use(ref, slot):
            outer_ref[rows, :] = ref[slot, :OUTER_ROWS].astype(F32)
            stage_ref[rows, :] = ref[slot, OUTER_ROWS:].astype(F32)

        pick(code_ref, low_ref, high_ref, (chunk // HALF, chunk % HALF), use)
    inner_ref[...] = stage_ref[...].T


def finish_attention_kernel(code_ref, low_ref, high_ref, *out_refs):
    half = pl.program_id(0)
    for part in range(HALF):
        rows = slice(part * SMALL_ROWS, (part + 1) * SMALL_ROWS)

        def use(ref, slot):
            for index, out_ref in enumerate(out_refs):
                out_ref[rows, :] = ref[
                    slot, index * SMALL_ROWS : (index + 1) * SMALL_ROWS
                ].astype(F32)

        pick(code_ref, low_ref, high_ref, (half, part), use)


def post_kernel(a_ref, b_ref, x_ref, grad_middle_ref, gain_ref, out_ref):
    back = (a_ref[0].astype(F32) + b_ref[0].astype(F32)).T
    x = x_ref[0].astype(F32)
    inv = lax.rsqrt(jnp.mean(x * x, -1, keepdims=True) + EPSILON)
    scaled = back * gain_ref[...]
    grad = inv * scaled - x * (inv * inv * inv) * jnp.mean(scaled * x, -1, keepdims=True)
    out_ref[0] = (grad_middle_ref[0] + grad).astype(BF16)


ANYWHERE = pl.BlockSpec(memory_space=pl.ANY)


def whole(shape):
    return pl.BlockSpec(shape, lambda *_: (0,) * len(shape))


def by_row(shape):
    return pl.BlockSpec((1,) + shape[1:], lambda i, *_: (i,) + (0,) * (len(shape) - 1))


def one_row(shape, row):
    return pl.BlockSpec((1,) + shape[1:], lambda *_: (row,) + (0,) * (len(shape) - 1))


def shaped(shape, dtype):
    return jax.ShapeDtypeStruct(shape, dtype)


def call(
    kernel,
    grid,
    prefetch,
    inputs,
    in_specs,
    outs,
    out_specs,
    scratch=(),
    flops=0,
    name=None,
    aliases=None,
):
    moved = sum(a.size * a.dtype.itemsize for a in inputs)
    moved += sum(o.size * o.dtype.itemsize for o in outs)
    return pl.pallas_call(
        kernel,
        out_shape=outs,
        grid_spec=pltpu.PrefetchScalarGridSpec(
            num_scalar_prefetch=len(prefetch),
            grid=grid,
            in_specs=in_specs,
            out_specs=out_specs,
            scratch_shapes=list(scratch),
        ),
        compiler_params=pltpu.CompilerParams(
            dimension_semantics=("arbitrary",) * len(grid), vmem_limit_bytes=VMEM_LIMIT
        ),
        cost_estimate=pl.CostEstimate(flops=flops, bytes_accessed=moved, transcendentals=0),
        input_output_aliases=aliases or {},
        name=name,
    )(*prefetch, *inputs)


def add(*parts):
    total = parts[0].astype(F32)
    for part in parts[1:]:
        total = total + part.astype(F32)
    return total


def make_body(rows, seq):
    both = ("rows", "seq")
    further = [1 << i for i in range(3, rows.bit_length() - 1)]

    def swap_rows(array, bit):
        return lax.ppermute(array, "rows", [(i, i ^ bit) for i in range(rows)])

    def swap_seq(array, bit):
        return lax.ppermute(array, "seq", [(i, i ^ bit) for i in range(seq)])

    def swap_step(array, step):
        def partner(r, z):
            first, second = ((0, 2), (0, 4)), ((1, 1), (1, 2))
            if r & 1:
                first, second = first[::-1], second[::-1]
            axis, bit = (first + second)[step]
            return (r, z ^ bit) if axis else (r ^ bit, z)

        pairs = []
        for r in range(rows):
            for z in range(seq):
                to_r, to_z = partner(r, z)
                pairs.append((r * seq + z, to_r * seq + to_z))
        return lax.ppermute(array, both, pairs)

    def codes():
        r, z = lax.axis_index("rows"), lax.axis_index("seq")
        core = r & 1
        b1, b2, z0, z1 = (r >> 1) & 1, (r >> 2) & 1, z & 1, (z >> 1) & 1
        even = b1 * 8 + b2 * 4 + z0 * 2 + z1
        odd = b2 * 8 + b1 * 4 + z1 * 2 + z0
        label = jnp.where(core == 0, even, odd)
        other = jnp.where(core == 0, odd, even)
        return jnp.stack([core, label, other]).astype(jnp.int32)

    def reduce_scatter(keep, arrived, hold=None):
        parts = [keep, arrived]
        size = keep.shape[0]
        outgoing = []
        for step in range(4):
            size //= 2
            send = add(*[part[size : 2 * size] for part in parts]).astype(BF16)
            outgoing.append(send)
            parts = [part[:size] for part in parts]
            parts.append(swap_step(send, step))
            if hold is not None and step == 0:
                parts[-1] = hold(send, parts[-1])
        total = add(*parts)
        for bit in further:
            total = total + swap_rows(total, bit)
        return total.astype(BF16)

    def all_gather(held):
        for step in (3, 2, 1, 0):
            held = jnp.concatenate([held, swap_step(held, step)])
        return held, swap_rows(held, 1)

    def body(
        block_input,
        cotangent,
        gain_attn,
        w_query,
        w_key,
        w_value,
        w_out,
        gain_mlp,
        w_inner,
        outer_weight,
        bias_table,
        lengths,
        observed,
    ):
        count, here = block_input.shape[0], block_input.shape[1]
        tokens = count * here
        last = count - 1
        place = lax.axis_index("seq").astype(jnp.int32).reshape(1)
        code = codes()
        gain_attn_row = gain_attn.reshape(1, D)
        gain_mlp_row = gain_mlp.reshape(1, D)

        mine = [block_input[row] for row in range(count)]
        x2 = [swap_seq(x, 2) for x in mine]
        x1 = [swap_seq(x, 1) for x in mine]
        seen = jnp.stack([observed] + [swap_seq(observed, j) for j in range(1, seq)], axis=1)
        x3 = [swap_seq(x, 1) for x in x2]

        stacked = (PAIRS, 2 * here, PACKED_LENGTH)
        bias = call(
            functools.partial(bias_kernel, here=here, seq=seq),
            (1,),
            (place,),
            (bias_table,),
            [whole(bias_table.shape)],
            [shaped(stacked, F32)],
            [whole(stacked)],
            [pltpu.VMEM((H, SPAN), F32)],
            name="bias",
        )[0]

        one = (here, D)
        own = (count, here, D)
        full = (count, PACKED_LENGTH, D)
        p_shape = (count,) + stacked
        square = whole((D, D))
        line = whole((1, D))

        kept = []
        sums = []
        normed_mlp, actives, grad_acts = [], [], []
        kept_shapes = [
            shaped(own, BF16),
            shaped(own, F32),
            shaped(own, F32),
            shaped(full, BF16),
            shaped(own, BF16),
            shaped(full, BF16),
            shaped(full, BF16),
            shaped(p_shape, BF16),
        ]
        sum_shapes = [shaped(own, F32)] * 2
        for row in range(count):
            inputs = [
                block_input,
                x1[row],
                x2[row],
                x3[row],
                seen,
                gain_attn_row,
                w_query,
                w_key,
                w_value,
                w_out,
                gain_mlp_row,
                bias,
            ]
            specs = [one_row(own, row)] + [whole(one)] * 3 + [one_row(seen.shape, row), line]
            specs += [square] * 4 + [line, whole(stacked)]
            first = len(inputs) + 2
            nm, *kept = call(
                functools.partial(attention_kernel, row=row, here=here, seq=seq),
                (1,),
                (place, lengths),
                inputs + kept,
                specs + [ANYWHERE] * len(kept),
                [shaped(one, BF16)] + kept_shapes,
                [whole(one)] + [one_row(s.shape, row) for s in kept_shapes],
                flops=8 * here * D * PACKED_LENGTH,
                name="attention",
                aliases={first + i: 1 + i for i in range(len(kept))},
            )
            normed_mlp.append(nm)
            if row == last:
                break
            sums_in = sums
            first = 4 + 1
            *sums, active, grad_act = call(
                functools.partial(mlp_kernel, deal=False, prior=0),
                (FF // FF_TILE,),
                (code,),
                [nm, cotangent, w_inner, outer_weight] + sums_in,
                [
                    whole(one),
                    one_row(own, row),
                    pl.BlockSpec((D, FF_TILE), lambda i, *_: (0, i)),
                    pl.BlockSpec((FF_TILE, D), lambda i, *_: (i, 0)),
                ]
                + [ANYWHERE] * len(sums_in),
                sum_shapes + [shaped((here, FF), BF16)] * 2,
                [one_row(own, row)] * 2
                + [pl.BlockSpec((here, FF_TILE), lambda i, *_: (0, i))] * 2,
                flops=8 * here * D * FF,
                name="mlp",
                aliases={first + i: i for i in range(len(sums_in))},
            )
            actives.append(active)
            grad_acts.append(grad_act)

        steps = FF // FF_TILE // 2
        part_shape = (HALF, 2 * OUTER_ROWS, D)

        def mlp_last(sums, own_half):
            which = code[0] if own_half else 1 - code[0]
            info = jnp.stack([which * steps, code[1] if own_half else code[2]])
            hidden = pl.BlockSpec((here, FF_TILE), lambda i, n: (0, n[0] + i))
            inputs = [normed_mlp[last], cotangent, w_inner, outer_weight]
            specs = [
                whole(one),
                one_row(own, last),
                pl.BlockSpec((D, FF_TILE), lambda i, n: (0, n[0] + i)),
                pl.BlockSpec((FF_TILE, D), lambda i, n: (n[0] + i, 0)),
            ]
            inputs += normed_mlp[:last] + actives + grad_acts + [cotangent]
            specs += [whole(one)] * last + [hidden] * (2 * last) + [whole(own)]
            first = len(inputs) + 1
            return call(
                functools.partial(mlp_kernel, deal=True, prior=last),
                (steps,),
                (info,),
                inputs + sums,
                specs + [one_row(own, last)] * 2,
                sum_shapes + [shaped(part_shape, BF16)],
                [one_row(own, last)] * 2 + [whole(part_shape)],
                flops=10 * here * D * FF,
                name="mlp_last",
                aliases={first: 0, first + 1: 1},
            )

        sums = [s.at[last].set(0.0) for s in sums]
        *sums, mlp_send = mlp_last(sums, False)
        mlp_arrived = swap_rows(mlp_send, 1)
        *sums, mlp_keep = mlp_last(sums, True)

        small_half = (HALF, 4 * SMALL_ROWS, D)
        dx_half = (seq // 2, count, D, here)
        dx_spec = pl.BlockSpec((seq // 2, 1, D, here), lambda i, *_: (0, i, 0, 0))
        results = []

        def back_call(pin, arrived):
            results.extend(
                call(
                    functools.partial(back_kernel, here=here, seq=seq),
                    (count,),
                    (place, code),
                    (cotangent, *sums, kept[1], kept[0], *kept[2:], gain_mlp_row, w_out)
                    + (w_query, w_key, w_value, pin),
                    [by_row(own)] * 6
                    + [by_row(full), by_row(own), by_row(full), by_row(full), by_row(p_shape)]
                    + [line]
                    + [square] * 4
                    + [ANYWHERE],
                    [shaped(own, BF16), shaped(own, F32)]
                    + [shaped(dx_half, BF16)] * 2
                    + [shaped(small_half, BF16)] * 2
                    + [shaped((H, 128), F32), shaped((8, D), F32), shaped((1, D), F32)],
                    [by_row(own)] * 2
                    + [dx_spec] * 2
                    + [whole(small_half)] * 2
                    + [whole((H, 128)), whole((8, D)), line],
                    [
                        pltpu.VMEM(stacked, F32),
                        pltpu.VMEM((8 * H, SPAN), F32),
                        pltpu.VMEM((D, D), F32),
                        pltpu.VMEM((D, D), F32),
                        pltpu.VMEM((D, D), F32),
                        pltpu.VMEM((D, D), F32),
                        pltpu.VMEM((D, D), F32),
                    ],
                    flops=20 * tokens * D * PACKED_LENGTH,
                    name="attention_back",
                )
            )
            return lax.optimization_barrier((arrived, results[6]))[0]

        mlp_part = reduce_scatter(mlp_keep, mlp_arrived, back_call)
        (
            block_output,
            grad_middle,
            dx_keep,
            dx_send,
            small_keep,
            small_send,
            table,
            gain_part,
            gain_mlp_part,
        ) = results

        half_sum = add(dx_keep, swap_seq(dx_send, 1)).astype(BF16)
        arrived = swap_seq(half_sum[1], 2)
        dx_shape = (count, D, here)
        input_grad = call(
            post_kernel,
            (count,),
            (),
            (half_sum[0], arrived, block_input, grad_middle, gain_attn_row),
            [by_row(dx_shape)] * 2 + [by_row(own)] * 2 + [line],
            [shaped(own, BF16)],
            [by_row(own)],
            name="post",
        )[0]

        small_part = reduce_scatter(small_keep, swap_rows(small_send, 1))
        mlp_low, mlp_high = all_gather(mlp_part)
        grad_outer, grad_inner = call(
            finish_mlp_kernel,
            (FF // FF_TILE,),
            (code,),
            (mlp_low, mlp_high),
            [whole(part_shape)] * 2,
            [shaped((FF, D), F32), shaped((D, FF), F32)],
            [
                pl.BlockSpec((FF_TILE, D), lambda i, *_: (i, 0)),
                pl.BlockSpec((D, FF_TILE), lambda i, *_: (0, i)),
            ],
            [pltpu.VMEM((FF_TILE, D), F32)],
            name="finish_mlp",
        )
        small_low, small_high = all_gather(small_part)
        grad_out, grad_query, grad_key, grad_value = call(
            finish_attention_kernel,
            (2,),
            (code,),
            (small_low, small_high),
            [whole(small_half)] * 2,
            [shaped((D, D), F32)] * 4,
            [pl.BlockSpec((D // 2, D), lambda i, *_: (i, 0))] * 4,
            name="finish_attention",
        )

        small = jnp.concatenate(
            [gain_part[:1] / gain_attn_row, gain_mlp_part, table.reshape(2, D)], axis=0
        )
        for bit in [1 << i for i in range(rows.bit_length() - 1)]:
            small = small + swap_rows(small, bit)
        for bit in [1 << i for i in range(seq.bit_length() - 1)]:
            small = small + swap_seq(small, bit)

        return (
            block_output,
            input_grad,
            small[0],
            grad_query,
            grad_key,
            grad_value,
            grad_out,
            small[1],
            grad_inner,
            grad_outer,
            small[2:].reshape(H, 128)[:, :BUCKETS].T,
        )

    return body


def solution(mesh):
    split = P("rows", "seq", None)
    placed = (split, split) + (P(),) * 9 + (P("rows", None), P("rows", "seq"))
    return jax.shard_map(
        make_body(mesh.shape["rows"], mesh.shape["seq"]),
        mesh=mesh,
        in_specs=placed,
        out_specs=(split, split) + (P(),) * 9,
        check_vma=False,
    )
```

time: 457 us -> 245 us (0.54)
  waiting for transfers between devices: 245 us -> 86.5 us
  matrix products: 65.1 us -> 0 us
  starting transfers between devices: 0.47 us -> 59.7 us
  Pallas kernels: 0 us -> 56.7 us
  blocking collectives: 52.5 us -> 0 us
  local copies, waits for them, and re-layouts: 70.4 us -> 27.6 us
  between operations: 14.3 us -> 1.5 us
    psum x1 -> x0, waiting for transfers between devices: 189 us -> none  [body(): lax.psum((grad_gain_attn, grad_query, grad_key, grad_value, grad_out, gra...]
    ppermute x0 -> x39, waiting for transfers between devices: none -> 86.5 us  [the longest x16 58.2 us: swap_step(): return lax.ppermute(array, both, pairs)]
    dot_general x26 -> x0, matrix products: 65.1 us -> none  [the longest x6 15 us: weight_grad(): lax.dot_general(left_side.reshape(-1, left_side.shape[-1]), right_side.re...]
    ppermute x0 -> x39, starting transfers between devices: none -> 59.7 us  [the longest x7 31 us: swap_rows(): return lax.ppermute(array, 'rows', [(i, i ^ bit) for i in range(rows)])]
    pallas_call x0 -> x12, Pallas kernels: none -> 56.7 us  [call(): pl.pallas_call(kernel, out_shape=outs, grid_spec=pltpu.PrefetchScalarGrid...]
    reduce_scatter x2 -> x0, waiting for transfers between devices: 46 us -> none  [the longest x1 33.9 us: body(): lax.psum_scatter(running[2].astype(jnp.bfloat16), 'seq', scatter_dimensio...]
    psum x1 -> x0, blocking collectives: 41.4 us -> none  [body(): lax.psum((grad_gain_attn, grad_query, grad_key, grad_value, grad_out, gra...]
    eq x2 -> x0, local copies, waits for them, and re-layouts: 37.4 us -> none  [the longest x1 37.3 us: scores_block(): buckets[None] == jnp.arange(BUCKETS, dtype=jnp.int32)[:, None, None]]
  transfers between devices with their start and end apart: 5 -> 39, of which waited for: 4 -> 16; matrix products, arithmetic and copies ran while one was open for 20% -> 5% of each run, Pallas kernels for 0% -> 17%
where the time goes in v1:
time: 245 us; the launch traced here: 243 us
  waiting for transfers between devices  86.5 us (35%)
  starting transfers between devices  59.7 us (24%)
  Pallas kernels  56.7 us (23%)
  local copies, waits for them, and re-layouts  27.6 us (11%)
  other arithmetic  11.1 us (5%)
    ppermute x16, waiting for transfers between devices, swap_step(): return lax.ppermute(array, both, pairs)  58.2 us
    pallas_call x12, Pallas kernels, call(): pl.pallas_call(kernel, out_shape=outs, grid_spec=pltpu.PrefetchScalarGrid...  56.7 us
    ppermute x7, starting transfers between devices, swap_rows(): return lax.ppermute(array, 'rows', [(i, i ^ bit) for i in range(rows)])  31 us
    ppermute x16, waiting for transfers between devices, swap_seq(): return lax.ppermute(array, 'seq', [(i, i ^ bit) for i in range(seq)])  24.9 us
    unnamed x135, local copies, waits for them, and re-layouts  22.6 us
    ppermute x16, starting transfers between devices, swap_seq(): return lax.ppermute(array, 'seq', [(i, i ^ bit) for i in range(seq)])  17.6 us
    ppermute x16, starting transfers between devices, swap_step(): return lax.ppermute(array, both, pairs)  11.1 us
    convert_element_type x8, other arithmetic, reduce_scatter(): send = add(*[part[size:2 * size] for part in parts]).astype(BF16)  5.83 us
  transfers between devices with their start and end apart: 39, of which 16 were waited for; matrix products, arithmetic and copies ran while one was open for 5% of the time, Pallas kernels for 17%

profile of v1, /device:TPU:1, one launch (start us, length us, event | category | flops | bytes accessed | tf_op | source)
XLA Modules:
  0.0 243.1 jit_solution(971754761970783665)
XLA Ops:
  0.7 1.8 slice_bitcast_fusion.2
  2.5 3.1 %collective-permute-start.10 = (bf16[128,512]{1,0:T(8,128)(2,1)S(1)}, bf16[128,512]{1,0:T(8,128)(2,1)S(1)}, u32[]{:S(2)}, u32[]{:S(2)}) collective-permute-start(bf16[128,512]{1,0:T(8,128)(2,1)S(1)} %get-tuple-element.155), channel_id=1, source_target_pairs={{0,2},{1,3},{2,0},{3,1},{4,6},{5,7},{6,4},{7,5},{8,10},{9,11},{10,... | collective-permute-start | bytes 393224 | tf_op jit(solution)/shard_map/ppermute | solution.py:497
  5.7 1.3 collective-permute-start.3
  7.0 1.3 collective-permute-start.4
  8.3 1.0 collective-permute-start.7
  9.9 1.2 collective-permute-start.9
  11.5 6.1 %collective-permute-start.1 = (bf16[128,512]{1,0:T(8,128)(2,1)}, bf16[128,512]{1,0:T(8,128)(2,1)}, u32[]{:S(2)}, u32[]{:S(2)}) collective-permute-start(bf16[128,512]{1,0:T(8,128)(2,1)} %get-tuple-element.157), channel_id=1, source_target_pairs={{0,2},{1,3},{2,0},{3,1},{4,6},{5,7},{6,4},{7,5},{8,10},{9,11},{10,... | collective-permute-start | bytes 393224 | tf_op jit(solution)/shard_map/ppermute | solution.py:497
  19.2 1.4 bias.1.bias_ref
  20.6 1.5 collective-permute-start.6
  22.9 1.4 collective-permute-start
  27.9 3.4 %attention.3 = (bf16[128,512]{1,0:T(8,128)(2,1)S(1)}, bf16[3,128,512]{2,1,0:T(8,128)(2,1)S(1)}, f32[3,128,512]{2,1,0:T(8,128)S(1)}, f32[3,128,512]{2,1,0:T(8,128...) custom-call(s32[1]{0:T(128)} %bitcast.place_ref, ...), custom_call_target="tpu_custom_call" | custom-call | flops 268435456 | bytes 15345664 | tf_op jit(solution)/shard_map/attention/pallas_call | solution.py:463
  31.3 4.3 %mlp.2 = (f32[3,128,512]{2,1,0:T(8,128)S(1)}, f32[3,128,512]{2,1,0:T(8,128)S(1)}, bf16[128,2048]{1,0:T(8,128)(2,1)S(1)}, bf16[128,2048]{1,0:T(8,128)(2,1)S(1)}) custom-call(s32[3]{0:T(128)S(1)} %pad_add_fusion.1.half_ref.code_ref, bf16[128,512]{1,0:T(8,128)(2,1)S(1)} %get-tuple-element.109.nm_ref.refs_0_, bf16[3,128,512]{2,1,0:T(8,128)(2,1)S(1)} %copy-done.5, ...), custom_call_target="tpu_custom_call" | custom-call | flops 1073741824 | bytes 7340032 | tf_op jit(solution)/shard_map/mlp/pallas_call | solution.py:463
  35.7 4.3 %attention.4 = (bf16[128,512]{1,0:T(8,128)(2,1)S(1)}, bf16[3,128,512]{2,1,0:T(8,128)(2,1)S(1)}, f32[3,128,512]{2,1,0:T(8,128)S(1)}, f32[3,128,512]{2,1,0:T(8,128...) custom-call(s32[1]{0:T(128)} %bitcast.place_ref, ...), custom_call_target="tpu_custom_call", output_to_operand_aliasing={{1}: (14, {}), {2}: (15, {}), {3}: (16, {}), {4}: (17, {}),... | custom-call | flops 268435456 | bytes 25569280 | tf_op jit(solution)/shard_map/attention/pallas_call | solution.py:463
  40.0 4.1 %mlp.3 = (f32[3,128,512]{2,1,0:T(8,128)S(1)}, f32[3,128,512]{2,1,0:T(8,128)S(1)}, bf16[128,2048]{1,0:T(8,128)(2,1)S(1)}, bf16[128,2048]{1,0:T(8,128)(2,1)S(1)}) custom-call(s32[3]{0:T(128)S(1)} %pad_add_fusion.1.half_ref.code_ref, bf16[128,512]{1,0:T(8,128)(2,1)S(1)} %get-tuple-element.110.nm_ref.refs_1_, ...), custom_call_target="tpu_custom_call", output_to_operand_aliasing={{0}: (5, {}), {1}: (6, {})} | custom-call | flops 1073741824 | bytes 8912896 | tf_op jit(solution)/shard_map/mlp/pallas_call | solution.py:463
  44.2 4.3 %attention.5 = (bf16[128,512]{1,0:T(8,128)(2,1)S(1)}, bf16[3,128,512]{2,1,0:T(8,128)(2,1)S(1)}, f32[3,128,512]{2,1,0:T(8,128)S(1)}, f32[3,128,512]{2,1,0:T(8,128...) custom-call(s32[1]{0:T(128)} %bitcast.place_ref, ...), custom_call_target="tpu_custom_call", output_to_operand_aliasing={{1}: (14, {}), {2}: (15, {}), {3}: (16, {}), {4}: (17, {}),... | custom-call | flops 268435456 | bytes 25569280 | tf_op jit(solution)/shard_map/attention/pallas_call | solution.py:463
  48.6 1.1 copy-done.6
  52.3 5.0 %mlp_last.2 = (f32[3,128,512]{2,1,0:T(8,128)S(1)}, f32[3,128,512]{2,1,0:T(8,128)S(1)}, bf16[16,128,512]{2,1,0:T(8,128)(2,1)}) custom-call(s32[2]{0:T(128)S(1)} %copy-done.58, bf16[128,512]{1,0:T(8,128)(2,1)S(1)} %get-tuple-element.108.nm_ref, bf16[3,128,512]{2,1,0:T(8,128)(2,1)S(1)} %copy-done.5, ...), custom_call_target="tpu_custom_call", output_to_operand_aliasing={{0}: (12, {}), {1}: (13, {})} | custom-call | flops 1342177280 | bytes 12713984 | tf_op jit(solution)/shard_map/mlp_last/pallas_call | solution.py:463
  58.2 2.1 collective-permute-start.12
  60.3 1.6 copy-done.2
  61.9 1.1 copy-done.13
  63.0 1.0 copy-done.37
  64.1 1.0 copy-done.39
  65.1 1.0 copy-done.41
  66.2 1.0 copy-done.43
  68.2 3.6 %mlp_last.3 = (f32[3,128,512]{2,1,0:T(8,128)S(1)}, f32[3,128,512]{2,1,0:T(8,128)S(1)}, bf16[16,128,512]{2,1,0:T(8,128)(2,1)S(1)}) custom-call(s32[2]{0:T(128)S(1)} %pad_add_fusion.2.half_ref, bf16[128,512]{1,0:T(8,128)(2,1)S(1)} %copy-done.48, bf16[3,128,512]{2,1,0:T(8,128)(2,1)S(1)} %copy-done.5, ...), custom_call_target="tpu_custom_call", output_to_operand_aliasing={{0}: (12, {}), {1}: (13, {})} | custom-call | flops 1342177280 | bytes 12713984 | tf_op jit(solution)/shard_map/mlp_last/pallas_call | solution.py:463
  72.7 1.7 add_convert_fusion.pin_ref
  74.5 1.4 collective-permute-start.30
  76.0 1.1 copy-done.15
  77.1 1.0 copy-done.35
  78.1 14.3 %attention_back.1 = (bf16[3,128,512]{2,1,0:T(8,128)(2,1)}, f32[3,128,512]{2,1,0:T(8,128)S(1)}, bf16[2,3,512,128]{3,2,1,0:T(8,128)(2,1)S(1)}, bf16[2,3,512,128]{3...) custom-call(s32[1]{0:T(128)} %bitcast.place_ref, ...), custom_call_target="tpu_custom_call" | custom-call | flops 2013265920 | bytes 20209664 | tf_op jit(solution)/shard_map/attention_back/pallas_call | solution.py:463
  92.4 1.6 add_convert_fusion.2
  94.1 1.3 collective-permute-start.31
  95.9 6.6 %collective-permute-done.31 = bf16[4,128,512]{2,1,0:T(8,128)(2,1)S(1)} collective-permute-done((bf16[4,128,512]{2,1,0:T(8,128)(2,1)S(1)}, bf16[4,128,512]{2,1,0:T(8,128)(2,1)S(1)}, u32[]{:S(2)}, u32[]{:S(2)}) %collective-permute-start.31) | collective-permute-done | bytes 524320 | tf_op jit(solution)/shard_map/ppermute | solution.py:512
  102.5 1.1 add_convert_fusion.4
  103.6 1.8 collective-permute-start.32
  105.4 7.1 %collective-permute-done.32 = bf16[2,128,512]{2,1,0:T(8,128)(2,1)S(1)} collective-permute-done((bf16[2,128,512]{2,1,0:T(8,128)(2,1)S(1)}, bf16[2,128,512]{2,1,0:T(8,128)(2,1)S(1)}, u32[]{:S(2)}, u32[]{:S(2)}) %collective-permute-start.32) | collective-permute-done | bytes 262176 | tf_op jit(solution)/shard_map/ppermute | solution.py:512
  112.5 1.0 add_convert_fusion.7
  114.0 3.4 %collective-permute-done.33 = bf16[1,128,512]{2,1,0:T(8,128)(2,1)S(1)} collective-permute-done((bf16[1,128,512]{2,1,0:T(8,128)(2,1)S(1)}, bf16[1,128,512]{2,1,0:T(8,128)(2,1)S(1)}, u32[]{:S(2)}, u32[]{:S(2)}) %collective-permute-start.33) | collective-permute-done | bytes 131104 | tf_op jit(solution)/shard_map/ppermute | solution.py:512
  117.4 1.0 constant_dynamic-update-slice_fusion.9
  119.3 3.1 %collective-permute-done.34 = bf16[1,128,512]{2,1,0:T(8,128)(2,1)S(1)} collective-permute-done((bf16[1,128,512]{2,1,0:T(8,128)(2,1)S(1)}, bf16[1,128,512]{2,1,0:T(8,128)(2,1)S(1)}, u32[]{:S(2)}, u32[]{:S(2)}) %collective-permute-start.34) | collective-permute-done | bytes 131104 | tf_op jit(solution)/shard_map/ppermute | solution.py:512
  122.4 1.7 collective-permute-start.35
  124.1 9.4 %collective-permute-done.35 = bf16[2,128,512]{2,1,0:T(8,128)(2,1)S(1)} collective-permute-done((bf16[2,128,512]{2,1,0:T(8,128)(2,1)S(1)}, bf16[2,128,512]{2,1,0:T(8,128)(2,1)S(1)}, u32[]{:S(2)}, u32[]{:S(2)}) %collective-permute-start.35) | collective-permute-done | bytes 262176 | tf_op jit(solution)/shard_map/ppermute | solution.py:512
  133.6 1.5 collective-permute-start.36
  135.3 9.5 %collective-permute-done.22 = bf16[4,64,512]{2,1,0:T(8,128)(2,1)S(1)} collective-permute-done((bf16[4,64,512]{2,1,0:T(8,128)(2,1)S(1)}, bf16[4,64,512]{2,1,0:T(8,128)(2,1)S(1)}, u32[]{:S(2)}, u32[]{:S(2)}) %collective-permute-start.22) | collective-permute-done | bytes 262176 | tf_op jit(solution)/shard_map/ppermute | solution.py:512
  145.1 1.2 collective-permute-start.37
  146.2 4.8 %collective-permute-done.23 = bf16[2,64,512]{2,1,0:T(8,128)(2,1)S(1)} collective-permute-done((bf16[2,64,512]{2,1,0:T(8,128)(2,1)S(1)}, bf16[2,64,512]{2,1,0:T(8,128)(2,1)S(1)}, u32[]{:S(2)}, u32[]{:S(2)}) %collective-permute-start.23) | collective-permute-done | bytes 131104 | tf_op jit(solution)/shard_map/ppermute | solution.py:512
  151.2 3.1 %collective-permute-done.24 = bf16[1,64,512]{2,1,0:T(8,128)(2,1)S(1)} collective-permute-done((bf16[1,64,512]{2,1,0:T(8,128)(2,1)S(1)}, bf16[1,64,512]{2,1,0:T(8,128)(2,1)S(1)}, u32[]{:S(2)}, u32[]{:S(2)}) %collective-permute-start.24) | collective-permute-done | bytes 65568 | tf_op jit(solution)/shard_map/ppermute | solution.py:512
  154.4 3.8 %collective-permute-done.25 = bf16[1,64,512]{2,1,0:T(8,128)(2,1)S(1)} collective-permute-done((bf16[1,64,512]{2,1,0:T(8,128)(2,1)S(1)}, bf16[1,64,512]{2,1,0:T(8,128)(2,1)S(1)}, u32[]{:S(2)}, u32[]{:S(2)}) %collective-permute-start.25) | collective-permute-done | bytes 65568 | tf_op jit(solution)/shard_map/ppermute | solution.py:512
  158.5 7.5 %collective-permute-done.26 = bf16[2,64,512]{2,1,0:T(8,128)(2,1)S(1)} collective-permute-done((bf16[2,64,512]{2,1,0:T(8,128)(2,1)S(1)}, bf16[2,64,512]{2,1,0:T(8,128)(2,1)S(1)}, u32[]{:S(2)}, u32[]{:S(2)}) %collective-permute-start.26) | collective-permute-done | bytes 131104 | tf_op jit(solution)/shard_map/ppermute | solution.py:512
  166.2 12.2 %collective-permute-start.38 = (bf16[16,128,512]{2,1,0:T(8,128)(2,1)S(1)}, bf16[16,128,512]{2,1,0:T(8,128)(2,1)}, u32[]{:S(2)}, u32[]{:S(2)}) collective-permute-start(bf16[16,128,512]{2,1,0:T(8,128)(2,1)S(1)} %constant_dynamic-update-slice_fusion.5.low_ref), channel_id=1, source_target_pairs={{0,4},{4,0},{8,12},{12,8},{16,20},{20,16},{24,28},{28,24},{1,5},{5... | collective-permute-start | bytes 6291464 | tf_op jit(solution)/shard_map/ppermute | solution.py:494
  180.5 7.6 %collective-permute-start.15 = (f32[4,512]{1,0:T(4,128)S(1)}, f32[4,512]{1,0:T(4,128)S(1)}, u32[]{:S(2)}, u32[]{:S(2)}) collective-permute-start(f32[4,512]{1,0:T(4,128)S(1)} %pad_maximum_fusion.6), channel_id=1, source_target_pairs={{0,4},{4,0},{8,12},{12,8},{16,20},{20,16},{24,28},{28,24},{1,5},{5... | collective-permute-start | bytes 24584 | tf_op jit(solution)/shard_map/ppermute | solution.py:494
  188.1 1.0 constant_dynamic-update-slice_fusion.1
  189.1 1.1 constant_dynamic-update-slice_fusion.low_ref
  190.2 6.3 %collective-permute-start.29 = (bf16[16,64,512]{2,1,0:T(8,128)(2,1)S(1)}, bf16[16,64,512]{2,1,0:T(8,128)(2,1)}, u32[]{:S(2)}, u32[]{:S(2)}) collective-permute-start(bf16[16,64,512]{2,1,0:T(8,128)(2,1)S(1)} %constant_dynamic-update-slice_fusion.low_ref), channel_id=1, source_target_pairs={{0,4},{4,0},{8,12},{12,8},{16,20},{20,16},{24,28},{28,24},{1,5},{5... | collective-permute-start | bytes 3145736 | tf_op jit(solution)/shard_map/ppermute | solution.py:494
  197.3 1.8 collective-permute-start.16
  199.1 1.3 collective-permute-done.16
  200.7 2.1 collective-permute-done.17
  202.8 2.5 %collective-permute-done.18 = f32[4,512]{1,0:T(4,128)S(1)} collective-permute-done((f32[4,512]{1,0:T(4,128)S(1)}, f32[4,512]{1,0:T(4,128)S(1)}, u32[]{:S(2)}, u32[]{:S(2)}) %collective-permute-start.18) | collective-permute-done | bytes 8224 | tf_op jit(solution)/shard_map/ppermute | solution.py:497
  205.5 3.3 %collective-permute-done.19 = f32[4,512]{1,0:T(4,128)S(1)} collective-permute-done((f32[4,512]{1,0:T(4,128)S(1)}, f32[4,512]{1,0:T(4,128)S(1)}, u32[]{:S(2)}, u32[]{:S(2)}) %collective-permute-start.19) | collective-permute-done | bytes 8224 | tf_op jit(solution)/shard_map/ppermute | solution.py:497
  209.4 1.6 add_convert_fusion.1
  212.5 18.7 %collective-permute-done.14.b_ref = bf16[3,512,128]{2,1,0:T(8,128)(2,1)S(1)} collective-permute-done((bf16[3,512,128]{2,1,0:T(8,128)(2,1)S(1)}, bf16[3,512,128]{2,1,0:T(8,128)(2,1)S(1)}, u32[]{:S(2)}, u32[]{:S(2)}) %collective-permute-start.14) | collective-permute-done | bytes 393248 | tf_op jit(solution)/shard_map/ppermute | solution.py:497
  231.2 1.8 post.1
  233.0 4.1 %finish_attention.1 = (f32[512,512]{1,0:T(8,128)}, f32[512,512]{1,0:T(8,128)}, f32[512,512]{1,0:T(8,128)}, f32[512,512]{1,0:T(8,128)}) custom-call(s32[3]{0:T(128)S(1)} %pad_add_fusion.1.half_ref.code_ref, bf16[16,64,512]{2,1,0:T(8,128)(2,1)S(1)} %constant_dynamic-update-slice_fusion.low_ref, bf16[16,64,512]{2,1,0:T(8,128)(2,1)} %collective-permute-done.29.high_ref), custom_call_target="tpu_custom_call" | custom-call | bytes 6291456 | tf_op jit(solution)/shard_map/finish_attention/pallas_call | solution.py:463
  237.1 6.0 %finish_mlp.1 = (f32[2048,512]{1,0:T(8,128)}, f32[512,2048]{1,0:T(8,128)}) custom-call(s32[3]{0:T(128)S(1)} %pad_add_fusion.1.half_ref.code_ref, bf16[16,128,512]{2,1,0:T(8,128)(2,1)S(1)} %constant_dynamic-update-slice_fusion.5.low_ref, bf16[16,128,512]{2,1,0:T(8,128)(2,1)} %collective-permute-done.38.high_ref), custom_call_target="tpu_custom_call" | custom-call | bytes 12582912 | tf_op jit(solution)/shard_map/finish_mlp/pallas_call | solution.py:463
  (203 shorter events, 20.7 us)
Async XLA Ops:
  0.6 24.4 %copy-start.16 = (bf16[3,128,512]{2,1,0:T(8,128)(2,1)S(1)}, bf16[3,128,512]{2,1,0:T(8,128)(2,1)}, u32[]{:S(2)}) copy-start(bf16[3,128,512]{2,1,0:T(8,128)(2,1)} %x_ref.1) | copy-start | bytes 1179652
  0.7 24.4 %copy-start.19 = (bf16[512,512]{1,0:T(8,128)(2,1)S(1)}, bf16[512,512]{1,0:T(8,128)(2,1)}, u32[]{:S(2)}) copy-start(bf16[512,512]{1,0:T(8,128)(2,1)} %wq_ref.7) | copy-start | bytes 1572868
  0.7 24.4 %copy-start.57 = (s32[3,4]{1,0:T(4,128)S(1)}, s32[3,4]{1,0:T(4,128)}, u32[]{:S(2)}) copy-start(s32[3,4]{1,0:T(4,128)} %lengths_ref.5) | copy-start | bytes 148
  0.7 24.4 %copy-start.56 = (f32[512]{0:T(512)S(1)}, f32[512]{0:T(512)}, u32[]{:S(2)}) copy-start(f32[512]{0:T(512)} %param.24) | copy-start | bytes 6148
  0.7 24.4 %copy-start.55 = (f32[512]{0:T(512)S(1)}, f32[512]{0:T(512)}, u32[]{:S(2)}) copy-start(f32[512]{0:T(512)} %param.19) | copy-start | bytes 6148
  2.5 15.1 %collective-permute-start.10 = (bf16[128,512]{1,0:T(8,128)(2,1)S(1)}, bf16[128,512]{1,0:T(8,128)(2,1)S(1)}, u32[]{:S(2)}, u32[]{:S(2)}) collective-permute-start(bf16[128,512]{1,0:T(8,128)(2,1)S(1)} %get-tuple-element.155), channel_id=1, source_target_pairs={{0,2},{1,3},{2,0},{3,1},{4,6},{5,7},{6,4},{7,5},{8,10},{9,11},{10,... | collective-permute-start | bytes 393224 | tf_op jit(solution)/shard_map/ppermute | solution.py:497
  5.7 4.3 %collective-permute-start.3 = (s32[3,128]{1,0:T(4,128)}, s32[3,128]{1,0:T(4,128)S(1)}, u32[]{:S(2)}, u32[]{:S(2)}) collective-permute-start(s32[3,128]{1,0:T(4,128)} %param.29), channel_id=1, source_target_pairs={{0,1},{1,0},{2,3},{3,2},{4,5},{5,4},{6,7},{7,6},{8,9},{9,8},{10,11... | collective-permute-start | bytes 4616 | tf_op jit(solution)/shard_map/ppermute | solution.py:497
  7.0 4.5 %collective-permute-start.5 = (s32[3,128]{1,0:T(4,128)}, s32[3,128]{1,0:T(4,128)S(1)}, u32[]{:S(2)}, u32[]{:S(2)}) collective-permute-start(s32[3,128]{1,0:T(4,128)} %param.29), channel_id=1, source_target_pairs={{0,3},{1,2},{2,1},{3,0},{4,7},{5,6},{6,5},{7,4},{8,11},{9,10},{10,... | collective-permute-start | bytes 4616 | tf_op jit(solution)/shard_map/ppermute | solution.py:497
  7.0 13.7 %collective-permute-start.4 = (s32[3,128]{1,0:T(4,128)}, s32[3,128]{1,0:T(4,128)S(1)}, u32[]{:S(2)}, u32[]{:S(2)}) collective-permute-start(s32[3,128]{1,0:T(4,128)} %param.29), channel_id=1, source_target_pairs={{0,2},{1,3},{2,0},{3,1},{4,6},{5,7},{6,4},{7,5},{8,10},{9,11},{10,... | collective-permute-start | bytes 4616 | tf_op jit(solution)/shard_map/ppermute | solution.py:497
  8.3 13.8 %collective-permute-start.7 = (bf16[128,512]{1,0:T(8,128)(2,1)}, bf16[128,512]{1,0:T(8,128)(2,1)}, u32[]{:S(2)}, u32[]{:S(2)}) collective-permute-start(bf16[128,512]{1,0:T(8,128)(2,1)} %get-tuple-element.156), channel_id=1, source_target_pairs={{0,2},{1,3},{2,0},{3,1},{4,6},{5,7},{6,4},{7,5},{8,10},{9,11},{10,... | collective-permute-start | bytes 393224 | tf_op jit(solution)/shard_map/ppermute | solution.py:497
  9.9 12.4 %collective-permute-start.9 = (bf16[128,512]{1,0:T(8,128)(2,1)S(1)}, bf16[128,512]{1,0:T(8,128)(2,1)S(1)}, u32[]{:S(2)}, u32[]{:S(2)}) collective-permute-start(bf16[128,512]{1,0:T(8,128)(2,1)S(1)} %get-tuple-element.155), channel_id=1, source_target_pairs={{0,1},{1,0},{2,3},{3,2},{4,5},{5,4},{6,7},{7,6},{8,9},{9,8},{10,11... | collective-permute-start | bytes 393224 | tf_op jit(solution)/shard_map/ppermute | solution.py:497
  11.5 12.8 %collective-permute-start.1 = (bf16[128,512]{1,0:T(8,128)(2,1)}, bf16[128,512]{1,0:T(8,128)(2,1)}, u32[]{:S(2)}, u32[]{:S(2)}) collective-permute-start(bf16[128,512]{1,0:T(8,128)(2,1)} %get-tuple-element.157), channel_id=1, source_target_pairs={{0,2},{1,3},{2,0},{3,1},{4,6},{5,7},{6,4},{7,5},{8,10},{9,11},{10,... | collective-permute-start | bytes 393224 | tf_op jit(solution)/shard_map/ppermute | solution.py:497
  17.7 6.8 %collective-permute-start.11 = (bf16[128,512]{1,0:T(8,128)(2,1)S(1)}, bf16[128,512]{1,0:T(8,128)(2,1)S(1)}, u32[]{:S(2)}, u32[]{:S(2)}) collective-permute-start(bf16[128,512]{1,0:T(8,128)(2,1)S(1)} %collective-permute-done.10.x2_ref), channel_id=1, source_target_pairs={{0,1},{1,0},{2,3},{3,2},{4,5},{5,4},{6,7},{7,6},{8,9},{9,8},{10,11... | collective-permute-start | bytes 393224 | tf_op jit(solution)/shard_map/ppermute | solution.py:497
  20.6 15.0 %collective-permute-start.6 = (bf16[128,512]{1,0:T(8,128)(2,1)}, bf16[128,512]{1,0:T(8,128)(2,1)S(1)}, u32[]{:S(2)}, u32[]{:S(2)}) collective-permute-start(bf16[128,512]{1,0:T(8,128)(2,1)} %get-tuple-element.156), channel_id=1, source_target_pairs={{0,1},{1,0},{2,3},{3,2},{4,5},{5,4},{6,7},{7,6},{8,9},{9,8},{10,11... | collective-permute-start | bytes 393224 | tf_op jit(solution)/shard_map/ppermute | solution.py:497
  22.2 13.5 %collective-permute-start.8 = (bf16[128,512]{1,0:T(8,128)(2,1)}, bf16[128,512]{1,0:T(8,128)(2,1)S(1)}, u32[]{:S(2)}, u32[]{:S(2)}) collective-permute-start(bf16[128,512]{1,0:T(8,128)(2,1)} %collective-permute-done.7.x2_ref), channel_id=1, source_target_pairs={{0,1},{1,0},{2,3},{3,2},{4,5},{5,4},{6,7},{7,6},{8,9},{9,8},{10,11... | collective-permute-start | bytes 393224 | tf_op jit(solution)/shard_map/ppermute | solution.py:497
  22.9 21.3 %collective-permute-start = (bf16[128,512]{1,0:T(8,128)(2,1)}, bf16[128,512]{1,0:T(8,128)(2,1)S(1)}, u32[]{:S(2)}, u32[]{:S(2)}) collective-permute-start(bf16[128,512]{1,0:T(8,128)(2,1)} %get-tuple-element.157), channel_id=1, source_target_pairs={{0,1},{1,0},{2,3},{3,2},{4,5},{5,4},{6,7},{7,6},{8,9},{9,8},{10,11... | collective-permute-start | bytes 393224 | tf_op jit(solution)/shard_map/ppermute | solution.py:497
  24.3 19.9 %collective-permute-start.2 = (bf16[128,512]{1,0:T(8,128)(2,1)}, bf16[128,512]{1,0:T(8,128)(2,1)S(1)}, u32[]{:S(2)}, u32[]{:S(2)}) collective-permute-start(bf16[128,512]{1,0:T(8,128)(2,1)} %collective-permute-done.1.x2_ref), channel_id=1, source_target_pairs={{0,1},{1,0},{2,3},{3,2},{4,5},{5,4},{6,7},{7,6},{8,9},{9,8},{10,11... | collective-permute-start | bytes 393224 | tf_op jit(solution)/shard_map/ppermute | solution.py:497
  35.6 16.6 %copy-start.36 = (bf16[128,2048]{1,0:T(8,128)(2,1)}, bf16[128,2048]{1,0:T(8,128)(2,1)S(1)}, u32[]{:S(2)}) copy-start(bf16[128,2048]{1,0:T(8,128)(2,1)S(1)} %get-tuple-element.111.refs_2_) | copy-start | bytes 1572868
  35.6 16.6 %copy-start.38 = (bf16[128,2048]{1,0:T(8,128)(2,1)}, bf16[128,2048]{1,0:T(8,128)(2,1)S(1)}, u32[]{:S(2)}) copy-start(bf16[128,2048]{1,0:T(8,128)(2,1)S(1)} %get-tuple-element.115.refs_4_) | copy-start | bytes 1572868
  44.1 8.1 %copy-start.40 = (bf16[128,2048]{1,0:T(8,128)(2,1)}, bf16[128,2048]{1,0:T(8,128)(2,1)S(1)}, u32[]{:S(2)}) copy-start(bf16[128,2048]{1,0:T(8,128)(2,1)S(1)} %get-tuple-element.114.refs_3_) | copy-start | bytes 1572868
  44.1 8.1 %copy-start.42 = (bf16[128,2048]{1,0:T(8,128)(2,1)}, bf16[128,2048]{1,0:T(8,128)(2,1)S(1)}, u32[]{:S(2)}) copy-start(bf16[128,2048]{1,0:T(8,128)(2,1)S(1)} %get-tuple-element.116.refs_5_) | copy-start | bytes 1572868
  44.2 8.1 %copy-start.58 = (s32[2]{0:T(128)S(1)}, s32[2]{0:T(128)}, u32[]{:S(2)}) copy-start(s32[2]{0:T(128)} %pad_add_fusion.3.half_ref) | copy-start | bytes 28
  58.2 14.6 %collective-permute-start.12 = (bf16[16,128,512]{2,1,0:T(8,128)(2,1)}, bf16[16,128,512]{2,1,0:T(8,128)(2,1)}, u32[]{:S(2)}, u32[]{:S(2)}) collective-permute-start(bf16[16,128,512]{2,1,0:T(8,128)(2,1)} %get-tuple-element.132), channel_id=1, source_target_pairs={{0,4},{4,0},{8,12},{12,8},{16,20},{20,16},{24,28},{28,24},{1,5},{5... | collective-permute-start | bytes 6291464 | tf_op jit(solution)/shard_map/ppermute | solution.py:494
  68.1 7.8 %copy-start.7 = (bf16[3,512,512]{2,1,0:T(8,128)(2,1)S(1)}, bf16[3,512,512]{2,1,0:T(8,128)(2,1)}, u32[]{:S(2)}) copy-start(bf16[3,512,512]{2,1,0:T(8,128)(2,1)} %copy-done.6) | copy-start | bytes 4718596
  68.1 7.8 %copy-start.9 = (bf16[3,512,512]{2,1,0:T(8,128)(2,1)S(1)}, bf16[3,512,512]{2,1,0:T(8,128)(2,1)}, u32[]{:S(2)}) copy-start(bf16[3,512,512]{2,1,0:T(8,128)(2,1)} %copy-done.8) | copy-start | bytes 4718596
  68.1 7.8 %copy-start.11 = (bf16[3,512,512]{2,1,0:T(8,128)(2,1)S(1)}, bf16[3,512,512]{2,1,0:T(8,128)(2,1)}, u32[]{:S(2)}) copy-start(bf16[3,512,512]{2,1,0:T(8,128)(2,1)} %copy-done.10) | copy-start | bytes 4718596
  68.1 7.8 %copy-start.21 = (bf16[512,512]{1,0:T(8,128)(2,1)S(1)}, bf16[512,512]{1,0:T(8,128)(2,1)}, u32[]{:S(2)}) copy-start(bf16[512,512]{1,0:T(8,128)(2,1)} %wq_ref.7) | copy-start | bytes 1572868
  68.1 7.8 %copy-start.23 = (bf16[512,512]{1,0:T(8,128)(2,1)S(1)}, bf16[512,512]{1,0:T(8,128)(2,1)}, u32[]{:S(2)}) copy-start(bf16[512,512]{1,0:T(8,128)(2,1)} %wk_ref.7) | copy-start | bytes 1572868
  68.1 7.8 %copy-start.25 = (bf16[512,512]{1,0:T(8,128)(2,1)S(1)}, bf16[512,512]{1,0:T(8,128)(2,1)}, u32[]{:S(2)}) copy-start(bf16[512,512]{1,0:T(8,128)(2,1)} %wv_ref.7) | copy-start | bytes 1572868
  68.2 7.8 %copy-start.27 = (bf16[512,512]{1,0:T(8,128)(2,1)S(1)}, bf16[512,512]{1,0:T(8,128)(2,1)}, u32[]{:S(2)}) copy-start(bf16[512,512]{1,0:T(8,128)(2,1)} %w_out_ref.7) | copy-start | bytes 1572868
  68.2 7.8 %copy-start.29 = (f32[3,128,512]{2,1,0:T(8,128)S(1)}, f32[3,128,512]{2,1,0:T(8,128)}, u32[]{:S(2)}) copy-start(f32[3,128,512]{2,1,0:T(8,128)} %copy-done.28) | copy-start | bytes 2359300
  68.2 7.8 %copy-start.31 = (f32[3,128,512]{2,1,0:T(8,128)S(1)}, f32[3,128,512]{2,1,0:T(8,128)}, u32[]{:S(2)}) copy-start(f32[3,128,512]{2,1,0:T(8,128)} %copy-done.30) | copy-start | bytes 2359300
  74.5 18.0 %collective-permute-start.30 = (bf16[8,128,512]{2,1,0:T(8,128)(2,1)S(1)}, bf16[8,128,512]{2,1,0:T(8,128)(2,1)S(1)}, u32[]{:S(2)}, u32[]{:S(2)}) collective-permute-start(bf16[8,128,512]{2,1,0:T(8,128)(2,1)S(1)} %add_convert_fusion.pin_ref), channel_id=1, source_target_pairs={{0,8},{1,9},{2,10},{3,11},{4,20},{5,21},{6,22},{7,23},{8,0},{9,1},... | collective-permute-start | bytes 3145736 | tf_op jit(solution)/shard_map/ppermute | solution.py:512
  92.4 21.1 %copy-start.44 = (f32[3,128,512]{2,1,0:T(8,128)}, f32[3,128,512]{2,1,0:T(8,128)S(1)}, u32[]{:S(2)}) copy-start(f32[3,128,512]{2,1,0:T(8,128)S(1)} %get-tuple-element.136.grad_middle_ref) | copy-start | bytes 2359300
  92.4 21.1 %copy-start.46 = (bf16[2,3,512,128]{3,2,1,0:T(8,128)(2,1)}, bf16[2,3,512,128]{3,2,1,0:T(8,128)(2,1)S(1)}, u32[]{:S(2)}) copy-start(bf16[2,3,512,128]{3,2,1,0:T(8,128)(2,1)S(1)} %get-tuple-element.134) | copy-start | bytes 2359300
  92.4 21.1 %copy-start.59 = (bf16[2,3,512,128]{3,2,1,0:T(8,128)(2,1)}, bf16[2,3,512,128]{3,2,1,0:T(8,128)(2,1)S(1)}, u32[]{:S(2)}) copy-start(bf16[2,3,512,128]{3,2,1,0:T(8,128)(2,1)S(1)} %get-tuple-element.135) | copy-start | bytes 2359300
  94.1 8.4 %collective-permute-start.31 = (bf16[4,128,512]{2,1,0:T(8,128)(2,1)S(1)}, bf16[4,128,512]{2,1,0:T(8,128)(2,1)S(1)}, u32[]{:S(2)}, u32[]{:S(2)}) collective-permute-start(bf16[4,128,512]{2,1,0:T(8,128)(2,1)S(1)} %add_convert_fusion.2), channel_id=1, source_target_pairs={{0,16},{1,17},{2,18},{3,19},{4,12},{5,13},{6,14},{7,15},{8,24},{9,... | collective-permute-start | bytes 1572872 | tf_op jit(solution)/shard_map/ppermute | solution.py:512
  95.4 23.5 %collective-permute-start.20 = (bf16[16,64,512]{2,1,0:T(8,128)(2,1)S(1)}, bf16[16,64,512]{2,1,0:T(8,128)(2,1)S(1)}, u32[]{:S(2)}, u32[]{:S(2)}) collective-permute-start(bf16[16,64,512]{2,1,0:T(8,128)(2,1)S(1)} %get-tuple-element.141), channel_id=1, source_target_pairs={{0,4},{4,0},{8,12},{12,8},{16,20},{20,16},{24,28},{28,24},{1,5},{5... | collective-permute-start | bytes 3145736 | tf_op jit(solution)/shard_map/ppermute | solution.py:494
  103.6 8.9 %collective-permute-start.32 = (bf16[2,128,512]{2,1,0:T(8,128)(2,1)S(1)}, bf16[2,128,512]{2,1,0:T(8,128)(2,1)S(1)}, u32[]{:S(2)}, u32[]{:S(2)}) collective-permute-start(bf16[2,128,512]{2,1,0:T(8,128)(2,1)S(1)} %add_convert_fusion.4), channel_id=1, source_target_pairs={{0,1},{1,0},{2,3},{3,2},{4,6},{5,7},{6,4},{7,5},{8,9},{9,8},{10,11... | collective-permute-start | bytes 786440 | tf_op jit(solution)/shard_map/ppermute | solution.py:512
  113.6 3.9 %collective-permute-start.33 = (bf16[1,128,512]{2,1,0:T(8,128)(2,1)S(1)}, bf16[1,128,512]{2,1,0:T(8,128)(2,1)S(1)}, u32[]{:S(2)}, u32[]{:S(2)}) collective-permute-start(bf16[1,128,512]{2,1,0:T(8,128)(2,1)S(1)} %add_convert_fusion.7), channel_id=1, source_target_pairs={{0,2},{1,3},{2,0},{3,1},{4,5},{5,4},{6,7},{7,6},{8,10},{9,11},{10,... | collective-permute-start | bytes 393224 | tf_op jit(solution)/shard_map/ppermute | solution.py:512
  118.4 3.9 %collective-permute-start.34 = (bf16[1,128,512]{2,1,0:T(8,128)(2,1)S(1)}, bf16[1,128,512]{2,1,0:T(8,128)(2,1)S(1)}, u32[]{:S(2)}, u32[]{:S(2)}) collective-permute-start(bf16[1,128,512]{2,1,0:T(8,128)(2,1)S(1)} %get-tuple-element.150), channel_id=1, source_target_pairs={{0,2},{1,3},{2,0},{3,1},{4,5},{5,4},{6,7},{7,6},{8,10},{9,11},{10,... | collective-permute-start | bytes 393224 | tf_op jit(solution)/shard_map/ppermute | solution.py:512
  119.0 16.1 %collective-permute-start.21 = (bf16[8,64,512]{2,1,0:T(8,128)(2,1)S(1)}, bf16[8,64,512]{2,1,0:T(8,128)(2,1)S(1)}, u32[]{:S(2)}, u32[]{:S(2)}) collective-permute-start(bf16[8,64,512]{2,1,0:T(8,128)(2,1)S(1)} %add_convert_fusion.3), channel_id=1, source_target_pairs={{0,8},{1,9},{2,10},{3,11},{4,20},{5,21},{6,22},{7,23},{8,0},{9,1},... | collective-permute-start | bytes 1572872 | tf_op jit(solution)/shard_map/ppermute | solution.py:512
  122.4 11.1 %collective-permute-start.35 = (bf16[2,128,512]{2,1,0:T(8,128)(2,1)S(1)}, bf16[2,128,512]{2,1,0:T(8,128)(2,1)S(1)}, u32[]{:S(2)}, u32[]{:S(2)}) collective-permute-start(bf16[2,128,512]{2,1,0:T(8,128)(2,1)S(1)} %pad_maximum_fusion.4), channel_id=1, source_target_pairs={{0,1},{1,0},{2,3},{3,2},{4,6},{5,7},{6,4},{7,5},{8,9},{9,8},{10,11... | collective-permute-start | bytes 786440 | tf_op jit(solution)/shard_map/ppermute | solution.py:512
  133.6 11.4 %collective-permute-start.36 = (bf16[4,128,512]{2,1,0:T(8,128)(2,1)S(1)}, bf16[4,128,512]{2,1,0:T(8,128)(2,1)S(1)}, u32[]{:S(2)}, u32[]{:S(2)}) collective-permute-start(bf16[4,128,512]{2,1,0:T(8,128)(2,1)S(1)} %pad_maximum_fusion.2), channel_id=1, source_target_pairs={{0,16},{1,17},{2,18},{3,19},{4,12},{5,13},{6,14},{7,15},{8,24},{9,... | collective-permute-start | bytes 1572872 | tf_op jit(solution)/shard_map/ppermute | solution.py:512
  135.2 9.6 %collective-permute-start.22 = (bf16[4,64,512]{2,1,0:T(8,128)(2,1)S(1)}, bf16[4,64,512]{2,1,0:T(8,128)(2,1)S(1)}, u32[]{:S(2)}, u32[]{:S(2)}) collective-permute-start(bf16[4,64,512]{2,1,0:T(8,128)(2,1)S(1)} %add_convert_fusion.5), channel_id=1, source_target_pairs={{0,16},{1,17},{2,18},{3,19},{4,12},{5,13},{6,14},{7,15},{8,24},{9,... | collective-permute-start | bytes 786440 | tf_op jit(solution)/shard_map/ppermute | solution.py:512
  144.8 6.2 %collective-permute-start.23 = (bf16[2,64,512]{2,1,0:T(8,128)(2,1)S(1)}, bf16[2,64,512]{2,1,0:T(8,128)(2,1)S(1)}, u32[]{:S(2)}, u32[]{:S(2)}) collective-permute-start(bf16[2,64,512]{2,1,0:T(8,128)(2,1)S(1)} %add_convert_fusion.8), channel_id=1, source_target_pairs={{0,1},{1,0},{2,3},{3,2},{4,6},{5,7},{6,4},{7,5},{8,9},{9,8},{10,11... | collective-permute-start | bytes 393224 | tf_op jit(solution)/shard_map/ppermute | solution.py:512
  145.1 21.1 %collective-permute-start.37 = (bf16[8,128,512]{2,1,0:T(8,128)(2,1)S(1)}, bf16[8,128,512]{2,1,0:T(8,128)(2,1)S(1)}, u32[]{:S(2)}, u32[]{:S(2)}) collective-permute-start(bf16[8,128,512]{2,1,0:T(8,128)(2,1)S(1)} %pad_maximum_fusion), channel_id=1, source_target_pairs={{0,8},{1,9},{2,10},{3,11},{4,20},{5,21},{6,22},{7,23},{8,0},{9,1},... | collective-permute-start | bytes 3145736 | tf_op jit(solution)/shard_map/ppermute | solution.py:512
  151.1 3.2 %collective-permute-start.24 = (bf16[1,64,512]{2,1,0:T(8,128)(2,1)S(1)}, bf16[1,64,512]{2,1,0:T(8,128)(2,1)S(1)}, u32[]{:S(2)}, u32[]{:S(2)}) collective-permute-start(bf16[1,64,512]{2,1,0:T(8,128)(2,1)S(1)} %add_convert_fusion.10), channel_id=1, source_target_pairs={{0,2},{1,3},{2,0},{3,1},{4,5},{5,4},{6,7},{7,6},{8,10},{9,11},{10,... | collective-permute-start | bytes 196616 | tf_op jit(solution)/shard_map/ppermute | solution.py:512
  154.3 3.9 %collective-permute-start.25 = (bf16[1,64,512]{2,1,0:T(8,128)(2,1)S(1)}, bf16[1,64,512]{2,1,0:T(8,128)(2,1)S(1)}, u32[]{:S(2)}, u32[]{:S(2)}) collective-permute-start(bf16[1,64,512]{2,1,0:T(8,128)(2,1)S(1)} %get-tuple-element.152), channel_id=1, source_target_pairs={{0,2},{1,3},{2,0},{3,1},{4,5},{5,4},{6,7},{7,6},{8,10},{9,11},{10,... | collective-permute-start | bytes 196616 | tf_op jit(solution)/shard_map/ppermute | solution.py:512
  158.2 7.7 %collective-permute-start.26 = (bf16[2,64,512]{2,1,0:T(8,128)(2,1)S(1)}, bf16[2,64,512]{2,1,0:T(8,128)(2,1)S(1)}, u32[]{:S(2)}, u32[]{:S(2)}) collective-permute-start(bf16[2,64,512]{2,1,0:T(8,128)(2,1)S(1)} %pad_maximum_fusion.5), channel_id=1, source_target_pairs={{0,1},{1,0},{2,3},{3,2},{4,6},{5,7},{6,4},{7,5},{8,9},{9,8},{10,11... | collective-permute-start | bytes 393224 | tf_op jit(solution)/shard_map/ppermute | solution.py:512
  166.0 12.4 %collective-permute-start.27 = (bf16[4,64,512]{2,1,0:T(8,128)(2,1)S(1)}, bf16[4,64,512]{2,1,0:T(8,128)(2,1)S(1)}, u32[]{:S(2)}, u32[]{:S(2)}) collective-permute-start(bf16[4,64,512]{2,1,0:T(8,128)(2,1)S(1)} %pad_maximum_fusion.3), channel_id=1, source_target_pairs={{0,16},{1,17},{2,18},{3,19},{4,12},{5,13},{6,14},{7,15},{8,24},{9,... | collective-permute-start | bytes 786440 | tf_op jit(solution)/shard_map/ppermute | solution.py:512
  166.2 70.9 %collective-permute-start.38 = (bf16[16,128,512]{2,1,0:T(8,128)(2,1)S(1)}, bf16[16,128,512]{2,1,0:T(8,128)(2,1)}, u32[]{:S(2)}, u32[]{:S(2)}) collective-permute-start(bf16[16,128,512]{2,1,0:T(8,128)(2,1)S(1)} %constant_dynamic-update-slice_fusion.5.low_ref), channel_id=1, source_target_pairs={{0,4},{4,0},{8,12},{12,8},{16,20},{20,16},{24,28},{28,24},{1,5},{5... | collective-permute-start | bytes 6291464 | tf_op jit(solution)/shard_map/ppermute | solution.py:494
  180.0 9.1 %collective-permute-start.28 = (bf16[8,64,512]{2,1,0:T(8,128)(2,1)}, bf16[8,64,512]{2,1,0:T(8,128)(2,1)}, u32[]{:S(2)}, u32[]{:S(2)}) collective-permute-start(bf16[8,64,512]{2,1,0:T(8,128)(2,1)} %pad_maximum_fusion.1), channel_id=1, source_target_pairs={{0,8},{1,9},{2,10},{3,11},{4,20},{5,21},{6,22},{7,23},{8,0},{9,1},... | collective-permute-start | bytes 1572872 | tf_op jit(solution)/shard_map/ppermute | solution.py:512
  180.4 8.8 %copy-start.63 = (f32[1,512]{1,0:T(1,128)}, f32[1,512]{1,0:T(1,128)S(1)}, u32[]{:S(2)}) copy-start(f32[1,512]{1,0:T(1,128)S(1)} %slice_divide_fusion) | copy-start | bytes 6148
  180.4 29.0 %collective-permute-start.13 = (bf16[2,3,512,128]{3,2,1,0:T(8,128)(2,1)}, bf16[2,3,512,128]{3,2,1,0:T(8,128)(2,1)}, u32[]{:S(2)}, u32[]{:S(2)}) collective-permute-start(bf16[2,3,512,128]{3,2,1,0:T(8,128)(2,1)} %copy-done.59), channel_id=1, source_target_pairs={{0,1},{1,0},{2,3},{3,2},{4,5},{5,4},{6,7},{7,6},{8,9},{9,8},{10,11... | collective-permute-start | bytes 2359304 | tf_op jit(solution)/shard_map/ppermute | solution.py:497
  180.5 16.1 %collective-permute-start.15 = (f32[4,512]{1,0:T(4,128)S(1)}, f32[4,512]{1,0:T(4,128)S(1)}, u32[]{:S(2)}, u32[]{:S(2)}) collective-permute-start(f32[4,512]{1,0:T(4,128)S(1)} %pad_maximum_fusion.6), channel_id=1, source_target_pairs={{0,4},{4,0},{8,12},{12,8},{16,20},{20,16},{24,28},{28,24},{1,5},{5... | collective-permute-start | bytes 24584 | tf_op jit(solution)/shard_map/ppermute | solution.py:494
  190.2 41.0 %copy-start.18 = (bf16[3,128,512]{2,1,0:T(8,128)(2,1)S(1)}, bf16[3,128,512]{2,1,0:T(8,128)(2,1)}, u32[]{:S(2)}) copy-start(bf16[3,128,512]{2,1,0:T(8,128)(2,1)} %x_ref.1) | copy-start | bytes 1179652
  190.2 42.8 %collective-permute-start.29 = (bf16[16,64,512]{2,1,0:T(8,128)(2,1)S(1)}, bf16[16,64,512]{2,1,0:T(8,128)(2,1)}, u32[]{:S(2)}, u32[]{:S(2)}) collective-permute-start(bf16[16,64,512]{2,1,0:T(8,128)(2,1)S(1)} %constant_dynamic-update-slice_fusion.low_ref), channel_id=1, source_target_pairs={{0,4},{4,0},{8,12},{12,8},{16,20},{20,16},{24,28},{28,24},{1,5},{5... | collective-permute-start | bytes 3145736 | tf_op jit(solution)/shard_map/ppermute | solution.py:494
  197.3 3.1 %collective-permute-start.16 = (f32[4,512]{1,0:T(4,128)S(1)}, f32[4,512]{1,0:T(4,128)S(1)}, u32[]{:S(2)}, u32[]{:S(2)}) collective-permute-start(f32[4,512]{1,0:T(4,128)S(1)} %fusion), channel_id=1, source_target_pairs={{0,8},{4,12},{8,0},{12,4},{16,24},{20,28},{24,16},{28,20},{1,9},{5... | collective-permute-start | bytes 24584 | tf_op jit(solution)/shard_map/ppermute | solution.py:494
  200.3 2.5 %collective-permute-start.17 = (f32[4,512]{1,0:T(4,128)S(1)}, f32[4,512]{1,0:T(4,128)S(1)}, u32[]{:S(2)}, u32[]{:S(2)}) collective-permute-start(f32[4,512]{1,0:T(4,128)S(1)} %add.139), channel_id=1, source_target_pairs={{0,16},{4,20},{8,24},{12,28},{16,0},{20,4},{24,8},{28,12},{1,17},{... | collective-permute-start | bytes 24584 | tf_op jit(solution)/shard_map/ppermute | solution.py:494
  202.8 2.5 %collective-permute-start.18 = (f32[4,512]{1,0:T(4,128)S(1)}, f32[4,512]{1,0:T(4,128)S(1)}, u32[]{:S(2)}, u32[]{:S(2)}) collective-permute-start(f32[4,512]{1,0:T(4,128)S(1)} %add.140), channel_id=1, source_target_pairs={{0,1},{1,0},{2,3},{3,2},{4,5},{5,4},{6,7},{7,6},{8,9},{9,8},{10,11... | collective-permute-start | bytes 24584 | tf_op jit(solution)/shard_map/ppermute | solution.py:497
  205.3 3.4 %collective-permute-start.19 = (f32[4,512]{1,0:T(4,128)S(1)}, f32[4,512]{1,0:T(4,128)S(1)}, u32[]{:S(2)}, u32[]{:S(2)}) collective-permute-start(f32[4,512]{1,0:T(4,128)S(1)} %add.141), channel_id=1, source_target_pairs={{0,2},{1,3},{2,0},{3,1},{4,6},{5,7},{6,4},{7,5},{8,10},{9,11},{10,... | collective-permute-start | bytes 24584 | tf_op jit(solution)/shard_map/ppermute | solution.py:497
  209.4 21.8 %copy-start.45 = (f32[3,128,512]{2,1,0:T(8,128)S(1)}, f32[3,128,512]{2,1,0:T(8,128)}, u32[]{:S(2)}) copy-start(f32[3,128,512]{2,1,0:T(8,128)} %copy-done.44) | copy-start | bytes 2359300
  211.1 20.1 %collective-permute-start.14 = (bf16[3,512,128]{2,1,0:T(8,128)(2,1)S(1)}, bf16[3,512,128]{2,1,0:T(8,128)(2,1)S(1)}, u32[]{:S(2)}, u32[]{:S(2)}) collective-permute-start(bf16[3,512,128]{2,1,0:T(8,128)(2,1)S(1)} %get-tuple-element.153), channel_id=1, source_target_pairs={{0,2},{1,3},{2,0},{3,1},{4,6},{5,7},{6,4},{7,5},{8,10},{9,11},{10,... | collective-permute-start | bytes 1179656 | tf_op jit(solution)/shard_map/ppermute | solution.py:497
  (39 other events, 103.5 us)

commit v2 on v1

v2 whole, which is shorter than its diff:
```python
import functools
import math

import jax
import jax.numpy as jnp
from jax import lax
from jax.experimental import pallas as pl
from jax.experimental.pallas import tpu as pltpu
from jax.sharding import PartitionSpec as P

D = 512
FF = 2048
H = 8
HD = 64
PAIRS = H // 2
BUCKETS = 32
PACKED_LENGTH = 512
EPSILON = 1e-06
BUCKET_EDGES = (12, 16, 23, 32, 46, 64, 91)
SPAN = 2 * PACKED_LENGTH
CHUNKS = 32
HALF = CHUNKS // 2
OUTER_ROWS = FF // CHUNKS
SMALL_ROWS = D // CHUNKS
FF_TILE = 512
MASKED = -1000000000.0
MIB = 1024 * 1024
F32 = jnp.float32
BF16 = jnp.bfloat16


def dot(left, right, contract=(1, 0), precision=None):
    return lax.dot_general(
        left,
        right,
        (((contract[0],), (contract[1],)), ((), ())),
        preferred_element_type=F32,
        precision=precision,
    )


def xor_pairs(size, bit):
    return [(i, i ^ bit) for i in range(size)]


def bucket_of(relative):
    distance = jnp.abs(relative)
    beyond = jnp.full(distance.shape, 8, jnp.int32)
    for edge_value in BUCKET_EDGES:
        beyond = beyond + (distance >= edge_value).astype(jnp.int32)
    near = jnp.where(distance < 8, distance, beyond)
    return jnp.where(relative > 0, 16, 0).astype(jnp.int32) + near


def bucket_rows(shape, bucket_axis):
    place_axis = 1 - bucket_axis
    relative = lax.broadcasted_iota(jnp.int32, shape, place_axis) - PACKED_LENGTH
    return (bucket_of(relative) == lax.broadcasted_iota(jnp.int32, shape, bucket_axis)).astype(F32)


def split_heads(pair):
    lane = lax.broadcasted_iota(jnp.int32, pair.shape, 1)
    zero = jnp.zeros_like(pair)
    return jnp.concatenate(
        [jnp.where(lane < HD, pair, zero), jnp.where(lane >= HD, pair, zero)], axis=0
    )


def join_heads(stacked):
    half = stacked.shape[0] // 2
    lane = lax.broadcasted_iota(jnp.int32, (half, stacked.shape[1]), 1)
    return jnp.where(lane < HD, stacked[:half], stacked[half:])


def prepare_kernel(place_ref, table_ref, *refs, here, seq):
    count = (len(refs) - 3) // 2
    sources, bias_ref, targets = refs[:count], refs[count], refs[count + 1 : 2 * count + 1]
    line_ref, sems = refs[2 * count + 1 :]
    copies = [
        pltpu.make_async_copy(source, target, sems.at[i])
        for i, (source, target) in enumerate(zip(sources, targets))
    ]
    for copy in copies:
        copy.start()
    line_ref[...] = dot(
        table_ref[...], bucket_rows((BUCKETS, SPAN), 0), (0, 0), lax.Precision.HIGHEST
    )
    me = place_ref[0]
    for block in range(seq):
        offset = ((me ^ block) - me) * here + PACKED_LENGTH - here
        window = line_ref[:, pl.ds(pl.multiple_of(offset, 128), 2 * here)]
        for head in range(H):
            spread = jnp.broadcast_to(window[head : head + 1], (here, 2 * here))
            skewed = pltpu.roll(spread, here, 1, stride=1, stride_axis=0)
            row = (head % 2) * here
            bias_ref[head // 2, row : row + here, block * here : (block + 1) * here] = skewed[
                :, :here
            ]
    for copy in copies:
        copy.wait()


def attention_kernel(
    place_ref,
    lengths_ref,
    x0_ref,
    x1_ref,
    x2_ref,
    x3_ref,
    seen0_ref,
    seen1_ref,
    seen2_ref,
    seen3_ref,
    gain_ref,
    wq_ref,
    wk_ref,
    wv_ref,
    w_out_ref,
    gain_mlp_ref,
    bias_ref,
    normed_mlp_ref,
    attended_ref,
    middle_ref,
    mixed_ref,
    normed_ref,
    q_ref,
    k_ref,
    v_ref,
    p_ref,
    *,
    row,
    here,
    seq,
):
    me = place_ref[0]
    own_x = x0_ref[0].astype(F32)
    x = jnp.concatenate(
        [own_x] + [ref.astype(F32) for ref in (x1_ref[0], x2_ref[0], x3_ref[...])], axis=0
    )
    inv = lax.rsqrt(jnp.mean(x * x, -1, keepdims=True) + EPSILON)
    normed = (x * inv * gain_ref[...]).astype(BF16)
    normed_ref[...] = normed
    q = dot(normed[:here], wq_ref[...]).astype(BF16)
    k = dot(normed, wk_ref[...]).astype(BF16)
    v = dot(normed, wv_ref[...]).astype(BF16)
    q_ref[...] = q
    k_ref[...] = k
    v_ref[...] = v
    ends = [lengths_ref[row, 0]]
    for part in range(1, lengths_ref.shape[1]):
        ends.append(ends[-1] + lengths_ref[row, part])

    def segment(place):
        total = jnp.zeros(place.shape, jnp.int32)
        for end in ends:
            total = total + (end <= place).astype(jnp.int32)
        return total

    query_place = me * here + lax.broadcasted_iota(jnp.int32, (here, 1), 0)
    lane = lax.broadcasted_iota(jnp.int32, (1, here), 1)
    key_place = jnp.concatenate([(me ^ block) * here + lane for block in range(seq)], axis=1)
    seen = jnp.concatenate(
        [ref[row : row + 1] for ref in (seen0_ref, seen1_ref, seen2_ref, seen3_ref)], axis=1
    )
    key_segment = jnp.where(seen == 1, segment(key_place), -1)
    allowed = (segment(query_place) == key_segment) | (query_place == key_place)
    allowed = jnp.concatenate([allowed.astype(jnp.int32)] * 2, axis=0) == 1
    attended = []
    for pair in range(PAIRS):
        lanes = slice(pair * 2 * HD, (pair + 1) * 2 * HD)
        scores = dot(split_heads(q[:, lanes]), k[:, lanes], (1, 1)) + bias_ref[pair]
        scores = jnp.where(allowed, scores, MASKED)
        exponent = jnp.exp(scores - jnp.max(scores, -1, keepdims=True))
        share = 1.0 / jnp.sum(exponent, -1, keepdims=True)
        probs = (exponent * share).astype(BF16)
        p_ref[pair] = probs
        mixed = join_heads(dot(probs, v[:, lanes]))
        mixed_ref[:, lanes] = mixed
        attended.append(mixed.astype(BF16))
    attended = jnp.concatenate(attended, axis=1)
    attended_ref[...] = attended
    middle = own_x + dot(attended, w_out_ref[...])
    middle_ref[...] = middle
    inv = lax.rsqrt(jnp.mean(middle * middle, -1, keepdims=True) + EPSILON)
    normed_mlp_ref[...] = (middle * inv * gain_mlp_ref[...]).astype(BF16)


def gelu_both(u):
    scale = 0.7978845608028654
    square = u * u
    t = jnp.tanh(u * (scale + (scale * 0.044715) * square))
    half_up = 0.5 + 0.5 * t
    slope = half_up + (0.5 * u) * (1.0 - t * t) * (scale + (3.0 * 0.044715 * scale) * square)
    return u * half_up, slope


def mlp_kernel(code_ref, *refs, rows, own_half):
    nm_refs = refs[:rows]
    g_ref, w_inner_ref, w_outer_ref, total_ref, back_ref, parts_ref = refs[rows:]
    step = pl.program_id(0)
    core = code_ref[0]
    which = core if own_half else 1 - core
    label = code_ref[1] if own_half else code_ref[2]
    first = pl.multiple_of((which * pl.num_programs(0) + step) * FF_TILE, FF_TILE)
    normed = jnp.concatenate([ref[...] for ref in nm_refs], axis=0)
    g = g_ref[...].reshape(normed.shape)
    w_inner = w_inner_ref[:, pl.ds(first, FF_TILE)]
    w_outer = w_outer_ref[pl.ds(first, FF_TILE), :]
    active_f, slope = gelu_both(dot(normed, w_inner))
    active = active_f.astype(BF16)
    grad_act = (dot(g, w_outer, (1, 1)) * slope).astype(BF16)

    @pl.when(step == 0)
    def _():
        total_ref[...] = jnp.zeros_like(total_ref)
        back_ref[...] = jnp.zeros_like(back_ref)

    total_ref[...] += dot(active, w_outer)
    back_ref[...] += dot(grad_act, w_inner, (1, 1))
    outer = dot(active, g, (0, 0)).astype(BF16)
    inner = dot(grad_act, normed, (0, 0)).astype(BF16)
    for part in range(FF_TILE // OUTER_ROWS):
        slot = (step * (FF_TILE // OUTER_ROWS) + part) ^ label
        rows = slice(part * OUTER_ROWS, (part + 1) * OUTER_ROWS)
        parts_ref[slot, :OUTER_ROWS] = outer[rows]
        parts_ref[slot, OUTER_ROWS:] = inner[rows]


def back_kernel(place_ref, code_ref, *refs, rows, here, seq):
    per_row = 9
    row_refs = [refs[i * per_row : (i + 1) * per_row] for i in range(rows)]
    refs = refs[rows * per_row :]
    (
        g_ref,
        total_a_ref,
        total_b_ref,
        back_a_ref,
        back_b_ref,
        gain_attn_ref,
        gain_mlp_ref,
        w_out_ref,
        wq_ref,
        wk_ref,
        wv_ref,
        pin_ref,
        block_output_ref,
        grad_middle_ref,
        dx_keep_ref,
        dx_send_ref,
        keep_ref,
        send_ref,
        rider_ref,
        table_sum_ref,
        line_ref,
        go_ref,
        gq_ref,
        gk_ref,
        gv_ref,
    ) = refs
    gain_mlp_grad = jnp.zeros((1, D), F32)
    for index in range(rows):
        _, attended_ref, middle_ref, mixed_ref, normed_ref, q_ref, k_ref, v_ref, p_ref = row_refs[
            index
        ]
        tokens = slice(index * here, (index + 1) * here)
        middle = middle_ref[...]
        back = back_a_ref[tokens] + back_b_ref[tokens]
        block_output_ref[index] = (middle + total_a_ref[tokens] + total_b_ref[tokens]).astype(BF16)
        inv = lax.rsqrt(jnp.mean(middle * middle, -1, keepdims=True) + EPSILON)
        gain_mlp_grad = gain_mlp_grad + jnp.sum(back * middle * inv, axis=0, keepdims=True)
        scaled = back * gain_mlp_ref[...]
        grad_middle = (
            g_ref[index].astype(F32)
            + inv * scaled
            - middle * (inv * inv * inv) * jnp.mean(scaled * middle, -1, keepdims=True)
        )
        grad_middle_ref[index] = grad_middle
        branch = grad_middle.astype(BF16)
        ga = dot(branch, w_out_ref[...], (1, 1)).astype(BF16)

        def accumulate(ref, value):
            if index == 0:
                ref[...] = value
            else:
                ref[...] += value

        accumulate(go_ref, dot(attended_ref[...], branch, (0, 0)))
        q = q_ref[...]
        k = k_ref[...]
        v = v_ref[...]
        normed = normed_ref[...]
        dq, dkt, dvt = [], [], []
        for pair in range(PAIRS):
            lanes = slice(pair * 2 * HD, (pair + 1) * 2 * HD)
            ga_split = split_heads(ga[:, lanes])
            q_split = split_heads(q[:, lanes])
            mixed = mixed_ref[:, lanes]
            probs = p_ref[pair]
            delta = jnp.sum(
                ga_split.astype(F32) * jnp.concatenate([mixed, mixed], axis=0), -1, keepdims=True
            )
            grad_probs = dot(ga_split, v[:, lanes], (1, 1))
            grad_scores_f = probs.astype(F32) * (grad_probs - delta)
            accumulate(table_sum_ref.at[pair], grad_scores_f)
            grad_scores = grad_scores_f.astype(BF16)
            dq.append(join_heads(dot(grad_scores, k[:, lanes])).astype(BF16))
            dkt.append(dot(q_split, grad_scores, (0, 0)).astype(BF16))
            dvt.append(dot(ga_split, probs, (0, 0)).astype(BF16))
        dq = jnp.concatenate(dq, axis=1)
        dkt = jnp.concatenate(dkt, axis=0)
        dvt = jnp.concatenate(dvt, axis=0)
        dxt = dot(wk_ref[...], dkt) + dot(wv_ref[...], dvt)
        own = dxt[:, :here] + dot(wq_ref[...], dq, (1, 1))
        pieces = [own] + [dxt[:, block * here : (block + 1) * here] for block in range(1, seq)]
        pieces = [piece.astype(BF16) for piece in pieces]
        dx_keep_ref[0, index] = pieces[0]
        dx_send_ref[1, index] = pieces[3]

        @pl.when(code_ref[0] == 0)
        def _():
            dx_keep_ref[1, index] = pieces[2]
            dx_send_ref[0, index] = pieces[1]

        @pl.when(code_ref[0] == 1)
        def _():
            dx_keep_ref[1, index] = pieces[1]
            dx_send_ref[0, index] = pieces[2]

        accumulate(gq_ref, dot(normed[:here], dq, (0, 0)))
        accumulate(gk_ref, dot(dkt, normed))
        accumulate(gv_ref, dot(dvt, normed))

    me = place_ref[0]
    line_ref[...] = jnp.zeros_like(line_ref)
    for block in range(seq):
        offset = ((me ^ block) - me) * here + PACKED_LENGTH - here
        window = pl.ds(pl.multiple_of(offset, 128), 2 * here)
        for head in range(H):
            row = (head % 2) * here
            tile = table_sum_ref[head // 2, row : row + here, block * here : (block + 1) * here]
            total = jnp.zeros((8, 2 * here), F32)
            empty = jnp.zeros((8, here), F32)
            for group in range(here // 8):
                wide = jnp.concatenate([tile[group * 8 : group * 8 + 8], empty], axis=1)
                total = total + pltpu.roll(wide, here - 8 * group, 1)
            line_ref[head * 8 : head * 8 + 8, window] += total
    lines = line_ref[...]
    sub = lax.broadcasted_iota(jnp.int32, lines.shape, 0)
    for bit in (1, 2, 4):
        lines = jnp.where((sub & bit) != 0, pltpu.roll(lines, SPAN - bit, 1), lines)
    by_head = jnp.concatenate(
        [jnp.sum(lines[h * 8 : h * 8 + 8], axis=0, keepdims=True) for h in range(H)], axis=0
    )
    table = dot(by_head, bucket_rows((SPAN, 128), 1), (1, 0), lax.Precision.HIGHEST)
    gk_ref[...] = gk_ref[...].T
    gv_ref[...] = gv_ref[...].T
    gain = (
        wq_ref[...].astype(F32) * gq_ref[...]
        + wk_ref[...].astype(F32) * gk_ref[...]
        + wv_ref[...].astype(F32) * gv_ref[...]
    )
    gain_grad = dot(jnp.ones((8, D), F32), gain, (1, 1), lax.Precision.HIGHEST)
    rider = jnp.concatenate(
        [
            jnp.concatenate([table, jnp.zeros((8, D - 128), F32)], axis=1),
            gain_grad[:1] / gain_attn_ref[...],
            gain_mlp_grad,
            jnp.zeros((6, D), F32),
        ],
        axis=0,
    )
    rider_ref[...] = rider
    high = rider.astype(BF16)
    base = HALF * 4 * SMALL_ROWS
    send_ref[base : base + 16, :] = high
    send_ref[base + 16 : base + 32, :] = (rider - high.astype(F32)).astype(BF16)
    core, label, other = code_ref[0], code_ref[1], code_ref[2]
    for index, grad_ref in enumerate((go_ref, gq_ref, gk_ref, gv_ref)):
        for slot in range(HALF):
            chunk = core * HALF + (slot ^ label)
            first = pl.multiple_of(chunk * SMALL_ROWS, SMALL_ROWS)
            rows_to = slice(index * SMALL_ROWS, (index + 1) * SMALL_ROWS)
            keep_ref[slot, rows_to] = grad_ref[pl.ds(first, SMALL_ROWS), :].astype(BF16)
            chunk = (1 - core) * HALF + (slot ^ other)
            first = pl.multiple_of(chunk * SMALL_ROWS, SMALL_ROWS)
            start = (slot * 4 + index) * SMALL_ROWS
            send_ref[start : start + SMALL_ROWS, :] = grad_ref[
                pl.ds(first, SMALL_ROWS), :
            ].astype(BF16)


def pick(code_ref, low_ref, high_ref, chunk, use):
    core, label, other = code_ref[0], code_ref[1], code_ref[2]

    @pl.when(core == chunk[0])
    def _():
        use(low_ref, chunk[1] ^ label)

    @pl.when(core != chunk[0])
    def _():
        use(high_ref, chunk[1] ^ other)


def finish_mlp_kernel(code_ref, low_ref, high_ref, outer_ref, inner_ref, stage_ref):
    step = pl.program_id(0)
    per_step = FF_TILE // OUTER_ROWS
    for part in range(per_step):
        chunk = step * per_step + part
        rows = slice(part * OUTER_ROWS, (part + 1) * OUTER_ROWS)

        def use(ref, slot):
            outer_ref[rows, :] = ref[slot, :OUTER_ROWS].astype(F32)
            stage_ref[rows, :] = ref[slot, OUTER_ROWS:].astype(F32)

        pick(code_ref, low_ref, high_ref, (chunk // HALF, chunk % HALF), use)
    inner_ref[...] = stage_ref[...].T


def finish_attention_kernel(code_ref, low_ref, high_ref, *out_refs):
    half = pl.program_id(0)
    for part in range(HALF):
        rows = slice(part * SMALL_ROWS, (part + 1) * SMALL_ROWS)

        def use(ref, slot):
            for index, out_ref in enumerate(out_refs):
                out_ref[rows, :] = ref[
                    slot, index * SMALL_ROWS : (index + 1) * SMALL_ROWS
                ].astype(F32)

        pick(code_ref, low_ref, high_ref, (half, part), use)


def post_kernel(a_ref, b_ref, x_ref, grad_middle_ref, gain_ref, out_ref):
    back = (a_ref[0].astype(F32) + b_ref[0].astype(F32)).T
    x = x_ref[0].astype(F32)
    inv = lax.rsqrt(jnp.mean(x * x, -1, keepdims=True) + EPSILON)
    scaled = back * gain_ref[...]
    grad = inv * scaled - x * (inv * inv * inv) * jnp.mean(scaled * x, -1, keepdims=True)
    out_ref[0] = (grad_middle_ref[0] + grad).astype(BF16)


ANYWHERE = pl.BlockSpec(memory_space=pl.ANY)


def whole(shape):
    return pl.BlockSpec(shape, lambda *_: (0,) * len(shape))


def by_row(shape):
    return pl.BlockSpec((1,) + shape[1:], lambda i, *_: (i,) + (0,) * (len(shape) - 1))


def one_row(shape, row):
    return pl.BlockSpec((1,) + shape[1:], lambda *_: (row,) + (0,) * (len(shape) - 1))


def shaped(shape, dtype):
    return jax.ShapeDtypeStruct(shape, dtype)


def call(
    kernel,
    grid,
    prefetch,
    inputs,
    in_specs,
    outs,
    out_specs,
    scratch=(),
    flops=0,
    name=None,
    aliases=None,
    vmem=16,
):
    moved = sum(a.size * a.dtype.itemsize for a in inputs)
    moved += sum(math.prod(o.shape) * o.dtype.itemsize for o in outs)
    return pl.pallas_call(
        kernel,
        out_shape=outs,
        grid_spec=pltpu.PrefetchScalarGridSpec(
            num_scalar_prefetch=len(prefetch),
            grid=grid,
            in_specs=in_specs,
            out_specs=out_specs,
            scratch_shapes=list(scratch),
        ),
        compiler_params=pltpu.CompilerParams(
            dimension_semantics=("arbitrary",) * len(grid), vmem_limit_bytes=vmem * MIB
        ),
        cost_estimate=pl.CostEstimate(flops=flops, bytes_accessed=moved, transcendentals=0),
        input_output_aliases=aliases or {},
        name=name,
    )(*prefetch, *inputs)


def add(*parts):
    total = parts[0].astype(F32)
    for part in parts[1:]:
        total = total + part.astype(F32)
    return total


def make_body(rows, seq):
    both = ("rows", "seq")
    further = [1 << i for i in range(3, rows.bit_length() - 1)]

    def swap_rows(array, bit):
        return lax.ppermute(array, "rows", [(i, i ^ bit) for i in range(rows)])

    def swap_seq(array, bit):
        return lax.ppermute(array, "seq", [(i, i ^ bit) for i in range(seq)])

    def swap_step(array, step):
        def partner(r, z):
            first, second = ((0, 2), (0, 4)), ((1, 1), (1, 2))
            if r & 1:
                first, second = first[::-1], second[::-1]
            axis, bit = (first + second)[step]
            return (r, z ^ bit) if axis else (r ^ bit, z)

        pairs = []
        for r in range(rows):
            for z in range(seq):
                to_r, to_z = partner(r, z)
                pairs.append((r * seq + z, to_r * seq + to_z))
        return lax.ppermute(array, both, pairs)

    def codes():
        r, z = lax.axis_index("rows"), lax.axis_index("seq")
        core = r & 1
        b1, b2, z0, z1 = (r >> 1) & 1, (r >> 2) & 1, z & 1, (z >> 1) & 1
        even = b1 * 8 + b2 * 4 + z0 * 2 + z1
        odd = b2 * 8 + b1 * 4 + z1 * 2 + z0
        label = jnp.where(core == 0, even, odd)
        other = jnp.where(core == 0, odd, even)
        return jnp.stack([core, label, other]).astype(jnp.int32)

    def after(array, *earlier):
        return lax.optimization_barrier((array, *earlier))[0]

    def halves(rider):
        high = rider.astype(BF16)
        return [high, (rider - high.astype(F32)).astype(BF16)]

    class Reduction:
        def __init__(self, wire, shape, rider=None):
            self.rider = rider
            self.parts = [None]
            self.step = 0
            self.arrived = (swap_rows(wire, 1), *shape[:2])

        def send(self, outgoing):
            slots, rows_each = outgoing.shape[:2]
            if self.rider is not None:
                flat = outgoing.reshape(slots * rows_each, D)
                outgoing = jnp.concatenate([flat] + halves(self.rider), axis=0)
            self.arrived = (swap_step(outgoing, self.step), slots, rows_each)
            self.step += 1

        def receive(self, *earlier):
            array, slots, rows_each = self.arrived
            array = after(array, *earlier)
            if self.rider is not None:
                size = slots * rows_each
                extra = array[size:].astype(F32)
                self.rider = self.rider + extra[:16] + extra[16:]
                array = array[:size].reshape(slots, rows_each, D)
            self.parts.append(array)

        def halve(self, *earlier):
            self.receive(*earlier)
            size = self.parts[0].shape[0] // 2
            outgoing = add(*[part[size:] for part in self.parts]).astype(BF16)
            self.parts = [part[:size] for part in self.parts]
            self.send(outgoing)
            return outgoing

        def total(self, *earlier):
            self.receive(*earlier)
            total = add(*self.parts)
            for bit in further:
                total = total + swap_rows(total, bit)
                if self.rider is not None:
                    self.rider = self.rider + swap_rows(self.rider, bit)
            self.held = total.astype(BF16)
            self.arrived = swap_step(self.held, 3)
            self.step = 2
            return self.held

        def double(self, *earlier):
            self.held = jnp.concatenate([self.held, after(self.arrived, *earlier)])
            if self.step >= 0:
                self.arrived = swap_step(self.held, self.step)
            else:
                self.arrived = swap_rows(self.held, 1)
            self.step -= 1
            return self.held

    def body(
        block_input,
        cotangent,
        gain_attn,
        w_query,
        w_key,
        w_value,
        w_out,
        gain_mlp,
        w_inner,
        outer_weight,
        bias_table,
        lengths,
        observed,
    ):
        count, here = block_input.shape[0], block_input.shape[1]
        tokens = count * here
        last = count - 1
        place = lax.axis_index("seq").astype(jnp.int32).reshape(1)
        code = codes()
        gain_attn_row = gain_attn.reshape(1, D)
        gain_mlp_row = gain_mlp.reshape(1, D)

        def in_hbm(array):
            return pltpu.with_memory_space_constraint(array, pltpu.HBM)

        stacked = (PAIRS, 2 * here, PACKED_LENGTH)
        one = (here, D)
        own = (count, here, D)
        full = (PACKED_LENGTH, D)
        square = whole((D, D))
        line = whole((1, D))

        x2 = swap_seq(block_input, 2)
        x1 = swap_seq(block_input, 1)
        seen = [observed] + [swap_seq(observed, j) for j in range(1, seq)]
        resident = (w_query, w_key, w_value, w_out, w_inner, outer_weight, cotangent)
        bias, *resident = call(
            functools.partial(prepare_kernel, here=here, seq=seq),
            (1,),
            (place,),
            (bias_table, *[in_hbm(array) for array in resident]),
            [whole(bias_table.shape)] + [ANYWHERE] * len(resident),
            [pltpu.VMEM(stacked, F32)]
            + [pltpu.VMEM(array.shape, array.dtype) for array in resident],
            [whole(stacked)] + [whole(array.shape) for array in resident],
            [pltpu.VMEM((H, SPAN), F32), pltpu.SemaphoreType.DMA((len(resident),))],
            name="prepare",
            vmem=4,
        )
        w_query, w_key, w_value, w_out, w_inner, outer_weight, cotangent = resident
        x2 = after(x2, bias)
        x3 = [swap_seq(x2[row], 1) for row in range(count)]

        kept = []
        kept_shapes = [
            pltpu.VMEM(one, BF16),
            pltpu.VMEM(one, BF16),
            pltpu.VMEM(one, F32),
            pltpu.VMEM(one, F32),
            pltpu.VMEM(full, BF16),
            pltpu.VMEM(one, BF16),
            pltpu.VMEM(full, BF16),
            pltpu.VMEM(full, BF16),
            pltpu.VMEM(stacked, BF16),
        ]
        for row in range(count):
            kept.append(
                call(
                    functools.partial(attention_kernel, row=row, here=here, seq=seq),
                    (1,),
                    (place, lengths),
                    [block_input, in_hbm(x1), in_hbm(x2), in_hbm(x3[row]), *seen]
                    + [gain_attn_row, w_query, w_key, w_value, w_out, gain_mlp_row, bias],
                    [one_row(own, row)] * 3
                    + [whole(one)]
                    + [whole(observed.shape)] * seq
                    + [line]
                    + [square] * 4
                    + [line, whole(stacked)],
                    kept_shapes,
                    [whole(shape.shape) for shape in kept_shapes],
                    flops=8 * here * D * PACKED_LENGTH,
                    name="attention",
                    vmem=12,
                )
            )
        normed_mlp = [part[0] for part in kept]

        flat = (tokens, D)
        steps = FF // FF_TILE // 2
        part_shape = (HALF, 2 * OUTER_ROWS, D)

        def mlp_part(own_half, nm):
            return call(
                functools.partial(mlp_kernel, rows=count, own_half=own_half),
                (steps,),
                (code,),
                (*nm, cotangent, w_inner, outer_weight),
                [whole(one)] * count + [whole(own), whole((D, FF)), whole((FF, D))],
                [pltpu.VMEM(flat, F32)] * 2 + [pltpu.HBM(part_shape, BF16)],
                [whole(flat)] * 2 + [whole(part_shape)],
                flops=6 * tokens * D * FF,
                name="mlp",
                vmem=20,
            )

        total_a, back_a, mlp_send = mlp_part(False, normed_mlp)
        mlp = Reduction(mlp_send, part_shape)
        nm = [after(normed_mlp[0], total_a)] + normed_mlp[1:]
        total_b, back_b, mlp_keep = mlp_part(True, nm)

        small_half = (HALF, 4 * SMALL_ROWS, D)
        small_wire = (HALF * 4 * SMALL_ROWS + 32, D)
        dx_half = (seq // 2, count, D, here)
        mlp.parts[0] = mlp_keep
        first_out = mlp.halve()
        (
            block_output,
            grad_middle,
            dx_keep,
            dx_send,
            small_keep,
            small_send,
            rider,
        ) = call(
            functools.partial(back_kernel, rows=count, here=here, seq=seq),
            (1,),
            (place, code),
            [array for part in kept for array in part]
            + [cotangent, total_a, total_b, back_a, back_b, gain_attn_row, gain_mlp_row]
            + [w_out, w_query, w_key, w_value, in_hbm(first_out)],
            [whole(shape.shape) for part in kept for shape in kept_shapes]
            + [whole(own)]
            + [whole(flat)] * 4
            + [line] * 2
            + [square] * 4
            + [ANYWHERE],
            [shaped(own, BF16), shaped(own, F32)]
            + [shaped(dx_half, BF16)] * 2
            + [shaped(small_half, BF16), shaped(small_wire, BF16), shaped((16, D), F32)],
            [whole(own)] * 2
            + [whole(dx_half)] * 2
            + [whole(small_half), whole(small_wire), whole((16, D))],
            [
                pltpu.VMEM(stacked, F32),
                pltpu.VMEM((8 * H, SPAN), F32),
                pltpu.VMEM((D, D), F32),
                pltpu.VMEM((D, D), F32),
                pltpu.VMEM((D, D), F32),
                pltpu.VMEM((D, D), F32),
            ],
            flops=20 * tokens * D * PACKED_LENGTH,
            name="attention_back",
            vmem=24,
        )
        small = Reduction(small_send, small_half, rider)
        small.parts[0] = small_keep
        dx_arrived = swap_step(dx_send, 2)
        done = mlp.halve(rider)
        done = small.halve(done)
        done = mlp.halve(done)
        done = small.halve(done)
        done = mlp.halve(done)
        done = small.halve(done)
        done = mlp.total(done)
        done = small.halve(done)
        done = mlp.double(done)
        done = small.total(done)
        done = mlp.double(done)
        done = small.double(done)
        done = small.double(done)
        done = mlp.double(done)
        half_sum = add(dx_keep, after(dx_arrived, done)).astype(BF16)
        dx_last = swap_step(half_sum[1], 3)
        done = small.double(half_sum)
        done = mlp.double(done)
        done = small.double(done)
        dx_shape = (count, D, here)
        input_grad = call(
            post_kernel,
            (count,),
            (),
            (half_sum[0], after(dx_last, done), block_input, grad_middle, gain_attn_row),
            [by_row(dx_shape)] * 2 + [by_row(own)] * 2 + [line],
            [shaped(own, BF16)],
            [by_row(own)],
            name="post",
        )[0]
        done = input_grad
        grad_outer, grad_inner = call(
            finish_mlp_kernel,
            (FF // FF_TILE,),
            (code,),
            (mlp.held, after(mlp.arrived, done)),
            [whole(part_shape)] * 2,
            [shaped((FF, D), F32), shaped((D, FF), F32)],
            [
                pl.BlockSpec((FF_TILE, D), lambda i, *_: (i, 0)),
                pl.BlockSpec((D, FF_TILE), lambda i, *_: (0, i)),
            ],
            [pltpu.VMEM((FF_TILE, D), F32)],
            name="finish_mlp",
        )
        grad_out, grad_query, grad_key, grad_value = call(
            finish_attention_kernel,
            (2,),
            (code,),
            (small.held, small.arrived),
            [whole(small_half)] * 2,
            [shaped((D, D), F32)] * 4,
            [pl.BlockSpec((D // 2, D), lambda i, *_: (i, 0))] * 4,
            name="finish_attention",
        )

        return (
            block_output,
            input_grad,
            small.rider[8],
            grad_query,
            grad_key,
            grad_value,
            grad_out,
            small.rider[9],
            grad_inner,
            grad_outer,
            small.rider[:H, :BUCKETS].T,
        )

    return body


def solution(mesh):
    split = P("rows", "seq", None)
    placed = (split, split) + (P(),) * 9 + (P("rows", None), P("rows", "seq"))
    return jax.shard_map(
        make_body(mesh.shape["rows"], mesh.shape["seq"]),
        mesh=mesh,
        in_specs=placed,
        out_specs=(split, split) + (P(),) * 9,
        check_vma=False,
    )
```

time: 245 us -> 203 us (0.83)
  starting transfers between devices: 59.7 us -> 40.2 us
  local copies, waits for them, and re-layouts: 27.6 us -> 14.5 us
  other arithmetic: 11.1 us -> 3.3 us
  Pallas kernels: 56.7 us -> 51.3 us
  waiting for transfers between devices: 86.5 us -> 89.2 us
    ppermute x16 -> x18, waiting for transfers between devices: 58.2 us -> 78.6 us  [swap_step(): return lax.ppermute(array, both, pairs)]
    ppermute x7 -> x4, starting transfers between devices: 31 us -> 14.7 us  [swap_rows(): return lax.ppermute(array, 'rows', [(i, i ^ bit) for i in range(rows)])]
    ppermute x16 -> x8, waiting for transfers between devices: 24.9 us -> 9.32 us  [swap_seq(): return lax.ppermute(array, 'seq', [(i, i ^ bit) for i in range(seq)])]
    unnamed x135 -> x57, local copies, waits for them, and re-layouts: 22.6 us -> 11.3 us
    ppermute x16 -> x8, starting transfers between devices: 17.6 us -> 10.5 us  [swap_seq(): return lax.ppermute(array, 'seq', [(i, i ^ bit) for i in range(seq)])]
    pallas_call x12 -> x10, Pallas kernels: 56.7 us -> 51.3 us  [call(): pl.pallas_call(kernel, out_shape=outs, grid_spec=pltpu.PrefetchScalarGrid...]
    convert_element_type x9 -> x18, other arithmetic: 7.48 us -> 2.69 us  [the longest x8 2.39 us: halve(): outgoing = add(*[part[size:] for part in self.parts]).astype(BF16)]
    ppermute x16 -> x18, starting transfers between devices: 11.1 us -> 15 us  [swap_step(): return lax.ppermute(array, both, pairs)]
  transfers between devices with their start and end apart: 39 -> 30, of which waited for: 16 -> 19; matrix products, arithmetic and copies ran while one was open for 5% -> 3% of each run, Pallas kernels for 17% -> 18%
where the time goes in v2:
time: 203 us; the launch traced here: 200 us
  waiting for transfers between devices  89.2 us (44%)
  Pallas kernels  51.3 us (25%)
  starting transfers between devices  40.2 us (20%)
  local copies, waits for them, and re-layouts  14.5 us (7%)
  other arithmetic  3.3 us (2%)
    ppermute x18, waiting for transfers between devices, swap_step(): return lax.ppermute(array, both, pairs)  78.6 us
    pallas_call x10, Pallas kernels, call(): pl.pallas_call(kernel, out_shape=outs, grid_spec=pltpu.PrefetchScalarGrid...  51.3 us
    ppermute x18, starting transfers between devices, swap_step(): return lax.ppermute(array, both, pairs)  15 us
    ppermute x4, starting transfers between devices, swap_rows(): return lax.ppermute(array, 'rows', [(i, i ^ bit) for i in range(rows)])  14.7 us
    unnamed x57, local copies, waits for them, and re-layouts  11.3 us
    ppermute x8, starting transfers between devices, swap_seq(): return lax.ppermute(array, 'seq', [(i, i ^ bit) for i in range(seq)])  10.5 us
    ppermute x8, waiting for transfers between devices, swap_seq(): return lax.ppermute(array, 'seq', [(i, i ^ bit) for i in range(seq)])  9.32 us
  transfers between devices with their start and end apart: 30, of which 19 were waited for; matrix products, arithmetic and copies ran while one was open for 3% of the time, Pallas kernels for 18%

profile of v2, /device:TPU:1, one launch (start us, length us, event | category | flops | bytes accessed | tf_op | source)
XLA Modules:
  0.0 199.6 jit_solution(13624363531585141382)
XLA Ops:
  0.6 3.2 %collective-permute-start.1 = (bf16[3,128,512]{2,1,0:T(8,128)(2,1)}, bf16[3,128,512]{2,1,0:T(8,128)(2,1)}, u32[]{:S(2)}, u32[]{:S(2)}) collective-permute-start(bf16[3,128,512]{2,1,0:T(8,128)(2,1)} %x_ref.1), channel_id=1, source_target_pairs={{0,2},{1,3},{2,0},{3,1},{4,6},{5,7},{6,4},{7,5},{8,10},{9,11},{10,... | collective-permute-start | bytes 1179656 | tf_op jit(solution)/shard_map/ppermute | solution.py:511
  3.8 1.3 collective-permute-start
  5.1 0.8 copy.24.table_ref
  5.9 4.1 %prepare.1 = (f32[4,256,512]{2,1,0:T(8,128)S(1)}, bf16[512,512]{1,0:T(8,128)(2,1)S(1)}, bf16[512,512]{1,0:T(8,128)(2,1)S(1)}, bf16[512,512]{1,0:T(8,128)(2,1)S(1...) custom-call(s32[1]{0:T(128)} %bitcast.place_ref, ...), custom_call_target="tpu_custom_call" | custom-call | bytes 15467520 | tf_op jit(solution)/shard_map/prepare/pallas_call | solution.py:477
  10.0 0.8 copy-done
  10.8 0.8 copy-done.3
  11.6 0.7 copy-done.7
  12.3 1.3 copy-done.15
  13.7 1.3 copy-done.17
  15.0 6.5 %collective-permute-done.1.x2_ref = bf16[3,128,512]{2,1,0:T(8,128)(2,1)} collective-permute-done((bf16[3,128,512]{2,1,0:T(8,128)(2,1)}, bf16[3,128,512]{2,1,0:T(8,128)(2,1)}, u32[]{:S(2)}, u32[]{:S(2)}) %collective-permute-start.1) | collective-permute-done | bytes 393248 | tf_op jit(solution)/shard_map/ppermute | solution.py:511
  21.5 1.8 slice_bitcast_fusion.2
  23.3 1.1 collective-permute-start.2
  24.4 2.8 %collective-permute-start.5 = (s32[3,128]{1,0:T(4,128)}, s32[3,128]{1,0:T(4,128)S(1)}, u32[]{:S(2)}, u32[]{:S(2)}) collective-permute-start(s32[3,128]{1,0:T(4,128)} %seen0_ref.5), channel_id=1, source_target_pairs={{0,3},{1,2},{2,1},{3,0},{4,7},{5,6},{6,5},{7,4},{8,11},{9,10},{10,... | collective-permute-start | bytes 4616 | tf_op jit(solution)/shard_map/ppermute | solution.py:511
  27.9 2.7 %collective-permute-done.5.seen3_ref = s32[3,128]{1,0:T(4,128)S(1)} collective-permute-done((s32[3,128]{1,0:T(4,128)}, s32[3,128]{1,0:T(4,128)S(1)}, u32[]{:S(2)}, u32[]{:S(2)}) %collective-permute-start.5) | collective-permute-done | bytes 1568 | tf_op jit(solution)/shard_map/ppermute | solution.py:511
  30.8 1.3 collective-permute-start.6
  32.2 1.0 copy-done.1
  33.2 1.0 copy-done.4
  34.3 0.7 copy-done.9
  34.9 0.7 copy-done.11
  35.6 0.7 copy-done.13
  36.3 4.4 %attention.3 = (bf16[128,512]{1,0:T(8,128)(2,1)S(1)}, bf16[128,512]{1,0:T(8,128)(2,1)S(1)}, f32[128,512]{1,0:T(8,128)S(1)}, f32[128,512]{1,0:T(8,128)S(1)}, bf16...) custom-call(s32[1]{0:T(128)} %bitcast.place_ref, ...), custom_call_target="tpu_custom_call" | custom-call | flops 268435456 | bytes 9054208 | tf_op jit(solution)/shard_map/attention/pallas_call | solution.py:477
  40.7 0.6 copy-done.24
  41.4 4.4 %attention.4 = (bf16[128,512]{1,0:T(8,128)(2,1)S(1)}, bf16[128,512]{1,0:T(8,128)(2,1)S(1)}, f32[128,512]{1,0:T(8,128)S(1)}, f32[128,512]{1,0:T(8,128)S(1)}, bf16...) custom-call(s32[1]{0:T(128)} %bitcast.place_ref, ...), custom_call_target="tpu_custom_call" | custom-call | flops 268435456 | bytes 9054208 | tf_op jit(solution)/shard_map/attention/pallas_call | solution.py:477
  45.9 0.6 copy-done.23
  46.5 4.6 %attention.5 = (bf16[128,512]{1,0:T(8,128)(2,1)S(1)}, bf16[128,512]{1,0:T(8,128)(2,1)S(1)}, f32[128,512]{1,0:T(8,128)S(1)}, f32[128,512]{1,0:T(8,128)S(1)}, bf16...) custom-call(s32[1]{0:T(128)} %bitcast.place_ref, ...), custom_call_target="tpu_custom_call" | custom-call | flops 268435456 | bytes 9054208 | tf_op jit(solution)/shard_map/attention/pallas_call | solution.py:477
  51.1 6.0 %mlp.2 = (f32[384,512]{1,0:T(8,128)S(1)}, f32[384,512]{1,0:T(8,128)S(1)}, bf16[16,128,512]{2,1,0:T(8,128)(2,1)}) custom-call(s32[3]{0:T(128)S(1)} %pad_add_fusion.code_ref, bf16[128,512]{1,0:T(8,128)(2,1)S(1)} %get-tuple-element.124.refs_0_, bf16[128,512]{1,0:T(8,128)(2,1)S(1)} %get-tuple-element.102.refs_1_.refs_9_, ...), custom_call_target="tpu_custom_call" | custom-call | flops 2415919104 | bytes 8650752 | tf_op jit(solution)/shard_map/mlp/pallas_call | solution.py:477
  57.2 1.9 collective-permute-start.8
  59.1 5.8 %mlp.3 = (f32[384,512]{1,0:T(8,128)S(1)}, f32[384,512]{1,0:T(8,128)S(1)}, bf16[16,128,512]{2,1,0:T(8,128)(2,1)}) custom-call(s32[3]{0:T(128)S(1)} %pad_add_fusion.code_ref, bf16[128,512]{1,0:T(8,128)(2,1)S(1)} %get-tuple-element.124.refs_0_, bf16[128,512]{1,0:T(8,128)(2,1)S(1)} %get-tuple-element.102.refs_1_.refs_9_, ...), custom_call_target="tpu_custom_call" | custom-call | flops 2415919104 | bytes 8650752 | tf_op jit(solution)/shard_map/mlp/pallas_call | solution.py:477
  64.9 1.6 add_convert_fusion.refs_38_
  66.5 1.3 collective-permute-start.10
  67.9 12.8 %attention_back.1 = (bf16[3,128,512]{2,1,0:T(8,128)(2,1)}, f32[3,128,512]{2,1,0:T(8,128)S(1)}, bf16[2,3,512,128]{3,2,1,0:T(8,128)(2,1)S(1)}, bf16[2,3,512,128]{3...) custom-call(s32[1]{0:T(128)} %bitcast.place_ref, ...), custom_call_target="tpu_custom_call" | custom-call | flops 2013265920 | bytes 22220800 | tf_op jit(solution)/shard_map/attention_back/pallas_call | solution.py:477
  81.1 1.0 collective-permute-start.11
  82.2 1.2 collective-permute-done.12
  83.6 1.2 collective-permute-start.14
  84.8 7.0 %collective-permute-done.11 = bf16[4,128,512]{2,1,0:T(8,128)(2,1)S(1)} collective-permute-done((bf16[4,128,512]{2,1,0:T(8,128)(2,1)S(1)}, bf16[4,128,512]{2,1,0:T(8,128)(2,1)S(1)}, u32[]{:S(2)}, u32[]{:S(2)}) %collective-permute-start.11) | collective-permute-done | bytes 524320 | tf_op jit(solution)/shard_map/ppermute | solution.py:526
  92.4 3.7 %collective-permute-done.14 = bf16[544,512]{1,0:T(8,128)(2,1)S(1)} collective-permute-done((bf16[544,512]{1,0:T(8,128)(2,1)S(1)}, bf16[544,512]{1,0:T(8,128)(2,1)S(1)}, u32[]{:S(2)}, u32[]{:S(2)}) %collective-permute-start.14) | collective-permute-done | bytes 557088 | tf_op jit(solution)/shard_map/ppermute | solution.py:526
  96.4 1.3 collective-permute-start.16
  97.6 3.5 %collective-permute-done.13 = bf16[2,128,512]{2,1,0:T(8,128)(2,1)S(1)} collective-permute-done((bf16[2,128,512]{2,1,0:T(8,128)(2,1)S(1)}, bf16[2,128,512]{2,1,0:T(8,128)(2,1)S(1)}, u32[]{:S(2)}, u32[]{:S(2)}) %collective-permute-start.13) | collective-permute-done | bytes 262176 | tf_op jit(solution)/shard_map/ppermute | solution.py:526
  101.3 1.0 collective-permute-done.16
  102.4 0.6 collective-permute-start.18
  103.0 2.1 %collective-permute-done.15 = bf16[1,128,512]{2,1,0:T(8,128)(2,1)S(1)} collective-permute-done((bf16[1,128,512]{2,1,0:T(8,128)(2,1)S(1)}, bf16[1,128,512]{2,1,0:T(8,128)(2,1)S(1)}, u32[]{:S(2)}, u32[]{:S(2)}) %collective-permute-start.15) | collective-permute-done | bytes 131104 | tf_op jit(solution)/shard_map/ppermute | solution.py:526
  105.3 7.1 %collective-permute-done.18 = bf16[160,512]{1,0:T(8,128)(2,1)S(1)} collective-permute-done((bf16[160,512]{1,0:T(8,128)(2,1)S(1)}, bf16[160,512]{1,0:T(8,128)(2,1)S(1)}, u32[]{:S(2)}, u32[]{:S(2)}) %collective-permute-start.18) | collective-permute-done | bytes 163872 | tf_op jit(solution)/shard_map/ppermute | solution.py:526
  112.5 1.1 collective-permute-done.17
  113.7 1.5 collective-permute-start.19
  115.3 2.5 %collective-permute-done.20 = bf16[96,512]{1,0:T(8,128)(2,1)S(1)} collective-permute-done((bf16[96,512]{1,0:T(8,128)(2,1)S(1)}, bf16[96,512]{1,0:T(8,128)(2,1)S(1)}, u32[]{:S(2)}, u32[]{:S(2)}) %collective-permute-start.20) | collective-permute-done | bytes 98336 | tf_op jit(solution)/shard_map/ppermute | solution.py:526
  117.9 6.5 %collective-permute-done.19 = bf16[2,128,512]{2,1,0:T(8,128)(2,1)S(1)} collective-permute-done((bf16[2,128,512]{2,1,0:T(8,128)(2,1)S(1)}, bf16[2,128,512]{2,1,0:T(8,128)(2,1)S(1)}, u32[]{:S(2)}, u32[]{:S(2)}) %collective-permute-start.19) | collective-permute-done | bytes 262176 | tf_op jit(solution)/shard_map/ppermute | solution.py:526
  124.4 1.2 collective-permute-start.21
  125.6 4.6 %collective-permute-done.22 = bf16[1,64,512]{2,1,0:T(8,128)(2,1)S(1)} collective-permute-done((bf16[1,64,512]{2,1,0:T(8,128)(2,1)S(1)}, bf16[1,64,512]{2,1,0:T(8,128)(2,1)S(1)}, u32[]{:S(2)}, u32[]{:S(2)}) %collective-permute-start.22) | collective-permute-done | bytes 65568 | tf_op jit(solution)/shard_map/ppermute | solution.py:526
  130.3 2.4 %collective-permute-start.9 = (bf16[2,3,512,128]{3,2,1,0:T(8,128)(2,1)S(1)}, bf16[2,3,512,128]{3,2,1,0:T(8,128)(2,1)S(1)}, u32[]{:S(2)}, u32[]{:S(2)}) collective-permute-start(bf16[2,3,512,128]{3,2,1,0:T(8,128)(2,1)S(1)} %get-tuple-element.132), channel_id=1, source_target_pairs={{0,1},{1,0},{2,3},{3,2},{4,6},{5,7},{6,4},{7,5},{8,9},{9,8},{10,11... | collective-permute-start | bytes 2359304 | tf_op jit(solution)/shard_map/ppermute | solution.py:526
  132.7 12.8 %collective-permute-done.23 = bf16[2,64,512]{2,1,0:T(8,128)(2,1)S(1)} collective-permute-done((bf16[2,64,512]{2,1,0:T(8,128)(2,1)S(1)}, bf16[2,64,512]{2,1,0:T(8,128)(2,1)S(1)}, u32[]{:S(2)}, u32[]{:S(2)}) %collective-permute-start.23) | collective-permute-done | bytes 131104 | tf_op jit(solution)/shard_map/ppermute | solution.py:526
  145.6 1.4 collective-permute-start.27
  147.1 0.9 collective-permute-start.25
  148.0 6.1 %collective-permute-done.9 = bf16[2,3,512,128]{3,2,1,0:T(8,128)(2,1)S(1)} collective-permute-done((bf16[2,3,512,128]{3,2,1,0:T(8,128)(2,1)S(1)}, bf16[2,3,512,128]{3,2,1,0:T(8,128)(2,1)S(1)}, u32[]{:S(2)}, u32[]{:S(2)}) %collective-permute-start.9) | collective-permute-done | bytes 786464 | tf_op jit(solution)/shard_map/ppermute | solution.py:526
  154.4 5.2 %collective-permute-done.27 = bf16[8,128,512]{2,1,0:T(8,128)(2,1)S(1)} collective-permute-done((bf16[8,128,512]{2,1,0:T(8,128)(2,1)S(1)}, bf16[8,128,512]{2,1,0:T(8,128)(2,1)S(1)}, u32[]{:S(2)}, u32[]{:S(2)}) %collective-permute-start.27) | collective-permute-done | bytes 1048608 | tf_op jit(solution)/shard_map/ppermute | solution.py:526
  159.7 11.6 %collective-permute-start.29 = (bf16[16,128,512]{2,1,0:T(8,128)(2,1)S(1)}, bf16[16,128,512]{2,1,0:T(8,128)(2,1)S(1)}, u32[]{:S(2)}, u32[]{:S(2)}) collective-permute-start(bf16[16,128,512]{2,1,0:T(8,128)(2,1)S(1)} %constant_dynamic-update-slice_fusion.low_ref), channel_id=1, source_target_pairs={{0,4},{4,0},{8,12},{12,8},{16,20},{20,16},{24,28},{28,24},{1,5},{5... | collective-permute-start | bytes 6291464 | tf_op jit(solution)/shard_map/ppermute | solution.py:508
  171.2 1.4 collective-permute-start.26
  172.7 6.9 %collective-permute-done.26 = bf16[8,64,512]{2,1,0:T(8,128)(2,1)S(1)} collective-permute-done((bf16[8,64,512]{2,1,0:T(8,128)(2,1)S(1)}, bf16[8,64,512]{2,1,0:T(8,128)(2,1)S(1)}, u32[]{:S(2)}, u32[]{:S(2)}) %collective-permute-start.26) | collective-permute-done | bytes 524320 | tf_op jit(solution)/shard_map/ppermute | solution.py:526
  179.6 1.0 collective-permute-start.28
  180.8 0.6 slice_bitcast_fusion.5
  181.4 0.6 fusion.6
  181.9 8.6 %collective-permute-done.24.b_ref = bf16[3,512,128]{2,1,0:T(8,128)(2,1)S(1)} collective-permute-done((bf16[3,512,128]{2,1,0:T(8,128)(2,1)S(1)}, bf16[3,512,128]{2,1,0:T(8,128)(2,1)S(1)}, u32[]{:S(2)}, u32[]{:S(2)}) %collective-permute-start.24) | collective-permute-done | bytes 393248 | tf_op jit(solution)/shard_map/ppermute | solution.py:526
  190.5 1.8 post.1
  192.3 2.9 %finish_attention.1 = (f32[512,512]{1,0:T(8,128)}, f32[512,512]{1,0:T(8,128)}, f32[512,512]{1,0:T(8,128)}, f32[512,512]{1,0:T(8,128)}) custom-call(s32[3]{0:T(128)S(1)} %pad_add_fusion.code_ref, bf16[16,64,512]{2,1,0:T(8,128)(2,1)S(1)} %constant_dynamic-update-slice_fusion.5.low_ref, bf16[16,64,512]{2,1,0:T(8,128)(2,1)S(1)} %collective-permute-done.28.high_ref), custom_call_target="tpu_custom_call" | custom-call | bytes 6291456 | tf_op jit(solution)/shard_map/finish_attention/pallas_call | solution.py:477
  195.2 4.4 %finish_mlp.1 = (f32[2048,512]{1,0:T(8,128)}, f32[512,2048]{1,0:T(8,128)}) custom-call(s32[3]{0:T(128)S(1)} %pad_add_fusion.code_ref, bf16[16,128,512]{2,1,0:T(8,128)(2,1)S(1)} %constant_dynamic-update-slice_fusion.low_ref, bf16[16,128,512]{2,1,0:T(8,128)(2,1)S(1)} %collective-permute-done.29.high_ref), custom_call_target="tpu_custom_call" | custom-call | bytes 12582912 | tf_op jit(solution)/shard_map/finish_mlp/pallas_call | solution.py:477
  (109 shorter events, 4.1 us)
Async XLA Ops:
  0.6 20.8 %collective-permute-start.1 = (bf16[3,128,512]{2,1,0:T(8,128)(2,1)}, bf16[3,128,512]{2,1,0:T(8,128)(2,1)}, u32[]{:S(2)}, u32[]{:S(2)}) collective-permute-start(bf16[3,128,512]{2,1,0:T(8,128)(2,1)} %x_ref.1), channel_id=1, source_target_pairs={{0,2},{1,3},{2,0},{3,1},{4,6},{5,7},{6,4},{7,5},{8,10},{9,11},{10,... | collective-permute-start | bytes 1179656 | tf_op jit(solution)/shard_map/ppermute | solution.py:511
  3.8 28.3 %collective-permute-start = (bf16[3,128,512]{2,1,0:T(8,128)(2,1)}, bf16[3,128,512]{2,1,0:T(8,128)(2,1)}, u32[]{:S(2)}, u32[]{:S(2)}) collective-permute-start(bf16[3,128,512]{2,1,0:T(8,128)(2,1)} %x_ref.1), channel_id=1, source_target_pairs={{0,1},{1,0},{2,3},{3,2},{4,5},{5,4},{6,7},{7,6},{8,9},{9,8},{10,11... | collective-permute-start | bytes 1179656 | tf_op jit(solution)/shard_map/ppermute | solution.py:511
  5.9 26.2 %copy-start.6 = (bf16[3,128,512]{2,1,0:T(8,128)(2,1)S(1)}, bf16[3,128,512]{2,1,0:T(8,128)(2,1)}, u32[]{:S(2)}) copy-start(bf16[3,128,512]{2,1,0:T(8,128)(2,1)} %x_ref.1) | copy-start | bytes 1179652
  10.0 0.8 copy-start
  10.8 0.8 copy-start.3
  11.6 0.7 copy-start.7
  12.3 1.3 copy-start.15
  13.7 1.3 copy-start.17
  23.3 8.9 %collective-permute-start.2 = (bf16[128,512]{1,0:T(8,128)(2,1)}, bf16[128,512]{1,0:T(8,128)(2,1)}, u32[]{:S(2)}, u32[]{:S(2)}) collective-permute-start(bf16[128,512]{1,0:T(8,128)(2,1)} %get-tuple-element.183), channel_id=1, source_target_pairs={{0,1},{1,0},{2,3},{3,2},{4,5},{5,4},{6,7},{7,6},{8,9},{9,8},{10,11... | collective-permute-start | bytes 393224 | tf_op jit(solution)/shard_map/ppermute | solution.py:511
  24.4 6.2 %collective-permute-start.5 = (s32[3,128]{1,0:T(4,128)}, s32[3,128]{1,0:T(4,128)S(1)}, u32[]{:S(2)}, u32[]{:S(2)}) collective-permute-start(s32[3,128]{1,0:T(4,128)} %seen0_ref.5), channel_id=1, source_target_pairs={{0,3},{1,2},{2,1},{3,0},{4,7},{5,6},{6,5},{7,4},{8,11},{9,10},{10,... | collective-permute-start | bytes 4616 | tf_op jit(solution)/shard_map/ppermute | solution.py:511
  27.2 3.5 %collective-permute-start.4 = (s32[3,128]{1,0:T(4,128)}, s32[3,128]{1,0:T(4,128)S(1)}, u32[]{:S(2)}, u32[]{:S(2)}) collective-permute-start(s32[3,128]{1,0:T(4,128)} %seen0_ref.5), channel_id=1, source_target_pairs={{0,2},{1,3},{2,0},{3,1},{4,6},{5,7},{6,4},{7,5},{8,10},{9,11},{10,... | collective-permute-start | bytes 4616 | tf_op jit(solution)/shard_map/ppermute | solution.py:511
  27.5 4.7 %collective-permute-start.3 = (s32[3,128]{1,0:T(4,128)}, s32[3,128]{1,0:T(4,128)S(1)}, u32[]{:S(2)}, u32[]{:S(2)}) collective-permute-start(s32[3,128]{1,0:T(4,128)} %seen0_ref.5), channel_id=1, source_target_pairs={{0,1},{1,0},{2,3},{3,2},{4,5},{5,4},{6,7},{7,6},{8,9},{9,8},{10,11... | collective-permute-start | bytes 4616 | tf_op jit(solution)/shard_map/ppermute | solution.py:511
  30.6 15.3 %collective-permute-start.7 = (bf16[128,512]{1,0:T(8,128)(2,1)}, bf16[128,512]{1,0:T(8,128)(2,1)S(1)}, u32[]{:S(2)}, u32[]{:S(2)}) collective-permute-start(bf16[128,512]{1,0:T(8,128)(2,1)} %get-tuple-element.181), channel_id=1, source_target_pairs={{0,1},{1,0},{2,3},{3,2},{4,5},{5,4},{6,7},{7,6},{8,9},{9,8},{10,11... | collective-permute-start | bytes 393224 | tf_op jit(solution)/shard_map/ppermute | solution.py:511
  30.8 10.0 %collective-permute-start.6 = (bf16[128,512]{1,0:T(8,128)(2,1)}, bf16[128,512]{1,0:T(8,128)(2,1)S(1)}, u32[]{:S(2)}, u32[]{:S(2)}) collective-permute-start(bf16[128,512]{1,0:T(8,128)(2,1)} %get-tuple-element.182), channel_id=1, source_target_pairs={{0,1},{1,0},{2,3},{3,2},{4,5},{5,4},{6,7},{7,6},{8,9},{9,8},{10,11... | collective-permute-start | bytes 393224 | tf_op jit(solution)/shard_map/ppermute | solution.py:511
  32.2 1.0 copy-start.1
  33.2 1.0 copy-start.4
  34.3 0.7 copy-start.9
  34.9 0.7 copy-start.11
  35.6 0.7 copy-start.13
  36.3 5.1 %copy-start.12 = (f32[512]{0:T(512)S(1)}, f32[512]{0:T(512)}, u32[]{:S(2)}) copy-start(f32[512]{0:T(512)} %param.20) | copy-start | bytes 6148
  36.3 5.1 %copy-start.14 = (s32[3,4]{1,0:T(4,128)S(1)}, s32[3,4]{1,0:T(4,128)}, u32[]{:S(2)}) copy-start(s32[3,4]{1,0:T(4,128)} %lengths_ref.5) | copy-start | bytes 148
  40.7 0.7 copy-start.24
  45.8 5.3 %copy-start.8 = (bf16[3,128,512]{2,1,0:T(8,128)(2,1)S(1)}, bf16[3,128,512]{2,1,0:T(8,128)(2,1)}, u32[]{:S(2)}) copy-start(bf16[3,128,512]{2,1,0:T(8,128)(2,1)} %copy-done.7) | copy-start | bytes 1179652
  45.8 5.3 %copy-start.16 = (bf16[512,2048]{1,0:T(8,128)(2,1)S(1)}, bf16[512,2048]{1,0:T(8,128)(2,1)}, u32[]{:S(2)}) copy-start(bf16[512,2048]{1,0:T(8,128)(2,1)} %copy-done.15) | copy-start | bytes 6291460
  45.8 5.3 %copy-start.18 = (bf16[2048,512]{1,0:T(8,128)(2,1)S(1)}, bf16[2048,512]{1,0:T(8,128)(2,1)}, u32[]{:S(2)}) copy-start(bf16[2048,512]{1,0:T(8,128)(2,1)} %copy-done.17) | copy-start | bytes 6291460
  45.9 0.7 copy-start.23
  57.2 7.7 %collective-permute-start.8 = (bf16[16,128,512]{2,1,0:T(8,128)(2,1)}, bf16[16,128,512]{2,1,0:T(8,128)(2,1)S(1)}, u32[]{:S(2)}, u32[]{:S(2)}) collective-permute-start(bf16[16,128,512]{2,1,0:T(8,128)(2,1)} %get-tuple-element.129), channel_id=1, source_target_pairs={{0,4},{4,0},{8,12},{12,8},{16,20},{20,16},{24,28},{28,24},{1,5},{5... | collective-permute-start | bytes 6291464 | tf_op jit(solution)/shard_map/ppermute | solution.py:508
  64.9 2.9 %copy-start.2 = (bf16[512,512]{1,0:T(8,128)(2,1)S(1)}, bf16[512,512]{1,0:T(8,128)(2,1)}, u32[]{:S(2)}) copy-start(bf16[512,512]{1,0:T(8,128)(2,1)} %copy-done) | copy-start | bytes 1572868
  64.9 2.9 %copy-start.5 = (bf16[512,512]{1,0:T(8,128)(2,1)S(1)}, bf16[512,512]{1,0:T(8,128)(2,1)}, u32[]{:S(2)}) copy-start(bf16[512,512]{1,0:T(8,128)(2,1)} %copy-done.3) | copy-start | bytes 1572868
  64.9 2.9 %copy-start.10 = (f32[512]{0:T(512)S(1)}, f32[512]{0:T(512)}, u32[]{:S(2)}) copy-start(f32[512]{0:T(512)} %param.15) | copy-start | bytes 6148
  66.5 1.3 copy-start.19
  66.5 14.4 %collective-permute-start.10 = (bf16[8,128,512]{2,1,0:T(8,128)(2,1)S(1)}, bf16[8,128,512]{2,1,0:T(8,128)(2,1)S(1)}, u32[]{:S(2)}, u32[]{:S(2)}) collective-permute-start(bf16[8,128,512]{2,1,0:T(8,128)(2,1)S(1)} %add_convert_fusion.refs_38_), channel_id=1, source_target_pairs={{0,8},{1,9},{2,10},{3,11},{4,20},{5,21},{6,22},{7,23},{8,0},{9,1},... | collective-permute-start | bytes 3145736 | tf_op jit(solution)/shard_map/ppermute | solution.py:526
  67.8 13.1 %copy-start.20 = (bf16[16,128,512]{2,1,0:T(8,128)(2,1)S(1)}, bf16[16,128,512]{2,1,0:T(8,128)(2,1)}, u32[]{:S(2)}) copy-start(bf16[16,128,512]{2,1,0:T(8,128)(2,1)} %get-tuple-element.128) | copy-start | bytes 6291460
  80.7 2.7 %collective-permute-start.12 = (bf16[1056,512]{1,0:T(8,128)(2,1)S(1)}, bf16[1056,512]{1,0:T(8,128)(2,1)S(1)}, u32[]{:S(2)}, u32[]{:S(2)}) collective-permute-start(bf16[1056,512]{1,0:T(8,128)(2,1)S(1)} %get-tuple-element.136), channel_id=1, source_target_pairs={{0,4},{4,0},{8,12},{12,8},{16,20},{20,16},{24,28},{28,24},{1,5},{5... | collective-permute-start | bytes 3244040 | tf_op jit(solution)/shard_map/ppermute | solution.py:508
  81.1 10.7 %collective-permute-start.11 = (bf16[4,128,512]{2,1,0:T(8,128)(2,1)S(1)}, bf16[4,128,512]{2,1,0:T(8,128)(2,1)S(1)}, u32[]{:S(2)}, u32[]{:S(2)}) collective-permute-start(bf16[4,128,512]{2,1,0:T(8,128)(2,1)S(1)} %add_convert_fusion.2), channel_id=1, source_target_pairs={{0,16},{1,17},{2,18},{3,19},{4,12},{5,13},{6,14},{7,15},{8,24},{9,... | collective-permute-start | bytes 1572872 | tf_op jit(solution)/shard_map/ppermute | solution.py:526
  83.4 1.4 copy-start.21
  83.6 12.5 %collective-permute-start.14 = (bf16[544,512]{1,0:T(8,128)(2,1)S(1)}, bf16[544,512]{1,0:T(8,128)(2,1)S(1)}, u32[]{:S(2)}, u32[]{:S(2)}) collective-permute-start(bf16[544,512]{1,0:T(8,128)(2,1)S(1)} %pad_maximum_fusion.1), channel_id=1, source_target_pairs={{0,8},{1,9},{2,10},{3,11},{4,20},{5,21},{6,22},{7,23},{8,0},{9,1},... | collective-permute-start | bytes 1671176 | tf_op jit(solution)/shard_map/ppermute | solution.py:526
  91.8 4.3 %slice-start = ((bf16[1056,512]{1,0:T(8,128)(2,1)}), bf16[256,512]{1,0:T(8,128)(2,1)S(1)}, s32[]{:S(2)}) async-start(bf16[1056,512]{1,0:T(8,128)(2,1)} %copy-done.21), calls=%async_computation | async-start | bytes 524288 | tf_op jit(solution)/shard_map/slice | solution.py:573
  92.0 10.3 %slice-start.1 = ((bf16[1056,512]{1,0:T(8,128)(2,1)}), bf16[128,512]{1,0:T(8,128)(2,1)S(1)}, s32[]{:S(2)}) async-start(bf16[1056,512]{1,0:T(8,128)(2,1)} %copy-done.21), calls=%async_computation.1 | async-start | bytes 262144 | tf_op jit(solution)/shard_map/slice | solution.py:573
  92.0 9.1 %collective-permute-start.13 = (bf16[2,128,512]{2,1,0:T(8,128)(2,1)S(1)}, bf16[2,128,512]{2,1,0:T(8,128)(2,1)S(1)}, u32[]{:S(2)}, u32[]{:S(2)}) collective-permute-start(bf16[2,128,512]{2,1,0:T(8,128)(2,1)S(1)} %add_convert_fusion.3), channel_id=1, source_target_pairs={{0,1},{1,0},{2,3},{3,2},{4,6},{5,7},{6,4},{7,5},{8,9},{9,8},{10,11... | collective-permute-start | bytes 786440 | tf_op jit(solution)/shard_map/ppermute | solution.py:526
  96.3 16.1 %copy-start.22 = (bf16[1056,512]{1,0:T(8,128)(2,1)S(1)}, bf16[1056,512]{1,0:T(8,128)(2,1)}, u32[]{:S(2)}) copy-start(bf16[1056,512]{1,0:T(8,128)(2,1)} %copy-done.21) | copy-start | bytes 3244036
  96.4 5.9 %collective-permute-start.16 = (bf16[288,512]{1,0:T(8,128)(2,1)S(1)}, bf16[288,512]{1,0:T(8,128)(2,1)S(1)}, u32[]{:S(2)}, u32[]{:S(2)}) collective-permute-start(bf16[288,512]{1,0:T(8,128)(2,1)S(1)} %pad_maximum_fusion.4), channel_id=1, source_target_pairs={{0,16},{1,17},{2,18},{3,19},{4,12},{5,13},{6,14},{7,15},{8,24},{9,... | collective-permute-start | bytes 884744 | tf_op jit(solution)/shard_map/ppermute | solution.py:526
  101.2 3.9 %collective-permute-start.15 = (bf16[1,128,512]{2,1,0:T(8,128)(2,1)S(1)}, bf16[1,128,512]{2,1,0:T(8,128)(2,1)S(1)}, u32[]{:S(2)}, u32[]{:S(2)}) collective-permute-start(bf16[1,128,512]{2,1,0:T(8,128)(2,1)S(1)} %add_convert_fusion.5), channel_id=1, source_target_pairs={{0,2},{1,3},{2,0},{3,1},{4,5},{5,4},{6,7},{7,6},{8,10},{9,11},{10,... | collective-permute-start | bytes 393224 | tf_op jit(solution)/shard_map/ppermute | solution.py:526
  102.4 10.0 %collective-permute-start.18 = (bf16[160,512]{1,0:T(8,128)(2,1)S(1)}, bf16[160,512]{1,0:T(8,128)(2,1)S(1)}, u32[]{:S(2)}, u32[]{:S(2)}) collective-permute-start(bf16[160,512]{1,0:T(8,128)(2,1)S(1)} %pad_maximum_fusion.7), channel_id=1, source_target_pairs={{0,1},{1,0},{2,3},{3,2},{4,6},{5,7},{6,4},{7,5},{8,9},{9,8},{10,11... | collective-permute-start | bytes 491528 | tf_op jit(solution)/shard_map/ppermute | solution.py:526
  105.2 8.4 %collective-permute-start.17 = (bf16[1,128,512]{2,1,0:T(8,128)(2,1)S(1)}, bf16[1,128,512]{2,1,0:T(8,128)(2,1)S(1)}, u32[]{:S(2)}, u32[]{:S(2)}) collective-permute-start(bf16[1,128,512]{2,1,0:T(8,128)(2,1)S(1)} %get-tuple-element.164), channel_id=1, source_target_pairs={{0,2},{1,3},{2,0},{3,1},{4,5},{5,4},{6,7},{7,6},{8,10},{9,11},{10,... | collective-permute-start | bytes 393224 | tf_op jit(solution)/shard_map/ppermute | solution.py:526
  113.6 4.2 %collective-permute-start.20 = (bf16[96,512]{1,0:T(8,128)(2,1)S(1)}, bf16[96,512]{1,0:T(8,128)(2,1)S(1)}, u32[]{:S(2)}, u32[]{:S(2)}) collective-permute-start(bf16[96,512]{1,0:T(8,128)(2,1)S(1)} %pad_maximum_fusion.9), channel_id=1, source_target_pairs={{0,2},{1,3},{2,0},{3,1},{4,5},{5,4},{6,7},{7,6},{8,10},{9,11},{10,... | collective-permute-start | bytes 294920 | tf_op jit(solution)/shard_map/ppermute | solution.py:526
  113.7 10.6 %collective-permute-start.19 = (bf16[2,128,512]{2,1,0:T(8,128)(2,1)S(1)}, bf16[2,128,512]{2,1,0:T(8,128)(2,1)S(1)}, u32[]{:S(2)}, u32[]{:S(2)}) collective-permute-start(bf16[2,128,512]{2,1,0:T(8,128)(2,1)S(1)} %pad_maximum_fusion.5), channel_id=1, source_target_pairs={{0,1},{1,0},{2,3},{3,2},{4,6},{5,7},{6,4},{7,5},{8,9},{9,8},{10,11... | collective-permute-start | bytes 786440 | tf_op jit(solution)/shard_map/ppermute | solution.py:526
  124.4 21.1 %collective-permute-start.21 = (bf16[4,128,512]{2,1,0:T(8,128)(2,1)S(1)}, bf16[4,128,512]{2,1,0:T(8,128)(2,1)S(1)}, u32[]{:S(2)}, u32[]{:S(2)}) collective-permute-start(bf16[4,128,512]{2,1,0:T(8,128)(2,1)S(1)} %pad_maximum_fusion.2), channel_id=1, source_target_pairs={{0,16},{1,17},{2,18},{3,19},{4,12},{5,13},{6,14},{7,15},{8,24},{9,... | collective-permute-start | bytes 1572872 | tf_op jit(solution)/shard_map/ppermute | solution.py:526
  125.6 4.6 %collective-permute-start.22 = (bf16[1,64,512]{2,1,0:T(8,128)(2,1)S(1)}, bf16[1,64,512]{2,1,0:T(8,128)(2,1)S(1)}, u32[]{:S(2)}, u32[]{:S(2)}) collective-permute-start(bf16[1,64,512]{2,1,0:T(8,128)(2,1)S(1)} %get-tuple-element.166), channel_id=1, source_target_pairs={{0,2},{1,3},{2,0},{3,1},{4,5},{5,4},{6,7},{7,6},{8,10},{9,11},{10,... | collective-permute-start | bytes 196616 | tf_op jit(solution)/shard_map/ppermute | solution.py:526
  130.2 15.2 %collective-permute-start.23 = (bf16[2,64,512]{2,1,0:T(8,128)(2,1)S(1)}, bf16[2,64,512]{2,1,0:T(8,128)(2,1)S(1)}, u32[]{:S(2)}, u32[]{:S(2)}) collective-permute-start(bf16[2,64,512]{2,1,0:T(8,128)(2,1)S(1)} %pad_maximum_fusion.8), channel_id=1, source_target_pairs={{0,1},{1,0},{2,3},{3,2},{4,6},{5,7},{6,4},{7,5},{8,9},{9,8},{10,11... | collective-permute-start | bytes 393224 | tf_op jit(solution)/shard_map/ppermute | solution.py:526
  130.3 23.8 %collective-permute-start.9 = (bf16[2,3,512,128]{3,2,1,0:T(8,128)(2,1)S(1)}, bf16[2,3,512,128]{3,2,1,0:T(8,128)(2,1)S(1)}, u32[]{:S(2)}, u32[]{:S(2)}) collective-permute-start(bf16[2,3,512,128]{3,2,1,0:T(8,128)(2,1)S(1)} %get-tuple-element.132), channel_id=1, source_target_pairs={{0,1},{1,0},{2,3},{3,2},{4,6},{5,7},{6,4},{7,5},{8,9},{9,8},{10,11... | collective-permute-start | bytes 2359304 | tf_op jit(solution)/shard_map/ppermute | solution.py:526
  145.6 14.0 %collective-permute-start.27 = (bf16[8,128,512]{2,1,0:T(8,128)(2,1)S(1)}, bf16[8,128,512]{2,1,0:T(8,128)(2,1)S(1)}, u32[]{:S(2)}, u32[]{:S(2)}) collective-permute-start(bf16[8,128,512]{2,1,0:T(8,128)(2,1)S(1)} %pad_maximum_fusion), channel_id=1, source_target_pairs={{0,8},{1,9},{2,10},{3,11},{4,20},{5,21},{6,22},{7,23},{8,0},{9,1},... | collective-permute-start | bytes 3145736 | tf_op jit(solution)/shard_map/ppermute | solution.py:526
  147.1 7.2 %collective-permute-start.25 = (bf16[4,64,512]{2,1,0:T(8,128)(2,1)S(1)}, bf16[4,64,512]{2,1,0:T(8,128)(2,1)S(1)}, u32[]{:S(2)}, u32[]{:S(2)}) collective-permute-start(bf16[4,64,512]{2,1,0:T(8,128)(2,1)S(1)} %pad_maximum_fusion.6), channel_id=1, source_target_pairs={{0,16},{1,17},{2,18},{3,19},{4,12},{5,13},{6,14},{7,15},{8,24},{9,... | collective-permute-start | bytes 786440 | tf_op jit(solution)/shard_map/ppermute | solution.py:526
  159.7 35.6 %collective-permute-start.29 = (bf16[16,128,512]{2,1,0:T(8,128)(2,1)S(1)}, bf16[16,128,512]{2,1,0:T(8,128)(2,1)S(1)}, u32[]{:S(2)}, u32[]{:S(2)}) collective-permute-start(bf16[16,128,512]{2,1,0:T(8,128)(2,1)S(1)} %constant_dynamic-update-slice_fusion.low_ref), channel_id=1, source_target_pairs={{0,4},{4,0},{8,12},{12,8},{16,20},{20,16},{24,28},{28,24},{1,5},{5... | collective-permute-start | bytes 6291464 | tf_op jit(solution)/shard_map/ppermute | solution.py:508
  171.2 8.3 %collective-permute-start.26 = (bf16[8,64,512]{2,1,0:T(8,128)(2,1)S(1)}, bf16[8,64,512]{2,1,0:T(8,128)(2,1)S(1)}, u32[]{:S(2)}, u32[]{:S(2)}) collective-permute-start(bf16[8,64,512]{2,1,0:T(8,128)(2,1)S(1)} %pad_maximum_fusion.3), channel_id=1, source_target_pairs={{0,8},{1,9},{2,10},{3,11},{4,20},{5,21},{6,22},{7,23},{8,0},{9,1},... | collective-permute-start | bytes 1572872 | tf_op jit(solution)/shard_map/ppermute | solution.py:526
  179.6 12.7 %collective-permute-start.28 = (bf16[16,64,512]{2,1,0:T(8,128)(2,1)S(1)}, bf16[16,64,512]{2,1,0:T(8,128)(2,1)S(1)}, u32[]{:S(2)}, u32[]{:S(2)}) collective-permute-start(bf16[16,64,512]{2,1,0:T(8,128)(2,1)S(1)} %constant_dynamic-update-slice_fusion.5.low_ref), channel_id=1, source_target_pairs={{0,4},{4,0},{8,12},{12,8},{16,20},{20,16},{24,28},{28,24},{1,5},{5... | collective-permute-start | bytes 3145736 | tf_op jit(solution)/shard_map/ppermute | solution.py:508
  180.7 9.8 %collective-permute-start.24 = (bf16[3,512,128]{2,1,0:T(8,128)(2,1)S(1)}, bf16[3,512,128]{2,1,0:T(8,128)(2,1)S(1)}, u32[]{:S(2)}, u32[]{:S(2)}) collective-permute-start(bf16[3,512,128]{2,1,0:T(8,128)(2,1)S(1)} %get-tuple-element.179), channel_id=1, source_target_pairs={{0,2},{1,3},{2,0},{3,1},{4,5},{5,4},{6,7},{7,6},{8,10},{9,11},{10,... | collective-permute-start | bytes 1179656 | tf_op jit(solution)/shard_map/ppermute | solution.py:526

commit v3 on v2

v3 whole, which is shorter than its diff:
```python
import functools
import math

import jax
import jax.numpy as jnp
from jax import lax
from jax.experimental import pallas as pl
from jax.experimental.pallas import tpu as pltpu
from jax.sharding import PartitionSpec as P

D = 512
FF = 2048
H = 8
HD = 64
PAIRS = H // 2
BUCKETS = 32
PACKED_LENGTH = 512
EPSILON = 1e-06
BUCKET_EDGES = (12, 16, 23, 32, 46, 64, 91)
SPAN = 2 * PACKED_LENGTH
CHUNKS = 32
HALF = CHUNKS // 2
OUTER_ROWS = FF // CHUNKS
SMALL_ROWS = D // CHUNKS
FF_TILE = 512
MASKED = -1000000000.0
MIB = 1024 * 1024
F32 = jnp.float32
BF16 = jnp.bfloat16


SMALL_HALVINGS = 3
BEFORE_ROW = 2
ORDER = (
    "outer",
    "inner",
    "dx_start",
    "small_start",
    "small",
    "outer",
    "inner",
    "small",
    "outer",
    "inner",
    "small",
    "outer",
    "inner",
    "small",
    "outer",
    "inner",
    "small",
    "dx",
    "outer",
    "inner",
    "small",
    "finish_outer",
    "small",
    "finish_inner",
    "post",
    "small",
)


def dot(left, right, contract=(1, 0), precision=None):
    return lax.dot_general(
        left,
        right,
        (((contract[0],), (contract[1],)), ((), ())),
        preferred_element_type=F32,
        precision=precision,
    )


def xor_pairs(size, bit):
    return [(i, i ^ bit) for i in range(size)]


def bucket_of(relative):
    distance = jnp.abs(relative)
    beyond = jnp.full(distance.shape, 8, jnp.int32)
    for edge_value in BUCKET_EDGES:
        beyond = beyond + (distance >= edge_value).astype(jnp.int32)
    near = jnp.where(distance < 8, distance, beyond)
    return jnp.where(relative > 0, 16, 0).astype(jnp.int32) + near


def bucket_rows(shape, bucket_axis):
    place_axis = 1 - bucket_axis
    relative = lax.broadcasted_iota(jnp.int32, shape, place_axis) - PACKED_LENGTH
    return (bucket_of(relative) == lax.broadcasted_iota(jnp.int32, shape, bucket_axis)).astype(F32)


def split_heads(pair):
    lane = lax.broadcasted_iota(jnp.int32, pair.shape, 1)
    zero = jnp.zeros_like(pair)
    return jnp.concatenate(
        [jnp.where(lane < HD, pair, zero), jnp.where(lane >= HD, pair, zero)], axis=0
    )


def join_heads(stacked):
    half = stacked.shape[0] // 2
    lane = lax.broadcasted_iota(jnp.int32, (half, stacked.shape[1]), 1)
    return jnp.where(lane < HD, stacked[:half], stacked[half:])


def pack_kernel(x_ref, seen_ref, wire_ref, first_ref, *row_refs, here):
    count = x_ref.shape[0]
    flags = seen_ref[...].astype(F32)
    flags = jnp.concatenate([flags, jnp.zeros((16 - count, here), F32)], axis=0)
    tail = jnp.concatenate([flags, jnp.zeros((16, D - here), F32)], axis=1).astype(BF16)
    for row in range(count):
        wire_ref[row * here : (row + 1) * here] = x_ref[row]
        if row:
            row_refs[row - 1][...] = x_ref[row]
    wire_ref[count * here :] = tail
    first_ref[:here] = x_ref[0]
    first_ref[here:] = tail


def prepare_kernel(place_ref, table_ref, *refs, here, seq):
    count = (len(refs) - 3) // 2
    sources, bias_ref, targets = refs[:count], refs[count], refs[count + 1 : 2 * count + 1]
    line_ref, sems = refs[2 * count + 1 :]
    copies = [
        pltpu.make_async_copy(source, target, sems.at[i])
        for i, (source, target) in enumerate(zip(sources, targets))
    ]
    for copy in copies:
        copy.start()
    line_ref[...] = dot(
        table_ref[...], bucket_rows((BUCKETS, SPAN), 0), (0, 0), lax.Precision.HIGHEST
    )
    me = place_ref[0]
    for block in range(seq):
        offset = ((me ^ block) - me) * here + PACKED_LENGTH - here
        window = line_ref[:, pl.ds(pl.multiple_of(offset, 128), 2 * here)]
        for head in range(H):
            spread = jnp.broadcast_to(window[head : head + 1], (here, 2 * here))
            skewed = pltpu.roll(spread, here, 1, stride=1, stride_axis=0)
            row = (head % 2) * here
            bias_ref[head // 2, row : row + here, block * here : (block + 1) * here] = skewed[
                :, :here
            ]
    for copy in copies:
        copy.wait()


def attention_kernel(
    place_ref,
    lengths_ref,
    x0_ref,
    x1_ref,
    x2_ref,
    x3_ref,
    seen_ref,
    x1_tail_ref,
    x2_tail_ref,
    x3_tail_ref,
    gain_ref,
    gain_mlp_ref,
    bias_ref,
    wq_ref,
    wk_ref,
    wv_ref,
    w_out_ref,
    *refs,
    row,
    here,
    seq,
):
    (
        normed_mlp_ref,
        attended_ref,
        middle_ref,
        mixed_ref,
        normed_ref,
        q_ref,
        k_ref,
        v_ref,
        p_ref,
    ) = refs[-9:]
    me = place_ref[0]
    own_x = x0_ref[0].astype(F32)
    x = jnp.concatenate(
        [own_x] + [ref.astype(F32) for ref in (x1_ref[...], x2_ref[...], x3_ref[...])], axis=0
    )
    inv = lax.rsqrt(jnp.mean(x * x, -1, keepdims=True) + EPSILON)
    normed = (x * inv * gain_ref[...]).astype(BF16)
    normed_ref[...] = normed
    q = dot(normed[:here], wq_ref[...]).astype(BF16)
    k = dot(normed, wk_ref[...]).astype(BF16)
    v = dot(normed, wv_ref[...]).astype(BF16)
    q_ref[...] = q
    k_ref[...] = k
    v_ref[...] = v
    ends = [lengths_ref[row, 0]]
    for part in range(1, lengths_ref.shape[1]):
        ends.append(ends[-1] + lengths_ref[row, part])

    def segment(place):
        total = jnp.zeros(place.shape, jnp.int32)
        for end in ends:
            total = total + (end <= place).astype(jnp.int32)
        return total

    query_place = me * here + lax.broadcasted_iota(jnp.int32, (here, 1), 0)
    lane = lax.broadcasted_iota(jnp.int32, (1, here), 1)
    key_place = jnp.concatenate([(me ^ block) * here + lane for block in range(seq)], axis=1)
    seen = jnp.concatenate(
        [seen_ref[row : row + 1].astype(F32)]
        + [
            ref[...].astype(F32)[row : row + 1, :here]
            for ref in (x1_tail_ref, x2_tail_ref, x3_tail_ref)
        ],
        axis=1,
    )
    key_segment = jnp.where(seen == 1.0, segment(key_place), -1)
    allowed = (segment(query_place) == key_segment) | (query_place == key_place)
    allowed = jnp.concatenate([allowed.astype(jnp.int32)] * 2, axis=0) == 1
    attended = []
    for pair in range(PAIRS):
        lanes = slice(pair * 2 * HD, (pair + 1) * 2 * HD)
        scores = dot(split_heads(q[:, lanes]), k[:, lanes], (1, 1)) + bias_ref[pair]
        scores = jnp.where(allowed, scores, MASKED)
        exponent = jnp.exp(scores - jnp.max(scores, -1, keepdims=True))
        share = 1.0 / jnp.sum(exponent, -1, keepdims=True)
        probs = (exponent * share).astype(BF16)
        p_ref[pair] = probs
        mixed = join_heads(dot(probs, v[:, lanes]))
        mixed_ref[:, lanes] = mixed
        attended.append(mixed.astype(BF16))
    attended = jnp.concatenate(attended, axis=1)
    attended_ref[...] = attended
    middle = own_x + dot(attended, w_out_ref[...])
    middle_ref[...] = middle
    inv = lax.rsqrt(jnp.mean(middle * middle, -1, keepdims=True) + EPSILON)
    normed_mlp_ref[...] = (middle * inv * gain_mlp_ref[...]).astype(BF16)


def gelu_both(u):
    scale = 0.7978845608028654
    square = u * u
    t = jnp.tanh(u * (scale + (scale * 0.044715) * square))
    half_up = 0.5 + 0.5 * t
    slope = half_up + (0.5 * u) * (1.0 - t * t) * (scale + (3.0 * 0.044715 * scale) * square)
    return u * half_up, slope


def mlp_kernel(code_ref, *refs, rows, own_half):
    nm_refs = refs[:rows]
    g_ref, w_inner_ref, w_outer_ref, total_ref, back_ref, outer_ref, inner_ref = refs[rows:]
    step = pl.program_id(0)
    label = code_ref[1] if own_half else code_ref[2]
    normed = jnp.concatenate([ref[...] for ref in nm_refs], axis=0)
    g = g_ref[...].reshape(normed.shape)
    w_inner = w_inner_ref[...]
    w_outer = w_outer_ref[...]
    active_f, slope = gelu_both(dot(normed, w_inner))
    active = active_f.astype(BF16)
    grad_act = (dot(g, w_outer, (1, 1)) * slope).astype(BF16)

    @pl.when(step == 0)
    def _():
        total_ref[...] = jnp.zeros_like(total_ref)
        back_ref[...] = jnp.zeros_like(back_ref)

    total_ref[...] += dot(active, w_outer)
    back_ref[...] += dot(grad_act, w_inner, (1, 1))
    outer = dot(active, g, (0, 0)).astype(BF16)
    inner = dot(grad_act, normed, (0, 0)).astype(BF16)
    for part in range(FF_TILE // OUTER_ROWS):
        slot = (step * (FF_TILE // OUTER_ROWS) + part) ^ label
        rows = slice(part * OUTER_ROWS, (part + 1) * OUTER_ROWS)
        outer_ref[slot] = outer[rows]
        inner_ref[slot] = inner[rows]


def back_kernel(place_ref, code_ref, *refs, row, last, here, seq):
    _, attended_ref, middle_ref, mixed_ref, normed_ref, q_ref, k_ref, v_ref, p_ref = refs[:9]
    (
        g_ref,
        total_a_ref,
        total_b_ref,
        back_a_ref,
        back_b_ref,
        gain_mlp_ref,
        w_out_ref,
        wq_ref,
        wk_ref,
        wv_ref,
        _,
    ) = refs[9:20]
    refs = refs[20:]
    old = refs[:6] if row else None
    refs = refs[6:] if row else refs
    if last:
        gain_attn_ref = refs[0]
        refs = refs[1:]
    if row:
        refs = refs[1:]
    block_output_ref, grad_middle_ref, dx_keep_ref, dx_send_ref = refs[:4]
    if last:
        keep_ref, send_ref, rider_ref, line_ref = refs[4:8]
        sums = refs[8:14]
    else:
        sums = refs[4:10]

    def accumulate(which, value, part=None):
        if part is None:
            sums[which][...] = value + old[which][...] if row else value
        else:
            sums[which][part] = value + old[which][part] if row else value

    index = row
    tokens = slice(index * here, (index + 1) * here)
    middle = middle_ref[...]
    back = back_a_ref[tokens] + back_b_ref[tokens]
    block_output_ref[0] = (middle + total_a_ref[tokens] + total_b_ref[tokens]).astype(BF16)
    inv = lax.rsqrt(jnp.mean(middle * middle, -1, keepdims=True) + EPSILON)
    accumulate(5, jnp.sum(back * middle * inv, axis=0, keepdims=True))
    scaled = back * gain_mlp_ref[...]
    grad_middle = (
        g_ref[row].astype(F32)
        + inv * scaled
        - middle * (inv * inv * inv) * jnp.mean(scaled * middle, -1, keepdims=True)
    )
    grad_middle_ref[...] = grad_middle
    branch = grad_middle.astype(BF16)
    ga = dot(branch, w_out_ref[...], (1, 1)).astype(BF16)

    accumulate(0, dot(attended_ref[...], branch, (0, 0)))
    q = q_ref[...]
    k = k_ref[...]
    v = v_ref[...]
    normed = normed_ref[...]
    dq, dkt, dvt = [], [], []
    for pair in range(PAIRS):
        lanes = slice(pair * 2 * HD, (pair + 1) * 2 * HD)
        ga_split = split_heads(ga[:, lanes])
        q_split = split_heads(q[:, lanes])
        mixed = mixed_ref[:, lanes]
        probs = p_ref[pair]
        delta = jnp.sum(
            ga_split.astype(F32) * jnp.concatenate([mixed, mixed], axis=0), -1, keepdims=True
        )
        grad_probs = dot(ga_split, v[:, lanes], (1, 1))
        grad_scores_f = probs.astype(F32) * (grad_probs - delta)
        accumulate(4, grad_scores_f, pair)
        grad_scores = grad_scores_f.astype(BF16)
        dq.append(join_heads(dot(grad_scores, k[:, lanes])).astype(BF16))
        dkt.append(dot(q_split, grad_scores, (0, 0)).astype(BF16))
        dvt.append(dot(ga_split, probs, (0, 0)).astype(BF16))
    dq = jnp.concatenate(dq, axis=1)
    dkt = jnp.concatenate(dkt, axis=0)
    dvt = jnp.concatenate(dvt, axis=0)
    dxt = dot(wk_ref[...], dkt) + dot(wv_ref[...], dvt)
    own = dxt[:, :here] + dot(wq_ref[...], dq, (1, 1))
    pieces = [own] + [dxt[:, block * here : (block + 1) * here] for block in range(1, seq)]
    pieces = [piece.astype(BF16) for piece in pieces]
    dx_keep_ref[0] = pieces[0]
    dx_send_ref[1] = pieces[3]

    @pl.when(code_ref[0] == 0)
    def _():
        dx_keep_ref[1] = pieces[2]
        dx_send_ref[0] = pieces[1]

    @pl.when(code_ref[0] == 1)
    def _():
        dx_keep_ref[1] = pieces[1]
        dx_send_ref[0] = pieces[2]

    accumulate(1, dot(normed[:here], dq, (0, 0)))
    accumulate(2, dot(dkt, normed))
    accumulate(3, dot(dvt, normed))

    if not last:
        return
    me = place_ref[0]
    line_ref[...] = jnp.zeros_like(line_ref)
    for block in range(seq):
        offset = ((me ^ block) - me) * here + PACKED_LENGTH - here
        window = pl.ds(pl.multiple_of(offset, 128), 2 * here)
        for head in range(H):
            row = (head % 2) * here
            tile = sums[4][head // 2, row : row + here, block * here : (block + 1) * here]
            total = jnp.zeros((8, 2 * here), F32)
            empty = jnp.zeros((8, here), F32)
            for group in range(here // 8):
                wide = jnp.concatenate([tile[group * 8 : group * 8 + 8], empty], axis=1)
                total = total + pltpu.roll(wide, here - 8 * group, 1)
            line_ref[head * 8 : head * 8 + 8, window] += total
    lines = line_ref[...]
    sub = lax.broadcasted_iota(jnp.int32, lines.shape, 0)
    for bit in (1, 2, 4):
        lines = jnp.where((sub & bit) != 0, pltpu.roll(lines, SPAN - bit, 1), lines)
    by_head = jnp.concatenate(
        [jnp.sum(lines[h * 8 : h * 8 + 8], axis=0, keepdims=True) for h in range(H)], axis=0
    )
    table = dot(by_head, bucket_rows((SPAN, 128), 1), (1, 0), lax.Precision.HIGHEST)
    go_ref, gq_ref, gk_ref, gv_ref = sums[:4]
    gk_ref[...] = gk_ref[...].T
    gv_ref[...] = gv_ref[...].T
    gain = (
        wq_ref[...].astype(F32) * gq_ref[...]
        + wk_ref[...].astype(F32) * gk_ref[...]
        + wv_ref[...].astype(F32) * gv_ref[...]
    )
    gain_grad = dot(jnp.ones((8, D), F32), gain, (1, 1), lax.Precision.HIGHEST)
    rider = jnp.concatenate(
        [
            jnp.concatenate([table, jnp.zeros((8, D - 128), F32)], axis=1),
            gain_grad[:1] / gain_attn_ref[...],
            sums[5][...],
            jnp.zeros((6, D), F32),
        ],
        axis=0,
    )
    rider_ref[...] = rider
    high = rider.astype(BF16)
    base = HALF * 4 * SMALL_ROWS
    send_ref[base : base + 16, :] = high
    send_ref[base + 16 : base + 32, :] = (rider - high.astype(F32)).astype(BF16)
    core, label, other = code_ref[0], code_ref[1], code_ref[2]
    for index, grad_ref in enumerate((go_ref, gq_ref, gk_ref, gv_ref)):
        for slot in range(HALF):
            chunk = core * HALF + (slot ^ label)
            first = pl.multiple_of(chunk * SMALL_ROWS, SMALL_ROWS)
            rows_to = slice(index * SMALL_ROWS, (index + 1) * SMALL_ROWS)
            keep_ref[slot, rows_to] = grad_ref[pl.ds(first, SMALL_ROWS), :].astype(BF16)
            chunk = (1 - core) * HALF + (slot ^ other)
            first = pl.multiple_of(chunk * SMALL_ROWS, SMALL_ROWS)
            start = (slot * 4 + index) * SMALL_ROWS
            send_ref[start : start + SMALL_ROWS, :] = grad_ref[
                pl.ds(first, SMALL_ROWS), :
            ].astype(BF16)


def pick(code_ref, low_ref, high_ref, chunk, use):
    core, label, other = code_ref[0], code_ref[1], code_ref[2]

    @pl.when(core == chunk[0])
    def _():
        use(low_ref, chunk[1] ^ label)

    @pl.when(core != chunk[0])
    def _():
        use(high_ref, chunk[1] ^ other)


def finish_mlp_kernel(code_ref, low_ref, high_ref, out_ref, stage_ref, *, turned):
    step = pl.program_id(0)
    per_step = FF_TILE // OUTER_ROWS
    target = stage_ref if turned else out_ref
    for part in range(per_step):
        chunk = step * per_step + part
        rows = slice(part * OUTER_ROWS, (part + 1) * OUTER_ROWS)

        def use(ref, slot):
            target[rows, :] = ref[slot].astype(F32)

        pick(code_ref, low_ref, high_ref, (chunk // HALF, chunk % HALF), use)
    if turned:
        out_ref[...] = stage_ref[...].T


def finish_attention_kernel(code_ref, half_ref, *refs, own_half):
    out_refs = refs[-4:]
    label = code_ref[1] if own_half else code_ref[2]
    for part in range(HALF):
        rows = slice(part * SMALL_ROWS, (part + 1) * SMALL_ROWS)
        for index, out_ref in enumerate(out_refs):
            out_ref[rows, :] = half_ref[
                part ^ label, index * SMALL_ROWS : (index + 1) * SMALL_ROWS
            ].astype(F32)


def post_kernel(a_ref, b_ref, x_ref, gain_ref, *refs):
    grad_middle_refs, out_ref = refs[:-1], refs[-1]
    for row, grad_middle_ref in enumerate(grad_middle_refs):
        back = (a_ref[row].astype(F32) + b_ref[row].astype(F32)).T
        x = x_ref[row].astype(F32)
        inv = lax.rsqrt(jnp.mean(x * x, -1, keepdims=True) + EPSILON)
        scaled = back * gain_ref[...]
        grad = inv * scaled - x * (inv * inv * inv) * jnp.mean(scaled * x, -1, keepdims=True)
        out_ref[row] = (grad_middle_ref[...] + grad).astype(BF16)


ANYWHERE = pl.BlockSpec(memory_space=pl.ANY)


def whole(shape):
    return pl.BlockSpec(shape, lambda *_: (0,) * len(shape))


def by_row(shape):
    return pl.BlockSpec((1,) + shape[1:], lambda i, *_: (i,) + (0,) * (len(shape) - 1))


def one_row(shape, row):
    return pl.BlockSpec((1,) + shape[1:], lambda *_: (row,) + (0,) * (len(shape) - 1))


def shaped(shape, dtype):
    return jax.ShapeDtypeStruct(shape, dtype)


def call(
    kernel,
    grid,
    prefetch,
    inputs,
    in_specs,
    outs,
    out_specs,
    scratch=(),
    flops=0,
    name=None,
    aliases=None,
    vmem=16,
):
    return pl.pallas_call(
        kernel,
        out_shape=outs,
        grid_spec=pltpu.PrefetchScalarGridSpec(
            num_scalar_prefetch=len(prefetch),
            grid=grid,
            in_specs=in_specs,
            out_specs=out_specs,
            scratch_shapes=list(scratch),
        ),
        compiler_params=pltpu.CompilerParams(
            dimension_semantics=("arbitrary",) * len(grid), vmem_limit_bytes=vmem * MIB
        ),
        cost_estimate=pl.CostEstimate(flops=flops, bytes_accessed=flops // 256, transcendentals=0),
        input_output_aliases=aliases or {},
        name=name,
    )(*prefetch, *inputs)


def add(*parts):
    total = parts[0].astype(F32)
    for part in parts[1:]:
        total = total + part.astype(F32)
    return total


def make_body(rows, seq):
    both = ("rows", "seq")
    further = [1 << i for i in range(3, rows.bit_length() - 1)]

    def swap_rows(array, bit):
        return lax.ppermute(array, "rows", [(i, i ^ bit) for i in range(rows)])

    def swap_seq(array, bit):
        return lax.ppermute(array, "seq", [(i, i ^ bit) for i in range(seq)])

    def swap_step(array, step):
        def partner(r, z):
            first, second = ((0, 2), (0, 4)), ((1, 1), (1, 2))
            if r & 1:
                first, second = first[::-1], second[::-1]
            axis, bit = (first + second)[step]
            return (r, z ^ bit) if axis else (r ^ bit, z)

        pairs = []
        for r in range(rows):
            for z in range(seq):
                to_r, to_z = partner(r, z)
                pairs.append((r * seq + z, to_r * seq + to_z))
        return lax.ppermute(array, both, pairs)

    def codes():
        r, z = lax.axis_index("rows"), lax.axis_index("seq")
        core = r & 1
        b1, b2, z0, z1 = (r >> 1) & 1, (r >> 2) & 1, z & 1, (z >> 1) & 1
        even = b1 * 8 + b2 * 4 + z0 * 2 + z1
        odd = b2 * 8 + b1 * 4 + z1 * 2 + z0
        label = jnp.where(core == 0, even, odd)
        other = jnp.where(core == 0, odd, even)
        return jnp.stack([core, label, other]).astype(jnp.int32)

    def after(array, *earlier):
        return lax.optimization_barrier((array, *earlier))[0]

    def two_parts(rider):
        high = rider.astype(BF16)
        return [high, (rider - high.astype(F32)).astype(BF16)]

    class Reduction:
        def __init__(self, wire, shape, halvings, rider=None):
            self.rider = rider
            self.slots, self.rows_each = shape[:2]
            self.halvings = halvings
            self.step = 0
            self.spreading = False
            self.parts = [None]
            self.arrived = swap_rows(wire, 1)

        def send(self, outgoing):
            if self.rider is not None:
                flat = outgoing.reshape(-1, D)
                outgoing = jnp.concatenate([flat] + two_parts(self.rider), axis=0)
            self.slots = outgoing.shape[0] if self.rider is None else flat.shape[0] // self.rows_each
            self.arrived = swap_step(outgoing, self.step)
            self.step += 1

        def receive(self, earlier):
            array = after(self.arrived, *earlier)
            if self.rider is not None:
                size = self.slots * self.rows_each
                extra = array[size:].astype(F32)
                high, low = two_parts(self.rider)
                self.rider = (high.astype(F32) + low.astype(F32)) + (extra[:16] + extra[16:])
                array = array[:size].reshape(self.slots, self.rows_each, D)
            return array

        def advance(self, *earlier):
            if self.spreading:
                held = jnp.concatenate([self.held, after(self.arrived, *earlier)])
            else:
                self.parts.append(self.receive(earlier))
                if self.step < self.halvings:
                    size = self.parts[0].shape[0] // 2
                    outgoing = add(*[part[size:] for part in self.parts]).astype(BF16)
                    self.parts = [part[:size] for part in self.parts]
                    self.send(outgoing)
                    return outgoing
                held = add(*self.parts)
                if self.step < 4:
                    held = held.astype(BF16)
                    size = 8 >> self.step
                    order = [slot ^ size for slot in range(held.shape[0])]
                    self.parts = [held]
                    self.send(jnp.concatenate([held[slot : slot + 1] for slot in order]))
                    return held
                for bit in further:
                    held = held + swap_rows(held, bit)
                    if self.rider is not None:
                        self.rider = self.rider + swap_rows(self.rider, bit)
                held = held.astype(BF16)
                self.spreading = True
                self.step = self.halvings
            self.held = held
            self.step -= 1
            if self.step >= 0:
                self.arrived = swap_step(held, self.step)
            else:
                self.arrived = swap_rows(held, 1)
            return held

    def body(
        block_input,
        cotangent,
        gain_attn,
        w_query,
        w_key,
        w_value,
        w_out,
        gain_mlp,
        w_inner,
        outer_weight,
        bias_table,
        lengths,
        observed,
    ):
        count, here = block_input.shape[0], block_input.shape[1]
        tokens = count * here
        last = count - 1
        place = lax.axis_index("seq").astype(jnp.int32).reshape(1)
        code = codes()
        gain_attn_row = gain_attn.reshape(1, D)
        gain_mlp_row = gain_mlp.reshape(1, D)

        def in_hbm(array):
            return pltpu.with_memory_space_constraint(array, pltpu.HBM)

        stacked = (PAIRS, 2 * here, PACKED_LENGTH)
        one = (here, D)
        own = (count, here, D)
        full = (PACKED_LENGTH, D)
        square = whole((D, D))
        line = whole((1, D))

        wire, *x2 = call(
            functools.partial(pack_kernel, here=here),
            (1,),
            (),
            (block_input, observed),
            [whole(own), whole(observed.shape)],
            [shaped((tokens + 16, D), BF16), shaped((here + 16, D), BF16)]
            + [shaped(one, BF16)] * (count - 1),
            [whole((tokens + 16, D)), whole((here + 16, D))] + [whole(one)] * (count - 1),
            name="pack",
            vmem=8,
        )
        x2 = [swap_seq(x, 2) for x in x2]
        x1 = swap_seq(wire, 1)
        *x2, bias_table = lax.optimization_barrier((*x2, bias_table))
        x3 = [swap_seq(x, 1) for x in x2]
        resident = (w_query, w_key, w_value, w_out)
        resident = call(
            functools.partial(prepare_kernel, here=here, seq=seq),
            (1,),
            (place,),
            (bias_table, *[in_hbm(array) for array in resident]),
            [whole(bias_table.shape)] + [ANYWHERE] * len(resident),
            [pltpu.VMEM(stacked, F32)]
            + [pltpu.VMEM(array.shape, array.dtype) for array in resident],
            [whole(stacked)] + [whole(array.shape) for array in resident],
            [pltpu.VMEM((H, SPAN), F32), pltpu.SemaphoreType.DMA((len(resident),))],
            name="prepare",
            vmem=4,
        )
        kept = []
        kept_shapes = [
            pltpu.VMEM(one, BF16),
            pltpu.VMEM(one, BF16),
            pltpu.VMEM(one, F32),
            pltpu.VMEM(one, F32),
            pltpu.VMEM(full, BF16),
            pltpu.VMEM(one, BF16),
            pltpu.VMEM(full, BF16),
            pltpu.VMEM(full, BF16),
            pltpu.VMEM(stacked, BF16),
        ]
        for row in range(count):
            *resident, nm, attended, middle, mixed, normed, q, k, v, p = call(
                functools.partial(attention_kernel, row=row, here=here, seq=seq),
                (1,),
                (place, lengths),
                [block_input, x1, x2[row], x3[row], observed, x1, x2[0], x3[0]]
                + [gain_attn_row, gain_mlp_row, *resident],
                [
                    one_row(own, row),
                    pl.BlockSpec(one, lambda *_, row=row: (row, 0)),
                    whole(one),
                    whole(one),
                    whole(observed.shape),
                    pl.BlockSpec((16, D), lambda *_: (tokens // 16, 0)),
                    pl.BlockSpec((16, D), lambda *_: (here // 16, 0)),
                    pl.BlockSpec((16, D), lambda *_: (here // 16, 0)),
                ]
                + [line] * 2
                + [whole(stacked)]
                + [square] * 4,
                [pltpu.VMEM(array.shape, array.dtype) for array in resident] + kept_shapes,
                [ANYWHERE] * len(resident) + [whole(shape.shape) for shape in kept_shapes],
                flops=8 * here * D * PACKED_LENGTH,
                name="attention",
                vmem=12,
                aliases={12 + i: i for i in range(len(resident))},
            )
            kept.append((nm, attended, middle, mixed, normed, q, k, v, p))
        _, w_query, w_key, w_value, w_out = resident
        normed_mlp = [part[0] for part in kept]

        flat = (tokens, D)
        steps = FF // FF_TILE // 2
        part_shape = (HALF, OUTER_ROWS, D)

        def mlp_part(own_half, nm):
            def tile(i, code):
                return (code[0] if own_half else 1 - code[0]) * steps + i

            return call(
                functools.partial(mlp_kernel, rows=count, own_half=own_half),
                (steps,),
                (code,),
                [*nm, in_hbm(cotangent), in_hbm(w_inner), in_hbm(outer_weight)],
                [whole(one)] * count
                + [
                    whole(own),
                    pl.BlockSpec((D, FF_TILE), lambda i, n: (0, tile(i, n))),
                    pl.BlockSpec((FF_TILE, D), lambda i, n: (tile(i, n), 0)),
                ],
                [pltpu.VMEM(flat, F32)] * 2 + [pltpu.HBM(part_shape, BF16)] * 2,
                [whole(flat)] * 2 + [whole(part_shape)] * 2,
                flops=6 * tokens * D * FF,
                name="mlp",
                vmem=20,
            )

        total_a, back_a, outer_send, inner_send = mlp_part(False, normed_mlp)
        chains = {
            "outer": Reduction(outer_send, part_shape, 3),
            "inner": Reduction(inner_send, part_shape, 3),
        }
        nm = [after(normed_mlp[0], total_a)] + normed_mlp[1:]
        total_b, back_b, outer_keep, inner_keep = mlp_part(True, nm)
        chains["outer"].parts[0] = outer_keep
        chains["inner"].parts[0] = inner_keep

        small_half = (HALF, 4 * SMALL_ROWS, D)
        small_wire = (HALF * 4 * SMALL_ROWS + 32, D)
        done = chains["outer"].advance()
        done = chains["inner"].advance(done)
        dx_half = (seq // 2, D, here)
        sum_shapes = [pltpu.VMEM((D, D), F32)] * 4
        sum_shapes += [pltpu.VMEM(stacked, F32), pltpu.VMEM((1, D), F32)]
        sums, block_output = (), ()
        grad_middles, dx_keeps, dx_sends = [], [], []
        for row in range(count):
            end = row == count - 1
            inputs = [*kept[row], cotangent, total_a, total_b, back_a, back_b, gain_mlp_row]
            inputs += [w_out, w_query, w_key, w_value, done, *sums]
            specs = [whole(shape.shape) for shape in kept_shapes] + [whole(own)]
            specs += [whole(flat)] * 4 + [line] + [square] * 4 + [ANYWHERE]
            specs += [whole(shape.shape) for shape in sum_shapes[: len(sums)]]
            if end:
                inputs.append(gain_attn_row)
                specs.append(line)
            if row:
                inputs.append(block_output)
                specs.append(ANYWHERE)
            aliases = {len(inputs) + 1: 0} if row else {}
            outs = [pltpu.HBM(own, BF16), pltpu.HBM(one, F32)] + [shaped(dx_half, BF16)] * 2
            out_specs = [one_row(own, row), whole(one)] + [whole(dx_half)] * 2
            if end:
                outs += [shaped(small_half, BF16), shaped(small_wire, BF16), shaped((16, D), F32)]
                out_specs += [whole(small_half), whole(small_wire), whole((16, D))]
                scratch = [pltpu.VMEM((8 * H, SPAN), F32)]
                scratch += [pltpu.VMEM(shape.shape, shape.dtype) for shape in sum_shapes]
            else:
                outs += sum_shapes
                out_specs += [whole(shape.shape) for shape in sum_shapes]
                scratch = []
                if row:
                    aliases |= {22 + i: 4 + i for i in range(len(sums))}
            block_output, grad_middle, dx_keep, dx_send, *sums = call(
                functools.partial(back_kernel, row=row, last=end, here=here, seq=seq),
                (1,),
                (place, code),
                inputs,
                specs,
                outs,
                out_specs,
                scratch,
                flops=20 * here * D * PACKED_LENGTH,
                name="attention_back",
                vmem=24 if end else 14,
                aliases=aliases,
            )
            done = grad_middle
            if row == BEFORE_ROW - 1:
                done = chains["outer"].advance(done)
                done = chains["inner"].advance(done)
            grad_middles.append(grad_middle)
            dx_keeps.append(dx_keep)
            dx_sends.append(dx_send)
        small_keep, small_send, rider = sums
        dx_arrived = [swap_step(dx_send, 2) for dx_send in dx_sends[:-1]]
        for event in ORDER:
            if event in chains:
                done = chains[event].advance(done)
            elif event == "small_start":
                chains["small"] = Reduction(
                    after(small_send, done), small_half, SMALL_HALVINGS, rider
                )
                chains["small"].parts[0] = small_keep
            elif event == "dx_start":
                *dx_arrived, done = lax.optimization_barrier((*dx_arrived, done))
                dx_half = [
                    [add(x[i], y[i]).astype(BF16) for x, y in zip(dx_keeps, dx_arrived)]
                    for i in range(2)
                ]
                dx_arrived = swap_step(after(dx_sends[-1], dx_half[0][-1]), 2)
                done = dx_half[1][-1]
            elif event == "dx":
                dx_arrived = after(dx_arrived, done)
                half_kept, half_sent = [
                    jnp.stack(dx_half[i] + [add(dx_keeps[-1][i], dx_arrived[i]).astype(BF16)])
                    for i in range(2)
                ]
                dx_last = swap_step(half_sent, 3)
                done = half_sent
            elif event == "post":
                input_grad = call(
                    post_kernel,
                    (1,),
                    (),
                    (half_kept, after(dx_last, done), block_input, gain_attn_row, *grad_middles),
                    [whole(half_kept.shape)] * 2 + [whole(own), line] + [whole(one)] * count,
                    [shaped(own, BF16)],
                    [whole(own)],
                    name="post",
                )[0]
                done = input_grad
            elif event == "finish_outer":
                chain = chains["outer"]
                grad_outer = call(
                    functools.partial(finish_mlp_kernel, turned=False),
                    (FF // FF_TILE,),
                    (code,),
                    (chain.held, after(chain.arrived, done)),
                    [whole(part_shape)] * 2,
                    [shaped((FF, D), F32)],
                    [pl.BlockSpec((FF_TILE, D), lambda i, *_: (i, 0))],
                    [pltpu.VMEM((8, 128), F32)],
                    name="finish_outer",
                )[0]
                done = grad_outer
            elif event == "finish_inner":
                chain = chains["inner"]
                grad_inner = call(
                    functools.partial(finish_mlp_kernel, turned=True),
                    (FF // FF_TILE,),
                    (code,),
                    (chain.held, after(chain.arrived, done)),
                    [whole(part_shape)] * 2,
                    [shaped((D, FF), F32)],
                    [pl.BlockSpec((D, FF_TILE), lambda i, *_: (0, i))],
                    [pltpu.VMEM((FF_TILE, D), F32)],
                    name="finish_inner",
                )[0]
                done = grad_inner
        chain = chains["small"]
        grads = ()
        for own_half in (True, False):
            half = chain.held if own_half else after(chain.arrived, grads[0])

            def half_of(i, code):
                return (code[0] if own_half else 1 - code[0], 0)

            grads = call(
                functools.partial(finish_attention_kernel, own_half=own_half),
                (1,),
                (code,),
                (half, *grads),
                [whole(small_half)] + [ANYWHERE] * len(grads),
                [shaped((D, D), F32)] * 4,
                [pl.BlockSpec((D // 2, D), half_of)] * 4,
                name="finish_attention",
                aliases={2 + i: i for i in range(len(grads))},
            )
        grad_out, grad_query, grad_key, grad_value = grads
        rider = chain.rider

        return (
            block_output,
            input_grad,
            rider[8],
            grad_query,
            grad_key,
            grad_value,
            grad_out,
            rider[9],
            grad_inner,
            grad_outer,
            rider[:H, :BUCKETS].T,
        )

    return body


def solution(mesh):
    split = P("rows", "seq", None)
    placed = (split, split) + (P(),) * 9 + (P("rows", None), P("rows", "seq"))
    return jax.shard_map(
        make_body(mesh.shape["rows"], mesh.shape["seq"]),
        mesh=mesh,
        in_specs=placed,
        out_specs=(split, split) + (P(),) * 9,
        check_vma=False,
    )
```

time: 203 us -> 173 us (0.85); the launches traced: 200 us -> 172 us
  waiting for transfers between devices: 89.2 us -> 55.2 us
  starting transfers between devices: 40.2 us -> 50.6 us
  local copies, waits for them, and re-layouts: 14.5 us -> 4.78 us
  Pallas kernels: 51.3 us -> 55.8 us
    ppermute x18 -> x25, waiting for transfers between devices: 78.6 us -> 42.8 us  [swap_step(): return lax.ppermute(array, both, pairs)]
    ppermute x18 -> x25, starting transfers between devices: 15 us -> 28.8 us  [swap_step(): return lax.ppermute(array, both, pairs)]
    unnamed x57 -> x26, local copies, waits for them, and re-layouts: 11.3 us -> 2.66 us
    ppermute x4 -> x6, starting transfers between devices: 14.7 us -> 10.2 us  [swap_rows(): return lax.ppermute(array, 'rows', [(i, i ^ bit) for i in range(rows)])]
    pallas_call x10 -> x15, Pallas kernels: 51.3 us -> 55.8 us  [call(): pl.pallas_call(kernel, out_shape=outs, grid_spec=pltpu.PrefetchScalarGrid...]
    ppermute x8 -> x7, waiting for transfers between devices: 9.32 us -> 12.3 us  [swap_seq(): return lax.ppermute(array, 'seq', [(i, i ^ bit) for i in range(seq)])]
    ppermute x8 -> x7, starting transfers between devices: 10.5 us -> 11.5 us  [swap_seq(): return lax.ppermute(array, 'seq', [(i, i ^ bit) for i in range(seq)])]
  transfers between devices with their start and end apart: 30 -> 38, of which waited for: 19 -> 15; matrix products, arithmetic and copies ran while one was open for 3% -> 4% of each run, Pallas kernels for 18% -> 25%
where the time goes in v3:
time: 173 us; the launch traced here: 172 us
  Pallas kernels  55.8 us (32%)
  waiting for transfers between devices  55.2 us (32%)
  starting transfers between devices  50.6 us (29%)
  local copies, waits for them, and re-layouts  4.78 us (3%)
  other arithmetic  4.65 us (3%)
    pallas_call x15, Pallas kernels, call(): pl.pallas_call(kernel, out_shape=outs, grid_spec=pltpu.PrefetchScalarGrid...  55.8 us
    ppermute x25, waiting for transfers between devices, swap_step(): return lax.ppermute(array, both, pairs)  42.8 us
    ppermute x25, starting transfers between devices, swap_step(): return lax.ppermute(array, both, pairs)  28.8 us
    ppermute x7, waiting for transfers between devices, swap_seq(): return lax.ppermute(array, 'seq', [(i, i ^ bit) for i in range(seq)])  12.3 us
    ppermute x7, starting transfers between devices, swap_seq(): return lax.ppermute(array, 'seq', [(i, i ^ bit) for i in range(seq)])  11.5 us
    ppermute x6, starting transfers between devices, swap_rows(): return lax.ppermute(array, 'rows', [(i, i ^ bit) for i in range(rows)])  10.2 us
  transfers between devices with their start and end apart: 38, of which 15 were waited for; matrix products, arithmetic and copies ran while one was open for 4% of the time, Pallas kernels for 25%

profile of v3, /device:TPU:1, one launch (start us, length us, event | category | flops | bytes accessed | tf_op | source)
XLA Modules:
  0.0 172.2 jit_solution(2319726650890439051)
XLA Ops:
  0.7 1.0 copy-done
  1.6 0.7 copy-done.8
  2.4 2.2 %collective-permute-start = (bf16[400,512]{1,0:T(8,128)(2,1)S(1)}, bf16[400,512]{1,0:T(8,128)(2,1)S(1)}, u32[]{:S(2)}, u32[]{:S(2)}) collective-permute-start(bf16[400,512]{1,0:T(8,128)(2,1)S(1)} %get-tuple-element.140), channel_id=1, source_target_pairs={{0,1},{1,0},{2,3},{3,2},{4,5},{5,4},{6,7},{7,6},{8,9},{9,8},{10,11... | collective-permute-start | bytes 1228808 | tf_op jit(solution)/shard_map/ppermute | solution.py:557
  4.6 2.3 %collective-permute-start.1 = (bf16[144,512]{1,0:T(8,128)(2,1)S(1)}, bf16[144,512]{1,0:T(8,128)(2,1)S(1)}, u32[]{:S(2)}, u32[]{:S(2)}) collective-permute-start(bf16[144,512]{1,0:T(8,128)(2,1)S(1)} %get-tuple-element.141), channel_id=1, source_target_pairs={{0,2},{1,3},{2,0},{3,1},{4,6},{5,7},{6,4},{7,5},{8,10},{9,11},{10,... | collective-permute-start | bytes 442376 | tf_op jit(solution)/shard_map/ppermute | solution.py:557
  7.0 2.3 %collective-permute-start.3 = (bf16[128,512]{1,0:T(8,128)(2,1)S(1)}, bf16[128,512]{1,0:T(8,128)(2,1)S(1)}, u32[]{:S(2)}, u32[]{:S(2)}) collective-permute-start(bf16[128,512]{1,0:T(8,128)(2,1)S(1)} %get-tuple-element.143), channel_id=1, source_target_pairs={{0,2},{1,3},{2,0},{3,1},{4,6},{5,7},{6,4},{7,5},{8,10},{9,11},{10,... | collective-permute-start | bytes 393224 | tf_op jit(solution)/shard_map/ppermute | solution.py:557
  9.3 9.5 %collective-permute-done.2.x2_ref = bf16[128,512]{1,0:T(8,128)(2,1)S(1)} collective-permute-done((bf16[128,512]{1,0:T(8,128)(2,1)S(1)}, bf16[128,512]{1,0:T(8,128)(2,1)S(1)}, u32[]{:S(2)}, u32[]{:S(2)}) %collective-permute-start.2) | collective-permute-done | bytes 131104 | tf_op jit(solution)/shard_map/ppermute | solution.py:557
  18.7 2.8 %collective-permute-done.3.x2_ref = bf16[128,512]{1,0:T(8,128)(2,1)S(1)} collective-permute-done((bf16[128,512]{1,0:T(8,128)(2,1)S(1)}, bf16[128,512]{1,0:T(8,128)(2,1)S(1)}, u32[]{:S(2)}, u32[]{:S(2)}) %collective-permute-start.3) | collective-permute-done | bytes 131104 | tf_op jit(solution)/shard_map/ppermute | solution.py:557
  21.6 3.2 %collective-permute-start.5 = (bf16[144,512]{1,0:T(8,128)(2,1)S(1)}, bf16[144,512]{1,0:T(8,128)(2,1)S(1)}, u32[]{:S(2)}, u32[]{:S(2)}) collective-permute-start(bf16[144,512]{1,0:T(8,128)(2,1)S(1)} %collective-permute-done.1.x2_ref.x2_tail_ref), channel_id=1, source_target_pairs={{0,1},{1,0},{2,3},{3,2},{4,5},{5,4},{6,7},{7,6},{8,9},{9,8},{10,11... | collective-permute-start | bytes 442376 | tf_op jit(solution)/shard_map/ppermute | solution.py:557
  24.8 1.4 collective-permute-start.6
  26.3 0.8 copy.51.table_ref
  27.1 2.7 %prepare.1 = (f32[4,256,512]{2,1,0:T(8,128)S(1)}, bf16[512,512]{1,0:T(8,128)(2,1)S(1)}, bf16[512,512]{1,0:T(8,128)(2,1)S(1)}, bf16[512,512]{1,0:T(8,128)(2,1)S(1)}, bf16[512,512]{1,0:T(8,128)(2,1)S(1)}) custom-call(s32[1]{0:T(128)} %bitcast.place_ref, f32[32,8]{1,0:T(8,128)S(1)} %copy.51.table_ref, bf16[512,512]{1,0:T(8,128)(2,1)} %refs_0_.1, ...), custom_call_target="tpu_custom_call" | custom-call | tf_op jit(solution)/shard_map/prepare/pallas_call | solution.py:523
  29.9 3.4 %attention.3 = (f32[4,256,512]{2,1,0:T(8,128)S(1)}, bf16[512,512]{1,0:T(8,128)(2,1)S(1)}, bf16[512,512]{1,0:T(8,128)(2,1)S(1)}, bf16[512,512]{1,0:T(8,128)(2,1)S...) custom-call(s32[1]{0:T(128)} %bitcast.place_ref, ...), custom_call_target="tpu_custom_call", output_to_operand_aliasing={{0}: (12, {}), {1}: (13, {}), {2}: (14, {}), {3}: (15, {}),... | custom-call | flops 268435456 | bytes 1048576 | tf_op jit(solution)/shard_map/attention/pallas_call | solution.py:523
  33.3 3.4 %attention.4 = (f32[4,256,512]{2,1,0:T(8,128)S(1)}, bf16[512,512]{1,0:T(8,128)(2,1)S(1)}, bf16[512,512]{1,0:T(8,128)(2,1)S(1)}, bf16[512,512]{1,0:T(8,128)(2,1)S...) custom-call(s32[1]{0:T(128)} %bitcast.place_ref, ...), custom_call_target="tpu_custom_call", output_to_operand_aliasing={{0}: (12, {}), {1}: (13, {}), {2}: (14, {}), {3}: (15, {}),... | custom-call | flops 268435456 | bytes 1048576 | tf_op jit(solution)/shard_map/attention/pallas_call | solution.py:523
  36.7 3.4 %attention.5 = (f32[4,256,512]{2,1,0:T(8,128)S(1)}, bf16[512,512]{1,0:T(8,128)(2,1)S(1)}, bf16[512,512]{1,0:T(8,128)(2,1)S(1)}, bf16[512,512]{1,0:T(8,128)(2,1)S...) custom-call(s32[1]{0:T(128)} %bitcast.place_ref, ...), custom_call_target="tpu_custom_call", output_to_operand_aliasing={{0}: (12, {}), {1}: (13, {}), {2}: (14, {}), {3}: (15, {}),... | custom-call | flops 268435456 | bytes 1048576 | tf_op jit(solution)/shard_map/attention/pallas_call | solution.py:523
  40.2 7.2 %mlp.2 = (f32[384,512]{1,0:T(8,128)S(1)}, f32[384,512]{1,0:T(8,128)S(1)}, bf16[16,64,512]{2,1,0:T(8,128)(2,1)}, bf16[16,64,512]{2,1,0:T(8,128)(2,1)}) custom-call(s32[3]{0:T(128)S(1)} %pad_add_fusion.code_ref, bf16[128,512]{1,0:T(8,128)(2,1)S(1)} %get-tuple-element.175.refs_0_, bf16[128,512]{1,0:T(8,128)(2,1)S(1)} %get-tuple-element.173.refs_1_.refs_0_, ...), custom_call_target="tpu_custom_call" | custom-call | flops 2415919104 | bytes 9437184 | tf_op jit(solution)/shard_map/mlp/pallas_call | solution.py:523
  47.4 2.6 %collective-permute-start.8 = (bf16[16,64,512]{2,1,0:T(8,128)(2,1)}, bf16[16,64,512]{2,1,0:T(8,128)(2,1)S(1)}, u32[]{:S(2)}, u32[]{:S(2)}) collective-permute-start(bf16[16,64,512]{2,1,0:T(8,128)(2,1)} %get-tuple-element.186), channel_id=1, source_target_pairs={{0,4},{4,0},{8,12},{12,8},{16,20},{20,16},{24,28},{28,24},{1,5},{5... | collective-permute-start | bytes 3145736 | tf_op jit(solution)/shard_map/ppermute | solution.py:554
  50.0 6.9 %mlp.3 = (f32[384,512]{1,0:T(8,128)S(1)}, f32[384,512]{1,0:T(8,128)S(1)}, bf16[16,64,512]{2,1,0:T(8,128)(2,1)}, bf16[16,64,512]{2,1,0:T(8,128)(2,1)}) custom-call(s32[3]{0:T(128)S(1)} %pad_add_fusion.code_ref, bf16[128,512]{1,0:T(8,128)(2,1)S(1)} %get-tuple-element.175.refs_0_, bf16[128,512]{1,0:T(8,128)(2,1)S(1)} %get-tuple-element.173.refs_1_.refs_0_, ...), custom_call_target="tpu_custom_call" | custom-call | flops 2415919104 | bytes 9437184 | tf_op jit(solution)/shard_map/mlp/pallas_call | solution.py:523
  56.9 1.2 add_convert_fusion.1
  58.1 1.3 collective-permute-start.10
  59.4 1.2 add_convert_fusion.refs_19_
  60.6 0.3 collective-permute-start.9
  60.9 4.5 %attention_back.3 = (bf16[3,128,512]{2,1,0:T(8,128)(2,1)}, f32[128,512]{1,0:T(8,128)}, bf16[2,512,128]{2,1,0:T(8,128)(2,1)S(1)}, bf16[2,512,128]{2,1,0:T(8,128)(...) custom-call(s32[1]{0:T(128)} %bitcast.place_ref, ...), custom_call_target="tpu_custom_call" | custom-call | flops 671088640 | bytes 2621440 | tf_op jit(solution)/shard_map/attention_back/pallas_call | solution.py:523
  65.4 0.9 copy-done.3
  66.4 5.1 %attention_back.4 = (bf16[3,128,512]{2,1,0:T(8,128)(2,1)}, f32[128,512]{1,0:T(8,128)}, bf16[2,512,128]{2,1,0:T(8,128)(2,1)S(1)}, bf16[2,512,128]{2,1,0:T(8,128)(...) custom-call(s32[1]{0:T(128)} %bitcast.place_ref, ...), custom_call_target="tpu_custom_call", output_to_operand_aliasing={{0}: (28, {}), {4}: (22, {}), {5}: (23, {}), {6}: (24, {}),... | custom-call | flops 671088640 | bytes 2621440 | tf_op jit(solution)/shard_map/attention_back/pallas_call | solution.py:523
  71.4 2.3 %collective-permute-start.12 = (bf16[2,512,128]{2,1,0:T(8,128)(2,1)S(1)}, bf16[2,512,128]{2,1,0:T(8,128)(2,1)S(1)}, u32[]{:S(2)}, u32[]{:S(2)}) collective-permute-start(bf16[2,512,128]{2,1,0:T(8,128)(2,1)S(1)} %get-tuple-element.225), channel_id=1, source_target_pairs={{0,1},{1,0},{2,3},{3,2},{4,6},{5,7},{6,4},{7,5},{8,9},{9,8},{10,11... | collective-permute-start | bytes 786440 | tf_op jit(solution)/shard_map/ppermute | solution.py:572
  73.9 1.3 collective-permute-start.14
  75.3 0.3 collective-permute-start.13
  75.6 6.6 %attention_back.5 = (bf16[3,128,512]{2,1,0:T(8,128)(2,1)}, f32[128,512]{1,0:T(8,128)}, bf16[2,512,128]{2,1,0:T(8,128)(2,1)S(1)}, bf16[2,512,128]{2,1,0:T(8,128)(...) custom-call(s32[1]{0:T(128)} %bitcast.place_ref, ...), custom_call_target="tpu_custom_call", output_to_operand_aliasing={{0}: (29, {})} | custom-call | flops 671088640 | bytes 2621440 | tf_op jit(solution)/shard_map/attention_back/pallas_call | solution.py:523
  82.4 3.6 %collective-permute-done.11 = bf16[2,512,128]{2,1,0:T(8,128)(2,1)S(1)} collective-permute-done((bf16[2,512,128]{2,1,0:T(8,128)(2,1)S(1)}, bf16[2,512,128]{2,1,0:T(8,128)(2,1)S(1)}, u32[]{:S(2)}, u32[]{:S(2)}) %collective-permute-start.11) | collective-permute-done | bytes 262176 | tf_op jit(solution)/shard_map/ppermute | solution.py:572
  86.2 2.1 %collective-permute-start.15 = (bf16[2,512,128]{2,1,0:T(8,128)(2,1)S(1)}, bf16[2,512,128]{2,1,0:T(8,128)(2,1)S(1)}, u32[]{:S(2)}, u32[]{:S(2)}) collective-permute-start(bf16[2,512,128]{2,1,0:T(8,128)(2,1)S(1)} %get-tuple-element.233), channel_id=1, source_target_pairs={{0,1},{1,0},{2,3},{3,2},{4,6},{5,7},{6,4},{7,5},{8,9},{9,8},{10,11... | collective-permute-start | bytes 786440 | tf_op jit(solution)/shard_map/ppermute | solution.py:572
  88.3 0.4 collective-permute-start.18
  88.6 2.0 %collective-permute-start.19 = (bf16[2,64,512]{2,1,0:T(8,128)(2,1)S(1)}, bf16[2,64,512]{2,1,0:T(8,128)(2,1)S(1)}, u32[]{:S(2)}, u32[]{:S(2)}) collective-permute-start(bf16[2,64,512]{2,1,0:T(8,128)(2,1)S(1)} %add_convert_fusion.15), channel_id=1, source_target_pairs={{0,1},{1,0},{2,3},{3,2},{4,6},{5,7},{6,4},{7,5},{8,9},{9,8},{10,11... | collective-permute-start | bytes 393224 | tf_op jit(solution)/shard_map/ppermute | solution.py:572
  90.9 8.6 %collective-permute-done.19 = bf16[2,64,512]{2,1,0:T(8,128)(2,1)S(1)} collective-permute-done((bf16[2,64,512]{2,1,0:T(8,128)(2,1)S(1)}, bf16[2,64,512]{2,1,0:T(8,128)(2,1)S(1)}, u32[]{:S(2)}, u32[]{:S(2)}) %collective-permute-start.19) | collective-permute-done | bytes 131104 | tf_op jit(solution)/shard_map/ppermute | solution.py:572
  99.8 3.4 %collective-permute-start.22 = (bf16[2,64,512]{2,1,0:T(8,128)(2,1)S(1)}, bf16[2,64,512]{2,1,0:T(8,128)(2,1)S(1)}, u32[]{:S(2)}, u32[]{:S(2)}) collective-permute-start(bf16[2,64,512]{2,1,0:T(8,128)(2,1)S(1)} %pad_maximum_fusion.16), channel_id=1, source_target_pairs={{0,2},{1,3},{2,0},{3,1},{4,5},{5,4},{6,7},{7,6},{8,10},{9,11},{10,... | collective-permute-start | bytes 393224 | tf_op jit(solution)/shard_map/ppermute | solution.py:572
  103.2 1.3 collective-permute-start.17
  104.6 7.3 %collective-permute-done.17 = bf16[544,512]{1,0:T(8,128)(2,1)S(1)} collective-permute-done((bf16[544,512]{1,0:T(8,128)(2,1)S(1)}, bf16[544,512]{1,0:T(8,128)(2,1)S(1)}, u32[]{:S(2)}, u32[]{:S(2)}) %collective-permute-start.17) | collective-permute-done | bytes 557088 | tf_op jit(solution)/shard_map/ppermute | solution.py:572
  112.1 1.0 collective-permute-start.25
  113.1 1.3 collective-permute-start.20
  114.4 1.5 collective-permute-start.24
  116.0 3.1 %collective-permute-done.20 = bf16[288,512]{1,0:T(8,128)(2,1)S(1)} collective-permute-done((bf16[288,512]{1,0:T(8,128)(2,1)S(1)}, bf16[288,512]{1,0:T(8,128)(2,1)S(1)}, u32[]{:S(2)}, u32[]{:S(2)}) %collective-permute-start.20) | collective-permute-done | bytes 294944 | tf_op jit(solution)/shard_map/ppermute | solution.py:572
  119.3 1.5 collective-permute-start.23
  120.8 1.3 collective-permute-start.28
  122.1 0.3 collective-permute-start.27
  122.4 3.6 %collective-permute-done.23 = bf16[160,512]{1,0:T(8,128)(2,1)S(1)} collective-permute-done((bf16[160,512]{1,0:T(8,128)(2,1)S(1)}, bf16[160,512]{1,0:T(8,128)(2,1)S(1)}, u32[]{:S(2)}, u32[]{:S(2)}) %collective-permute-start.23) | collective-permute-done | bytes 163872 | tf_op jit(solution)/shard_map/ppermute | solution.py:572
  126.4 1.3 collective-permute-start.31
  127.8 1.4 collective-permute-done.27
  129.3 1.3 collective-permute-start.30
  131.0 6.6 %collective-permute-done.31 = bf16[8,64,512]{2,1,0:T(8,128)(2,1)S(1)} collective-permute-done((bf16[8,64,512]{2,1,0:T(8,128)(2,1)S(1)}, bf16[8,64,512]{2,1,0:T(8,128)(2,1)S(1)}, u32[]{:S(2)}, u32[]{:S(2)}) %collective-permute-start.31) | collective-permute-done | bytes 524320 | tf_op jit(solution)/shard_map/ppermute | solution.py:572
  137.7 1.3 collective-permute-start.35
  139.0 1.7 collective-permute-start.33
  140.7 2.5 %collective-permute-done.30 = bf16[8,64,512]{2,1,0:T(8,128)(2,1)S(1)} collective-permute-done((bf16[8,64,512]{2,1,0:T(8,128)(2,1)S(1)}, bf16[8,64,512]{2,1,0:T(8,128)(2,1)S(1)}, u32[]{:S(2)}, u32[]{:S(2)}) %collective-permute-start.30) | collective-permute-done | bytes 524320 | tf_op jit(solution)/shard_map/ppermute | solution.py:572
  143.3 1.3 collective-permute-start.32
  144.9 1.5 collective-permute-start.34
  146.5 3.2 %finish_outer.1 = f32[2048,512]{1,0:T(8,128)} custom-call(s32[3]{0:T(128)S(1)} %pad_add_fusion.code_ref, bf16[16,64,512]{2,1,0:T(8,128)(2,1)S(1)} %pad_maximum_fusion.low_ref, bf16[16,64,512]{2,1,0:T(8,128)(2,1)S(1)} %collective-permute-done.35.high_ref), custom_call_target="tpu_custom_call" | custom-call | tf_op jit(solution)/shard_map/finish_outer/pallas_call | solution.py:523
  149.7 0.8 collective-permute-done.34
  150.6 1.3 collective-permute-start.36
  152.0 4.1 %finish_inner.1 = f32[512,2048]{1,0:T(8,128)} custom-call(s32[3]{0:T(128)S(1)} %pad_add_fusion.code_ref, bf16[16,64,512]{2,1,0:T(8,128)(2,1)S(1)} %pad_maximum_fusion.1.low_ref, bf16[16,64,512]{2,1,0:T(8,128)(2,1)S(1)} %collective-permute-done.32.high_ref), custom_call_target="tpu_custom_call" | custom-call | tf_op jit(solution)/shard_map/finish_inner/pallas_call | solution.py:523
  156.1 4.8 %collective-permute-done.29.b_ref = bf16[3,512,128]{2,1,0:T(8,128)(2,1)S(1)} collective-permute-done((bf16[3,512,128]{2,1,0:T(8,128)(2,1)S(1)}, bf16[3,512,128]{2,1,0:T(8,128)(2,1)S(1)}, u32[]{:S(2)}, u32[]{:S(2)}) %collective-permute-start.29) | collective-permute-done | bytes 393248 | tf_op jit(solution)/shard_map/ppermute | solution.py:572
  160.8 1.3 post.1
  162.2 4.9 %collective-permute-start.37 = (bf16[16,64,512]{2,1,0:T(8,128)(2,1)S(1)}, bf16[16,64,512]{2,1,0:T(8,128)(2,1)S(1)}, u32[]{:S(2)}, u32[]{:S(2)}) collective-permute-start(bf16[16,64,512]{2,1,0:T(8,128)(2,1)S(1)} %pad_maximum_fusion.2.half_ref), channel_id=1, source_target_pairs={{0,4},{4,0},{8,12},{12,8},{16,20},{20,16},{24,28},{28,24},{1,5},{5... | collective-permute-start | bytes 3145736 | tf_op jit(solution)/shard_map/ppermute | solution.py:554
  167.1 0.6 slice_bitcast_fusion
  167.7 0.6 fusion.29
  168.3 1.9 %finish_attention.2 = (f32[512,512]{1,0:T(8,128)}, f32[512,512]{1,0:T(8,128)}, f32[512,512]{1,0:T(8,128)}, f32[512,512]{1,0:T(8,128)}) custom-call(s32[3]{0:T(128)S(1)} %pad_add_fusion.code_ref, bf16[16,64,512]{2,1,0:T(8,128)(2,1)S(1)} %pad_maximum_fusion.2.half_ref), custom_call_target="tpu_custom_call" | custom-call | tf_op jit(solution)/shard_map/finish_attention/pallas_call | solution.py:523
  170.2 1.9 %finish_attention.3 = (f32[512,512]{1,0:T(8,128)}, f32[512,512]{1,0:T(8,128)}, f32[512,512]{1,0:T(8,128)}, f32[512,512]{1,0:T(8,128)}) custom-call(s32[3]{0:T(128)S(1)} %pad_add_fusion.code_ref, bf16[16,64,512]{2,1,0:T(8,128)(2,1)S(1)} %collective-permute-done.37.half_ref, ...), custom_call_target="tpu_custom_call", output_to_operand_aliasing={{0}: (2, {}), {1}: (3, {}), {2}: (4, {}), {3}: (5, {})} | custom-call | tf_op jit(solution)/shard_map/finish_attention/pallas_call | solution.py:523
  (117 shorter events, 3.5 us)
Async XLA Ops:
  0.6 1.0 copy-start
  1.6 0.7 copy-start.8
  2.3 27.5 %copy-start.1 = (bf16[3,128,512]{2,1,0:T(8,128)(2,1)S(1)}, bf16[3,128,512]{2,1,0:T(8,128)(2,1)}, u32[]{:S(2)}) copy-start(bf16[3,128,512]{2,1,0:T(8,128)(2,1)} %x_ref.3) | copy-start | bytes 1179652
  2.3 27.5 %copy-start.6 = (f32[512]{0:T(512)S(1)}, f32[512]{0:T(512)}, u32[]{:S(2)}) copy-start(f32[512]{0:T(512)} %param.20) | copy-start | bytes 6148
  2.3 27.5 %copy-start.7 = (f32[512]{0:T(512)S(1)}, f32[512]{0:T(512)}, u32[]{:S(2)}) copy-start(f32[512]{0:T(512)} %param.15) | copy-start | bytes 6148
  2.3 27.5 %copy-start.9 = (s32[3,128]{1,0:T(4,128)S(1)}, s32[3,128]{1,0:T(4,128)}, u32[]{:S(2)}) copy-start(s32[3,128]{1,0:T(4,128)} %seen_ref.7) | copy-start | bytes 4612
  2.3 27.5 %copy-start.10 = (s32[3,4]{1,0:T(4,128)S(1)}, s32[3,4]{1,0:T(4,128)}, u32[]{:S(2)}) copy-start(s32[3,4]{1,0:T(4,128)} %lengths_ref.5) | copy-start | bytes 148
  2.4 27.4 %collective-permute-start = (bf16[400,512]{1,0:T(8,128)(2,1)S(1)}, bf16[400,512]{1,0:T(8,128)(2,1)S(1)}, u32[]{:S(2)}, u32[]{:S(2)}) collective-permute-start(bf16[400,512]{1,0:T(8,128)(2,1)S(1)} %get-tuple-element.140), channel_id=1, source_target_pairs={{0,1},{1,0},{2,3},{3,2},{4,5},{5,4},{6,7},{7,6},{8,9},{9,8},{10,11... | collective-permute-start | bytes 1228808 | tf_op jit(solution)/shard_map/ppermute | solution.py:557
  4.6 17.0 %collective-permute-start.1 = (bf16[144,512]{1,0:T(8,128)(2,1)S(1)}, bf16[144,512]{1,0:T(8,128)(2,1)S(1)}, u32[]{:S(2)}, u32[]{:S(2)}) collective-permute-start(bf16[144,512]{1,0:T(8,128)(2,1)S(1)} %get-tuple-element.141), channel_id=1, source_target_pairs={{0,2},{1,3},{2,0},{3,1},{4,6},{5,7},{6,4},{7,5},{8,10},{9,11},{10,... | collective-permute-start | bytes 442376 | tf_op jit(solution)/shard_map/ppermute | solution.py:557
  6.9 11.8 %collective-permute-start.2 = (bf16[128,512]{1,0:T(8,128)(2,1)S(1)}, bf16[128,512]{1,0:T(8,128)(2,1)S(1)}, u32[]{:S(2)}, u32[]{:S(2)}) collective-permute-start(bf16[128,512]{1,0:T(8,128)(2,1)S(1)} %get-tuple-element.142), channel_id=1, source_target_pairs={{0,2},{1,3},{2,0},{3,1},{4,6},{5,7},{6,4},{7,5},{8,10},{9,11},{10,... | collective-permute-start | bytes 393224 | tf_op jit(solution)/shard_map/ppermute | solution.py:557
  7.0 14.6 %collective-permute-start.3 = (bf16[128,512]{1,0:T(8,128)(2,1)S(1)}, bf16[128,512]{1,0:T(8,128)(2,1)S(1)}, u32[]{:S(2)}, u32[]{:S(2)}) collective-permute-start(bf16[128,512]{1,0:T(8,128)(2,1)S(1)} %get-tuple-element.143), channel_id=1, source_target_pairs={{0,2},{1,3},{2,0},{3,1},{4,6},{5,7},{6,4},{7,5},{8,10},{9,11},{10,... | collective-permute-start | bytes 393224 | tf_op jit(solution)/shard_map/ppermute | solution.py:557
  21.6 8.2 %collective-permute-start.5 = (bf16[144,512]{1,0:T(8,128)(2,1)S(1)}, bf16[144,512]{1,0:T(8,128)(2,1)S(1)}, u32[]{:S(2)}, u32[]{:S(2)}) collective-permute-start(bf16[144,512]{1,0:T(8,128)(2,1)S(1)} %collective-permute-done.1.x2_ref.x2_tail_ref), channel_id=1, source_target_pairs={{0,1},{1,0},{2,3},{3,2},{4,5},{5,4},{6,7},{7,6},{8,9},{9,8},{10,11... | collective-permute-start | bytes 442376 | tf_op jit(solution)/shard_map/ppermute | solution.py:557
  24.8 12.0 %collective-permute-start.4 = (bf16[128,512]{1,0:T(8,128)(2,1)S(1)}, bf16[128,512]{1,0:T(8,128)(2,1)S(1)}, u32[]{:S(2)}, u32[]{:S(2)}) collective-permute-start(bf16[128,512]{1,0:T(8,128)(2,1)S(1)} %collective-permute-done.3.x2_ref), channel_id=1, source_target_pairs={{0,1},{1,0},{2,3},{3,2},{4,5},{5,4},{6,7},{7,6},{8,9},{9,8},{10,11... | collective-permute-start | bytes 393224 | tf_op jit(solution)/shard_map/ppermute | solution.py:557
  24.8 8.5 %collective-permute-start.6 = (bf16[128,512]{1,0:T(8,128)(2,1)S(1)}, bf16[128,512]{1,0:T(8,128)(2,1)S(1)}, u32[]{:S(2)}, u32[]{:S(2)}) collective-permute-start(bf16[128,512]{1,0:T(8,128)(2,1)S(1)} %collective-permute-done.2.x2_ref), channel_id=1, source_target_pairs={{0,1},{1,0},{2,3},{3,2},{4,5},{5,4},{6,7},{7,6},{8,9},{9,8},{10,11... | collective-permute-start | bytes 393224 | tf_op jit(solution)/shard_map/ppermute | solution.py:557
  47.4 9.5 %collective-permute-start.8 = (bf16[16,64,512]{2,1,0:T(8,128)(2,1)}, bf16[16,64,512]{2,1,0:T(8,128)(2,1)S(1)}, u32[]{:S(2)}, u32[]{:S(2)}) collective-permute-start(bf16[16,64,512]{2,1,0:T(8,128)(2,1)} %get-tuple-element.186), channel_id=1, source_target_pairs={{0,4},{4,0},{8,12},{12,8},{16,20},{20,16},{24,28},{28,24},{1,5},{5... | collective-permute-start | bytes 3145736 | tf_op jit(solution)/shard_map/ppermute | solution.py:554
  50.0 9.4 %collective-permute-start.7 = (bf16[16,64,512]{2,1,0:T(8,128)(2,1)}, bf16[16,64,512]{2,1,0:T(8,128)(2,1)S(1)}, u32[]{:S(2)}, u32[]{:S(2)}) collective-permute-start(bf16[16,64,512]{2,1,0:T(8,128)(2,1)} %get-tuple-element.184), channel_id=1, source_target_pairs={{0,4},{4,0},{8,12},{12,8},{16,20},{20,16},{24,28},{28,24},{1,5},{5... | collective-permute-start | bytes 3145736 | tf_op jit(solution)/shard_map/ppermute | solution.py:554
  56.8 4.0 %copy-start.2 = (bf16[3,128,512]{2,1,0:T(8,128)(2,1)S(1)}, bf16[3,128,512]{2,1,0:T(8,128)(2,1)}, u32[]{:S(2)}) copy-start(bf16[3,128,512]{2,1,0:T(8,128)(2,1)} %refs_9_.5) | copy-start | bytes 1179652
  58.1 15.7 %collective-permute-start.10 = (bf16[8,64,512]{2,1,0:T(8,128)(2,1)S(1)}, bf16[8,64,512]{2,1,0:T(8,128)(2,1)S(1)}, u32[]{:S(2)}, u32[]{:S(2)}) collective-permute-start(bf16[8,64,512]{2,1,0:T(8,128)(2,1)S(1)} %add_convert_fusion.1), channel_id=1, source_target_pairs={{0,8},{1,9},{2,10},{3,11},{4,20},{5,21},{6,22},{7,23},{8,0},{9,1},... | collective-permute-start | bytes 1572872 | tf_op jit(solution)/shard_map/ppermute | solution.py:572
  60.6 14.6 %collective-permute-start.9 = (bf16[8,64,512]{2,1,0:T(8,128)(2,1)S(1)}, bf16[8,64,512]{2,1,0:T(8,128)(2,1)S(1)}, u32[]{:S(2)}, u32[]{:S(2)}) collective-permute-start(bf16[8,64,512]{2,1,0:T(8,128)(2,1)S(1)} %add_convert_fusion.refs_19_), channel_id=1, source_target_pairs={{0,8},{1,9},{2,10},{3,11},{4,20},{5,21},{6,22},{7,23},{8,0},{9,1},... | collective-permute-start | bytes 1572872 | tf_op jit(solution)/shard_map/ppermute | solution.py:572
  65.4 0.9 copy-start.3
  66.4 7.4 %copy-start.12 = (bf16[16,64,512]{2,1,0:T(8,128)(2,1)S(1)}, bf16[16,64,512]{2,1,0:T(8,128)(2,1)}, u32[]{:S(2)}) copy-start(bf16[16,64,512]{2,1,0:T(8,128)(2,1)} %get-tuple-element.185) | copy-start | bytes 3145732
  66.4 8.8 %copy-start.11 = (bf16[16,64,512]{2,1,0:T(8,128)(2,1)S(1)}, bf16[16,64,512]{2,1,0:T(8,128)(2,1)}, u32[]{:S(2)}) copy-start(bf16[16,64,512]{2,1,0:T(8,128)(2,1)} %get-tuple-element.183) | copy-start | bytes 3145732
  71.4 11.0 %collective-permute-start.12 = (bf16[2,512,128]{2,1,0:T(8,128)(2,1)S(1)}, bf16[2,512,128]{2,1,0:T(8,128)(2,1)S(1)}, u32[]{:S(2)}, u32[]{:S(2)}) collective-permute-start(bf16[2,512,128]{2,1,0:T(8,128)(2,1)S(1)} %get-tuple-element.225), channel_id=1, source_target_pairs={{0,1},{1,0},{2,3},{3,2},{4,6},{5,7},{6,4},{7,5},{8,9},{9,8},{10,11... | collective-permute-start | bytes 786440 | tf_op jit(solution)/shard_map/ppermute | solution.py:572
  73.7 12.2 %collective-permute-start.11 = (bf16[2,512,128]{2,1,0:T(8,128)(2,1)S(1)}, bf16[2,512,128]{2,1,0:T(8,128)(2,1)S(1)}, u32[]{:S(2)}, u32[]{:S(2)}) collective-permute-start(bf16[2,512,128]{2,1,0:T(8,128)(2,1)S(1)} %get-tuple-element.224), channel_id=1, source_target_pairs={{0,1},{1,0},{2,3},{3,2},{4,6},{5,7},{6,4},{7,5},{8,9},{9,8},{10,11... | collective-permute-start | bytes 786440 | tf_op jit(solution)/shard_map/ppermute | solution.py:572
  73.9 8.3 %collective-permute-start.14 = (bf16[4,64,512]{2,1,0:T(8,128)(2,1)S(1)}, bf16[4,64,512]{2,1,0:T(8,128)(2,1)S(1)}, u32[]{:S(2)}, u32[]{:S(2)}) collective-permute-start(bf16[4,64,512]{2,1,0:T(8,128)(2,1)S(1)} %add_convert_fusion.3), channel_id=1, source_target_pairs={{0,16},{1,17},{2,18},{3,19},{4,12},{5,13},{6,14},{7,15},{8,24},{9,... | collective-permute-start | bytes 786440 | tf_op jit(solution)/shard_map/ppermute | solution.py:572
  75.3 7.0 %collective-permute-start.13 = (bf16[4,64,512]{2,1,0:T(8,128)(2,1)S(1)}, bf16[4,64,512]{2,1,0:T(8,128)(2,1)S(1)}, u32[]{:S(2)}, u32[]{:S(2)}) collective-permute-start(bf16[4,64,512]{2,1,0:T(8,128)(2,1)S(1)} %add_convert_fusion.2.refs_19_), channel_id=1, source_target_pairs={{0,16},{1,17},{2,18},{3,19},{4,12},{5,13},{6,14},{7,15},{8,24},{9,... | collective-permute-start | bytes 786440 | tf_op jit(solution)/shard_map/ppermute | solution.py:572
  86.1 4.5 %collective-permute-start.16 = (bf16[1056,512]{1,0:T(8,128)(2,1)S(1)}, bf16[1056,512]{1,0:T(8,128)(2,1)S(1)}, u32[]{:S(2)}, u32[]{:S(2)}) collective-permute-start(bf16[1056,512]{1,0:T(8,128)(2,1)S(1)} %get-tuple-element.236), channel_id=1, source_target_pairs={{0,4},{4,0},{8,12},{12,8},{16,20},{20,16},{24,28},{28,24},{1,5},{5... | collective-permute-start | bytes 3244040 | tf_op jit(solution)/shard_map/ppermute | solution.py:554
  86.2 44.6 %collective-permute-start.15 = (bf16[2,512,128]{2,1,0:T(8,128)(2,1)S(1)}, bf16[2,512,128]{2,1,0:T(8,128)(2,1)S(1)}, u32[]{:S(2)}, u32[]{:S(2)}) collective-permute-start(bf16[2,512,128]{2,1,0:T(8,128)(2,1)S(1)} %get-tuple-element.233), channel_id=1, source_target_pairs={{0,1},{1,0},{2,3},{3,2},{4,6},{5,7},{6,4},{7,5},{8,9},{9,8},{10,11... | collective-permute-start | bytes 786440 | tf_op jit(solution)/shard_map/ppermute | solution.py:572
  88.3 11.4 %collective-permute-start.18 = (bf16[2,64,512]{2,1,0:T(8,128)(2,1)S(1)}, bf16[2,64,512]{2,1,0:T(8,128)(2,1)S(1)}, u32[]{:S(2)}, u32[]{:S(2)}) collective-permute-start(bf16[2,64,512]{2,1,0:T(8,128)(2,1)S(1)} %add_convert_fusion.14), channel_id=1, source_target_pairs={{0,1},{1,0},{2,3},{3,2},{4,6},{5,7},{6,4},{7,5},{8,9},{9,8},{10,11... | collective-permute-start | bytes 393224 | tf_op jit(solution)/shard_map/ppermute | solution.py:572
  88.6 10.9 %collective-permute-start.19 = (bf16[2,64,512]{2,1,0:T(8,128)(2,1)S(1)}, bf16[2,64,512]{2,1,0:T(8,128)(2,1)S(1)}, u32[]{:S(2)}, u32[]{:S(2)}) collective-permute-start(bf16[2,64,512]{2,1,0:T(8,128)(2,1)S(1)} %add_convert_fusion.15), channel_id=1, source_target_pairs={{0,1},{1,0},{2,3},{3,2},{4,6},{5,7},{6,4},{7,5},{8,9},{9,8},{10,11... | collective-permute-start | bytes 393224 | tf_op jit(solution)/shard_map/ppermute | solution.py:572
  99.8 12.3 %collective-permute-start.22 = (bf16[2,64,512]{2,1,0:T(8,128)(2,1)S(1)}, bf16[2,64,512]{2,1,0:T(8,128)(2,1)S(1)}, u32[]{:S(2)}, u32[]{:S(2)}) collective-permute-start(bf16[2,64,512]{2,1,0:T(8,128)(2,1)S(1)} %pad_maximum_fusion.16), channel_id=1, source_target_pairs={{0,2},{1,3},{2,0},{3,1},{4,5},{5,4},{6,7},{7,6},{8,10},{9,11},{10,... | collective-permute-start | bytes 393224 | tf_op jit(solution)/shard_map/ppermute | solution.py:572
  103.2 8.7 %collective-permute-start.17 = (bf16[544,512]{1,0:T(8,128)(2,1)S(1)}, bf16[544,512]{1,0:T(8,128)(2,1)S(1)}, u32[]{:S(2)}, u32[]{:S(2)}) collective-permute-start(bf16[544,512]{1,0:T(8,128)(2,1)S(1)} %pad_maximum_fusion.3), channel_id=1, source_target_pairs={{0,8},{1,9},{2,10},{3,11},{4,20},{5,21},{6,22},{7,23},{8,0},{9,1},... | collective-permute-start | bytes 1671176 | tf_op jit(solution)/shard_map/ppermute | solution.py:572
  104.5 8.6 %collective-permute-start.21 = (bf16[2,64,512]{2,1,0:T(8,128)(2,1)S(1)}, bf16[2,64,512]{2,1,0:T(8,128)(2,1)S(1)}, u32[]{:S(2)}, u32[]{:S(2)}) collective-permute-start(bf16[2,64,512]{2,1,0:T(8,128)(2,1)S(1)} %pad_maximum_fusion.15), channel_id=1, source_target_pairs={{0,2},{1,3},{2,0},{3,1},{4,5},{5,4},{6,7},{7,6},{8,10},{9,11},{10,... | collective-permute-start | bytes 393224 | tf_op jit(solution)/shard_map/ppermute | solution.py:572
  112.1 7.1 %collective-permute-start.25 = (bf16[2,64,512]{2,1,0:T(8,128)(2,1)S(1)}, bf16[2,64,512]{2,1,0:T(8,128)(2,1)S(1)}, u32[]{:S(2)}, u32[]{:S(2)}) collective-permute-start(bf16[2,64,512]{2,1,0:T(8,128)(2,1)S(1)} %add_convert_fusion.8), channel_id=1, source_target_pairs={{0,1},{1,0},{2,3},{3,2},{4,6},{5,7},{6,4},{7,5},{8,9},{9,8},{10,11... | collective-permute-start | bytes 393224 | tf_op jit(solution)/shard_map/ppermute | solution.py:572
  113.1 5.9 %collective-permute-start.20 = (bf16[288,512]{1,0:T(8,128)(2,1)S(1)}, bf16[288,512]{1,0:T(8,128)(2,1)S(1)}, u32[]{:S(2)}, u32[]{:S(2)}) collective-permute-start(bf16[288,512]{1,0:T(8,128)(2,1)S(1)} %pad_maximum_fusion.9), channel_id=1, source_target_pairs={{0,16},{1,17},{2,18},{3,19},{4,12},{5,13},{6,14},{7,15},{8,24},{9,... | collective-permute-start | bytes 884744 | tf_op jit(solution)/shard_map/ppermute | solution.py:572
  114.4 7.6 %collective-permute-start.24 = (bf16[2,64,512]{2,1,0:T(8,128)(2,1)S(1)}, bf16[2,64,512]{2,1,0:T(8,128)(2,1)S(1)}, u32[]{:S(2)}, u32[]{:S(2)}) collective-permute-start(bf16[2,64,512]{2,1,0:T(8,128)(2,1)S(1)} %add_convert_fusion.7), channel_id=1, source_target_pairs={{0,1},{1,0},{2,3},{3,2},{4,6},{5,7},{6,4},{7,5},{8,9},{9,8},{10,11... | collective-permute-start | bytes 393224 | tf_op jit(solution)/shard_map/ppermute | solution.py:572
  119.3 6.8 %collective-permute-start.23 = (bf16[160,512]{1,0:T(8,128)(2,1)S(1)}, bf16[160,512]{1,0:T(8,128)(2,1)S(1)}, u32[]{:S(2)}, u32[]{:S(2)}) collective-permute-start(bf16[160,512]{1,0:T(8,128)(2,1)S(1)} %pad_maximum_fusion.13), channel_id=1, source_target_pairs={{0,1},{1,0},{2,3},{3,2},{4,6},{5,7},{6,4},{7,5},{8,9},{9,8},{10,11... | collective-permute-start | bytes 491528 | tf_op jit(solution)/shard_map/ppermute | solution.py:572
  120.8 5.6 %collective-permute-start.28 = (bf16[4,64,512]{2,1,0:T(8,128)(2,1)S(1)}, bf16[4,64,512]{2,1,0:T(8,128)(2,1)S(1)}, u32[]{:S(2)}, u32[]{:S(2)}) collective-permute-start(bf16[4,64,512]{2,1,0:T(8,128)(2,1)S(1)} %pad_maximum_fusion.10), channel_id=1, source_target_pairs={{0,16},{1,17},{2,18},{3,19},{4,12},{5,13},{6,14},{7,15},{8,24},{9,... | collective-permute-start | bytes 786440 | tf_op jit(solution)/shard_map/ppermute | solution.py:572
  122.1 7.1 %collective-permute-start.27 = (bf16[4,64,512]{2,1,0:T(8,128)(2,1)S(1)}, bf16[4,64,512]{2,1,0:T(8,128)(2,1)S(1)}, u32[]{:S(2)}, u32[]{:S(2)}) collective-permute-start(bf16[4,64,512]{2,1,0:T(8,128)(2,1)S(1)} %pad_maximum_fusion.11), channel_id=1, source_target_pairs={{0,16},{1,17},{2,18},{3,19},{4,12},{5,13},{6,14},{7,15},{8,24},{9,... | collective-permute-start | bytes 786440 | tf_op jit(solution)/shard_map/ppermute | solution.py:572
  126.3 4.5 %collective-permute-start.26 = (bf16[160,512]{1,0:T(8,128)(2,1)S(1)}, bf16[160,512]{1,0:T(8,128)(2,1)S(1)}, u32[]{:S(2)}, u32[]{:S(2)}) collective-permute-start(bf16[160,512]{1,0:T(8,128)(2,1)S(1)} %pad_maximum_fusion.14), channel_id=1, source_target_pairs={{0,2},{1,3},{2,0},{3,1},{4,5},{5,4},{6,7},{7,6},{8,10},{9,11},{10,... | collective-permute-start | bytes 491528 | tf_op jit(solution)/shard_map/ppermute | solution.py:572
  126.4 11.1 %collective-permute-start.31 = (bf16[8,64,512]{2,1,0:T(8,128)(2,1)S(1)}, bf16[8,64,512]{2,1,0:T(8,128)(2,1)S(1)}, u32[]{:S(2)}, u32[]{:S(2)}) collective-permute-start(bf16[8,64,512]{2,1,0:T(8,128)(2,1)S(1)} %pad_maximum_fusion.4), channel_id=1, source_target_pairs={{0,8},{1,9},{2,10},{3,11},{4,20},{5,21},{6,22},{7,23},{8,0},{9,1},... | collective-permute-start | bytes 1572872 | tf_op jit(solution)/shard_map/ppermute | solution.py:572
  129.3 13.9 %collective-permute-start.30 = (bf16[8,64,512]{2,1,0:T(8,128)(2,1)S(1)}, bf16[8,64,512]{2,1,0:T(8,128)(2,1)S(1)}, u32[]{:S(2)}, u32[]{:S(2)}) collective-permute-start(bf16[8,64,512]{2,1,0:T(8,128)(2,1)S(1)} %pad_maximum_fusion.5), channel_id=1, source_target_pairs={{0,8},{1,9},{2,10},{3,11},{4,20},{5,21},{6,22},{7,23},{8,0},{9,1},... | collective-permute-start | bytes 1572872 | tf_op jit(solution)/shard_map/ppermute | solution.py:572
  137.7 8.8 %collective-permute-start.35 = (bf16[16,64,512]{2,1,0:T(8,128)(2,1)S(1)}, bf16[16,64,512]{2,1,0:T(8,128)(2,1)S(1)}, u32[]{:S(2)}, u32[]{:S(2)}) collective-permute-start(bf16[16,64,512]{2,1,0:T(8,128)(2,1)S(1)} %pad_maximum_fusion.low_ref), channel_id=1, source_target_pairs={{0,4},{4,0},{8,12},{12,8},{16,20},{20,16},{24,28},{28,24},{1,5},{5... | collective-permute-start | bytes 3145736 | tf_op jit(solution)/shard_map/ppermute | solution.py:554
  139.0 5.9 %collective-permute-start.33 = (bf16[2,64,512]{2,1,0:T(8,128)(2,1)S(1)}, bf16[2,64,512]{2,1,0:T(8,128)(2,1)S(1)}, u32[]{:S(2)}, u32[]{:S(2)}) collective-permute-start(bf16[2,64,512]{2,1,0:T(8,128)(2,1)S(1)} %fusion.2), channel_id=1, source_target_pairs={{0,1},{1,0},{2,3},{3,2},{4,6},{5,7},{6,4},{7,5},{8,9},{9,8},{10,11... | collective-permute-start | bytes 393224 | tf_op jit(solution)/shard_map/ppermute | solution.py:572
  143.3 8.6 %collective-permute-start.32 = (bf16[16,64,512]{2,1,0:T(8,128)(2,1)S(1)}, bf16[16,64,512]{2,1,0:T(8,128)(2,1)S(1)}, u32[]{:S(2)}, u32[]{:S(2)}) collective-permute-start(bf16[16,64,512]{2,1,0:T(8,128)(2,1)S(1)} %pad_maximum_fusion.1.low_ref), channel_id=1, source_target_pairs={{0,4},{4,0},{8,12},{12,8},{16,20},{20,16},{24,28},{28,24},{1,5},{5... | collective-permute-start | bytes 3145736 | tf_op jit(solution)/shard_map/ppermute | solution.py:554
  144.9 5.6 %collective-permute-start.34 = (bf16[4,64,512]{2,1,0:T(8,128)(2,1)S(1)}, bf16[4,64,512]{2,1,0:T(8,128)(2,1)S(1)}, u32[]{:S(2)}, u32[]{:S(2)}) collective-permute-start(bf16[4,64,512]{2,1,0:T(8,128)(2,1)S(1)} %pad_maximum_fusion.12), channel_id=1, source_target_pairs={{0,16},{1,17},{2,18},{3,19},{4,12},{5,13},{6,14},{7,15},{8,24},{9,... | collective-permute-start | bytes 786440 | tf_op jit(solution)/shard_map/ppermute | solution.py:572
  150.6 11.5 %collective-permute-start.36 = (bf16[8,64,512]{2,1,0:T(8,128)(2,1)S(1)}, bf16[8,64,512]{2,1,0:T(8,128)(2,1)S(1)}, u32[]{:S(2)}, u32[]{:S(2)}) collective-permute-start(bf16[8,64,512]{2,1,0:T(8,128)(2,1)S(1)} %pad_maximum_fusion.6), channel_id=1, source_target_pairs={{0,8},{1,9},{2,10},{3,11},{4,20},{5,21},{6,22},{7,23},{8,0},{9,1},... | collective-permute-start | bytes 1572872 | tf_op jit(solution)/shard_map/ppermute | solution.py:572
  151.9 9.0 %collective-permute-start.29 = (bf16[3,512,128]{2,1,0:T(8,128)(2,1)S(1)}, bf16[3,512,128]{2,1,0:T(8,128)(2,1)S(1)}, u32[]{:S(2)}, u32[]{:S(2)}) collective-permute-start(bf16[3,512,128]{2,1,0:T(8,128)(2,1)S(1)} %pad_maximum_fusion.8), channel_id=1, source_target_pairs={{0,2},{1,3},{2,0},{3,1},{4,5},{5,4},{6,7},{7,6},{8,10},{9,11},{10,... | collective-permute-start | bytes 1179656 | tf_op jit(solution)/shard_map/ppermute | solution.py:572
  151.9 8.9 %copy-start.4 = (f32[128,512]{1,0:T(8,128)S(1)}, f32[128,512]{1,0:T(8,128)}, u32[]{:S(2)}) copy-start(f32[128,512]{1,0:T(8,128)} %get-tuple-element.212.refs_1_) | copy-start | bytes 786436
  151.9 8.9 %copy-start.5 = (f32[128,512]{1,0:T(8,128)S(1)}, f32[128,512]{1,0:T(8,128)}, u32[]{:S(2)}) copy-start(f32[128,512]{1,0:T(8,128)} %get-tuple-element.226.refs_2_) | copy-start | bytes 786436
  162.2 8.0 %collective-permute-start.37 = (bf16[16,64,512]{2,1,0:T(8,128)(2,1)S(1)}, bf16[16,64,512]{2,1,0:T(8,128)(2,1)S(1)}, u32[]{:S(2)}, u32[]{:S(2)}) collective-permute-start(bf16[16,64,512]{2,1,0:T(8,128)(2,1)S(1)} %pad_maximum_fusion.2.half_ref), channel_id=1, source_target_pairs={{0,4},{4,0},{8,12},{12,8},{16,20},{20,16},{24,28},{28,24},{1,5},{5... | collective-permute-start | bytes 3145736 | tf_op jit(solution)/shard_map/ppermute | solution.py:554

commit v4 on v3

--- a/solution.py
+++ b/solution.py
@@ -23,6 +23,7 @@
 OUTER_ROWS = FF // CHUNKS
 SMALL_ROWS = D // CHUNKS
 FF_TILE = 512
+HALF_FF = FF // 2
 MASKED = -1000000000.0
 MIB = 1024 * 1024
 F32 = jnp.float32
@@ -31,32 +32,35 @@
 
 SMALL_HALVINGS = 3
 BEFORE_ROW = 2
+EARLY = ("outer", "inner", )
 ORDER = (
     "outer",
+    "small_start",
+    "rider",
     "inner",
-    "dx_start",
-    "small_start",
+    "outer",
     "small",
+    "dx_first",
+    "inner",
     "outer",
     "inner",
     "small",
+    "small",
+    "dx_start",
     "outer",
+    "small",
     "inner",
-    "small",
-    "outer",
-    "inner",
-    "small",
     "outer",
     "inner",
     "small",
     "dx",
     "outer",
+    "small",
+    "small",
+    "post",
     "inner",
-    "small",
     "finish_outer",
-    "small",
     "finish_inner",
-    "post",
     "small",
 )
 
@@ -104,18 +108,22 @@
     return jnp.where(lane < HD, stacked[:half], stacked[half:])
 
 
-def pack_kernel(x_ref, seen_ref, wire_ref, first_ref, *row_refs, here):
+def pack_kernel(x_ref, seen_ref, *out_refs, here, rows, tail):
     count = x_ref.shape[0]
-    flags = seen_ref[...].astype(F32)
-    flags = jnp.concatenate([flags, jnp.zeros((16 - count, here), F32)], axis=0)
-    tail = jnp.concatenate([flags, jnp.zeros((16, D - here), F32)], axis=1).astype(BF16)
-    for row in range(count):
-        wire_ref[row * here : (row + 1) * here] = x_ref[row]
-        if row:
-            row_refs[row - 1][...] = x_ref[row]
-    wire_ref[count * here :] = tail
-    first_ref[:here] = x_ref[0]
-    first_ref[here:] = tail
+    for out_ref, group in zip(out_refs, rows):
+        for place, row in enumerate(group):
+            out_ref[place * here : (place + 1) * here] = x_ref[row]
+    if tail:
+        flags = seen_ref[...].astype(F32)
+        flags = jnp.concatenate([flags, jnp.zeros((16 - count, here), F32)], axis=0)
+        flags = jnp.concatenate([flags, jnp.zeros((16, D - here), F32)], axis=1)
+        out_refs[0][len(rows[0]) * here :] = flags.astype(BF16)
+
+
+def split_kernel(wire_ref, *out_refs, here):
+    for row, out_ref in enumerate(out_refs):
+        out_ref[:here] = wire_ref[row * here : (row + 1) * here]
+    out_refs[0][here:] = wire_ref[len(out_refs) * here :]
 
 
 def prepare_kernel(place_ref, table_ref, *refs, here, seq):
@@ -149,6 +157,7 @@
 def attention_kernel(
     place_ref,
     lengths_ref,
+    code_ref,
     x0_ref,
     x1_ref,
     x2_ref,
@@ -168,7 +177,15 @@
     row,
     here,
     seq,
+    fetch,
 ):
+    if fetch:
+        copies = [
+            pltpu.make_async_copy(refs[i], refs[i - 4], refs[-1].at[i]) for i in range(3)
+        ]
+        for copy in copies:
+            copy.start()
+        refs = refs[:-4]
     (
         normed_mlp_ref,
         attended_ref,
@@ -224,10 +241,13 @@
         scores = dot(split_heads(q[:, lanes]), k[:, lanes], (1, 1)) + bias_ref[pair]
         scores = jnp.where(allowed, scores, MASKED)
         exponent = jnp.exp(scores - jnp.max(scores, -1, keepdims=True))
-        share = 1.0 / jnp.sum(exponent, -1, keepdims=True)
-        probs = (exponent * share).astype(BF16)
-        p_ref[pair] = probs
-        mixed = join_heads(dot(probs, v[:, lanes]))
+        ones = jnp.ones((PACKED_LENGTH, 128), BF16)
+        both = dot(exponent.astype(BF16), jnp.concatenate([v[:, lanes], ones], axis=1))
+        share = 1.0 / both[:, 128:]
+        mixed = join_heads(both[:, :128] * share)
+        for first in range(0, PACKED_LENGTH, 128):
+            part = slice(first, first + 128)
+            p_ref[pair, :, part] = (exponent[:, part] * share).astype(BF16)
         mixed_ref[:, lanes] = mixed
         attended.append(mixed.astype(BF16))
     attended = jnp.concatenate(attended, axis=1)
@@ -236,6 +256,9 @@
     middle_ref[...] = middle
     inv = lax.rsqrt(jnp.mean(middle * middle, -1, keepdims=True) + EPSILON)
     normed_mlp_ref[...] = (middle * inv * gain_mlp_ref[...]).astype(BF16)
+    if fetch:
+        for copy in copies:
+            copy.wait()
 
 
 def gelu_both(u):
@@ -249,28 +272,25 @@
 
 def mlp_kernel(code_ref, *refs, rows, own_half):
     nm_refs = refs[:rows]
-    g_ref, w_inner_ref, w_outer_ref, total_ref, back_ref, outer_ref, inner_ref = refs[rows:]
-    step = pl.program_id(0)
+    g_ref, w_inner_ref, w_outer_ref = refs[rows : rows + 3]
+    refs = refs[rows + 3 :]
+    total_ref, back_ref, outer_ref, inner_ref = refs
     label = code_ref[1] if own_half else code_ref[2]
     normed = jnp.concatenate([ref[...] for ref in nm_refs], axis=0)
     g = g_ref[...].reshape(normed.shape)
-    w_inner = w_inner_ref[...]
-    w_outer = w_outer_ref[...]
+    half = code_ref[0] if own_half else 1 - code_ref[0]
+    hidden = pl.ds(pl.multiple_of(half * HALF_FF, HALF_FF), HALF_FF)
+    w_inner = w_inner_ref[:, hidden]
+    w_outer = w_outer_ref[hidden, :]
     active_f, slope = gelu_both(dot(normed, w_inner))
     active = active_f.astype(BF16)
     grad_act = (dot(g, w_outer, (1, 1)) * slope).astype(BF16)
-
-    @pl.when(step == 0)
-    def _():
-        total_ref[...] = jnp.zeros_like(total_ref)
-        back_ref[...] = jnp.zeros_like(back_ref)
-
-    total_ref[...] += dot(active, w_outer)
-    back_ref[...] += dot(grad_act, w_inner, (1, 1))
+    total_ref[...] = dot(active, w_outer)
+    back_ref[...] = dot(grad_act, w_inner, (1, 1))
     outer = dot(active, g, (0, 0)).astype(BF16)
     inner = dot(grad_act, normed, (0, 0)).astype(BF16)
-    for part in range(FF_TILE // OUTER_ROWS):
-        slot = (step * (FF_TILE // OUTER_ROWS) + part) ^ label
+    for part in range(HALF):
+        slot = part ^ label
         rows = slice(part * OUTER_ROWS, (part + 1) * OUTER_ROWS)
         outer_ref[slot] = outer[rows]
         inner_ref[slot] = inner[rows]
@@ -294,17 +314,12 @@
     refs = refs[20:]
     old = refs[:6] if row else None
     refs = refs[6:] if row else refs
-    if last:
-        gain_attn_ref = refs[0]
-        refs = refs[1:]
     if row:
         refs = refs[1:]
     block_output_ref, grad_middle_ref, dx_keep_ref, dx_send_ref = refs[:4]
+    sums = refs[4:10]
     if last:
-        keep_ref, send_ref, rider_ref, line_ref = refs[4:8]
-        sums = refs[8:14]
-    else:
-        sums = refs[4:10]
+        keep_ref, send_ref = refs[10:12]
 
     def accumulate(which, value, part=None):
         if part is None:
@@ -354,10 +369,15 @@
     dq = jnp.concatenate(dq, axis=1)
     dkt = jnp.concatenate(dkt, axis=0)
     dvt = jnp.concatenate(dvt, axis=0)
-    dxt = dot(wk_ref[...], dkt) + dot(wv_ref[...], dvt)
-    own = dxt[:, :here] + dot(wq_ref[...], dq, (1, 1))
-    pieces = [own] + [dxt[:, block * here : (block + 1) * here] for block in range(1, seq)]
-    pieces = [piece.astype(BF16) for piece in pieces]
+    chunks = [slice(first, first + 128) for first in range(0, D, 128)]
+    pieces = [[] for _ in range(seq)]
+    for rows in chunks:
+        dxt = dot(wk_ref[rows], dkt) + dot(wv_ref[rows], dvt)
+        own = dxt[:, :here] + dot(wq_ref[rows], dq, (1, 1))
+        pieces[0].append(own.astype(BF16))
+        for block in range(1, seq):
+            pieces[block].append(dxt[:, block * here : (block + 1) * here].astype(BF16))
+    pieces = [jnp.concatenate(piece, axis=0) for piece in pieces]
     dx_keep_ref[0] = pieces[0]
     dx_send_ref[1] = pieces[3]
 
@@ -372,11 +392,44 @@
         dx_send_ref[0] = pieces[2]
 
     accumulate(1, dot(normed[:here], dq, (0, 0)))
-    accumulate(2, dot(dkt, normed))
-    accumulate(3, dot(dvt, normed))
+    for rows in chunks:
+        accumulate(2, dot(dkt[rows], normed), rows)
+        accumulate(3, dot(dvt[rows], normed), rows)
 
     if not last:
         return
+    go_ref, gq_ref, gk_ref, gv_ref = sums[:4]
+    gk_ref[...] = gk_ref[...].T
+    gv_ref[...] = gv_ref[...].T
+    core, label, other = code_ref[0], code_ref[1], code_ref[2]
+    for index, grad_ref in enumerate((go_ref, gq_ref, gk_ref, gv_ref)):
+        for slot in range(HALF):
+            chunk = core * HALF + (slot ^ label)
+            first = pl.multiple_of(chunk * SMALL_ROWS, SMALL_ROWS)
+            rows_to = slice(index * SMALL_ROWS, (index + 1) * SMALL_ROWS)
+            keep_ref[slot, rows_to] = grad_ref[pl.ds(first, SMALL_ROWS), :].astype(BF16)
+            chunk = (1 - core) * HALF + (slot ^ other)
+            first = pl.multiple_of(chunk * SMALL_ROWS, SMALL_ROWS)
+            send_ref[slot, rows_to] = grad_ref[pl.ds(first, SMALL_ROWS), :].astype(BF16)
+
+
+def rider_kernel(
+    place_ref,
+    gq_ref,
+    gk_ref,
+    gv_ref,
+    table_sum_ref,
+    gain_mlp_ref,
+    gain_attn_ref,
+    wq_ref,
+    wk_ref,
+    wv_ref,
+    rider_ref,
+    line_ref,
+    *,
+    here,
+    seq,
+):
     me = place_ref[0]
     line_ref[...] = jnp.zeros_like(line_ref)
     for block in range(seq):
@@ -384,7 +437,7 @@
         window = pl.ds(pl.multiple_of(offset, 128), 2 * here)
         for head in range(H):
             row = (head % 2) * here
-            tile = sums[4][head // 2, row : row + here, block * here : (block + 1) * here]
+            tile = table_sum_ref[head // 2, row : row + here, block * here : (block + 1) * here]
             total = jnp.zeros((8, 2 * here), F32)
             empty = jnp.zeros((8, here), F32)
             for group in range(here // 8):
@@ -399,9 +452,6 @@
         [jnp.sum(lines[h * 8 : h * 8 + 8], axis=0, keepdims=True) for h in range(H)], axis=0
     )
     table = dot(by_head, bucket_rows((SPAN, 128), 1), (1, 0), lax.Precision.HIGHEST)
-    go_ref, gq_ref, gk_ref, gv_ref = sums[:4]
-    gk_ref[...] = gk_ref[...].T
-    gv_ref[...] = gv_ref[...].T
     gain = (
         wq_ref[...].astype(F32) * gq_ref[...]
         + wk_ref[...].astype(F32) * gk_ref[...]
@@ -412,29 +462,12 @@
         [
             jnp.concatenate([table, jnp.zeros((8, D - 128), F32)], axis=1),
             gain_grad[:1] / gain_attn_ref[...],
-            sums[5][...],
+            gain_mlp_ref[...],
             jnp.zeros((6, D), F32),
         ],
         axis=0,
     )
     rider_ref[...] = rider
-    high = rider.astype(BF16)
-    base = HALF * 4 * SMALL_ROWS
-    send_ref[base : base + 16, :] = high
-    send_ref[base + 16 : base + 32, :] = (rider - high.astype(F32)).astype(BF16)
-    core, label, other = code_ref[0], code_ref[1], code_ref[2]
-    for index, grad_ref in enumerate((go_ref, gq_ref, gk_ref, gv_ref)):
-        for slot in range(HALF):
-            chunk = core * HALF + (slot ^ label)
-            first = pl.multiple_of(chunk * SMALL_ROWS, SMALL_ROWS)
-            rows_to = slice(index * SMALL_ROWS, (index + 1) * SMALL_ROWS)
-            keep_ref[slot, rows_to] = grad_ref[pl.ds(first, SMALL_ROWS), :].astype(BF16)
-            chunk = (1 - core) * HALF + (slot ^ other)
-            first = pl.multiple_of(chunk * SMALL_ROWS, SMALL_ROWS)
-            start = (slot * 4 + index) * SMALL_ROWS
-            send_ref[start : start + SMALL_ROWS, :] = grad_ref[
-                pl.ds(first, SMALL_ROWS), :
-            ].astype(BF16)
 
 
 def pick(code_ref, low_ref, high_ref, chunk, use):
@@ -589,14 +622,18 @@
         return [high, (rider - high.astype(F32)).astype(BF16)]
 
     class Reduction:
-        def __init__(self, wire, shape, halvings, rider=None):
-            self.rider = rider
+        def __init__(self, wire, shape, halvings):
+            self.rider = self.side = None
             self.slots, self.rows_each = shape[:2]
             self.halvings = halvings
             self.step = 0
             self.spreading = False
             self.parts = [None]
             self.arrived = swap_rows(wire, 1)
+
+        def attach(self, rider):
+            self.rider = rider
+            self.side = swap_rows(jnp.concatenate(two_parts(rider), axis=0), 1)
 
         def send(self, outgoing):
             if self.rider is not None:
@@ -610,10 +647,12 @@
             array = after(self.arrived, *earlier)
             if self.rider is not None:
                 size = self.slots * self.rows_each
-                extra = array[size:].astype(F32)
+                extra = (array[size:] if self.side is None else self.side).astype(F32)
                 high, low = two_parts(self.rider)
                 self.rider = (high.astype(F32) + low.astype(F32)) + (extra[:16] + extra[16:])
-                array = array[:size].reshape(self.slots, self.rows_each, D)
+                if self.side is None:
+                    array = array[:size].reshape(self.slots, self.rows_each, D)
+                self.side = None
             return array
 
         def advance(self, *earlier):
@@ -683,20 +722,34 @@
         square = whole((D, D))
         line = whole((1, D))
 
-        wire, *x2 = call(
-            functools.partial(pack_kernel, here=here),
+        def pack(rows, tail, *pins):
+            shapes = [(len(group) * here + (16 if tail and not i else 0), D) for i, group in enumerate(rows)]
+            return call(
+                functools.partial(pack_kernel, here=here, rows=rows, tail=tail),
+                (1,),
+                (),
+                (in_hbm(block_input), in_hbm(after(observed, *pins))),
+                [whole(own), whole(observed.shape)],
+                [shaped(shape, BF16) for shape in shapes],
+                [whole(shape) for shape in shapes],
+                name="pack",
+                vmem=8,
+            )
+
+        wire = pack([list(range(count))], True)[0]
+        x2 = swap_seq(wire, 2)
+        x1 = swap_seq(wire, 1)
+        x2 = call(
+            functools.partial(split_kernel, here=here),
             (1,),
             (),
-            (block_input, observed),
-            [whole(own), whole(observed.shape)],
-            [shaped((tokens + 16, D), BF16), shaped((here + 16, D), BF16)]
-            + [shaped(one, BF16)] * (count - 1),
-            [whole((tokens + 16, D)), whole((here + 16, D))] + [whole(one)] * (count - 1),
-            name="pack",
-            vmem=8,
+            (x2,),
+            [whole(wire.shape)],
+            [shaped((here + 16, D), BF16)] + [shaped(one, BF16)] * (count - 1),
+            [whole((here + 16, D))] + [whole(one)] * (count - 1),
+            name="split",
+            vmem=4,
         )
-        x2 = [swap_seq(x, 2) for x in x2]
-        x1 = swap_seq(wire, 1)
         *x2, bias_table = lax.optimization_barrier((*x2, bias_table))
         x3 = [swap_seq(x, 1) for x in x2]
         resident = (w_query, w_key, w_value, w_out)
@@ -725,13 +778,17 @@
             pltpu.VMEM(full, BF16),
             pltpu.VMEM(stacked, BF16),
         ]
+        fetched_shapes = [pltpu.VMEM(shape, BF16) for shape in ((D, FF), (FF, D), own)]
+        mlp_sources = [in_hbm(array) for array in (w_inner, outer_weight, cotangent)]
         for row in range(count):
-            *resident, nm, attended, middle, mixed, normed, q, k, v, p = call(
-                functools.partial(attention_kernel, row=row, here=here, seq=seq),
+            fetch = row == count - 1
+            shapes = kept_shapes + (fetched_shapes if fetch else [])
+            outs = call(
+                functools.partial(attention_kernel, row=row, here=here, seq=seq, fetch=fetch),
                 (1,),
-                (place, lengths),
+                (place, lengths, code),
                 [block_input, x1, x2[row], x3[row], observed, x1, x2[0], x3[0]]
-                + [gain_attn_row, gain_mlp_row, *resident],
+                + [gain_attn_row, gain_mlp_row, *resident, *(mlp_sources if fetch else [])],
                 [
                     one_row(own, row),
                     pl.BlockSpec(one, lambda *_, row=row: (row, 0)),
@@ -744,44 +801,41 @@
                 ]
                 + [line] * 2
                 + [whole(stacked)]
-                + [square] * 4,
-                [pltpu.VMEM(array.shape, array.dtype) for array in resident] + kept_shapes,
-                [ANYWHERE] * len(resident) + [whole(shape.shape) for shape in kept_shapes],
+                + [square] * 4
+                + [ANYWHERE] * (3 if fetch else 0),
+                [pltpu.VMEM(array.shape, array.dtype) for array in resident] + shapes,
+                [ANYWHERE] * len(resident) + [whole(shape.shape) for shape in shapes],
+                [pltpu.SemaphoreType.DMA((3,))] if fetch else [],
                 flops=8 * here * D * PACKED_LENGTH,
                 name="attention",
                 vmem=12,
-                aliases={12 + i: i for i in range(len(resident))},
+                aliases={13 + i: i for i in range(len(resident))},
             )
-            kept.append((nm, attended, middle, mixed, normed, q, k, v, p))
+            resident = outs[: len(resident)]
+            kept.append(tuple(outs[len(resident) : len(resident) + len(kept_shapes)]))
+            fetched = outs[len(resident) + len(kept_shapes) :]
         _, w_query, w_key, w_value, w_out = resident
         normed_mlp = [part[0] for part in kept]
 
         flat = (tokens, D)
-        steps = FF // FF_TILE // 2
         part_shape = (HALF, OUTER_ROWS, D)
 
         def mlp_part(own_half, nm):
-            def tile(i, code):
-                return (code[0] if own_half else 1 - code[0]) * steps + i
-
+            shapes = [pltpu.VMEM(flat, F32)] * 2 + [pltpu.VMEM(part_shape, BF16)] * 2
             return call(
                 functools.partial(mlp_kernel, rows=count, own_half=own_half),
-                (steps,),
+                (1,),
                 (code,),
-                [*nm, in_hbm(cotangent), in_hbm(w_inner), in_hbm(outer_weight)],
-                [whole(one)] * count
-                + [
-                    whole(own),
-                    pl.BlockSpec((D, FF_TILE), lambda i, n: (0, tile(i, n))),
-                    pl.BlockSpec((FF_TILE, D), lambda i, n: (tile(i, n), 0)),
-                ],
-                [pltpu.VMEM(flat, F32)] * 2 + [pltpu.HBM(part_shape, BF16)] * 2,
-                [whole(flat)] * 2 + [whole(part_shape)] * 2,
+                [*nm, cotangent, *fetched],
+                [whole(one)] * count + [whole(own), whole((D, FF)), whole((FF, D))],
+                shapes,
+                [whole(shape.shape) for shape in shapes],
                 flops=6 * tokens * D * FF,
                 name="mlp",
-                vmem=20,
+                vmem=16,
             )
 
+        *fetched, cotangent = fetched
         total_a, back_a, outer_send, inner_send = mlp_part(False, normed_mlp)
         chains = {
             "outer": Reduction(outer_send, part_shape, 3),
@@ -793,7 +847,6 @@
         chains["inner"].parts[0] = inner_keep
 
         small_half = (HALF, 4 * SMALL_ROWS, D)
-        small_wire = (HALF * 4 * SMALL_ROWS + 32, D)
         done = chains["outer"].advance()
         done = chains["inner"].advance(done)
         dx_half = (seq // 2, D, here)
@@ -808,26 +861,19 @@
             specs = [whole(shape.shape) for shape in kept_shapes] + [whole(own)]
             specs += [whole(flat)] * 4 + [line] + [square] * 4 + [ANYWHERE]
             specs += [whole(shape.shape) for shape in sum_shapes[: len(sums)]]
-            if end:
-                inputs.append(gain_attn_row)
-                specs.append(line)
             if row:
                 inputs.append(block_output)
                 specs.append(ANYWHERE)
             aliases = {len(inputs) + 1: 0} if row else {}
-            outs = [pltpu.HBM(own, BF16), pltpu.HBM(one, F32)] + [shaped(dx_half, BF16)] * 2
+            outs = [pltpu.HBM(own, BF16), pltpu.VMEM(one, F32)] + [pltpu.VMEM(dx_half, BF16)] * 2
             out_specs = [one_row(own, row), whole(one)] + [whole(dx_half)] * 2
+            outs += sum_shapes
+            out_specs += [whole(shape.shape) for shape in sum_shapes]
+            if row:
+                aliases |= {22 + i: 4 + i for i in range(len(sums))}
             if end:
-                outs += [shaped(small_half, BF16), shaped(small_wire, BF16), shaped((16, D), F32)]
-                out_specs += [whole(small_half), whole(small_wire), whole((16, D))]
-                scratch = [pltpu.VMEM((8 * H, SPAN), F32)]
-                scratch += [pltpu.VMEM(shape.shape, shape.dtype) for shape in sum_shapes]
-            else:
-                outs += sum_shapes
-                out_specs += [whole(shape.shape) for shape in sum_shapes]
-                scratch = []
-                if row:
-                    aliases |= {22 + i: 4 + i for i in range(len(sums))}
+                outs += [pltpu.VMEM(small_half, BF16)] * 2
+                out_specs += [whole(small_half)] * 2
             block_output, grad_middle, dx_keep, dx_send, *sums = call(
                 functools.partial(back_kernel, row=row, last=end, here=here, seq=seq),
                 (1,),
@@ -836,37 +882,55 @@
                 specs,
                 outs,
                 out_specs,
-                scratch,
                 flops=20 * here * D * PACKED_LENGTH,
                 name="attention_back",
-                vmem=24 if end else 14,
+                vmem=16,
                 aliases=aliases,
             )
             done = grad_middle
             if row == BEFORE_ROW - 1:
-                done = chains["outer"].advance(done)
-                done = chains["inner"].advance(done)
+                for event in EARLY:
+                    done = chains[event].advance(done)
             grad_middles.append(grad_middle)
             dx_keeps.append(dx_keep)
             dx_sends.append(dx_send)
-        small_keep, small_send, rider = sums
+        *sums, small_keep, small_send = sums
+
+        def make_rider(pin):
+            _, gq, gk, gv, table_sum, gain_mlp_sum = sums
+            return call(
+                functools.partial(rider_kernel, here=here, seq=seq),
+                (1,),
+                (place,),
+                (gq, gk, gv, table_sum, after(gain_mlp_sum, pin), gain_attn_row)
+                + (w_query, w_key, w_value),
+                [square] * 3 + [whole(stacked)] + [line] * 2 + [square] * 3,
+                [pltpu.VMEM((16, D), F32)],
+                [whole((16, D))],
+                [pltpu.VMEM((8 * H, SPAN), F32)],
+                name="rider",
+                vmem=8,
+            )[0]
+
         dx_arrived = [swap_step(dx_send, 2) for dx_send in dx_sends[:-1]]
         for event in ORDER:
             if event in chains:
                 done = chains[event].advance(done)
             elif event == "small_start":
-                chains["small"] = Reduction(
-                    after(small_send, done), small_half, SMALL_HALVINGS, rider
-                )
+                chains["small"] = Reduction(after(small_send, done), small_half, SMALL_HALVINGS)
                 chains["small"].parts[0] = small_keep
-            elif event == "dx_start":
+            elif event == "rider":
+                done = make_rider(done)
+                chains["small"].attach(done)
+            elif event == "dx_first":
                 *dx_arrived, done = lax.optimization_barrier((*dx_arrived, done))
                 dx_half = [
                     [add(x[i], y[i]).astype(BF16) for x, y in zip(dx_keeps, dx_arrived)]
                     for i in range(2)
                 ]
-                dx_arrived = swap_step(after(dx_sends[-1], dx_half[0][-1]), 2)
-                done = dx_half[1][-1]
+                *dx_half[0], done = lax.optimization_barrier((*dx_half[0], dx_half[1][-1]))
+            elif event == "dx_start":
+                dx_arrived = swap_step(after(dx_sends[-1], done), 2)
             elif event == "dx":
                 dx_arrived = after(dx_arrived, done)
                 half_kept, half_sent = [

time: 173 us -> 150 us (0.87)
  waiting for transfers between devices: 55.2 us -> 45.7 us
  Pallas kernels: 55.8 us -> 48.3 us
  local copies, waits for them, and re-layouts: 4.78 us -> 2.07 us
  other arithmetic: 4.65 us -> 2.53 us
    ppermute x25, waiting for transfers between devices: 42.8 us -> 28.3 us  [swap_step(): return lax.ppermute(array, both, pairs)]
    pallas_call x15 -> x17, Pallas kernels: 55.8 us -> 48.3 us  [call(): pl.pallas_call(kernel, out_shape=outs, grid_spec=pltpu.PrefetchScalarGrid...]
    ppermute x7 -> x5, waiting for transfers between devices: 12.3 us -> 17.4 us  [swap_seq(): return lax.ppermute(array, 'seq', [(i, i ^ bit) for i in range(seq)])]
    ppermute x6 -> x7, starting transfers between devices: 10.2 us -> 15.2 us  [swap_rows(): return lax.ppermute(array, 'rows', [(i, i ^ bit) for i in range(rows)])]
    ppermute x7 -> x5, starting transfers between devices: 11.5 us -> 7.16 us  [swap_seq(): return lax.ppermute(array, 'seq', [(i, i ^ bit) for i in range(seq)])]
    unnamed x26 -> x10, local copies, waits for them, and re-layouts: 2.66 us -> 0.02 us
    convert_element_type x9, other arithmetic: 3.1 us -> 0.96 us  [advance(): outgoing = add(*[part[size:] for part in self.parts]).astype(BF16)]
  transfers between devices with their start and end apart: 38 -> 37, of which waited for: 15 -> 16; matrix products, arithmetic and copies ran while one was open for 4% -> 3% of each run, Pallas kernels for 25% -> 26%
where the time goes in v4:
time: 150 us
  starting transfers between devices  50.3 us (34%)
  Pallas kernels  48.3 us (32%)
  waiting for transfers between devices  45.7 us (30%)
  other arithmetic  2.53 us (2%)
  local copies, waits for them, and re-layouts  2.07 us (1%)
    pallas_call x17, Pallas kernels, call(): pl.pallas_call(kernel, out_shape=outs, grid_spec=pltpu.PrefetchScalarGrid...  48.3 us
    ppermute x25, waiting for transfers between devices, swap_step(): return lax.ppermute(array, both, pairs)  28.3 us
    ppermute x25, starting transfers between devices, swap_step(): return lax.ppermute(array, both, pairs)  27.9 us
    ppermute x5, waiting for transfers between devices, swap_seq(): return lax.ppermute(array, 'seq', [(i, i ^ bit) for i in range(seq)])  17.4 us
    ppermute x7, starting transfers between devices, swap_rows(): return lax.ppermute(array, 'rows', [(i, i ^ bit) for i in range(rows)])  15.2 us
    ppermute x5, starting transfers between devices, swap_seq(): return lax.ppermute(array, 'seq', [(i, i ^ bit) for i in range(seq)])  7.16 us
  transfers between devices with their start and end apart: 37, of which 16 were waited for; matrix products, arithmetic and copies ran while one was open for 3% of the time, Pallas kernels for 26%

profile of v4, /device:TPU:1, one launch (start us, length us, event | category | flops | bytes accessed | tf_op | source)
XLA Modules:
  0.0 150.2 jit_solution(6972279267844775377)
XLA Ops:
  0.7 1.1 pack.1
  1.8 3.2 %collective-permute-start.1 = (bf16[400,512]{1,0:T(8,128)(2,1)S(1)}, bf16[400,512]{1,0:T(8,128)(2,1)S(1)}, u32[]{:S(2)}, u32[]{:S(2)}) collective-permute-start(bf16[400,512]{1,0:T(8,128)(2,1)S(1)} %pack.1), channel_id=1, source_target_pairs={{0,2},{1,3},{2,0},{3,1},{4,6},{5,7},{6,4},{7,5},{8,10},{9,11},{10,... | collective-permute-start | bytes 1228808 | tf_op jit(solution)/shard_map/ppermute | solution.py:590
  5.0 1.3 collective-permute-start
  6.3 16.7 %collective-permute-done.1.wire_ref = bf16[400,512]{1,0:T(8,128)(2,1)S(1)} collective-permute-done((bf16[400,512]{1,0:T(8,128)(2,1)S(1)}, bf16[400,512]{1,0:T(8,128)(2,1)S(1)}, u32[]{:S(2)}, u32[]{:S(2)}) %collective-permute-start.1) | collective-permute-done | bytes 409632 | tf_op jit(solution)/shard_map/ppermute | solution.py:590
  23.0 1.2 collective-permute-start.3
  24.6 1.1 collective-permute-start.4
  25.8 0.8 copy.57.table_ref
  26.5 2.7 %prepare.1 = (f32[4,256,512]{2,1,0:T(8,128)S(1)}, bf16[512,512]{1,0:T(8,128)(2,1)S(1)}, bf16[512,512]{1,0:T(8,128)(2,1)S(1)}, bf16[512,512]{1,0:T(8,128)(2,1)S(1)}, bf16[512,512]{1,0:T(8,128)(2,1)S(1)}) custom-call(s32[1]{0:T(128)} %bitcast.place_ref, f32[32,8]{1,0:T(8,128)S(1)} %copy.57.table_ref, bf16[512,512]{1,0:T(8,128)(2,1)} %refs_0_.2, ...), custom_call_target="tpu_custom_call" | custom-call | tf_op jit(solution)/shard_map/prepare/pallas_call | solution.py:556
  29.3 2.8 %attention.3 = (f32[4,256,512]{2,1,0:T(8,128)S(1)}, bf16[512,512]{1,0:T(8,128)(2,1)S(1)}, bf16[512,512]{1,0:T(8,128)(2,1)S(1)}, bf16[512,512]{1,0:T(8,128)(2,1)S...) custom-call(s32[1]{0:T(128)} %bitcast.place_ref, ...), custom_call_target="tpu_custom_call", output_to_operand_aliasing={{0}: (13, {}), {1}: (14, {}), {2}: (15, {}), {3}: (16, {}),... | custom-call | flops 268435456 | bytes 1048576 | tf_op jit(solution)/shard_map/attention/pallas_call | solution.py:556
  32.1 0.6 collective-permute-done.4.x3_ref
  32.8 2.8 %attention.4 = (f32[4,256,512]{2,1,0:T(8,128)S(1)}, bf16[512,512]{1,0:T(8,128)(2,1)S(1)}, bf16[512,512]{1,0:T(8,128)(2,1)S(1)}, bf16[512,512]{1,0:T(8,128)(2,1)S...) custom-call(s32[1]{0:T(128)} %bitcast.place_ref, ...), custom_call_target="tpu_custom_call", output_to_operand_aliasing={{0}: (13, {}), {1}: (14, {}), {2}: (15, {}), {3}: (16, {}),... | custom-call | flops 268435456 | bytes 1048576 | tf_op jit(solution)/shard_map/attention/pallas_call | solution.py:556
  35.5 3.1 %attention.5 = (f32[4,256,512]{2,1,0:T(8,128)S(1)}, bf16[512,512]{1,0:T(8,128)(2,1)S(1)}, bf16[512,512]{1,0:T(8,128)(2,1)S(1)}, bf16[512,512]{1,0:T(8,128)(2,1)S...) custom-call(s32[1]{0:T(128)} %bitcast.place_ref, ...), custom_call_target="tpu_custom_call", output_to_operand_aliasing={{0}: (13, {}), {1}: (14, {}), {2}: (15, {}), {3}: (16, {}),... | custom-call | flops 268435456 | bytes 1048576 | tf_op jit(solution)/shard_map/attention/pallas_call | solution.py:556
  38.6 3.7 %mlp.2 = (f32[384,512]{1,0:T(8,128)S(1)}, f32[384,512]{1,0:T(8,128)S(1)}, bf16[16,64,512]{2,1,0:T(8,128)(2,1)S(1)}, bf16[16,64,512]{2,1,0:T(8,128)(2,1)S(1)}) custom-call(s32[3]{0:T(128)S(1)} %pad_add_fusion.code_ref, bf16[128,512]{1,0:T(8,128)(2,1)S(1)} %get-tuple-element.186.refs_0_, bf16[128,512]{1,0:T(8,128)(2,1)S(1)} %get-tuple-element.182.refs_1_.refs_0_, ...), custom_call_target="tpu_custom_call" | custom-call | flops 2415919104 | bytes 9437184 | tf_op jit(solution)/shard_map/mlp/pallas_call | solution.py:556
  42.3 2.3 %collective-permute-start.6 = (bf16[16,64,512]{2,1,0:T(8,128)(2,1)S(1)}, bf16[16,64,512]{2,1,0:T(8,128)(2,1)S(1)}, u32[]{:S(2)}, u32[]{:S(2)}) collective-permute-start(bf16[16,64,512]{2,1,0:T(8,128)(2,1)S(1)} %get-tuple-element.197), channel_id=1, source_target_pairs={{0,4},{4,0},{8,12},{12,8},{16,20},{20,16},{24,28},{28,24},{1,5},{5... | collective-permute-start | bytes 3145736 | tf_op jit(solution)/shard_map/ppermute | solution.py:587
  44.7 3.9 %mlp.3 = (f32[384,512]{1,0:T(8,128)S(1)}, f32[384,512]{1,0:T(8,128)S(1)}, bf16[16,64,512]{2,1,0:T(8,128)(2,1)S(1)}, bf16[16,64,512]{2,1,0:T(8,128)(2,1)S(1)}) custom-call(s32[3]{0:T(128)S(1)} %pad_add_fusion.code_ref, bf16[128,512]{1,0:T(8,128)(2,1)S(1)} %get-tuple-element.186.refs_0_, bf16[128,512]{1,0:T(8,128)(2,1)S(1)} %get-tuple-element.182.refs_1_.refs_0_, ...), custom_call_target="tpu_custom_call" | custom-call | flops 2415919104 | bytes 9437184 | tf_op jit(solution)/shard_map/mlp/pallas_call | solution.py:556
  48.8 1.1 collective-permute-start.8
  50.0 0.5 collective-permute-start.7
  50.5 3.9 %attention_back.3 = (bf16[3,128,512]{2,1,0:T(8,128)(2,1)}, f32[128,512]{1,0:T(8,128)S(1)}, bf16[2,512,128]{2,1,0:T(8,128)(2,1)S(1)}, bf16[2,512,128]{2,1,0:T(8,1...) custom-call(s32[1]{0:T(128)} %bitcast.place_ref, ...), custom_call_target="tpu_custom_call" | custom-call | flops 671088640 | bytes 2621440 | tf_op jit(solution)/shard_map/attention_back/pallas_call | solution.py:556
  54.5 4.3 %attention_back.4 = (bf16[3,128,512]{2,1,0:T(8,128)(2,1)}, f32[128,512]{1,0:T(8,128)S(1)}, bf16[2,512,128]{2,1,0:T(8,128)(2,1)S(1)}, bf16[2,512,128]{2,1,0:T(8,1...) custom-call(s32[1]{0:T(128)} %bitcast.place_ref, ...), custom_call_target="tpu_custom_call", output_to_operand_aliasing={{0}: (28, {}), {4}: (22, {}), {5}: (23, {}), {6}: (24, {}),... | custom-call | flops 671088640 | bytes 2621440 | tf_op jit(solution)/shard_map/attention_back/pallas_call | solution.py:556
  58.8 2.8 %collective-permute-start.10 = (bf16[2,512,128]{2,1,0:T(8,128)(2,1)S(1)}, bf16[2,512,128]{2,1,0:T(8,128)(2,1)S(1)}, u32[]{:S(2)}, u32[]{:S(2)}) collective-permute-start(bf16[2,512,128]{2,1,0:T(8,128)(2,1)S(1)} %get-tuple-element.236), channel_id=1, source_target_pairs={{0,1},{1,0},{2,3},{3,2},{4,6},{5,7},{6,4},{7,5},{8,9},{9,8},{10,11... | collective-permute-start | bytes 786440 | tf_op jit(solution)/shard_map/ppermute | solution.py:605
  61.8 1.3 collective-permute-start.11
  63.2 0.8 collective-permute-start.14
  63.9 5.4 %attention_back.5 = (bf16[3,128,512]{2,1,0:T(8,128)(2,1)}, f32[128,512]{1,0:T(8,128)S(1)}, bf16[2,512,128]{2,1,0:T(8,128)(2,1)S(1)}, bf16[2,512,128]{2,1,0:T(8,1...) custom-call(s32[1]{0:T(128)} %bitcast.place_ref, ...), custom_call_target="tpu_custom_call", output_to_operand_aliasing={{0}: (28, {}), {4}: (22, {}), {5}: (23, {}), {6}: (24, {}),... | custom-call | flops 671088640 | bytes 2621440 | tf_op jit(solution)/shard_map/attention_back/pallas_call | solution.py:556
  69.4 3.1 %collective-permute-start.13 = (bf16[2,64,512]{2,1,0:T(8,128)(2,1)S(1)}, bf16[2,64,512]{2,1,0:T(8,128)(2,1)S(1)}, u32[]{:S(2)}, u32[]{:S(2)}) collective-permute-start(bf16[2,64,512]{2,1,0:T(8,128)(2,1)S(1)} %add_convert_fusion.16), channel_id=1, source_target_pairs={{0,1},{1,0},{2,3},{3,2},{4,6},{5,7},{6,4},{7,5},{8,9},{9,8},{10,11... | collective-permute-start | bytes 393224 | tf_op jit(solution)/shard_map/ppermute | solution.py:605
  72.5 2.2 %rider.1 = f32[16,512]{1,0:T(8,128)S(1)} custom-call(s32[1]{0:T(128)} %bitcast.place_ref, f32[512,512]{1,0:T(8,128)S(1)} %get-tuple-element.242.gq_ref, f32[512,512]{1,0:T(8,128)S(1)} %get-tuple-element.243.gk_ref, f32[512,512]{1,0:T(8,128)S(1)} %get-tuple-element.244.gv_ref, f32[4,256,512]{2,1,0:T(8,128)S(1)} %get-tuple-element.245.table_sum_ref, ...), custom_call_target="tpu_custom_call" | custom-call | tf_op jit(solution)/shard_map/rider/pallas_call | solution.py:556
  75.1 3.2 %collective-permute-start.17 = (bf16[2,64,512]{2,1,0:T(8,128)(2,1)S(1)}, bf16[2,64,512]{2,1,0:T(8,128)(2,1)S(1)}, u32[]{:S(2)}, u32[]{:S(2)}) collective-permute-start(bf16[2,64,512]{2,1,0:T(8,128)(2,1)S(1)} %add_convert_fusion.15), channel_id=1, source_target_pairs={{0,1},{1,0},{2,3},{3,2},{4,6},{5,7},{6,4},{7,5},{8,9},{9,8},{10,11... | collective-permute-start | bytes 393224 | tf_op jit(solution)/shard_map/ppermute | solution.py:605
  78.6 3.6 %collective-permute-done.17 = bf16[2,64,512]{2,1,0:T(8,128)(2,1)S(1)} collective-permute-done((bf16[2,64,512]{2,1,0:T(8,128)(2,1)S(1)}, bf16[2,64,512]{2,1,0:T(8,128)(2,1)S(1)}, u32[]{:S(2)}, u32[]{:S(2)}) %collective-permute-start.17) | collective-permute-done | bytes 131104 | tf_op jit(solution)/shard_map/ppermute | solution.py:605
  82.6 1.3 collective-permute-start.18
  83.9 0.6 collective-permute-done.19
  84.5 2.6 %collective-permute-done.18 = bf16[2,64,512]{2,1,0:T(8,128)(2,1)S(1)} collective-permute-done((bf16[2,64,512]{2,1,0:T(8,128)(2,1)S(1)}, bf16[2,64,512]{2,1,0:T(8,128)(2,1)S(1)}, u32[]{:S(2)}, u32[]{:S(2)}) %collective-permute-start.18) | collective-permute-done | bytes 131104 | tf_op jit(solution)/shard_map/ppermute | solution.py:605
  87.2 3.7 %collective-permute-done.16 = bf16[544,512]{1,0:T(8,128)(2,1)S(1)} collective-permute-done((bf16[544,512]{1,0:T(8,128)(2,1)S(1)}, bf16[544,512]{1,0:T(8,128)(2,1)S(1)}, u32[]{:S(2)}, u32[]{:S(2)}) %collective-permute-start.16) | collective-permute-done | bytes 557088 | tf_op jit(solution)/shard_map/ppermute | solution.py:605
  91.1 1.0 collective-permute-start.20
  92.1 1.5 %collective-permute-start.25 = (bf16[2,64,512]{2,1,0:T(8,128)(2,1)S(1)}, bf16[2,64,512]{2,1,0:T(8,128)(2,1)S(1)}, u32[]{:S(2)}, u32[]{:S(2)}) collective-permute-start(bf16[2,64,512]{2,1,0:T(8,128)(2,1)S(1)} %add_convert_fusion.9), channel_id=1, source_target_pairs={{0,1},{1,0},{2,3},{3,2},{4,6},{5,7},{6,4},{7,5},{8,9},{9,8},{10,11... | collective-permute-start | bytes 393224 | tf_op jit(solution)/shard_map/ppermute | solution.py:605
  93.7 0.8 collective-permute-start.23
  94.5 2.5 %collective-permute-done.20 = bf16[288,512]{1,0:T(8,128)(2,1)S(1)} collective-permute-done((bf16[288,512]{1,0:T(8,128)(2,1)S(1)}, bf16[288,512]{1,0:T(8,128)(2,1)S(1)}, u32[]{:S(2)}, u32[]{:S(2)}) %collective-permute-start.20) | collective-permute-done | bytes 294944 | tf_op jit(solution)/shard_map/ppermute | solution.py:605
  97.2 1.7 %collective-permute-start.22 = (bf16[160,512]{1,0:T(8,128)(2,1)S(1)}, bf16[160,512]{1,0:T(8,128)(2,1)S(1)}, u32[]{:S(2)}, u32[]{:S(2)}) collective-permute-start(bf16[160,512]{1,0:T(8,128)(2,1)S(1)} %pad_maximum_fusion.13), channel_id=1, source_target_pairs={{0,1},{1,0},{2,3},{3,2},{4,6},{5,7},{6,4},{7,5},{8,9},{9,8},{10,11... | collective-permute-start | bytes 491528 | tf_op jit(solution)/shard_map/ppermute | solution.py:605
  99.1 2.1 %collective-permute-done.23 = bf16[2,64,512]{2,1,0:T(8,128)(2,1)S(1)} collective-permute-done((bf16[2,64,512]{2,1,0:T(8,128)(2,1)S(1)}, bf16[2,64,512]{2,1,0:T(8,128)(2,1)S(1)}, u32[]{:S(2)}, u32[]{:S(2)}) %collective-permute-start.23) | collective-permute-done | bytes 131104 | tf_op jit(solution)/shard_map/ppermute | solution.py:605
  101.2 0.5 collective-permute-start.27
  101.7 0.5 collective-permute-start.21
  102.2 2.4 %collective-permute-done.22 = bf16[160,512]{1,0:T(8,128)(2,1)S(1)} collective-permute-done((bf16[160,512]{1,0:T(8,128)(2,1)S(1)}, bf16[160,512]{1,0:T(8,128)(2,1)S(1)}, u32[]{:S(2)}, u32[]{:S(2)}) %collective-permute-start.22) | collective-permute-done | bytes 163872 | tf_op jit(solution)/shard_map/ppermute | solution.py:605
  104.8 0.6 collective-permute-start.26
  105.5 0.7 collective-permute-start.24
  106.2 0.6 collective-permute-done.27
  106.8 0.5 collective-permute-start.30
  107.3 3.1 %collective-permute-done.26 = bf16[4,64,512]{2,1,0:T(8,128)(2,1)S(1)} collective-permute-done((bf16[4,64,512]{2,1,0:T(8,128)(2,1)S(1)}, bf16[4,64,512]{2,1,0:T(8,128)(2,1)S(1)}, u32[]{:S(2)}, u32[]{:S(2)}) %collective-permute-start.26) | collective-permute-done | bytes 262176 | tf_op jit(solution)/shard_map/ppermute | solution.py:605
  110.5 0.5 collective-permute-start.33
  111.0 2.8 %collective-permute-done.24 = bf16[160,512]{1,0:T(8,128)(2,1)S(1)} collective-permute-done((bf16[160,512]{1,0:T(8,128)(2,1)S(1)}, bf16[160,512]{1,0:T(8,128)(2,1)S(1)}, u32[]{:S(2)}, u32[]{:S(2)}) %collective-permute-start.24) | collective-permute-done | bytes 163872 | tf_op jit(solution)/shard_map/ppermute | solution.py:605
  113.8 1.0 collective-permute-start.29
  114.9 2.4 %collective-permute-start.28 = (bf16[3,512,128]{2,1,0:T(8,128)(2,1)S(1)}, bf16[3,512,128]{2,1,0:T(8,128)(2,1)S(1)}, u32[]{:S(2)}, u32[]{:S(2)}) collective-permute-start(bf16[3,512,128]{2,1,0:T(8,128)(2,1)S(1)} %pad_maximum_fusion.8), channel_id=1, source_target_pairs={{0,2},{1,3},{2,0},{3,1},{4,5},{5,4},{6,7},{7,6},{8,10},{9,11},{10,... | collective-permute-start | bytes 1179656 | tf_op jit(solution)/shard_map/ppermute | solution.py:605
  117.3 1.7 %collective-permute-done.30 = bf16[8,64,512]{2,1,0:T(8,128)(2,1)S(1)} collective-permute-done((bf16[8,64,512]{2,1,0:T(8,128)(2,1)S(1)}, bf16[8,64,512]{2,1,0:T(8,128)(2,1)S(1)}, u32[]{:S(2)}, u32[]{:S(2)}) %collective-permute-start.30) | collective-permute-done | bytes 524320 | tf_op jit(solution)/shard_map/ppermute | solution.py:605
  119.2 0.9 collective-permute-done.29
  120.1 1.7 %collective-permute-start.31 = (bf16[4,64,512]{2,1,0:T(8,128)(2,1)S(1)}, bf16[4,64,512]{2,1,0:T(8,128)(2,1)S(1)}, u32[]{:S(2)}, u32[]{:S(2)}) collective-permute-start(bf16[4,64,512]{2,1,0:T(8,128)(2,1)S(1)} %pad_maximum_fusion.12), channel_id=1, source_target_pairs={{0,16},{1,17},{2,18},{3,19},{4,12},{5,13},{6,14},{7,15},{8,24},{9,... | collective-permute-start | bytes 786440 | tf_op jit(solution)/shard_map/ppermute | solution.py:605
  121.9 6.1 %collective-permute-start.35 = (bf16[16,64,512]{2,1,0:T(8,128)(2,1)S(1)}, bf16[16,64,512]{2,1,0:T(8,128)(2,1)S(1)}, u32[]{:S(2)}, u32[]{:S(2)}) collective-permute-start(bf16[16,64,512]{2,1,0:T(8,128)(2,1)S(1)} %pad_maximum_fusion.low_ref), channel_id=1, source_target_pairs={{0,4},{4,0},{8,12},{12,8},{16,20},{20,16},{24,28},{28,24},{1,5},{5... | collective-permute-start | bytes 3145736 | tf_op jit(solution)/shard_map/ppermute | solution.py:587
  128.1 0.7 collective-permute-done.31
  128.9 1.3 post.1
  130.2 5.1 %collective-permute-start.34 = (bf16[16,64,512]{2,1,0:T(8,128)(2,1)S(1)}, bf16[16,64,512]{2,1,0:T(8,128)(2,1)S(1)}, u32[]{:S(2)}, u32[]{:S(2)}) collective-permute-start(bf16[16,64,512]{2,1,0:T(8,128)(2,1)S(1)} %pad_maximum_fusion.1.low_ref), channel_id=1, source_target_pairs={{0,4},{4,0},{8,12},{12,8},{16,20},{20,16},{24,28},{28,24},{1,5},{5... | collective-permute-start | bytes 3145736 | tf_op jit(solution)/shard_map/ppermute | solution.py:587
  135.6 3.2 %finish_outer.1 = f32[2048,512]{1,0:T(8,128)} custom-call(s32[3]{0:T(128)S(1)} %pad_add_fusion.code_ref, bf16[16,64,512]{2,1,0:T(8,128)(2,1)S(1)} %pad_maximum_fusion.low_ref, bf16[16,64,512]{2,1,0:T(8,128)(2,1)S(1)} %collective-permute-done.35.high_ref), custom_call_target="tpu_custom_call" | custom-call | tf_op jit(solution)/shard_map/finish_outer/pallas_call | solution.py:556
  138.8 4.1 %finish_inner.1 = f32[512,2048]{1,0:T(8,128)} custom-call(s32[3]{0:T(128)S(1)} %pad_add_fusion.code_ref, bf16[16,64,512]{2,1,0:T(8,128)(2,1)S(1)} %pad_maximum_fusion.1.low_ref, bf16[16,64,512]{2,1,0:T(8,128)(2,1)S(1)} %collective-permute-done.34.high_ref), custom_call_target="tpu_custom_call" | custom-call | tf_op jit(solution)/shard_map/finish_inner/pallas_call | solution.py:556
  142.9 0.8 collective-permute-done.32
  143.8 1.3 collective-permute-start.36
  145.1 0.6 slice_bitcast_fusion
  145.7 0.6 fusion.29
  146.3 1.9 %finish_attention.2 = (f32[512,512]{1,0:T(8,128)}, f32[512,512]{1,0:T(8,128)}, f32[512,512]{1,0:T(8,128)}, f32[512,512]{1,0:T(8,128)}) custom-call(s32[3]{0:T(128)S(1)} %pad_add_fusion.code_ref, bf16[16,64,512]{2,1,0:T(8,128)(2,1)S(1)} %pad_maximum_fusion.2.half_ref), custom_call_target="tpu_custom_call" | custom-call | tf_op jit(solution)/shard_map/finish_attention/pallas_call | solution.py:556
  148.2 1.9 %finish_attention.3 = (f32[512,512]{1,0:T(8,128)}, f32[512,512]{1,0:T(8,128)}, f32[512,512]{1,0:T(8,128)}, f32[512,512]{1,0:T(8,128)}) custom-call(s32[3]{0:T(128)S(1)} %pad_add_fusion.code_ref, bf16[16,64,512]{2,1,0:T(8,128)(2,1)S(1)} %collective-permute-done.36.half_ref, ...), custom_call_target="tpu_custom_call", output_to_operand_aliasing={{0}: (2, {}), {1}: (3, {}), {2}: (4, {}), {3}: (5, {})} | custom-call | tf_op jit(solution)/shard_map/finish_attention/pallas_call | solution.py:556
  (100 shorter events, 3.9 us)
Async XLA Ops:
  0.6 28.6 %copy-start.3 = (s32[3,128]{1,0:T(4,128)S(1)}, s32[3,128]{1,0:T(4,128)}, u32[]{:S(2)}) copy-start(s32[3,128]{1,0:T(4,128)} %seen_ref.6) | copy-start | bytes 4612
  0.7 28.6 %copy-start = (bf16[3,128,512]{2,1,0:T(8,128)(2,1)S(1)}, bf16[3,128,512]{2,1,0:T(8,128)(2,1)}, u32[]{:S(2)}) copy-start(bf16[3,128,512]{2,1,0:T(8,128)(2,1)} %x_ref.3) | copy-start | bytes 1179652
  0.7 28.6 %copy-start.4 = (s32[3,4]{1,0:T(4,128)S(1)}, s32[3,4]{1,0:T(4,128)}, u32[]{:S(2)}) copy-start(s32[3,4]{1,0:T(4,128)} %lengths_ref.5) | copy-start | bytes 148
  0.7 28.6 %copy-start.1 = (f32[512]{0:T(512)S(1)}, f32[512]{0:T(512)}, u32[]{:S(2)}) copy-start(f32[512]{0:T(512)} %param.20) | copy-start | bytes 6148
  0.7 28.6 %copy-start.2 = (f32[512]{0:T(512)S(1)}, f32[512]{0:T(512)}, u32[]{:S(2)}) copy-start(f32[512]{0:T(512)} %param.15) | copy-start | bytes 6148
  1.8 21.2 %collective-permute-start.1 = (bf16[400,512]{1,0:T(8,128)(2,1)S(1)}, bf16[400,512]{1,0:T(8,128)(2,1)S(1)}, u32[]{:S(2)}, u32[]{:S(2)}) collective-permute-start(bf16[400,512]{1,0:T(8,128)(2,1)S(1)} %pack.1), channel_id=1, source_target_pairs={{0,2},{1,3},{2,0},{3,1},{4,6},{5,7},{6,4},{7,5},{8,10},{9,11},{10,... | collective-permute-start | bytes 1228808 | tf_op jit(solution)/shard_map/ppermute | solution.py:590
  5.0 24.3 %collective-permute-start = (bf16[400,512]{1,0:T(8,128)(2,1)S(1)}, bf16[400,512]{1,0:T(8,128)(2,1)S(1)}, u32[]{:S(2)}, u32[]{:S(2)}) collective-permute-start(bf16[400,512]{1,0:T(8,128)(2,1)S(1)} %pack.1), channel_id=1, source_target_pairs={{0,1},{1,0},{2,3},{3,2},{4,5},{5,4},{6,7},{7,6},{8,9},{9,8},{10,11... | collective-permute-start | bytes 1228808 | tf_op jit(solution)/shard_map/ppermute | solution.py:590
  23.0 6.2 %collective-permute-start.3 = (bf16[144,512]{1,0:T(8,128)(2,1)S(1)}, bf16[144,512]{1,0:T(8,128)(2,1)S(1)}, u32[]{:S(2)}, u32[]{:S(2)}) collective-permute-start(bf16[144,512]{1,0:T(8,128)(2,1)S(1)} %get-tuple-element.153.x2_ref.x2_tail_ref), channel_id=1, source_target_pairs={{0,1},{1,0},{2,3},{3,2},{4,5},{5,4},{6,7},{7,6},{8,9},{9,8},{10,11... | collective-permute-start | bytes 442376 | tf_op jit(solution)/shard_map/ppermute | solution.py:590
  24.2 11.3 %collective-permute-start.2 = (bf16[128,512]{1,0:T(8,128)(2,1)S(1)}, bf16[128,512]{1,0:T(8,128)(2,1)S(1)}, u32[]{:S(2)}, u32[]{:S(2)}) collective-permute-start(bf16[128,512]{1,0:T(8,128)(2,1)S(1)} %get-tuple-element.152.x2_ref), channel_id=1, source_target_pairs={{0,1},{1,0},{2,3},{3,2},{4,5},{5,4},{6,7},{7,6},{8,9},{9,8},{10,11... | collective-permute-start | bytes 393224 | tf_op jit(solution)/shard_map/ppermute | solution.py:590
  24.6 8.2 %collective-permute-start.4 = (bf16[128,512]{1,0:T(8,128)(2,1)S(1)}, bf16[128,512]{1,0:T(8,128)(2,1)S(1)}, u32[]{:S(2)}, u32[]{:S(2)}) collective-permute-start(bf16[128,512]{1,0:T(8,128)(2,1)S(1)} %get-tuple-element.154.x2_ref), channel_id=1, source_target_pairs={{0,1},{1,0},{2,3},{3,2},{4,5},{5,4},{6,7},{7,6},{8,9},{9,8},{10,11... | collective-permute-start | bytes 393224 | tf_op jit(solution)/shard_map/ppermute | solution.py:590
  42.3 6.3 %collective-permute-start.6 = (bf16[16,64,512]{2,1,0:T(8,128)(2,1)S(1)}, bf16[16,64,512]{2,1,0:T(8,128)(2,1)S(1)}, u32[]{:S(2)}, u32[]{:S(2)}) collective-permute-start(bf16[16,64,512]{2,1,0:T(8,128)(2,1)S(1)} %get-tuple-element.197), channel_id=1, source_target_pairs={{0,4},{4,0},{8,12},{12,8},{16,20},{20,16},{24,28},{28,24},{1,5},{5... | collective-permute-start | bytes 3145736 | tf_op jit(solution)/shard_map/ppermute | solution.py:587
  44.6 5.2 %collective-permute-start.5 = (bf16[16,64,512]{2,1,0:T(8,128)(2,1)S(1)}, bf16[16,64,512]{2,1,0:T(8,128)(2,1)S(1)}, u32[]{:S(2)}, u32[]{:S(2)}) collective-permute-start(bf16[16,64,512]{2,1,0:T(8,128)(2,1)S(1)} %get-tuple-element.195), channel_id=1, source_target_pairs={{0,4},{4,0},{8,12},{12,8},{16,20},{20,16},{24,28},{28,24},{1,5},{5... | collective-permute-start | bytes 3145736 | tf_op jit(solution)/shard_map/ppermute | solution.py:587
  48.8 12.9 %collective-permute-start.8 = (bf16[8,64,512]{2,1,0:T(8,128)(2,1)S(1)}, bf16[8,64,512]{2,1,0:T(8,128)(2,1)S(1)}, u32[]{:S(2)}, u32[]{:S(2)}) collective-permute-start(bf16[8,64,512]{2,1,0:T(8,128)(2,1)S(1)} %add_convert_fusion.2), channel_id=1, source_target_pairs={{0,8},{1,9},{2,10},{3,11},{4,20},{5,21},{6,22},{7,23},{8,0},{9,1},... | collective-permute-start | bytes 1572872 | tf_op jit(solution)/shard_map/ppermute | solution.py:605
  50.0 13.1 %collective-permute-start.7 = (bf16[8,64,512]{2,1,0:T(8,128)(2,1)S(1)}, bf16[8,64,512]{2,1,0:T(8,128)(2,1)S(1)}, u32[]{:S(2)}, u32[]{:S(2)}) collective-permute-start(bf16[8,64,512]{2,1,0:T(8,128)(2,1)S(1)} %add_convert_fusion.1.refs_19_), channel_id=1, source_target_pairs={{0,8},{1,9},{2,10},{3,11},{4,20},{5,21},{6,22},{7,23},{8,0},{9,1},... | collective-permute-start | bytes 1572872 | tf_op jit(solution)/shard_map/ppermute | solution.py:605
  58.8 35.7 %collective-permute-start.10 = (bf16[2,512,128]{2,1,0:T(8,128)(2,1)S(1)}, bf16[2,512,128]{2,1,0:T(8,128)(2,1)S(1)}, u32[]{:S(2)}, u32[]{:S(2)}) collective-permute-start(bf16[2,512,128]{2,1,0:T(8,128)(2,1)S(1)} %get-tuple-element.236), channel_id=1, source_target_pairs={{0,1},{1,0},{2,3},{3,2},{4,6},{5,7},{6,4},{7,5},{8,9},{9,8},{10,11... | collective-permute-start | bytes 786440 | tf_op jit(solution)/shard_map/ppermute | solution.py:605
  61.6 32.9 %collective-permute-start.9 = (bf16[2,512,128]{2,1,0:T(8,128)(2,1)S(1)}, bf16[2,512,128]{2,1,0:T(8,128)(2,1)S(1)}, u32[]{:S(2)}, u32[]{:S(2)}) collective-permute-start(bf16[2,512,128]{2,1,0:T(8,128)(2,1)S(1)} %get-tuple-element.235), channel_id=1, source_target_pairs={{0,1},{1,0},{2,3},{3,2},{4,6},{5,7},{6,4},{7,5},{8,9},{9,8},{10,11... | collective-permute-start | bytes 786440 | tf_op jit(solution)/shard_map/ppermute | solution.py:605
  61.8 7.6 %collective-permute-start.11 = (bf16[4,64,512]{2,1,0:T(8,128)(2,1)S(1)}, bf16[4,64,512]{2,1,0:T(8,128)(2,1)S(1)}, u32[]{:S(2)}, u32[]{:S(2)}) collective-permute-start(bf16[4,64,512]{2,1,0:T(8,128)(2,1)S(1)} %add_convert_fusion.4), channel_id=1, source_target_pairs={{0,16},{1,17},{2,18},{3,19},{4,12},{5,13},{6,14},{7,15},{8,24},{9,... | collective-permute-start | bytes 786440 | tf_op jit(solution)/shard_map/ppermute | solution.py:605
  63.2 11.6 %collective-permute-start.14 = (bf16[4,64,512]{2,1,0:T(8,128)(2,1)S(1)}, bf16[4,64,512]{2,1,0:T(8,128)(2,1)S(1)}, u32[]{:S(2)}, u32[]{:S(2)}) collective-permute-start(bf16[4,64,512]{2,1,0:T(8,128)(2,1)S(1)} %add_convert_fusion.3.refs_19_), channel_id=1, source_target_pairs={{0,16},{1,17},{2,18},{3,19},{4,12},{5,13},{6,14},{7,15},{8,24},{9,... | collective-permute-start | bytes 786440 | tf_op jit(solution)/shard_map/ppermute | solution.py:605
  69.4 8.9 %collective-permute-start.13 = (bf16[2,64,512]{2,1,0:T(8,128)(2,1)S(1)}, bf16[2,64,512]{2,1,0:T(8,128)(2,1)S(1)}, u32[]{:S(2)}, u32[]{:S(2)}) collective-permute-start(bf16[2,64,512]{2,1,0:T(8,128)(2,1)S(1)} %add_convert_fusion.16), channel_id=1, source_target_pairs={{0,1},{1,0},{2,3},{3,2},{4,6},{5,7},{6,4},{7,5},{8,9},{9,8},{10,11... | collective-permute-start | bytes 393224 | tf_op jit(solution)/shard_map/ppermute | solution.py:605
  74.8 3.5 %collective-permute-start.15 = (bf16[32,512]{1,0:T(8,128)(2,1)S(1)}, bf16[32,512]{1,0:T(8,128)(2,1)S(1)}, u32[]{:S(2)}, u32[]{:S(2)}) collective-permute-start(bf16[32,512]{1,0:T(8,128)(2,1)S(1)} %pad_maximum_fusion.18), channel_id=1, source_target_pairs={{0,4},{4,0},{8,12},{12,8},{16,20},{20,16},{24,28},{28,24},{1,5},{5... | collective-permute-start | bytes 98312 | tf_op jit(solution)/shard_map/ppermute | solution.py:587
  75.1 7.0 %collective-permute-start.17 = (bf16[2,64,512]{2,1,0:T(8,128)(2,1)S(1)}, bf16[2,64,512]{2,1,0:T(8,128)(2,1)S(1)}, u32[]{:S(2)}, u32[]{:S(2)}) collective-permute-start(bf16[2,64,512]{2,1,0:T(8,128)(2,1)S(1)} %add_convert_fusion.15), channel_id=1, source_target_pairs={{0,1},{1,0},{2,3},{3,2},{4,6},{5,7},{6,4},{7,5},{8,9},{9,8},{10,11... | collective-permute-start | bytes 393224 | tf_op jit(solution)/shard_map/ppermute | solution.py:605
  78.3 4.0 %collective-permute-start.12 = (bf16[16,64,512]{2,1,0:T(8,128)(2,1)S(1)}, bf16[16,64,512]{2,1,0:T(8,128)(2,1)S(1)}, u32[]{:S(2)}, u32[]{:S(2)}) collective-permute-start(bf16[16,64,512]{2,1,0:T(8,128)(2,1)S(1)} %get-tuple-element.241), channel_id=1, source_target_pairs={{0,4},{4,0},{8,12},{12,8},{16,20},{20,16},{24,28},{28,24},{1,5},{5... | collective-permute-start | bytes 3145736 | tf_op jit(solution)/shard_map/ppermute | solution.py:587
  78.5 6.0 %collective-permute-start.19 = (bf16[2,64,512]{2,1,0:T(8,128)(2,1)S(1)}, bf16[2,64,512]{2,1,0:T(8,128)(2,1)S(1)}, u32[]{:S(2)}, u32[]{:S(2)}) collective-permute-start(bf16[2,64,512]{2,1,0:T(8,128)(2,1)S(1)} %pad_maximum_fusion.16), channel_id=1, source_target_pairs={{0,2},{1,3},{2,0},{3,1},{4,5},{5,4},{6,7},{7,6},{8,10},{9,11},{10,... | collective-permute-start | bytes 393224 | tf_op jit(solution)/shard_map/ppermute | solution.py:605
  82.5 8.4 %collective-permute-start.16 = (bf16[544,512]{1,0:T(8,128)(2,1)S(1)}, bf16[544,512]{1,0:T(8,128)(2,1)S(1)}, u32[]{:S(2)}, u32[]{:S(2)}) collective-permute-start(bf16[544,512]{1,0:T(8,128)(2,1)S(1)} %pad_maximum_fusion.3), channel_id=1, source_target_pairs={{0,8},{1,9},{2,10},{3,11},{4,20},{5,21},{6,22},{7,23},{8,0},{9,1},... | collective-permute-start | bytes 1671176 | tf_op jit(solution)/shard_map/ppermute | solution.py:605
  82.6 4.6 %collective-permute-start.18 = (bf16[2,64,512]{2,1,0:T(8,128)(2,1)S(1)}, bf16[2,64,512]{2,1,0:T(8,128)(2,1)S(1)}, u32[]{:S(2)}, u32[]{:S(2)}) collective-permute-start(bf16[2,64,512]{2,1,0:T(8,128)(2,1)S(1)} %pad_maximum_fusion.15), channel_id=1, source_target_pairs={{0,2},{1,3},{2,0},{3,1},{4,5},{5,4},{6,7},{7,6},{8,10},{9,11},{10,... | collective-permute-start | bytes 393224 | tf_op jit(solution)/shard_map/ppermute | solution.py:605
  91.1 5.9 %collective-permute-start.20 = (bf16[288,512]{1,0:T(8,128)(2,1)S(1)}, bf16[288,512]{1,0:T(8,128)(2,1)S(1)}, u32[]{:S(2)}, u32[]{:S(2)}) collective-permute-start(bf16[288,512]{1,0:T(8,128)(2,1)S(1)} %pad_maximum_fusion.9), channel_id=1, source_target_pairs={{0,16},{1,17},{2,18},{3,19},{4,12},{5,13},{6,14},{7,15},{8,24},{9,... | collective-permute-start | bytes 884744 | tf_op jit(solution)/shard_map/ppermute | solution.py:605
  92.1 12.6 %collective-permute-start.25 = (bf16[2,64,512]{2,1,0:T(8,128)(2,1)S(1)}, bf16[2,64,512]{2,1,0:T(8,128)(2,1)S(1)}, u32[]{:S(2)}, u32[]{:S(2)}) collective-permute-start(bf16[2,64,512]{2,1,0:T(8,128)(2,1)S(1)} %add_convert_fusion.9), channel_id=1, source_target_pairs={{0,1},{1,0},{2,3},{3,2},{4,6},{5,7},{6,4},{7,5},{8,9},{9,8},{10,11... | collective-permute-start | bytes 393224 | tf_op jit(solution)/shard_map/ppermute | solution.py:605
  93.7 7.5 %collective-permute-start.23 = (bf16[2,64,512]{2,1,0:T(8,128)(2,1)S(1)}, bf16[2,64,512]{2,1,0:T(8,128)(2,1)S(1)}, u32[]{:S(2)}, u32[]{:S(2)}) collective-permute-start(bf16[2,64,512]{2,1,0:T(8,128)(2,1)S(1)} %add_convert_fusion.10), channel_id=1, source_target_pairs={{0,1},{1,0},{2,3},{3,2},{4,6},{5,7},{6,4},{7,5},{8,9},{9,8},{10,11... | collective-permute-start | bytes 393224 | tf_op jit(solution)/shard_map/ppermute | solution.py:605
  97.2 7.4 %collective-permute-start.22 = (bf16[160,512]{1,0:T(8,128)(2,1)S(1)}, bf16[160,512]{1,0:T(8,128)(2,1)S(1)}, u32[]{:S(2)}, u32[]{:S(2)}) collective-permute-start(bf16[160,512]{1,0:T(8,128)(2,1)S(1)} %pad_maximum_fusion.13), channel_id=1, source_target_pairs={{0,1},{1,0},{2,3},{3,2},{4,6},{5,7},{6,4},{7,5},{8,9},{9,8},{10,11... | collective-permute-start | bytes 491528 | tf_op jit(solution)/shard_map/ppermute | solution.py:605
  101.2 5.6 %collective-permute-start.27 = (bf16[4,64,512]{2,1,0:T(8,128)(2,1)S(1)}, bf16[4,64,512]{2,1,0:T(8,128)(2,1)S(1)}, u32[]{:S(2)}, u32[]{:S(2)}) collective-permute-start(bf16[4,64,512]{2,1,0:T(8,128)(2,1)S(1)} %pad_maximum_fusion.10), channel_id=1, source_target_pairs={{0,16},{1,17},{2,18},{3,19},{4,12},{5,13},{6,14},{7,15},{8,24},{9,... | collective-permute-start | bytes 786440 | tf_op jit(solution)/shard_map/ppermute | solution.py:605
  101.7 13.1 %collective-permute-start.21 = (bf16[2,512,128]{2,1,0:T(8,128)(2,1)S(1)}, bf16[2,512,128]{2,1,0:T(8,128)(2,1)S(1)}, u32[]{:S(2)}, u32[]{:S(2)}) collective-permute-start(bf16[2,512,128]{2,1,0:T(8,128)(2,1)S(1)} %get-tuple-element.262), channel_id=1, source_target_pairs={{0,1},{1,0},{2,3},{3,2},{4,6},{5,7},{6,4},{7,5},{8,9},{9,8},{10,11... | collective-permute-start | bytes 786440 | tf_op jit(solution)/shard_map/ppermute | solution.py:605
  104.8 5.6 %collective-permute-start.26 = (bf16[4,64,512]{2,1,0:T(8,128)(2,1)S(1)}, bf16[4,64,512]{2,1,0:T(8,128)(2,1)S(1)}, u32[]{:S(2)}, u32[]{:S(2)}) collective-permute-start(bf16[4,64,512]{2,1,0:T(8,128)(2,1)S(1)} %pad_maximum_fusion.11), channel_id=1, source_target_pairs={{0,16},{1,17},{2,18},{3,19},{4,12},{5,13},{6,14},{7,15},{8,24},{9,... | collective-permute-start | bytes 786440 | tf_op jit(solution)/shard_map/ppermute | solution.py:605
  105.5 8.3 %collective-permute-start.24 = (bf16[160,512]{1,0:T(8,128)(2,1)S(1)}, bf16[160,512]{1,0:T(8,128)(2,1)S(1)}, u32[]{:S(2)}, u32[]{:S(2)}) collective-permute-start(bf16[160,512]{1,0:T(8,128)(2,1)S(1)} %pad_maximum_fusion.14), channel_id=1, source_target_pairs={{0,2},{1,3},{2,0},{3,1},{4,5},{5,4},{6,7},{7,6},{8,10},{9,11},{10,... | collective-permute-start | bytes 491528 | tf_op jit(solution)/shard_map/ppermute | solution.py:605
  106.8 12.3 %collective-permute-start.30 = (bf16[8,64,512]{2,1,0:T(8,128)(2,1)S(1)}, bf16[8,64,512]{2,1,0:T(8,128)(2,1)S(1)}, u32[]{:S(2)}, u32[]{:S(2)}) collective-permute-start(bf16[8,64,512]{2,1,0:T(8,128)(2,1)S(1)} %pad_maximum_fusion.4), channel_id=1, source_target_pairs={{0,8},{1,9},{2,10},{3,11},{4,20},{5,21},{6,22},{7,23},{8,0},{9,1},... | collective-permute-start | bytes 1572872 | tf_op jit(solution)/shard_map/ppermute | solution.py:605
  110.5 19.7 %collective-permute-start.33 = (bf16[8,64,512]{2,1,0:T(8,128)(2,1)S(1)}, bf16[8,64,512]{2,1,0:T(8,128)(2,1)S(1)}, u32[]{:S(2)}, u32[]{:S(2)}) collective-permute-start(bf16[8,64,512]{2,1,0:T(8,128)(2,1)S(1)} %pad_maximum_fusion.5), channel_id=1, source_target_pairs={{0,8},{1,9},{2,10},{3,11},{4,20},{5,21},{6,22},{7,23},{8,0},{9,1},... | collective-permute-start | bytes 1572872 | tf_op jit(solution)/shard_map/ppermute | solution.py:605
  113.8 6.3 %collective-permute-start.29 = (bf16[2,64,512]{2,1,0:T(8,128)(2,1)S(1)}, bf16[2,64,512]{2,1,0:T(8,128)(2,1)S(1)}, u32[]{:S(2)}, u32[]{:S(2)}) collective-permute-start(bf16[2,64,512]{2,1,0:T(8,128)(2,1)S(1)} %fusion.1), channel_id=1, source_target_pairs={{0,1},{1,0},{2,3},{3,2},{4,6},{5,7},{6,4},{7,5},{8,9},{9,8},{10,11... | collective-permute-start | bytes 393224 | tf_op jit(solution)/shard_map/ppermute | solution.py:605
  114.9 13.9 %collective-permute-start.28 = (bf16[3,512,128]{2,1,0:T(8,128)(2,1)S(1)}, bf16[3,512,128]{2,1,0:T(8,128)(2,1)S(1)}, u32[]{:S(2)}, u32[]{:S(2)}) collective-permute-start(bf16[3,512,128]{2,1,0:T(8,128)(2,1)S(1)} %pad_maximum_fusion.8), channel_id=1, source_target_pairs={{0,2},{1,3},{2,0},{3,1},{4,5},{5,4},{6,7},{7,6},{8,10},{9,11},{10,... | collective-permute-start | bytes 1179656 | tf_op jit(solution)/shard_map/ppermute | solution.py:605
  120.1 8.7 %collective-permute-start.31 = (bf16[4,64,512]{2,1,0:T(8,128)(2,1)S(1)}, bf16[4,64,512]{2,1,0:T(8,128)(2,1)S(1)}, u32[]{:S(2)}, u32[]{:S(2)}) collective-permute-start(bf16[4,64,512]{2,1,0:T(8,128)(2,1)S(1)} %pad_maximum_fusion.12), channel_id=1, source_target_pairs={{0,16},{1,17},{2,18},{3,19},{4,12},{5,13},{6,14},{7,15},{8,24},{9,... | collective-permute-start | bytes 786440 | tf_op jit(solution)/shard_map/ppermute | solution.py:605
  121.9 13.6 %collective-permute-start.35 = (bf16[16,64,512]{2,1,0:T(8,128)(2,1)S(1)}, bf16[16,64,512]{2,1,0:T(8,128)(2,1)S(1)}, u32[]{:S(2)}, u32[]{:S(2)}) collective-permute-start(bf16[16,64,512]{2,1,0:T(8,128)(2,1)S(1)} %pad_maximum_fusion.low_ref), channel_id=1, source_target_pairs={{0,4},{4,0},{8,12},{12,8},{16,20},{20,16},{24,28},{28,24},{1,5},{5... | collective-permute-start | bytes 3145736 | tf_op jit(solution)/shard_map/ppermute | solution.py:587
  130.2 8.5 %collective-permute-start.34 = (bf16[16,64,512]{2,1,0:T(8,128)(2,1)S(1)}, bf16[16,64,512]{2,1,0:T(8,128)(2,1)S(1)}, u32[]{:S(2)}, u32[]{:S(2)}) collective-permute-start(bf16[16,64,512]{2,1,0:T(8,128)(2,1)S(1)} %pad_maximum_fusion.1.low_ref), channel_id=1, source_target_pairs={{0,4},{4,0},{8,12},{12,8},{16,20},{20,16},{24,28},{28,24},{1,5},{5... | collective-permute-start | bytes 3145736 | tf_op jit(solution)/shard_map/ppermute | solution.py:587
  135.4 8.3 %collective-permute-start.32 = (bf16[8,64,512]{2,1,0:T(8,128)(2,1)S(1)}, bf16[8,64,512]{2,1,0:T(8,128)(2,1)S(1)}, u32[]{:S(2)}, u32[]{:S(2)}) collective-permute-start(bf16[8,64,512]{2,1,0:T(8,128)(2,1)S(1)} %pad_maximum_fusion.6), channel_id=1, source_target_pairs={{0,8},{1,9},{2,10},{3,11},{4,20},{5,21},{6,22},{7,23},{8,0},{9,1},... | collective-permute-start | bytes 1572872 | tf_op jit(solution)/shard_map/ppermute | solution.py:605
  143.8 4.4 %collective-permute-start.36 = (bf16[16,64,512]{2,1,0:T(8,128)(2,1)S(1)}, bf16[16,64,512]{2,1,0:T(8,128)(2,1)S(1)}, u32[]{:S(2)}, u32[]{:S(2)}) collective-permute-start(bf16[16,64,512]{2,1,0:T(8,128)(2,1)S(1)} %pad_maximum_fusion.2.half_ref), channel_id=1, source_target_pairs={{0,4},{4,0},{8,12},{12,8},{16,20},{20,16},{24,28},{28,24},{1,5},{5... | collective-permute-start | bytes 3145736 | tf_op jit(solution)/shard_map/ppermute | solution.py:587

commit v5 on v4

--- a/solution.py
+++ b/solution.py
@@ -22,7 +22,6 @@
 HALF = CHUNKS // 2
 OUTER_ROWS = FF // CHUNKS
 SMALL_ROWS = D // CHUNKS
-FF_TILE = 512
 HALF_FF = FF // 2
 MASKED = -1000000000.0
 MIB = 1024 * 1024
@@ -47,21 +46,25 @@
     "small",
     "small",
     "dx_start",
+    "small",
+    "outer",
+    "inner",
     "outer",
     "small",
     "inner",
-    "outer",
-    "inner",
-    "small",
     "dx",
     "outer",
     "small",
     "small",
     "post",
     "inner",
-    "finish_outer",
-    "finish_inner",
+    "own_outer",
+    "other_outer",
+    "own_inner",
+    "other_inner",
     "small",
+    "own_small",
+    "other_small",
 )
 
 
@@ -75,8 +78,12 @@
     )
 
 
-def xor_pairs(size, bit):
-    return [(i, i ^ bit) for i in range(size)]
+def dot_ones(values, ones, contract, swapped=False):
+    high = values.astype(BF16)
+    low = (values - high.astype(F32)).astype(BF16)
+    if swapped:
+        return dot(ones, high, contract) + dot(ones, low, contract)
+    return dot(high, ones, contract) + dot(low, ones, contract)
 
 
 def bucket_of(relative):
@@ -451,13 +458,13 @@
     by_head = jnp.concatenate(
         [jnp.sum(lines[h * 8 : h * 8 + 8], axis=0, keepdims=True) for h in range(H)], axis=0
     )
-    table = dot(by_head, bucket_rows((SPAN, 128), 1), (1, 0), lax.Precision.HIGHEST)
+    table = dot_ones(by_head, bucket_rows((SPAN, 128), 1).astype(BF16), (1, 0))
     gain = (
         wq_ref[...].astype(F32) * gq_ref[...]
         + wk_ref[...].astype(F32) * gk_ref[...]
         + wv_ref[...].astype(F32) * gv_ref[...]
     )
-    gain_grad = dot(jnp.ones((8, D), F32), gain, (1, 1), lax.Precision.HIGHEST)
+    gain_grad = dot_ones(gain, jnp.ones((8, D), BF16), (1, 1), True)
     rider = jnp.concatenate(
         [
             jnp.concatenate([table, jnp.zeros((8, D - 128), F32)], axis=1),
@@ -470,43 +477,43 @@
     rider_ref[...] = rider
 
 
-def pick(code_ref, low_ref, high_ref, chunk, use):
-    core, label, other = code_ref[0], code_ref[1], code_ref[2]
-
-    @pl.when(core == chunk[0])
-    def _():
-        use(low_ref, chunk[1] ^ label)
-
-    @pl.when(core != chunk[0])
-    def _():
-        use(high_ref, chunk[1] ^ other)
-
-
-def finish_mlp_kernel(code_ref, low_ref, high_ref, out_ref, stage_ref, *, turned):
-    step = pl.program_id(0)
-    per_step = FF_TILE // OUTER_ROWS
-    target = stage_ref if turned else out_ref
-    for part in range(per_step):
-        chunk = step * per_step + part
-        rows = slice(part * OUTER_ROWS, (part + 1) * OUTER_ROWS)
-
-        def use(ref, slot):
-            target[rows, :] = ref[slot].astype(F32)
-
-        pick(code_ref, low_ref, high_ref, (chunk // HALF, chunk % HALF), use)
-    if turned:
-        out_ref[...] = stage_ref[...].T
+def finish_mlp_kernel(code_ref, half_ref, *refs, own_half, turned):
+    out_ref, stage_ref, sems = refs[-3:]
+    half = code_ref[0] if own_half else 1 - code_ref[0]
+    label = code_ref[1] if own_half else code_ref[2]
+    groups = stage_ref.shape[0]
+    per_group = HALF // groups
+    size = per_group * OUTER_ROWS
+    copies = []
+    for group in range(groups):
+        pieces = [half_ref[(group * per_group + i) ^ label].astype(F32) for i in range(per_group)]
+        piece = jnp.concatenate(pieces, axis=0)
+        stage_ref[group] = piece.T if turned else piece
+        place = pl.ds(pl.multiple_of((half * groups + group) * size, size), size)
+        target = out_ref.at[:, place] if turned else out_ref.at[place]
+        copies.append(pltpu.make_async_copy(stage_ref.at[group], target, sems.at[group]))
+        copies[-1].start()
+    for copy in copies:
+        copy.wait()
 
 
 def finish_attention_kernel(code_ref, half_ref, *refs, own_half):
-    out_refs = refs[-4:]
+    out_refs, stage_ref, sems = refs[-6:-2], refs[-2], refs[-1]
+    half = code_ref[0] if own_half else 1 - code_ref[0]
     label = code_ref[1] if own_half else code_ref[2]
-    for part in range(HALF):
-        rows = slice(part * SMALL_ROWS, (part + 1) * SMALL_ROWS)
-        for index, out_ref in enumerate(out_refs):
-            out_ref[rows, :] = half_ref[
-                part ^ label, index * SMALL_ROWS : (index + 1) * SMALL_ROWS
-            ].astype(F32)
+    place = pl.ds(pl.multiple_of(half * (D // 2), D // 2), D // 2)
+    copies = []
+    for index, out_ref in enumerate(out_refs):
+        part = slice(index * SMALL_ROWS, (index + 1) * SMALL_ROWS)
+        for slot in range(HALF):
+            rows = slice(slot * SMALL_ROWS, (slot + 1) * SMALL_ROWS)
+            stage_ref[index, rows] = half_ref[slot ^ label, part].astype(F32)
+        copies.append(
+            pltpu.make_async_copy(stage_ref.at[index], out_ref.at[place], sems.at[index])
+        )
+        copies[-1].start()
+    for copy in copies:
+        copy.wait()
 
 
 def post_kernel(a_ref, b_ref, x_ref, gain_ref, *refs):
@@ -913,6 +920,38 @@
             )[0]
 
         dx_arrived = [swap_step(dx_send, 2) for dx_send in dx_sends[:-1]]
+
+        grads = {}
+
+        def finish(name, own_half, pin):
+            chain = chains[name]
+            groups = 4
+            if name == "small":
+                kernel = finish_attention_kernel
+                shapes, stage = [(D, D)] * 4, (4, D // 2, D)
+            else:
+                turned = name == "inner"
+                kernel = functools.partial(finish_mlp_kernel, turned=turned)
+                size = HALF_FF // groups
+                shapes = [(D, FF) if turned else (FF, D)]
+                stage = (groups, D, size) if turned else (groups, size, D)
+            half = after(chain.held if own_half else chain.arrived, pin)
+            before = grads.get(name, ())
+            grads[name] = call(
+                functools.partial(kernel, own_half=own_half),
+                (1,),
+                (code,),
+                (half, *before),
+                [whole(half.shape)] + [ANYWHERE] * len(before),
+                [pltpu.HBM(shape, F32) for shape in shapes],
+                [ANYWHERE] * len(shapes),
+                [pltpu.VMEM(stage, F32), pltpu.SemaphoreType.DMA((stage[0],))],
+                name="finish_" + name,
+                vmem=10,
+                aliases={2 + i: i for i in range(len(before))},
+            )
+            return grads[name][0]
+
         for event in ORDER:
             if event in chains:
                 done = chains[event].advance(done)
@@ -951,55 +990,12 @@
                     name="post",
                 )[0]
                 done = input_grad
-            elif event == "finish_outer":
-                chain = chains["outer"]
-                grad_outer = call(
-                    functools.partial(finish_mlp_kernel, turned=False),
-                    (FF // FF_TILE,),
-                    (code,),
-                    (chain.held, after(chain.arrived, done)),
-                    [whole(part_shape)] * 2,
-                    [shaped((FF, D), F32)],
-                    [pl.BlockSpec((FF_TILE, D), lambda i, *_: (i, 0))],
-                    [pltpu.VMEM((8, 128), F32)],
-                    name="finish_outer",
-                )[0]
-                done = grad_outer
-            elif event == "finish_inner":
-                chain = chains["inner"]
-                grad_inner = call(
-                    functools.partial(finish_mlp_kernel, turned=True),
-                    (FF // FF_TILE,),
-                    (code,),
-                    (chain.held, after(chain.arrived, done)),
-                    [whole(part_shape)] * 2,
-                    [shaped((D, FF), F32)],
-                    [pl.BlockSpec((D, FF_TILE), lambda i, *_: (0, i))],
-                    [pltpu.VMEM((FF_TILE, D), F32)],
-                    name="finish_inner",
-                )[0]
-                done = grad_inner
-        chain = chains["small"]
-        grads = ()
-        for own_half in (True, False):
-            half = chain.held if own_half else after(chain.arrived, grads[0])
-
-            def half_of(i, code):
-                return (code[0] if own_half else 1 - code[0], 0)
-
-            grads = call(
-                functools.partial(finish_attention_kernel, own_half=own_half),
-                (1,),
-                (code,),
-                (half, *grads),
-                [whole(small_half)] + [ANYWHERE] * len(grads),
-                [shaped((D, D), F32)] * 4,
-                [pl.BlockSpec((D // 2, D), half_of)] * 4,
-                name="finish_attention",
-                aliases={2 + i: i for i in range(len(grads))},
-            )
-        grad_out, grad_query, grad_key, grad_value = grads
-        rider = chain.rider
+            else:
+                which, name = event.split("_")
+                done = finish(name, which == "own", done)
+        (grad_outer,), (grad_inner,) = grads["outer"], grads["inner"]
+        grad_out, grad_query, grad_key, grad_value = grads["small"]
+        rider = chains["small"].rider
 
         return (
             block_output,

time: 150 us -> 149 us (level)
  starting transfers between devices: 50.3 us -> 45 us
  waiting for transfers between devices: 45.7 us -> 49.8 us
    ppermute x7, starting transfers between devices: 15.2 us -> 8.24 us  [swap_rows(): return lax.ppermute(array, 'rows', [(i, i ^ bit) for i in range(rows)])]
    ppermute x25, waiting for transfers between devices: 28.3 us -> 32.4 us  [swap_step(): return lax.ppermute(array, both, pairs)]
    ppermute x25, starting transfers between devices: 27.9 us -> 29.6 us  [swap_step(): return lax.ppermute(array, both, pairs)]
    pallas_call x17 -> x19, Pallas kernels: 48.3 us -> 48.3 us  [call(): pl.pallas_call(kernel, out_shape=outs, grid_spec=pltpu.PrefetchScalarGrid...]
  transfers between devices with their start and end apart: 37 -> 37, of which waited for: 16 -> 12; matrix products, arithmetic and copies ran while one was open for 3% -> 3% of each run, Pallas kernels for 26% -> 26%
where the time goes in v5:
time: 149 us
  waiting for transfers between devices  49.8 us (33%)
  Pallas kernels  48.3 us (32%)
  starting transfers between devices  45 us (30%)
  other arithmetic  2.52 us (2%)
  local copies, waits for them, and re-layouts  2.07 us (1%)
  between operations  1.51 us (1%)
    pallas_call x19, Pallas kernels, call(): pl.pallas_call(kernel, out_shape=outs, grid_spec=pltpu.PrefetchScalarGrid...  48.3 us
    ppermute x25, waiting for transfers between devices, swap_step(): return lax.ppermute(array, both, pairs)  32.4 us
    ppermute x25, starting transfers between devices, swap_step(): return lax.ppermute(array, both, pairs)  29.6 us
    ppermute x5, waiting for transfers between devices, swap_seq(): return lax.ppermute(array, 'seq', [(i, i ^ bit) for i in range(seq)])  17.4 us
    ppermute x7, starting transfers between devices, swap_rows(): return lax.ppermute(array, 'rows', [(i, i ^ bit) for i in range(rows)])  8.24 us
    ppermute x5, starting transfers between devices, swap_seq(): return lax.ppermute(array, 'seq', [(i, i ^ bit) for i in range(seq)])  7.16 us
  transfers between devices with their start and end apart: 37, of which 12 were waited for; matrix products, arithmetic and copies ran while one was open for 3% of the time, Pallas kernels for 26%

profile of v5, /device:TPU:1, one launch (start us, length us, event | category | flops | bytes accessed | tf_op | source)
XLA Modules:
  0.0 149.2 jit_solution(3911571441507132030)
XLA Ops:
  0.7 1.1 pack.1
  1.8 3.2 %collective-permute-start.1 = (bf16[400,512]{1,0:T(8,128)(2,1)S(1)}, bf16[400,512]{1,0:T(8,128)(2,1)S(1)}, u32[]{:S(2)}, u32[]{:S(2)}) collective-permute-start(bf16[400,512]{1,0:T(8,128)(2,1)S(1)} %pack.1), channel_id=1, source_target_pairs={{0,2},{1,3},{2,0},{3,1},{4,6},{5,7},{6,4},{7,5},{8,10},{9,11},{10,... | collective-permute-start | bytes 1228808 | tf_op jit(solution)/shard_map/ppermute | solution.py:597
  5.0 1.3 collective-permute-start
  6.3 16.7 %collective-permute-done.1.wire_ref = bf16[400,512]{1,0:T(8,128)(2,1)S(1)} collective-permute-done((bf16[400,512]{1,0:T(8,128)(2,1)S(1)}, bf16[400,512]{1,0:T(8,128)(2,1)S(1)}, u32[]{:S(2)}, u32[]{:S(2)}) %collective-permute-start.1) | collective-permute-done | bytes 409632 | tf_op jit(solution)/shard_map/ppermute | solution.py:597
  23.0 1.2 collective-permute-start.3
  24.2 0.3 collective-permute-start.2
  24.6 1.1 collective-permute-start.4
  25.8 0.8 copy.59.table_ref
  26.5 2.7 %prepare.1 = (f32[4,256,512]{2,1,0:T(8,128)S(1)}, bf16[512,512]{1,0:T(8,128)(2,1)S(1)}, bf16[512,512]{1,0:T(8,128)(2,1)S(1)}, bf16[512,512]{1,0:T(8,128)(2,1)S(1)}, bf16[512,512]{1,0:T(8,128)(2,1)S(1)}) custom-call(s32[1]{0:T(128)} %bitcast.place_ref, f32[32,8]{1,0:T(8,128)S(1)} %copy.59.table_ref, bf16[512,512]{1,0:T(8,128)(2,1)} %refs_0_.2, ...), custom_call_target="tpu_custom_call" | custom-call | tf_op jit(solution)/shard_map/prepare/pallas_call | solution.py:563
  29.3 2.8 %attention.3 = (f32[4,256,512]{2,1,0:T(8,128)S(1)}, bf16[512,512]{1,0:T(8,128)(2,1)S(1)}, bf16[512,512]{1,0:T(8,128)(2,1)S(1)}, bf16[512,512]{1,0:T(8,128)(2,1)S...) custom-call(s32[1]{0:T(128)} %bitcast.place_ref, ...), custom_call_target="tpu_custom_call", output_to_operand_aliasing={{0}: (13, {}), {1}: (14, {}), {2}: (15, {}), {3}: (16, {}),... | custom-call | flops 268435456 | bytes 1048576 | tf_op jit(solution)/shard_map/attention/pallas_call | solution.py:563
  32.1 0.6 collective-permute-done.4.x3_ref
  32.8 2.8 %attention.4 = (f32[4,256,512]{2,1,0:T(8,128)S(1)}, bf16[512,512]{1,0:T(8,128)(2,1)S(1)}, bf16[512,512]{1,0:T(8,128)(2,1)S(1)}, bf16[512,512]{1,0:T(8,128)(2,1)S...) custom-call(s32[1]{0:T(128)} %bitcast.place_ref, ...), custom_call_target="tpu_custom_call", output_to_operand_aliasing={{0}: (13, {}), {1}: (14, {}), {2}: (15, {}), {3}: (16, {}),... | custom-call | flops 268435456 | bytes 1048576 | tf_op jit(solution)/shard_map/attention/pallas_call | solution.py:563
  35.5 3.1 %attention.5 = (f32[4,256,512]{2,1,0:T(8,128)S(1)}, bf16[512,512]{1,0:T(8,128)(2,1)S(1)}, bf16[512,512]{1,0:T(8,128)(2,1)S(1)}, bf16[512,512]{1,0:T(8,128)(2,1)S...) custom-call(s32[1]{0:T(128)} %bitcast.place_ref, ...), custom_call_target="tpu_custom_call", output_to_operand_aliasing={{0}: (13, {}), {1}: (14, {}), {2}: (15, {}), {3}: (16, {}),... | custom-call | flops 268435456 | bytes 1048576 | tf_op jit(solution)/shard_map/attention/pallas_call | solution.py:563
  38.6 3.7 %mlp.2 = (f32[384,512]{1,0:T(8,128)S(1)}, f32[384,512]{1,0:T(8,128)S(1)}, bf16[16,64,512]{2,1,0:T(8,128)(2,1)S(1)}, bf16[16,64,512]{2,1,0:T(8,128)(2,1)S(1)}) custom-call(s32[3]{0:T(128)S(1)} %pad_add_fusion.code_ref, bf16[128,512]{1,0:T(8,128)(2,1)S(1)} %get-tuple-element.189.refs_0_, bf16[128,512]{1,0:T(8,128)(2,1)S(1)} %get-tuple-element.185.refs_1_.refs_0_, ...), custom_call_target="tpu_custom_call" | custom-call | flops 2415919104 | bytes 9437184 | tf_op jit(solution)/shard_map/mlp/pallas_call | solution.py:563
  42.3 2.3 %collective-permute-start.6 = (bf16[16,64,512]{2,1,0:T(8,128)(2,1)S(1)}, bf16[16,64,512]{2,1,0:T(8,128)(2,1)S(1)}, u32[]{:S(2)}, u32[]{:S(2)}) collective-permute-start(bf16[16,64,512]{2,1,0:T(8,128)(2,1)S(1)} %get-tuple-element.200), channel_id=1, source_target_pairs={{0,4},{4,0},{8,12},{12,8},{16,20},{20,16},{24,28},{28,24},{1,5},{5... | collective-permute-start | bytes 3145736 | tf_op jit(solution)/shard_map/ppermute | solution.py:594
  44.7 3.9 %mlp.3 = (f32[384,512]{1,0:T(8,128)S(1)}, f32[384,512]{1,0:T(8,128)S(1)}, bf16[16,64,512]{2,1,0:T(8,128)(2,1)S(1)}, bf16[16,64,512]{2,1,0:T(8,128)(2,1)S(1)}) custom-call(s32[3]{0:T(128)S(1)} %pad_add_fusion.code_ref, bf16[128,512]{1,0:T(8,128)(2,1)S(1)} %get-tuple-element.189.refs_0_, bf16[128,512]{1,0:T(8,128)(2,1)S(1)} %get-tuple-element.185.refs_1_.refs_0_, ...), custom_call_target="tpu_custom_call" | custom-call | flops 2415919104 | bytes 9437184 | tf_op jit(solution)/shard_map/mlp/pallas_call | solution.py:563
  48.8 1.1 collective-permute-start.8
  50.0 0.5 collective-permute-start.7
  50.5 3.9 %attention_back.3 = (bf16[3,128,512]{2,1,0:T(8,128)(2,1)}, f32[128,512]{1,0:T(8,128)S(1)}, bf16[2,512,128]{2,1,0:T(8,128)(2,1)S(1)}, bf16[2,512,128]{2,1,0:T(8,1...) custom-call(s32[1]{0:T(128)} %bitcast.place_ref, ...), custom_call_target="tpu_custom_call" | custom-call | flops 671088640 | bytes 2621440 | tf_op jit(solution)/shard_map/attention_back/pallas_call | solution.py:563
  54.5 4.3 %attention_back.4 = (bf16[3,128,512]{2,1,0:T(8,128)(2,1)}, f32[128,512]{1,0:T(8,128)S(1)}, bf16[2,512,128]{2,1,0:T(8,128)(2,1)S(1)}, bf16[2,512,128]{2,1,0:T(8,1...) custom-call(s32[1]{0:T(128)} %bitcast.place_ref, ...), custom_call_target="tpu_custom_call", output_to_operand_aliasing={{0}: (28, {}), {4}: (22, {}), {5}: (23, {}), {6}: (24, {}),... | custom-call | flops 671088640 | bytes 2621440 | tf_op jit(solution)/shard_map/attention_back/pallas_call | solution.py:563
  58.8 2.8 %collective-permute-start.10 = (bf16[2,512,128]{2,1,0:T(8,128)(2,1)S(1)}, bf16[2,512,128]{2,1,0:T(8,128)(2,1)S(1)}, u32[]{:S(2)}, u32[]{:S(2)}) collective-permute-start(bf16[2,512,128]{2,1,0:T(8,128)(2,1)S(1)} %get-tuple-element.239), channel_id=1, source_target_pairs={{0,1},{1,0},{2,3},{3,2},{4,6},{5,7},{6,4},{7,5},{8,9},{9,8},{10,11... | collective-permute-start | bytes 786440 | tf_op jit(solution)/shard_map/ppermute | solution.py:612
  61.8 1.3 collective-permute-start.11
  63.2 0.8 collective-permute-start.14
  63.9 5.5 %attention_back.5 = (bf16[3,128,512]{2,1,0:T(8,128)(2,1)}, f32[128,512]{1,0:T(8,128)S(1)}, bf16[2,512,128]{2,1,0:T(8,128)(2,1)S(1)}, bf16[2,512,128]{2,1,0:T(8,1...) custom-call(s32[1]{0:T(128)} %bitcast.place_ref, ...), custom_call_target="tpu_custom_call", output_to_operand_aliasing={{0}: (28, {}), {4}: (22, {}), {5}: (23, {}), {6}: (24, {}),... | custom-call | flops 671088640 | bytes 2621440 | tf_op jit(solution)/shard_map/attention_back/pallas_call | solution.py:563
  69.5 3.1 %collective-permute-start.13 = (bf16[2,64,512]{2,1,0:T(8,128)(2,1)S(1)}, bf16[2,64,512]{2,1,0:T(8,128)(2,1)S(1)}, u32[]{:S(2)}, u32[]{:S(2)}) collective-permute-start(bf16[2,64,512]{2,1,0:T(8,128)(2,1)S(1)} %add_convert_fusion.16), channel_id=1, source_target_pairs={{0,1},{1,0},{2,3},{3,2},{4,6},{5,7},{6,4},{7,5},{8,9},{9,8},{10,11... | collective-permute-start | bytes 393224 | tf_op jit(solution)/shard_map/ppermute | solution.py:612
  72.5 1.6 %rider.1 = f32[16,512]{1,0:T(8,128)S(1)} custom-call(s32[1]{0:T(128)} %bitcast.place_ref, f32[512,512]{1,0:T(8,128)S(1)} %get-tuple-element.245.gq_ref, f32[512,512]{1,0:T(8,128)S(1)} %get-tuple-element.246.gk_ref, f32[512,512]{1,0:T(8,128)S(1)} %get-tuple-element.247.gv_ref, f32[4,256,512]{2,1,0:T(8,128)S(1)} %get-tuple-element.248.table_sum_ref, ...), custom_call_target="tpu_custom_call" | custom-call | tf_op jit(solution)/shard_map/rider/pallas_call | solution.py:563
  74.2 0.3 collective-permute-start.15
  74.5 3.2 %collective-permute-start.17 = (bf16[2,64,512]{2,1,0:T(8,128)(2,1)S(1)}, bf16[2,64,512]{2,1,0:T(8,128)(2,1)S(1)}, u32[]{:S(2)}, u32[]{:S(2)}) collective-permute-start(bf16[2,64,512]{2,1,0:T(8,128)(2,1)S(1)} %add_convert_fusion.15), channel_id=1, source_target_pairs={{0,1},{1,0},{2,3},{3,2},{4,6},{5,7},{6,4},{7,5},{8,9},{9,8},{10,11... | collective-permute-start | bytes 393224 | tf_op jit(solution)/shard_map/ppermute | solution.py:612
  78.0 3.6 %collective-permute-done.17 = bf16[2,64,512]{2,1,0:T(8,128)(2,1)S(1)} collective-permute-done((bf16[2,64,512]{2,1,0:T(8,128)(2,1)S(1)}, bf16[2,64,512]{2,1,0:T(8,128)(2,1)S(1)}, u32[]{:S(2)}, u32[]{:S(2)}) %collective-permute-start.17) | collective-permute-done | bytes 131104 | tf_op jit(solution)/shard_map/ppermute | solution.py:612
  82.0 1.3 collective-permute-start.18
  83.3 1.3 collective-permute-done.19
  84.6 1.6 %collective-permute-done.18 = bf16[2,64,512]{2,1,0:T(8,128)(2,1)S(1)} collective-permute-done((bf16[2,64,512]{2,1,0:T(8,128)(2,1)S(1)}, bf16[2,64,512]{2,1,0:T(8,128)(2,1)S(1)}, u32[]{:S(2)}, u32[]{:S(2)}) %collective-permute-start.18) | collective-permute-done | bytes 131104 | tf_op jit(solution)/shard_map/ppermute | solution.py:612
  86.2 4.1 %collective-permute-done.16 = bf16[544,512]{1,0:T(8,128)(2,1)S(1)} collective-permute-done((bf16[544,512]{1,0:T(8,128)(2,1)S(1)}, bf16[544,512]{1,0:T(8,128)(2,1)S(1)}, u32[]{:S(2)}, u32[]{:S(2)}) %collective-permute-start.16) | collective-permute-done | bytes 557088 | tf_op jit(solution)/shard_map/ppermute | solution.py:612
  90.5 1.0 collective-permute-start.20
  91.5 1.6 %collective-permute-start.22 = (bf16[2,64,512]{2,1,0:T(8,128)(2,1)S(1)}, bf16[2,64,512]{2,1,0:T(8,128)(2,1)S(1)}, u32[]{:S(2)}, u32[]{:S(2)}) collective-permute-start(bf16[2,64,512]{2,1,0:T(8,128)(2,1)S(1)} %add_convert_fusion.9), channel_id=1, source_target_pairs={{0,1},{1,0},{2,3},{3,2},{4,6},{5,7},{6,4},{7,5},{8,9},{9,8},{10,11... | collective-permute-start | bytes 393224 | tf_op jit(solution)/shard_map/ppermute | solution.py:612
  93.1 0.8 collective-permute-start.23
  93.9 2.6 %collective-permute-done.20 = bf16[288,512]{1,0:T(8,128)(2,1)S(1)} collective-permute-done((bf16[288,512]{1,0:T(8,128)(2,1)S(1)}, bf16[288,512]{1,0:T(8,128)(2,1)S(1)}, u32[]{:S(2)}, u32[]{:S(2)}) %collective-permute-start.20) | collective-permute-done | bytes 294944 | tf_op jit(solution)/shard_map/ppermute | solution.py:612
  96.6 1.7 %collective-permute-start.24 = (bf16[160,512]{1,0:T(8,128)(2,1)S(1)}, bf16[160,512]{1,0:T(8,128)(2,1)S(1)}, u32[]{:S(2)}, u32[]{:S(2)}) collective-permute-start(bf16[160,512]{1,0:T(8,128)(2,1)S(1)} %pad_maximum_fusion.13), channel_id=1, source_target_pairs={{0,1},{1,0},{2,3},{3,2},{4,6},{5,7},{6,4},{7,5},{8,9},{9,8},{10,11... | collective-permute-start | bytes 491528 | tf_op jit(solution)/shard_map/ppermute | solution.py:612
  98.5 0.8 collective-permute-start.21
  99.3 5.7 %collective-permute-done.24 = bf16[160,512]{1,0:T(8,128)(2,1)S(1)} collective-permute-done((bf16[160,512]{1,0:T(8,128)(2,1)S(1)}, bf16[160,512]{1,0:T(8,128)(2,1)S(1)}, u32[]{:S(2)}, u32[]{:S(2)}) %collective-permute-start.24) | collective-permute-done | bytes 163872 | tf_op jit(solution)/shard_map/ppermute | solution.py:612
  105.1 0.8 collective-permute-start.27
  106.0 1.8 %collective-permute-start.26 = (bf16[160,512]{1,0:T(8,128)(2,1)S(1)}, bf16[160,512]{1,0:T(8,128)(2,1)S(1)}, u32[]{:S(2)}, u32[]{:S(2)}) collective-permute-start(bf16[160,512]{1,0:T(8,128)(2,1)S(1)} %pad_maximum_fusion.14), channel_id=1, source_target_pairs={{0,2},{1,3},{2,0},{3,1},{4,5},{5,4},{6,7},{7,6},{8,10},{9,11},{10,... | collective-permute-start | bytes 491528 | tf_op jit(solution)/shard_map/ppermute | solution.py:612
  107.7 0.3 collective-permute-start.25
  108.0 2.7 %collective-permute-done.27 = bf16[4,64,512]{2,1,0:T(8,128)(2,1)S(1)} collective-permute-done((bf16[4,64,512]{2,1,0:T(8,128)(2,1)S(1)}, bf16[4,64,512]{2,1,0:T(8,128)(2,1)S(1)}, u32[]{:S(2)}, u32[]{:S(2)}) %collective-permute-start.27) | collective-permute-done | bytes 262176 | tf_op jit(solution)/shard_map/ppermute | solution.py:612
  110.8 0.9 collective-permute-start.30
  111.7 3.1 %collective-permute-done.26 = bf16[160,512]{1,0:T(8,128)(2,1)S(1)} collective-permute-done((bf16[160,512]{1,0:T(8,128)(2,1)S(1)}, bf16[160,512]{1,0:T(8,128)(2,1)S(1)}, u32[]{:S(2)}, u32[]{:S(2)}) %collective-permute-start.26) | collective-permute-done | bytes 163872 | tf_op jit(solution)/shard_map/ppermute | solution.py:612
  114.8 1.4 collective-permute-start.29
  116.5 2.3 %collective-permute-start.28 = (bf16[3,512,128]{2,1,0:T(8,128)(2,1)S(1)}, bf16[3,512,128]{2,1,0:T(8,128)(2,1)S(1)}, u32[]{:S(2)}, u32[]{:S(2)}) collective-permute-start(bf16[3,512,128]{2,1,0:T(8,128)(2,1)S(1)} %pad_maximum_fusion.8), channel_id=1, source_target_pairs={{0,2},{1,3},{2,0},{3,1},{4,5},{5,4},{6,7},{7,6},{8,10},{9,11},{10,... | collective-permute-start | bytes 1179656 | tf_op jit(solution)/shard_map/ppermute | solution.py:612
  118.8 2.3 %collective-permute-done.30 = bf16[8,64,512]{2,1,0:T(8,128)(2,1)S(1)} collective-permute-done((bf16[8,64,512]{2,1,0:T(8,128)(2,1)S(1)}, bf16[8,64,512]{2,1,0:T(8,128)(2,1)S(1)}, u32[]{:S(2)}, u32[]{:S(2)}) %collective-permute-start.30) | collective-permute-done | bytes 524320 | tf_op jit(solution)/shard_map/ppermute | solution.py:612
  121.3 1.2 collective-permute-start.31
  122.6 1.7 %collective-permute-start.35 = (bf16[16,64,512]{2,1,0:T(8,128)(2,1)S(1)}, bf16[16,64,512]{2,1,0:T(8,128)(2,1)S(1)}, u32[]{:S(2)}, u32[]{:S(2)}) collective-permute-start(bf16[16,64,512]{2,1,0:T(8,128)(2,1)S(1)} %pad_maximum_fusion.half_ref), channel_id=1, source_target_pairs={{0,4},{4,0},{8,12},{12,8},{16,20},{20,16},{24,28},{28,24},{1,5},{5... | collective-permute-start | bytes 3145736 | tf_op jit(solution)/shard_map/ppermute | solution.py:594
  124.3 5.5 %collective-permute-done.31 = bf16[4,64,512]{2,1,0:T(8,128)(2,1)S(1)} collective-permute-done((bf16[4,64,512]{2,1,0:T(8,128)(2,1)S(1)}, bf16[4,64,512]{2,1,0:T(8,128)(2,1)S(1)}, u32[]{:S(2)}, u32[]{:S(2)}) %collective-permute-start.31) | collective-permute-done | bytes 262176 | tf_op jit(solution)/shard_map/ppermute | solution.py:612
  129.8 1.3 post.1
  131.2 3.3 %collective-permute-start.34 = (bf16[16,64,512]{2,1,0:T(8,128)(2,1)S(1)}, bf16[16,64,512]{2,1,0:T(8,128)(2,1)S(1)}, u32[]{:S(2)}, u32[]{:S(2)}) collective-permute-start(bf16[16,64,512]{2,1,0:T(8,128)(2,1)S(1)} %pad_maximum_fusion.1.half_ref), channel_id=1, source_target_pairs={{0,4},{4,0},{8,12},{12,8},{16,20},{20,16},{24,28},{28,24},{1,5},{5... | collective-permute-start | bytes 3145736 | tf_op jit(solution)/shard_map/ppermute | solution.py:594
  134.5 0.8 collective-permute-start.32
  135.3 1.9 %finish_outer.2.refs_0_ = f32[2048,512]{1,0:T(8,128)} custom-call(s32[3]{0:T(128)S(1)} %pad_add_fusion.code_ref, bf16[16,64,512]{2,1,0:T(8,128)(2,1)S(1)} %pad_maximum_fusion.half_ref), custom_call_target="tpu_custom_call" | custom-call | tf_op jit(solution)/shard_map/finish_outer/pallas_call | solution.py:563
  137.3 1.9 %finish_outer.3 = f32[2048,512]{1,0:T(8,128)} custom-call(s32[3]{0:T(128)S(1)} %pad_add_fusion.code_ref, bf16[16,64,512]{2,1,0:T(8,128)(2,1)S(1)} %collective-permute-done.35.half_ref, f32[2048,512]{1,0:T(8,128)} %finish_outer.2.refs_0_), custom_call_target="tpu_custom_call", output_to_operand_aliasing={{}: (2, {})} | custom-call | tf_op jit(solution)/shard_map/finish_outer/pallas_call | solution.py:563
  139.2 2.0 %finish_inner.2.refs_0_ = f32[512,2048]{1,0:T(8,128)} custom-call(s32[3]{0:T(128)S(1)} %pad_add_fusion.code_ref, bf16[16,64,512]{2,1,0:T(8,128)(2,1)S(1)} %pad_maximum_fusion.1.half_ref), custom_call_target="tpu_custom_call" | custom-call | tf_op jit(solution)/shard_map/finish_inner/pallas_call | solution.py:563
  141.2 2.0 %finish_inner.3 = f32[512,2048]{1,0:T(8,128)} custom-call(s32[3]{0:T(128)S(1)} %pad_add_fusion.code_ref, bf16[16,64,512]{2,1,0:T(8,128)(2,1)S(1)} %collective-permute-done.34.half_ref, f32[512,2048]{1,0:T(8,128)} %finish_inner.2.refs_0_), custom_call_target="tpu_custom_call", output_to_operand_aliasing={{}: (2, {})} | custom-call | tf_op jit(solution)/shard_map/finish_inner/pallas_call | solution.py:563
  143.4 0.6 collective-permute-start.36
  144.0 0.6 slice_bitcast_fusion
  144.6 0.6 fusion.29
  145.2 1.9 %finish_small.2 = (f32[512,512]{1,0:T(8,128)}, f32[512,512]{1,0:T(8,128)}, f32[512,512]{1,0:T(8,128)}, f32[512,512]{1,0:T(8,128)}) custom-call(s32[3]{0:T(128)S(1)} %pad_add_fusion.code_ref, bf16[16,64,512]{2,1,0:T(8,128)(2,1)S(1)} %pad_maximum_fusion.2.half_ref), custom_call_target="tpu_custom_call" | custom-call | tf_op jit(solution)/shard_map/finish_small/pallas_call | solution.py:563
  147.1 1.9 %finish_small.3 = (f32[512,512]{1,0:T(8,128)}, f32[512,512]{1,0:T(8,128)}, f32[512,512]{1,0:T(8,128)}, f32[512,512]{1,0:T(8,128)}) custom-call(s32[3]{0:T(128)S(1)} %pad_add_fusion.code_ref, bf16[16,64,512]{2,1,0:T(8,128)(2,1)S(1)} %collective-permute-done.36.half_ref, ...), custom_call_target="tpu_custom_call", output_to_operand_aliasing={{0}: (2, {}), {1}: (3, {}), {2}: (4, {}), {3}: (5, {})} | custom-call | tf_op jit(solution)/shard_map/finish_small/pallas_call | solution.py:563
  (102 shorter events, 3.1 us)
Async XLA Ops:
  0.6 28.6 %copy-start.3 = (s32[3,128]{1,0:T(4,128)S(1)}, s32[3,128]{1,0:T(4,128)}, u32[]{:S(2)}) copy-start(s32[3,128]{1,0:T(4,128)} %seen_ref.6) | copy-start | bytes 4612
  0.7 28.6 %copy-start = (bf16[3,128,512]{2,1,0:T(8,128)(2,1)S(1)}, bf16[3,128,512]{2,1,0:T(8,128)(2,1)}, u32[]{:S(2)}) copy-start(bf16[3,128,512]{2,1,0:T(8,128)(2,1)} %x_ref.3) | copy-start | bytes 1179652
  0.7 28.6 %copy-start.4 = (s32[3,4]{1,0:T(4,128)S(1)}, s32[3,4]{1,0:T(4,128)}, u32[]{:S(2)}) copy-start(s32[3,4]{1,0:T(4,128)} %lengths_ref.5) | copy-start | bytes 148
  0.7 28.6 %copy-start.1 = (f32[512]{0:T(512)S(1)}, f32[512]{0:T(512)}, u32[]{:S(2)}) copy-start(f32[512]{0:T(512)} %param.20) | copy-start | bytes 6148
  0.7 28.6 %copy-start.2 = (f32[512]{0:T(512)S(1)}, f32[512]{0:T(512)}, u32[]{:S(2)}) copy-start(f32[512]{0:T(512)} %param.15) | copy-start | bytes 6148
  1.8 21.2 %collective-permute-start.1 = (bf16[400,512]{1,0:T(8,128)(2,1)S(1)}, bf16[400,512]{1,0:T(8,128)(2,1)S(1)}, u32[]{:S(2)}, u32[]{:S(2)}) collective-permute-start(bf16[400,512]{1,0:T(8,128)(2,1)S(1)} %pack.1), channel_id=1, source_target_pairs={{0,2},{1,3},{2,0},{3,1},{4,6},{5,7},{6,4},{7,5},{8,10},{9,11},{10,... | collective-permute-start | bytes 1228808 | tf_op jit(solution)/shard_map/ppermute | solution.py:597
  5.0 24.3 %collective-permute-start = (bf16[400,512]{1,0:T(8,128)(2,1)S(1)}, bf16[400,512]{1,0:T(8,128)(2,1)S(1)}, u32[]{:S(2)}, u32[]{:S(2)}) collective-permute-start(bf16[400,512]{1,0:T(8,128)(2,1)S(1)} %pack.1), channel_id=1, source_target_pairs={{0,1},{1,0},{2,3},{3,2},{4,5},{5,4},{6,7},{7,6},{8,9},{9,8},{10,11... | collective-permute-start | bytes 1228808 | tf_op jit(solution)/shard_map/ppermute | solution.py:597
  23.0 6.2 %collective-permute-start.3 = (bf16[144,512]{1,0:T(8,128)(2,1)S(1)}, bf16[144,512]{1,0:T(8,128)(2,1)S(1)}, u32[]{:S(2)}, u32[]{:S(2)}) collective-permute-start(bf16[144,512]{1,0:T(8,128)(2,1)S(1)} %get-tuple-element.156.x2_ref.x2_tail_ref), channel_id=1, source_target_pairs={{0,1},{1,0},{2,3},{3,2},{4,5},{5,4},{6,7},{7,6},{8,9},{9,8},{10,11... | collective-permute-start | bytes 442376 | tf_op jit(solution)/shard_map/ppermute | solution.py:597
  24.2 11.3 %collective-permute-start.2 = (bf16[128,512]{1,0:T(8,128)(2,1)S(1)}, bf16[128,512]{1,0:T(8,128)(2,1)S(1)}, u32[]{:S(2)}, u32[]{:S(2)}) collective-permute-start(bf16[128,512]{1,0:T(8,128)(2,1)S(1)} %get-tuple-element.155.x2_ref), channel_id=1, source_target_pairs={{0,1},{1,0},{2,3},{3,2},{4,5},{5,4},{6,7},{7,6},{8,9},{9,8},{10,11... | collective-permute-start | bytes 393224 | tf_op jit(solution)/shard_map/ppermute | solution.py:597
  24.6 8.2 %collective-permute-start.4 = (bf16[128,512]{1,0:T(8,128)(2,1)S(1)}, bf16[128,512]{1,0:T(8,128)(2,1)S(1)}, u32[]{:S(2)}, u32[]{:S(2)}) collective-permute-start(bf16[128,512]{1,0:T(8,128)(2,1)S(1)} %get-tuple-element.157.x2_ref), channel_id=1, source_target_pairs={{0,1},{1,0},{2,3},{3,2},{4,5},{5,4},{6,7},{7,6},{8,9},{9,8},{10,11... | collective-permute-start | bytes 393224 | tf_op jit(solution)/shard_map/ppermute | solution.py:597
  42.3 6.3 %collective-permute-start.6 = (bf16[16,64,512]{2,1,0:T(8,128)(2,1)S(1)}, bf16[16,64,512]{2,1,0:T(8,128)(2,1)S(1)}, u32[]{:S(2)}, u32[]{:S(2)}) collective-permute-start(bf16[16,64,512]{2,1,0:T(8,128)(2,1)S(1)} %get-tuple-element.200), channel_id=1, source_target_pairs={{0,4},{4,0},{8,12},{12,8},{16,20},{20,16},{24,28},{28,24},{1,5},{5... | collective-permute-start | bytes 3145736 | tf_op jit(solution)/shard_map/ppermute | solution.py:594
  44.6 5.2 %collective-permute-start.5 = (bf16[16,64,512]{2,1,0:T(8,128)(2,1)S(1)}, bf16[16,64,512]{2,1,0:T(8,128)(2,1)S(1)}, u32[]{:S(2)}, u32[]{:S(2)}) collective-permute-start(bf16[16,64,512]{2,1,0:T(8,128)(2,1)S(1)} %get-tuple-element.198), channel_id=1, source_target_pairs={{0,4},{4,0},{8,12},{12,8},{16,20},{20,16},{24,28},{28,24},{1,5},{5... | collective-permute-start | bytes 3145736 | tf_op jit(solution)/shard_map/ppermute | solution.py:594
  48.8 12.9 %collective-permute-start.8 = (bf16[8,64,512]{2,1,0:T(8,128)(2,1)S(1)}, bf16[8,64,512]{2,1,0:T(8,128)(2,1)S(1)}, u32[]{:S(2)}, u32[]{:S(2)}) collective-permute-start(bf16[8,64,512]{2,1,0:T(8,128)(2,1)S(1)} %add_convert_fusion.2), channel_id=1, source_target_pairs={{0,8},{1,9},{2,10},{3,11},{4,20},{5,21},{6,22},{7,23},{8,0},{9,1},... | collective-permute-start | bytes 1572872 | tf_op jit(solution)/shard_map/ppermute | solution.py:612
  50.0 13.1 %collective-permute-start.7 = (bf16[8,64,512]{2,1,0:T(8,128)(2,1)S(1)}, bf16[8,64,512]{2,1,0:T(8,128)(2,1)S(1)}, u32[]{:S(2)}, u32[]{:S(2)}) collective-permute-start(bf16[8,64,512]{2,1,0:T(8,128)(2,1)S(1)} %add_convert_fusion.1.refs_19_), channel_id=1, source_target_pairs={{0,8},{1,9},{2,10},{3,11},{4,20},{5,21},{6,22},{7,23},{8,0},{9,1},... | collective-permute-start | bytes 1572872 | tf_op jit(solution)/shard_map/ppermute | solution.py:612
  58.8 35.1 %collective-permute-start.10 = (bf16[2,512,128]{2,1,0:T(8,128)(2,1)S(1)}, bf16[2,512,128]{2,1,0:T(8,128)(2,1)S(1)}, u32[]{:S(2)}, u32[]{:S(2)}) collective-permute-start(bf16[2,512,128]{2,1,0:T(8,128)(2,1)S(1)} %get-tuple-element.239), channel_id=1, source_target_pairs={{0,1},{1,0},{2,3},{3,2},{4,6},{5,7},{6,4},{7,5},{8,9},{9,8},{10,11... | collective-permute-start | bytes 786440 | tf_op jit(solution)/shard_map/ppermute | solution.py:612
  61.6 32.3 %collective-permute-start.9 = (bf16[2,512,128]{2,1,0:T(8,128)(2,1)S(1)}, bf16[2,512,128]{2,1,0:T(8,128)(2,1)S(1)}, u32[]{:S(2)}, u32[]{:S(2)}) collective-permute-start(bf16[2,512,128]{2,1,0:T(8,128)(2,1)S(1)} %get-tuple-element.238), channel_id=1, source_target_pairs={{0,1},{1,0},{2,3},{3,2},{4,6},{5,7},{6,4},{7,5},{8,9},{9,8},{10,11... | collective-permute-start | bytes 786440 | tf_op jit(solution)/shard_map/ppermute | solution.py:612
  61.8 7.6 %collective-permute-start.11 = (bf16[4,64,512]{2,1,0:T(8,128)(2,1)S(1)}, bf16[4,64,512]{2,1,0:T(8,128)(2,1)S(1)}, u32[]{:S(2)}, u32[]{:S(2)}) collective-permute-start(bf16[4,64,512]{2,1,0:T(8,128)(2,1)S(1)} %add_convert_fusion.4), channel_id=1, source_target_pairs={{0,16},{1,17},{2,18},{3,19},{4,12},{5,13},{6,14},{7,15},{8,24},{9,... | collective-permute-start | bytes 786440 | tf_op jit(solution)/shard_map/ppermute | solution.py:612
  63.2 11.0 %collective-permute-start.14 = (bf16[4,64,512]{2,1,0:T(8,128)(2,1)S(1)}, bf16[4,64,512]{2,1,0:T(8,128)(2,1)S(1)}, u32[]{:S(2)}, u32[]{:S(2)}) collective-permute-start(bf16[4,64,512]{2,1,0:T(8,128)(2,1)S(1)} %add_convert_fusion.3.refs_19_), channel_id=1, source_target_pairs={{0,16},{1,17},{2,18},{3,19},{4,12},{5,13},{6,14},{7,15},{8,24},{9,... | collective-permute-start | bytes 786440 | tf_op jit(solution)/shard_map/ppermute | solution.py:612
  69.5 8.3 %collective-permute-start.13 = (bf16[2,64,512]{2,1,0:T(8,128)(2,1)S(1)}, bf16[2,64,512]{2,1,0:T(8,128)(2,1)S(1)}, u32[]{:S(2)}, u32[]{:S(2)}) collective-permute-start(bf16[2,64,512]{2,1,0:T(8,128)(2,1)S(1)} %add_convert_fusion.16), channel_id=1, source_target_pairs={{0,1},{1,0},{2,3},{3,2},{4,6},{5,7},{6,4},{7,5},{8,9},{9,8},{10,11... | collective-permute-start | bytes 393224 | tf_op jit(solution)/shard_map/ppermute | solution.py:612
  74.2 3.5 %collective-permute-start.15 = (bf16[32,512]{1,0:T(8,128)(2,1)S(1)}, bf16[32,512]{1,0:T(8,128)(2,1)S(1)}, u32[]{:S(2)}, u32[]{:S(2)}) collective-permute-start(bf16[32,512]{1,0:T(8,128)(2,1)S(1)} %pad_maximum_fusion.18), channel_id=1, source_target_pairs={{0,4},{4,0},{8,12},{12,8},{16,20},{20,16},{24,28},{28,24},{1,5},{5... | collective-permute-start | bytes 98312 | tf_op jit(solution)/shard_map/ppermute | solution.py:594
  74.5 7.1 %collective-permute-start.17 = (bf16[2,64,512]{2,1,0:T(8,128)(2,1)S(1)}, bf16[2,64,512]{2,1,0:T(8,128)(2,1)S(1)}, u32[]{:S(2)}, u32[]{:S(2)}) collective-permute-start(bf16[2,64,512]{2,1,0:T(8,128)(2,1)S(1)} %add_convert_fusion.15), channel_id=1, source_target_pairs={{0,1},{1,0},{2,3},{3,2},{4,6},{5,7},{6,4},{7,5},{8,9},{9,8},{10,11... | collective-permute-start | bytes 393224 | tf_op jit(solution)/shard_map/ppermute | solution.py:612
  77.7 4.0 %collective-permute-start.12 = (bf16[16,64,512]{2,1,0:T(8,128)(2,1)S(1)}, bf16[16,64,512]{2,1,0:T(8,128)(2,1)S(1)}, u32[]{:S(2)}, u32[]{:S(2)}) collective-permute-start(bf16[16,64,512]{2,1,0:T(8,128)(2,1)S(1)} %get-tuple-element.244), channel_id=1, source_target_pairs={{0,4},{4,0},{8,12},{12,8},{16,20},{20,16},{24,28},{28,24},{1,5},{5... | collective-permute-start | bytes 3145736 | tf_op jit(solution)/shard_map/ppermute | solution.py:594
  77.9 6.7 %collective-permute-start.19 = (bf16[2,64,512]{2,1,0:T(8,128)(2,1)S(1)}, bf16[2,64,512]{2,1,0:T(8,128)(2,1)S(1)}, u32[]{:S(2)}, u32[]{:S(2)}) collective-permute-start(bf16[2,64,512]{2,1,0:T(8,128)(2,1)S(1)} %pad_maximum_fusion.16), channel_id=1, source_target_pairs={{0,2},{1,3},{2,0},{3,1},{4,5},{5,4},{6,7},{7,6},{8,10},{9,11},{10,... | collective-permute-start | bytes 393224 | tf_op jit(solution)/shard_map/ppermute | solution.py:612
  81.9 8.4 %collective-permute-start.16 = (bf16[544,512]{1,0:T(8,128)(2,1)S(1)}, bf16[544,512]{1,0:T(8,128)(2,1)S(1)}, u32[]{:S(2)}, u32[]{:S(2)}) collective-permute-start(bf16[544,512]{1,0:T(8,128)(2,1)S(1)} %pad_maximum_fusion.3), channel_id=1, source_target_pairs={{0,8},{1,9},{2,10},{3,11},{4,20},{5,21},{6,22},{7,23},{8,0},{9,1},... | collective-permute-start | bytes 1671176 | tf_op jit(solution)/shard_map/ppermute | solution.py:612
  82.0 4.2 %collective-permute-start.18 = (bf16[2,64,512]{2,1,0:T(8,128)(2,1)S(1)}, bf16[2,64,512]{2,1,0:T(8,128)(2,1)S(1)}, u32[]{:S(2)}, u32[]{:S(2)}) collective-permute-start(bf16[2,64,512]{2,1,0:T(8,128)(2,1)S(1)} %pad_maximum_fusion.15), channel_id=1, source_target_pairs={{0,2},{1,3},{2,0},{3,1},{4,5},{5,4},{6,7},{7,6},{8,10},{9,11},{10,... | collective-permute-start | bytes 393224 | tf_op jit(solution)/shard_map/ppermute | solution.py:612
  90.5 5.9 %collective-permute-start.20 = (bf16[288,512]{1,0:T(8,128)(2,1)S(1)}, bf16[288,512]{1,0:T(8,128)(2,1)S(1)}, u32[]{:S(2)}, u32[]{:S(2)}) collective-permute-start(bf16[288,512]{1,0:T(8,128)(2,1)S(1)} %pad_maximum_fusion.9), channel_id=1, source_target_pairs={{0,16},{1,17},{2,18},{3,19},{4,12},{5,13},{6,14},{7,15},{8,24},{9,... | collective-permute-start | bytes 884744 | tf_op jit(solution)/shard_map/ppermute | solution.py:612
  91.5 16.2 %collective-permute-start.22 = (bf16[2,64,512]{2,1,0:T(8,128)(2,1)S(1)}, bf16[2,64,512]{2,1,0:T(8,128)(2,1)S(1)}, u32[]{:S(2)}, u32[]{:S(2)}) collective-permute-start(bf16[2,64,512]{2,1,0:T(8,128)(2,1)S(1)} %add_convert_fusion.9), channel_id=1, source_target_pairs={{0,1},{1,0},{2,3},{3,2},{4,6},{5,7},{6,4},{7,5},{8,9},{9,8},{10,11... | collective-permute-start | bytes 393224 | tf_op jit(solution)/shard_map/ppermute | solution.py:612
  93.1 12.0 %collective-permute-start.23 = (bf16[2,64,512]{2,1,0:T(8,128)(2,1)S(1)}, bf16[2,64,512]{2,1,0:T(8,128)(2,1)S(1)}, u32[]{:S(2)}, u32[]{:S(2)}) collective-permute-start(bf16[2,64,512]{2,1,0:T(8,128)(2,1)S(1)} %add_convert_fusion.10), channel_id=1, source_target_pairs={{0,1},{1,0},{2,3},{3,2},{4,6},{5,7},{6,4},{7,5},{8,9},{9,8},{10,11... | collective-permute-start | bytes 393224 | tf_op jit(solution)/shard_map/ppermute | solution.py:612
  96.6 8.3 %collective-permute-start.24 = (bf16[160,512]{1,0:T(8,128)(2,1)S(1)}, bf16[160,512]{1,0:T(8,128)(2,1)S(1)}, u32[]{:S(2)}, u32[]{:S(2)}) collective-permute-start(bf16[160,512]{1,0:T(8,128)(2,1)S(1)} %pad_maximum_fusion.13), channel_id=1, source_target_pairs={{0,1},{1,0},{2,3},{3,2},{4,6},{5,7},{6,4},{7,5},{8,9},{9,8},{10,11... | collective-permute-start | bytes 491528 | tf_op jit(solution)/shard_map/ppermute | solution.py:612
  98.5 17.9 %collective-permute-start.21 = (bf16[2,512,128]{2,1,0:T(8,128)(2,1)S(1)}, bf16[2,512,128]{2,1,0:T(8,128)(2,1)S(1)}, u32[]{:S(2)}, u32[]{:S(2)}) collective-permute-start(bf16[2,512,128]{2,1,0:T(8,128)(2,1)S(1)} %get-tuple-element.265), channel_id=1, source_target_pairs={{0,1},{1,0},{2,3},{3,2},{4,6},{5,7},{6,4},{7,5},{8,9},{9,8},{10,11... | collective-permute-start | bytes 786440 | tf_op jit(solution)/shard_map/ppermute | solution.py:612
  105.1 5.6 %collective-permute-start.27 = (bf16[4,64,512]{2,1,0:T(8,128)(2,1)S(1)}, bf16[4,64,512]{2,1,0:T(8,128)(2,1)S(1)}, u32[]{:S(2)}, u32[]{:S(2)}) collective-permute-start(bf16[4,64,512]{2,1,0:T(8,128)(2,1)S(1)} %pad_maximum_fusion.10), channel_id=1, source_target_pairs={{0,16},{1,17},{2,18},{3,19},{4,12},{5,13},{6,14},{7,15},{8,24},{9,... | collective-permute-start | bytes 786440 | tf_op jit(solution)/shard_map/ppermute | solution.py:612
  106.0 8.8 %collective-permute-start.26 = (bf16[160,512]{1,0:T(8,128)(2,1)S(1)}, bf16[160,512]{1,0:T(8,128)(2,1)S(1)}, u32[]{:S(2)}, u32[]{:S(2)}) collective-permute-start(bf16[160,512]{1,0:T(8,128)(2,1)S(1)} %pad_maximum_fusion.14), channel_id=1, source_target_pairs={{0,2},{1,3},{2,0},{3,1},{4,5},{5,4},{6,7},{7,6},{8,10},{9,11},{10,... | collective-permute-start | bytes 491528 | tf_op jit(solution)/shard_map/ppermute | solution.py:612
  107.7 8.5 %collective-permute-start.25 = (bf16[4,64,512]{2,1,0:T(8,128)(2,1)S(1)}, bf16[4,64,512]{2,1,0:T(8,128)(2,1)S(1)}, u32[]{:S(2)}, u32[]{:S(2)}) collective-permute-start(bf16[4,64,512]{2,1,0:T(8,128)(2,1)S(1)} %pad_maximum_fusion.11), channel_id=1, source_target_pairs={{0,16},{1,17},{2,18},{3,19},{4,12},{5,13},{6,14},{7,15},{8,24},{9,... | collective-permute-start | bytes 786440 | tf_op jit(solution)/shard_map/ppermute | solution.py:612
  110.8 10.3 %collective-permute-start.30 = (bf16[8,64,512]{2,1,0:T(8,128)(2,1)S(1)}, bf16[8,64,512]{2,1,0:T(8,128)(2,1)S(1)}, u32[]{:S(2)}, u32[]{:S(2)}) collective-permute-start(bf16[8,64,512]{2,1,0:T(8,128)(2,1)S(1)} %pad_maximum_fusion.4), channel_id=1, source_target_pairs={{0,8},{1,9},{2,10},{3,11},{4,20},{5,21},{6,22},{7,23},{8,0},{9,1},... | collective-permute-start | bytes 1572872 | tf_op jit(solution)/shard_map/ppermute | solution.py:612
  114.8 6.4 %collective-permute-start.29 = (bf16[2,64,512]{2,1,0:T(8,128)(2,1)S(1)}, bf16[2,64,512]{2,1,0:T(8,128)(2,1)S(1)}, u32[]{:S(2)}, u32[]{:S(2)}) collective-permute-start(bf16[2,64,512]{2,1,0:T(8,128)(2,1)S(1)} %fusion.1), channel_id=1, source_target_pairs={{0,1},{1,0},{2,3},{3,2},{4,6},{5,7},{6,4},{7,5},{8,9},{9,8},{10,11... | collective-permute-start | bytes 393224 | tf_op jit(solution)/shard_map/ppermute | solution.py:612
  116.3 14.8 %collective-permute-start.33 = (bf16[8,64,512]{2,1,0:T(8,128)(2,1)S(1)}, bf16[8,64,512]{2,1,0:T(8,128)(2,1)S(1)}, u32[]{:S(2)}, u32[]{:S(2)}) collective-permute-start(bf16[8,64,512]{2,1,0:T(8,128)(2,1)S(1)} %pad_maximum_fusion.5), channel_id=1, source_target_pairs={{0,8},{1,9},{2,10},{3,11},{4,20},{5,21},{6,22},{7,23},{8,0},{9,1},... | collective-permute-start | bytes 1572872 | tf_op jit(solution)/shard_map/ppermute | solution.py:612
  116.5 13.3 %collective-permute-start.28 = (bf16[3,512,128]{2,1,0:T(8,128)(2,1)S(1)}, bf16[3,512,128]{2,1,0:T(8,128)(2,1)S(1)}, u32[]{:S(2)}, u32[]{:S(2)}) collective-permute-start(bf16[3,512,128]{2,1,0:T(8,128)(2,1)S(1)} %pad_maximum_fusion.8), channel_id=1, source_target_pairs={{0,2},{1,3},{2,0},{3,1},{4,5},{5,4},{6,7},{7,6},{8,10},{9,11},{10,... | collective-permute-start | bytes 1179656 | tf_op jit(solution)/shard_map/ppermute | solution.py:612
  121.3 8.5 %collective-permute-start.31 = (bf16[4,64,512]{2,1,0:T(8,128)(2,1)S(1)}, bf16[4,64,512]{2,1,0:T(8,128)(2,1)S(1)}, u32[]{:S(2)}, u32[]{:S(2)}) collective-permute-start(bf16[4,64,512]{2,1,0:T(8,128)(2,1)S(1)} %pad_maximum_fusion.12), channel_id=1, source_target_pairs={{0,16},{1,17},{2,18},{3,19},{4,12},{5,13},{6,14},{7,15},{8,24},{9,... | collective-permute-start | bytes 786440 | tf_op jit(solution)/shard_map/ppermute | solution.py:612
  122.6 14.7 %collective-permute-start.35 = (bf16[16,64,512]{2,1,0:T(8,128)(2,1)S(1)}, bf16[16,64,512]{2,1,0:T(8,128)(2,1)S(1)}, u32[]{:S(2)}, u32[]{:S(2)}) collective-permute-start(bf16[16,64,512]{2,1,0:T(8,128)(2,1)S(1)} %pad_maximum_fusion.half_ref), channel_id=1, source_target_pairs={{0,4},{4,0},{8,12},{12,8},{16,20},{20,16},{24,28},{28,24},{1,5},{5... | collective-permute-start | bytes 3145736 | tf_op jit(solution)/shard_map/ppermute | solution.py:594
  131.2 10.0 %collective-permute-start.34 = (bf16[16,64,512]{2,1,0:T(8,128)(2,1)S(1)}, bf16[16,64,512]{2,1,0:T(8,128)(2,1)S(1)}, u32[]{:S(2)}, u32[]{:S(2)}) collective-permute-start(bf16[16,64,512]{2,1,0:T(8,128)(2,1)S(1)} %pad_maximum_fusion.1.half_ref), channel_id=1, source_target_pairs={{0,4},{4,0},{8,12},{12,8},{16,20},{20,16},{24,28},{28,24},{1,5},{5... | collective-permute-start | bytes 3145736 | tf_op jit(solution)/shard_map/ppermute | solution.py:594
  134.5 8.7 %collective-permute-start.32 = (bf16[8,64,512]{2,1,0:T(8,128)(2,1)S(1)}, bf16[8,64,512]{2,1,0:T(8,128)(2,1)S(1)}, u32[]{:S(2)}, u32[]{:S(2)}) collective-permute-start(bf16[8,64,512]{2,1,0:T(8,128)(2,1)S(1)} %pad_maximum_fusion.6), channel_id=1, source_target_pairs={{0,8},{1,9},{2,10},{3,11},{4,20},{5,21},{6,22},{7,23},{8,0},{9,1},... | collective-permute-start | bytes 1572872 | tf_op jit(solution)/shard_map/ppermute | solution.py:612
  143.4 3.7 %collective-permute-start.36 = (bf16[16,64,512]{2,1,0:T(8,128)(2,1)S(1)}, bf16[16,64,512]{2,1,0:T(8,128)(2,1)S(1)}, u32[]{:S(2)}, u32[]{:S(2)}) collective-permute-start(bf16[16,64,512]{2,1,0:T(8,128)(2,1)S(1)} %pad_maximum_fusion.2.half_ref), channel_id=1, source_target_pairs={{0,4},{4,0},{8,12},{12,8},{16,20},{20,16},{24,28},{28,24},{1,5},{5... | collective-permute-start | bytes 3145736 | tf_op jit(solution)/shard_map/ppermute | solution.py:594

commit v6 on v5

--- a/solution.py
+++ b/solution.py
@@ -51,17 +51,15 @@
     "inner",
     "outer",
     "small",
+    "dx",
     "inner",
-    "dx",
     "outer",
     "small",
     "small",
     "post",
     "inner",
-    "own_outer",
-    "other_outer",
-    "own_inner",
-    "other_inner",
+    "all_outer",
+    "all_inner",
     "small",
     "own_small",
     "other_small",
@@ -477,22 +475,22 @@
     rider_ref[...] = rider
 
 
-def finish_mlp_kernel(code_ref, half_ref, *refs, own_half, turned):
-    out_ref, stage_ref, sems = refs[-3:]
-    half = code_ref[0] if own_half else 1 - code_ref[0]
-    label = code_ref[1] if own_half else code_ref[2]
-    groups = stage_ref.shape[0]
+def finish_mlp_kernel(code_ref, own_ref, other_ref, out_ref, stage_ref, sems, *, turned):
+    core, label, other = code_ref[0], code_ref[1], code_ref[2]
+    groups = stage_ref.shape[0] // 2
     per_group = HALF // groups
     size = per_group * OUTER_ROWS
     copies = []
-    for group in range(groups):
-        pieces = [half_ref[(group * per_group + i) ^ label].astype(F32) for i in range(per_group)]
-        piece = jnp.concatenate(pieces, axis=0)
-        stage_ref[group] = piece.T if turned else piece
-        place = pl.ds(pl.multiple_of((half * groups + group) * size, size), size)
-        target = out_ref.at[:, place] if turned else out_ref.at[place]
-        copies.append(pltpu.make_async_copy(stage_ref.at[group], target, sems.at[group]))
-        copies[-1].start()
+    for index, (half, ref, code) in enumerate(((core, own_ref, label), (1 - core, other_ref, other))):
+        for group in range(groups):
+            slots = [(group * per_group + i) ^ code for i in range(per_group)]
+            piece = jnp.concatenate([ref[slot].astype(F32) for slot in slots], axis=0)
+            stage = index * groups + group
+            stage_ref[stage] = piece.T if turned else piece
+            place = pl.ds(pl.multiple_of((half * groups + group) * size, size), size)
+            target = out_ref.at[:, place] if turned else out_ref.at[place]
+            copies.append(pltpu.make_async_copy(stage_ref.at[stage], target, sems.at[stage]))
+            copies[-1].start()
     for copy in copies:
         copy.wait()
 
@@ -923,34 +921,42 @@
 
         grads = {}
 
-        def finish(name, own_half, pin):
+        def finish_mlp(name, pin):
             chain = chains[name]
-            groups = 4
-            if name == "small":
-                kernel = finish_attention_kernel
-                shapes, stage = [(D, D)] * 4, (4, D // 2, D)
-            else:
-                turned = name == "inner"
-                kernel = functools.partial(finish_mlp_kernel, turned=turned)
-                size = HALF_FF // groups
-                shapes = [(D, FF) if turned else (FF, D)]
-                stage = (groups, D, size) if turned else (groups, size, D)
+            turned = name == "inner"
+            groups = 2
+            size = HALF_FF // groups
+            stage = (2 * groups, D, size) if turned else (2 * groups, size, D)
+            return call(
+                functools.partial(finish_mlp_kernel, turned=turned),
+                (1,),
+                (code,),
+                (chain.held, after(chain.arrived, pin)),
+                [whole(part_shape)] * 2,
+                [pltpu.HBM((D, FF) if turned else (FF, D), F32)],
+                [ANYWHERE],
+                [pltpu.VMEM(stage, F32), pltpu.SemaphoreType.DMA((2 * groups,))],
+                name="finish_" + name,
+                vmem=12,
+            )
+
+        def finish_small(own_half, pin):
+            chain = chains["small"]
+            before = grads.get("small", ())
             half = after(chain.held if own_half else chain.arrived, pin)
-            before = grads.get(name, ())
-            grads[name] = call(
-                functools.partial(kernel, own_half=own_half),
+            return call(
+                functools.partial(finish_attention_kernel, own_half=own_half),
                 (1,),
                 (code,),
                 (half, *before),
                 [whole(half.shape)] + [ANYWHERE] * len(before),
-                [pltpu.HBM(shape, F32) for shape in shapes],
-                [ANYWHERE] * len(shapes),
-                [pltpu.VMEM(stage, F32), pltpu.SemaphoreType.DMA((stage[0],))],
-                name="finish_" + name,
+                [pltpu.HBM((D, D), F32)] * 4,
+                [ANYWHERE] * 4,
+                [pltpu.VMEM((4, D // 2, D), F32), pltpu.SemaphoreType.DMA((4,))],
+                name="finish_small",
                 vmem=10,
                 aliases={2 + i: i for i in range(len(before))},
             )
-            return grads[name][0]
 
         for event in ORDER:
             if event in chains:
@@ -992,7 +998,11 @@
                 done = input_grad
             else:
                 which, name = event.split("_")
-                done = finish(name, which == "own", done)
+                if name == "small":
+                    grads[name] = finish_small(which == "own", done)
+                else:
+                    grads[name] = finish_mlp(name, done)
+                done = grads[name][0]
         (grad_outer,), (grad_inner,) = grads["outer"], grads["inner"]
         grad_out, grad_query, grad_key, grad_value = grads["small"]
         rider = chains["small"].rider

time: 149 us -> 148 us (level)
  Pallas kernels: 48.3 us -> 45.9 us
  waiting for transfers between devices: 49.8 us -> 51.6 us
    pallas_call x19 -> x17, Pallas kernels: 48.3 us -> 45.9 us  [call(): pl.pallas_call(kernel, out_shape=outs, grid_spec=pltpu.PrefetchScalarGrid...]
    ppermute x25, waiting for transfers between devices: 32.4 us -> 34.2 us  [swap_step(): return lax.ppermute(array, both, pairs)]
  transfers between devices with their start and end apart: 37 -> 37, of which waited for: 12 -> 14; matrix products, arithmetic and copies ran while one was open for 3% -> 3% of each run, Pallas kernels for 26% -> 24%
where the time goes in v6:
time: 148 us
  waiting for transfers between devices  51.6 us (35%)
  Pallas kernels  45.9 us (31%)
  starting transfers between devices  44.3 us (30%)
  other arithmetic  2.52 us (2%)
  local copies, waits for them, and re-layouts  2.07 us (1%)
    pallas_call x17, Pallas kernels, call(): pl.pallas_call(kernel, out_shape=outs, grid_spec=pltpu.PrefetchScalarGrid...  45.9 us
    ppermute x25, waiting for transfers between devices, swap_step(): return lax.ppermute(array, both, pairs)  34.2 us
    ppermute x25, starting transfers between devices, swap_step(): return lax.ppermute(array, both, pairs)  28.1 us
    ppermute x5, waiting for transfers between devices, swap_seq(): return lax.ppermute(array, 'seq', [(i, i ^ bit) for i in range(seq)])  17.4 us
    ppermute x7, starting transfers between devices, swap_rows(): return lax.ppermute(array, 'rows', [(i, i ^ bit) for i in range(rows)])  8.95 us
    ppermute x5, starting transfers between devices, swap_seq(): return lax.ppermute(array, 'seq', [(i, i ^ bit) for i in range(seq)])  7.16 us
  transfers between devices with their start and end apart: 37, of which 14 were waited for; matrix products, arithmetic and copies ran while one was open for 3% of the time, Pallas kernels for 24%

profile of v6, /device:TPU:1, one launch (start us, length us, event | category | flops | bytes accessed | tf_op | source)
XLA Modules:
  0.0 147.8 jit_solution(8613509848051037796)
XLA Ops:
  0.7 1.1 pack.1
  1.8 3.2 %collective-permute-start.1 = (bf16[400,512]{1,0:T(8,128)(2,1)S(1)}, bf16[400,512]{1,0:T(8,128)(2,1)S(1)}, u32[]{:S(2)}, u32[]{:S(2)}) collective-permute-start(bf16[400,512]{1,0:T(8,128)(2,1)S(1)} %pack.1), channel_id=1, source_target_pairs={{0,2},{1,3},{2,0},{3,1},{4,6},{5,7},{6,4},{7,5},{8,10},{9,11},{10,... | collective-permute-start | bytes 1228808 | tf_op jit(solution)/shard_map/ppermute | solution.py:595
  5.0 1.3 collective-permute-start
  6.3 16.7 %collective-permute-done.1.wire_ref = bf16[400,512]{1,0:T(8,128)(2,1)S(1)} collective-permute-done((bf16[400,512]{1,0:T(8,128)(2,1)S(1)}, bf16[400,512]{1,0:T(8,128)(2,1)S(1)}, u32[]{:S(2)}, u32[]{:S(2)}) %collective-permute-start.1) | collective-permute-done | bytes 409632 | tf_op jit(solution)/shard_map/ppermute | solution.py:595
  23.0 1.2 collective-permute-start.3
  24.2 0.3 collective-permute-start.2
  24.6 1.1 collective-permute-start.4
  25.8 0.8 copy.57.table_ref
  26.5 2.7 %prepare.1 = (f32[4,256,512]{2,1,0:T(8,128)S(1)}, bf16[512,512]{1,0:T(8,128)(2,1)S(1)}, bf16[512,512]{1,0:T(8,128)(2,1)S(1)}, bf16[512,512]{1,0:T(8,128)(2,1)S(1)}, bf16[512,512]{1,0:T(8,128)(2,1)S(1)}) custom-call(s32[1]{0:T(128)} %bitcast.place_ref, f32[32,8]{1,0:T(8,128)S(1)} %copy.57.table_ref, bf16[512,512]{1,0:T(8,128)(2,1)} %refs_0_.2, ...), custom_call_target="tpu_custom_call" | custom-call | tf_op jit(solution)/shard_map/prepare/pallas_call | solution.py:561
  29.3 2.8 %attention.3 = (f32[4,256,512]{2,1,0:T(8,128)S(1)}, bf16[512,512]{1,0:T(8,128)(2,1)S(1)}, bf16[512,512]{1,0:T(8,128)(2,1)S(1)}, bf16[512,512]{1,0:T(8,128)(2,1)S...) custom-call(s32[1]{0:T(128)} %bitcast.place_ref, ...), custom_call_target="tpu_custom_call", output_to_operand_aliasing={{0}: (13, {}), {1}: (14, {}), {2}: (15, {}), {3}: (16, {}),... | custom-call | flops 268435456 | bytes 1048576 | tf_op jit(solution)/shard_map/attention/pallas_call | solution.py:561
  32.1 0.6 collective-permute-done.4.x3_ref
  32.8 2.8 %attention.4 = (f32[4,256,512]{2,1,0:T(8,128)S(1)}, bf16[512,512]{1,0:T(8,128)(2,1)S(1)}, bf16[512,512]{1,0:T(8,128)(2,1)S(1)}, bf16[512,512]{1,0:T(8,128)(2,1)S...) custom-call(s32[1]{0:T(128)} %bitcast.place_ref, ...), custom_call_target="tpu_custom_call", output_to_operand_aliasing={{0}: (13, {}), {1}: (14, {}), {2}: (15, {}), {3}: (16, {}),... | custom-call | flops 268435456 | bytes 1048576 | tf_op jit(solution)/shard_map/attention/pallas_call | solution.py:561
  35.5 3.1 %attention.5 = (f32[4,256,512]{2,1,0:T(8,128)S(1)}, bf16[512,512]{1,0:T(8,128)(2,1)S(1)}, bf16[512,512]{1,0:T(8,128)(2,1)S(1)}, bf16[512,512]{1,0:T(8,128)(2,1)S...) custom-call(s32[1]{0:T(128)} %bitcast.place_ref, ...), custom_call_target="tpu_custom_call", output_to_operand_aliasing={{0}: (13, {}), {1}: (14, {}), {2}: (15, {}), {3}: (16, {}),... | custom-call | flops 268435456 | bytes 1048576 | tf_op jit(solution)/shard_map/attention/pallas_call | solution.py:561
  38.6 3.7 %mlp.2 = (f32[384,512]{1,0:T(8,128)S(1)}, f32[384,512]{1,0:T(8,128)S(1)}, bf16[16,64,512]{2,1,0:T(8,128)(2,1)S(1)}, bf16[16,64,512]{2,1,0:T(8,128)(2,1)S(1)}) custom-call(s32[3]{0:T(128)S(1)} %pad_add_fusion.code_ref, bf16[128,512]{1,0:T(8,128)(2,1)S(1)} %get-tuple-element.187.refs_0_, bf16[128,512]{1,0:T(8,128)(2,1)S(1)} %get-tuple-element.183.refs_1_.refs_0_, ...), custom_call_target="tpu_custom_call" | custom-call | flops 2415919104 | bytes 9437184 | tf_op jit(solution)/shard_map/mlp/pallas_call | solution.py:561
  42.3 2.3 %collective-permute-start.6 = (bf16[16,64,512]{2,1,0:T(8,128)(2,1)S(1)}, bf16[16,64,512]{2,1,0:T(8,128)(2,1)S(1)}, u32[]{:S(2)}, u32[]{:S(2)}) collective-permute-start(bf16[16,64,512]{2,1,0:T(8,128)(2,1)S(1)} %get-tuple-element.198), channel_id=1, source_target_pairs={{0,4},{4,0},{8,12},{12,8},{16,20},{20,16},{24,28},{28,24},{1,5},{5... | collective-permute-start | bytes 3145736 | tf_op jit(solution)/shard_map/ppermute | solution.py:592
  44.7 3.9 %mlp.3 = (f32[384,512]{1,0:T(8,128)S(1)}, f32[384,512]{1,0:T(8,128)S(1)}, bf16[16,64,512]{2,1,0:T(8,128)(2,1)S(1)}, bf16[16,64,512]{2,1,0:T(8,128)(2,1)S(1)}) custom-call(s32[3]{0:T(128)S(1)} %pad_add_fusion.code_ref, bf16[128,512]{1,0:T(8,128)(2,1)S(1)} %get-tuple-element.187.refs_0_, bf16[128,512]{1,0:T(8,128)(2,1)S(1)} %get-tuple-element.183.refs_1_.refs_0_, ...), custom_call_target="tpu_custom_call" | custom-call | flops 2415919104 | bytes 9437184 | tf_op jit(solution)/shard_map/mlp/pallas_call | solution.py:561
  48.6 0.1 add_convert_fusion.2
  48.8 1.1 collective-permute-start.8
  50.0 0.5 collective-permute-start.7
  50.5 3.9 %attention_back.3 = (bf16[3,128,512]{2,1,0:T(8,128)(2,1)}, f32[128,512]{1,0:T(8,128)S(1)}, bf16[2,512,128]{2,1,0:T(8,128)(2,1)S(1)}, bf16[2,512,128]{2,1,0:T(8,1...) custom-call(s32[1]{0:T(128)} %bitcast.place_ref, ...), custom_call_target="tpu_custom_call" | custom-call | flops 671088640 | bytes 2621440 | tf_op jit(solution)/shard_map/attention_back/pallas_call | solution.py:561
  54.5 4.3 %attention_back.4 = (bf16[3,128,512]{2,1,0:T(8,128)(2,1)}, f32[128,512]{1,0:T(8,128)S(1)}, bf16[2,512,128]{2,1,0:T(8,128)(2,1)S(1)}, bf16[2,512,128]{2,1,0:T(8,1...) custom-call(s32[1]{0:T(128)} %bitcast.place_ref, ...), custom_call_target="tpu_custom_call", output_to_operand_aliasing={{0}: (28, {}), {4}: (22, {}), {5}: (23, {}), {6}: (24, {}),... | custom-call | flops 671088640 | bytes 2621440 | tf_op jit(solution)/shard_map/attention_back/pallas_call | solution.py:561
  58.8 2.8 %collective-permute-start.10 = (bf16[2,512,128]{2,1,0:T(8,128)(2,1)S(1)}, bf16[2,512,128]{2,1,0:T(8,128)(2,1)S(1)}, u32[]{:S(2)}, u32[]{:S(2)}) collective-permute-start(bf16[2,512,128]{2,1,0:T(8,128)(2,1)S(1)} %get-tuple-element.237), channel_id=1, source_target_pairs={{0,1},{1,0},{2,3},{3,2},{4,6},{5,7},{6,4},{7,5},{8,9},{9,8},{10,11... | collective-permute-start | bytes 786440 | tf_op jit(solution)/shard_map/ppermute | solution.py:610
  61.8 1.3 collective-permute-start.11
  63.2 0.8 collective-permute-start.14
  63.9 5.4 %attention_back.5 = (bf16[3,128,512]{2,1,0:T(8,128)(2,1)}, f32[128,512]{1,0:T(8,128)S(1)}, bf16[2,512,128]{2,1,0:T(8,128)(2,1)S(1)}, bf16[2,512,128]{2,1,0:T(8,1...) custom-call(s32[1]{0:T(128)} %bitcast.place_ref, ...), custom_call_target="tpu_custom_call", output_to_operand_aliasing={{0}: (28, {}), {4}: (22, {}), {5}: (23, {}), {6}: (24, {}),... | custom-call | flops 671088640 | bytes 2621440 | tf_op jit(solution)/shard_map/attention_back/pallas_call | solution.py:561
  69.4 3.1 %collective-permute-start.13 = (bf16[2,64,512]{2,1,0:T(8,128)(2,1)S(1)}, bf16[2,64,512]{2,1,0:T(8,128)(2,1)S(1)}, u32[]{:S(2)}, u32[]{:S(2)}) collective-permute-start(bf16[2,64,512]{2,1,0:T(8,128)(2,1)S(1)} %add_convert_fusion.16), channel_id=1, source_target_pairs={{0,1},{1,0},{2,3},{3,2},{4,6},{5,7},{6,4},{7,5},{8,9},{9,8},{10,11... | collective-permute-start | bytes 393224 | tf_op jit(solution)/shard_map/ppermute | solution.py:610
  72.5 1.6 %rider.1 = f32[16,512]{1,0:T(8,128)S(1)} custom-call(s32[1]{0:T(128)} %bitcast.place_ref, f32[512,512]{1,0:T(8,128)S(1)} %get-tuple-element.243.gq_ref, f32[512,512]{1,0:T(8,128)S(1)} %get-tuple-element.244.gk_ref, f32[512,512]{1,0:T(8,128)S(1)} %get-tuple-element.245.gv_ref, f32[4,256,512]{2,1,0:T(8,128)S(1)} %get-tuple-element.246.table_sum_ref, ...), custom_call_target="tpu_custom_call" | custom-call | tf_op jit(solution)/shard_map/rider/pallas_call | solution.py:561
  74.2 0.3 collective-permute-start.15
  74.5 3.2 %collective-permute-start.17 = (bf16[2,64,512]{2,1,0:T(8,128)(2,1)S(1)}, bf16[2,64,512]{2,1,0:T(8,128)(2,1)S(1)}, u32[]{:S(2)}, u32[]{:S(2)}) collective-permute-start(bf16[2,64,512]{2,1,0:T(8,128)(2,1)S(1)} %add_convert_fusion.15), channel_id=1, source_target_pairs={{0,1},{1,0},{2,3},{3,2},{4,6},{5,7},{6,4},{7,5},{8,9},{9,8},{10,11... | collective-permute-start | bytes 393224 | tf_op jit(solution)/shard_map/ppermute | solution.py:610
  78.0 3.6 %collective-permute-done.17 = bf16[2,64,512]{2,1,0:T(8,128)(2,1)S(1)} collective-permute-done((bf16[2,64,512]{2,1,0:T(8,128)(2,1)S(1)}, bf16[2,64,512]{2,1,0:T(8,128)(2,1)S(1)}, u32[]{:S(2)}, u32[]{:S(2)}) %collective-permute-start.17) | collective-permute-done | bytes 131104 | tf_op jit(solution)/shard_map/ppermute | solution.py:610
  82.0 1.3 collective-permute-start.18
  83.3 0.9 collective-permute-done.19
  84.2 2.4 %collective-permute-done.18 = bf16[2,64,512]{2,1,0:T(8,128)(2,1)S(1)} collective-permute-done((bf16[2,64,512]{2,1,0:T(8,128)(2,1)S(1)}, bf16[2,64,512]{2,1,0:T(8,128)(2,1)S(1)}, u32[]{:S(2)}, u32[]{:S(2)}) %collective-permute-start.18) | collective-permute-done | bytes 131104 | tf_op jit(solution)/shard_map/ppermute | solution.py:610
  86.6 3.7 %collective-permute-done.16 = bf16[544,512]{1,0:T(8,128)(2,1)S(1)} collective-permute-done((bf16[544,512]{1,0:T(8,128)(2,1)S(1)}, bf16[544,512]{1,0:T(8,128)(2,1)S(1)}, u32[]{:S(2)}, u32[]{:S(2)}) %collective-permute-start.16) | collective-permute-done | bytes 557088 | tf_op jit(solution)/shard_map/ppermute | solution.py:610
  90.5 1.0 collective-permute-start.20
  91.5 1.5 %collective-permute-start.26 = (bf16[2,64,512]{2,1,0:T(8,128)(2,1)S(1)}, bf16[2,64,512]{2,1,0:T(8,128)(2,1)S(1)}, u32[]{:S(2)}, u32[]{:S(2)}) collective-permute-start(bf16[2,64,512]{2,1,0:T(8,128)(2,1)S(1)} %add_convert_fusion.9), channel_id=1, source_target_pairs={{0,1},{1,0},{2,3},{3,2},{4,6},{5,7},{6,4},{7,5},{8,9},{9,8},{10,11... | collective-permute-start | bytes 393224 | tf_op jit(solution)/shard_map/ppermute | solution.py:610
  93.0 0.8 collective-permute-start.24
  93.9 2.5 %collective-permute-done.20 = bf16[288,512]{1,0:T(8,128)(2,1)S(1)} collective-permute-done((bf16[288,512]{1,0:T(8,128)(2,1)S(1)}, bf16[288,512]{1,0:T(8,128)(2,1)S(1)}, u32[]{:S(2)}, u32[]{:S(2)}) %collective-permute-start.20) | collective-permute-done | bytes 294944 | tf_op jit(solution)/shard_map/ppermute | solution.py:610
  96.6 1.7 %collective-permute-start.22 = (bf16[160,512]{1,0:T(8,128)(2,1)S(1)}, bf16[160,512]{1,0:T(8,128)(2,1)S(1)}, u32[]{:S(2)}, u32[]{:S(2)}) collective-permute-start(bf16[160,512]{1,0:T(8,128)(2,1)S(1)} %pad_maximum_fusion.13), channel_id=1, source_target_pairs={{0,1},{1,0},{2,3},{3,2},{4,6},{5,7},{6,4},{7,5},{8,9},{9,8},{10,11... | collective-permute-start | bytes 491528 | tf_op jit(solution)/shard_map/ppermute | solution.py:610
  98.5 0.8 collective-permute-start.21
  99.2 5.6 %collective-permute-done.22 = bf16[160,512]{1,0:T(8,128)(2,1)S(1)} collective-permute-done((bf16[160,512]{1,0:T(8,128)(2,1)S(1)}, bf16[160,512]{1,0:T(8,128)(2,1)S(1)}, u32[]{:S(2)}, u32[]{:S(2)}) %collective-permute-start.22) | collective-permute-done | bytes 163872 | tf_op jit(solution)/shard_map/ppermute | solution.py:610
  105.1 0.7 collective-permute-start.25
  105.9 0.8 collective-permute-start.23
  106.7 0.5 collective-permute-start.30
  107.2 3.5 %collective-permute-done.25 = bf16[4,64,512]{2,1,0:T(8,128)(2,1)S(1)} collective-permute-done((bf16[4,64,512]{2,1,0:T(8,128)(2,1)S(1)}, bf16[4,64,512]{2,1,0:T(8,128)(2,1)S(1)}, u32[]{:S(2)}, u32[]{:S(2)}) %collective-permute-start.25) | collective-permute-done | bytes 262176 | tf_op jit(solution)/shard_map/ppermute | solution.py:610
  110.7 0.9 collective-permute-start.29
  111.7 3.0 %collective-permute-done.23 = bf16[160,512]{1,0:T(8,128)(2,1)S(1)} collective-permute-done((bf16[160,512]{1,0:T(8,128)(2,1)S(1)}, bf16[160,512]{1,0:T(8,128)(2,1)S(1)}, u32[]{:S(2)}, u32[]{:S(2)}) %collective-permute-start.23) | collective-permute-done | bytes 163872 | tf_op jit(solution)/shard_map/ppermute | solution.py:610
  114.9 3.4 %collective-permute-start.27 = (bf16[3,512,128]{2,1,0:T(8,128)(2,1)S(1)}, bf16[3,512,128]{2,1,0:T(8,128)(2,1)S(1)}, u32[]{:S(2)}, u32[]{:S(2)}) collective-permute-start(bf16[3,512,128]{2,1,0:T(8,128)(2,1)S(1)} %pad_maximum_fusion.8), channel_id=1, source_target_pairs={{0,2},{1,3},{2,0},{3,1},{4,5},{5,4},{6,7},{7,6},{8,10},{9,11},{10,... | collective-permute-start | bytes 1179656 | tf_op jit(solution)/shard_map/ppermute | solution.py:610
  118.5 2.7 %collective-permute-done.29 = bf16[8,64,512]{2,1,0:T(8,128)(2,1)S(1)} collective-permute-done((bf16[8,64,512]{2,1,0:T(8,128)(2,1)S(1)}, bf16[8,64,512]{2,1,0:T(8,128)(2,1)S(1)}, u32[]{:S(2)}, u32[]{:S(2)}) %collective-permute-start.29) | collective-permute-done | bytes 524320 | tf_op jit(solution)/shard_map/ppermute | solution.py:610
  121.3 0.2 collective-permute-done.28
  121.5 1.0 collective-permute-start.31
  122.6 3.6 %collective-permute-start.35 = (bf16[16,64,512]{2,1,0:T(8,128)(2,1)S(1)}, bf16[16,64,512]{2,1,0:T(8,128)(2,1)S(1)}, u32[]{:S(2)}, u32[]{:S(2)}) collective-permute-start(bf16[16,64,512]{2,1,0:T(8,128)(2,1)S(1)} %pad_maximum_fusion.own_ref), channel_id=1, source_target_pairs={{0,4},{4,0},{8,12},{12,8},{16,20},{20,16},{24,28},{28,24},{1,5},{5... | collective-permute-start | bytes 3145736 | tf_op jit(solution)/shard_map/ppermute | solution.py:592
  126.2 3.8 %collective-permute-done.31 = bf16[4,64,512]{2,1,0:T(8,128)(2,1)S(1)} collective-permute-done((bf16[4,64,512]{2,1,0:T(8,128)(2,1)S(1)}, bf16[4,64,512]{2,1,0:T(8,128)(2,1)S(1)}, u32[]{:S(2)}, u32[]{:S(2)}) %collective-permute-start.31) | collective-permute-done | bytes 262176 | tf_op jit(solution)/shard_map/ppermute | solution.py:610
  130.1 1.3 post.1
  131.4 1.7 %collective-permute-start.34 = (bf16[16,64,512]{2,1,0:T(8,128)(2,1)S(1)}, bf16[16,64,512]{2,1,0:T(8,128)(2,1)S(1)}, u32[]{:S(2)}, u32[]{:S(2)}) collective-permute-start(bf16[16,64,512]{2,1,0:T(8,128)(2,1)S(1)} %pad_maximum_fusion.1.own_ref), channel_id=1, source_target_pairs={{0,4},{4,0},{8,12},{12,8},{16,20},{20,16},{24,28},{28,24},{1,5},{5... | collective-permute-start | bytes 3145736 | tf_op jit(solution)/shard_map/ppermute | solution.py:592
  133.1 0.6 collective-permute-start.32
  133.7 2.7 %finish_outer.1 = f32[2048,512]{1,0:T(8,128)} custom-call(s32[3]{0:T(128)S(1)} %pad_add_fusion.code_ref, bf16[16,64,512]{2,1,0:T(8,128)(2,1)S(1)} %pad_maximum_fusion.own_ref, bf16[16,64,512]{2,1,0:T(8,128)(2,1)S(1)} %collective-permute-done.35.other_ref), custom_call_target="tpu_custom_call" | custom-call | tf_op jit(solution)/shard_map/finish_outer/pallas_call | solution.py:561
  136.4 2.8 %finish_inner.1 = f32[512,2048]{1,0:T(8,128)} custom-call(s32[3]{0:T(128)S(1)} %pad_add_fusion.code_ref, bf16[16,64,512]{2,1,0:T(8,128)(2,1)S(1)} %pad_maximum_fusion.1.own_ref, bf16[16,64,512]{2,1,0:T(8,128)(2,1)S(1)} %collective-permute-done.34.other_ref), custom_call_target="tpu_custom_call" | custom-call | tf_op jit(solution)/shard_map/finish_inner/pallas_call | solution.py:561
  139.2 2.3 %collective-permute-done.32 = bf16[8,64,512]{2,1,0:T(8,128)(2,1)S(1)} collective-permute-done((bf16[8,64,512]{2,1,0:T(8,128)(2,1)S(1)}, bf16[8,64,512]{2,1,0:T(8,128)(2,1)S(1)}, u32[]{:S(2)}, u32[]{:S(2)}) %collective-permute-start.32) | collective-permute-done | bytes 524320 | tf_op jit(solution)/shard_map/ppermute | solution.py:610
  141.6 1.0 collective-permute-start.36
  142.6 0.6 slice_bitcast_fusion
  143.2 0.6 fusion.29
  143.8 1.9 %finish_small.2 = (f32[512,512]{1,0:T(8,128)}, f32[512,512]{1,0:T(8,128)}, f32[512,512]{1,0:T(8,128)}, f32[512,512]{1,0:T(8,128)}) custom-call(s32[3]{0:T(128)S(1)} %pad_add_fusion.code_ref, bf16[16,64,512]{2,1,0:T(8,128)(2,1)S(1)} %pad_maximum_fusion.2.half_ref), custom_call_target="tpu_custom_call" | custom-call | tf_op jit(solution)/shard_map/finish_small/pallas_call | solution.py:561
  145.7 1.9 %finish_small.3 = (f32[512,512]{1,0:T(8,128)}, f32[512,512]{1,0:T(8,128)}, f32[512,512]{1,0:T(8,128)}, f32[512,512]{1,0:T(8,128)}) custom-call(s32[3]{0:T(128)S(1)} %pad_add_fusion.code_ref, bf16[16,64,512]{2,1,0:T(8,128)(2,1)S(1)} %collective-permute-done.36.half_ref, ...), custom_call_target="tpu_custom_call", output_to_operand_aliasing={{0}: (2, {}), {1}: (3, {}), {2}: (4, {}), {3}: (5, {})} | custom-call | tf_op jit(solution)/shard_map/finish_small/pallas_call | solution.py:561
  (100 shorter events, 3.0 us)
Async XLA Ops:
  0.6 28.6 %copy-start.3 = (s32[3,128]{1,0:T(4,128)S(1)}, s32[3,128]{1,0:T(4,128)}, u32[]{:S(2)}) copy-start(s32[3,128]{1,0:T(4,128)} %seen_ref.6) | copy-start | bytes 4612
  0.7 28.6 %copy-start = (bf16[3,128,512]{2,1,0:T(8,128)(2,1)S(1)}, bf16[3,128,512]{2,1,0:T(8,128)(2,1)}, u32[]{:S(2)}) copy-start(bf16[3,128,512]{2,1,0:T(8,128)(2,1)} %x_ref.3) | copy-start | bytes 1179652
  0.7 28.6 %copy-start.4 = (s32[3,4]{1,0:T(4,128)S(1)}, s32[3,4]{1,0:T(4,128)}, u32[]{:S(2)}) copy-start(s32[3,4]{1,0:T(4,128)} %lengths_ref.5) | copy-start | bytes 148
  0.7 28.6 %copy-start.1 = (f32[512]{0:T(512)S(1)}, f32[512]{0:T(512)}, u32[]{:S(2)}) copy-start(f32[512]{0:T(512)} %param.20) | copy-start | bytes 6148
  0.7 28.6 %copy-start.2 = (f32[512]{0:T(512)S(1)}, f32[512]{0:T(512)}, u32[]{:S(2)}) copy-start(f32[512]{0:T(512)} %param.15) | copy-start | bytes 6148
  1.8 21.2 %collective-permute-start.1 = (bf16[400,512]{1,0:T(8,128)(2,1)S(1)}, bf16[400,512]{1,0:T(8,128)(2,1)S(1)}, u32[]{:S(2)}, u32[]{:S(2)}) collective-permute-start(bf16[400,512]{1,0:T(8,128)(2,1)S(1)} %pack.1), channel_id=1, source_target_pairs={{0,2},{1,3},{2,0},{3,1},{4,6},{5,7},{6,4},{7,5},{8,10},{9,11},{10,... | collective-permute-start | bytes 1228808 | tf_op jit(solution)/shard_map/ppermute | solution.py:595
  5.0 24.3 %collective-permute-start = (bf16[400,512]{1,0:T(8,128)(2,1)S(1)}, bf16[400,512]{1,0:T(8,128)(2,1)S(1)}, u32[]{:S(2)}, u32[]{:S(2)}) collective-permute-start(bf16[400,512]{1,0:T(8,128)(2,1)S(1)} %pack.1), channel_id=1, source_target_pairs={{0,1},{1,0},{2,3},{3,2},{4,5},{5,4},{6,7},{7,6},{8,9},{9,8},{10,11... | collective-permute-start | bytes 1228808 | tf_op jit(solution)/shard_map/ppermute | solution.py:595
  23.0 6.2 %collective-permute-start.3 = (bf16[144,512]{1,0:T(8,128)(2,1)S(1)}, bf16[144,512]{1,0:T(8,128)(2,1)S(1)}, u32[]{:S(2)}, u32[]{:S(2)}) collective-permute-start(bf16[144,512]{1,0:T(8,128)(2,1)S(1)} %get-tuple-element.154.x2_ref.x2_tail_ref), channel_id=1, source_target_pairs={{0,1},{1,0},{2,3},{3,2},{4,5},{5,4},{6,7},{7,6},{8,9},{9,8},{10,11... | collective-permute-start | bytes 442376 | tf_op jit(solution)/shard_map/ppermute | solution.py:595
  24.2 11.3 %collective-permute-start.2 = (bf16[128,512]{1,0:T(8,128)(2,1)S(1)}, bf16[128,512]{1,0:T(8,128)(2,1)S(1)}, u32[]{:S(2)}, u32[]{:S(2)}) collective-permute-start(bf16[128,512]{1,0:T(8,128)(2,1)S(1)} %get-tuple-element.153.x2_ref), channel_id=1, source_target_pairs={{0,1},{1,0},{2,3},{3,2},{4,5},{5,4},{6,7},{7,6},{8,9},{9,8},{10,11... | collective-permute-start | bytes 393224 | tf_op jit(solution)/shard_map/ppermute | solution.py:595
  24.6 8.2 %collective-permute-start.4 = (bf16[128,512]{1,0:T(8,128)(2,1)S(1)}, bf16[128,512]{1,0:T(8,128)(2,1)S(1)}, u32[]{:S(2)}, u32[]{:S(2)}) collective-permute-start(bf16[128,512]{1,0:T(8,128)(2,1)S(1)} %get-tuple-element.155.x2_ref), channel_id=1, source_target_pairs={{0,1},{1,0},{2,3},{3,2},{4,5},{5,4},{6,7},{7,6},{8,9},{9,8},{10,11... | collective-permute-start | bytes 393224 | tf_op jit(solution)/shard_map/ppermute | solution.py:595
  42.3 6.3 %collective-permute-start.6 = (bf16[16,64,512]{2,1,0:T(8,128)(2,1)S(1)}, bf16[16,64,512]{2,1,0:T(8,128)(2,1)S(1)}, u32[]{:S(2)}, u32[]{:S(2)}) collective-permute-start(bf16[16,64,512]{2,1,0:T(8,128)(2,1)S(1)} %get-tuple-element.198), channel_id=1, source_target_pairs={{0,4},{4,0},{8,12},{12,8},{16,20},{20,16},{24,28},{28,24},{1,5},{5... | collective-permute-start | bytes 3145736 | tf_op jit(solution)/shard_map/ppermute | solution.py:592
  44.6 5.2 %collective-permute-start.5 = (bf16[16,64,512]{2,1,0:T(8,128)(2,1)S(1)}, bf16[16,64,512]{2,1,0:T(8,128)(2,1)S(1)}, u32[]{:S(2)}, u32[]{:S(2)}) collective-permute-start(bf16[16,64,512]{2,1,0:T(8,128)(2,1)S(1)} %get-tuple-element.196), channel_id=1, source_target_pairs={{0,4},{4,0},{8,12},{12,8},{16,20},{20,16},{24,28},{28,24},{1,5},{5... | collective-permute-start | bytes 3145736 | tf_op jit(solution)/shard_map/ppermute | solution.py:592
  48.8 12.9 %collective-permute-start.8 = (bf16[8,64,512]{2,1,0:T(8,128)(2,1)S(1)}, bf16[8,64,512]{2,1,0:T(8,128)(2,1)S(1)}, u32[]{:S(2)}, u32[]{:S(2)}) collective-permute-start(bf16[8,64,512]{2,1,0:T(8,128)(2,1)S(1)} %add_convert_fusion.2), channel_id=1, source_target_pairs={{0,8},{1,9},{2,10},{3,11},{4,20},{5,21},{6,22},{7,23},{8,0},{9,1},... | collective-permute-start | bytes 1572872 | tf_op jit(solution)/shard_map/ppermute | solution.py:610
  50.0 13.1 %collective-permute-start.7 = (bf16[8,64,512]{2,1,0:T(8,128)(2,1)S(1)}, bf16[8,64,512]{2,1,0:T(8,128)(2,1)S(1)}, u32[]{:S(2)}, u32[]{:S(2)}) collective-permute-start(bf16[8,64,512]{2,1,0:T(8,128)(2,1)S(1)} %add_convert_fusion.1.refs_19_), channel_id=1, source_target_pairs={{0,8},{1,9},{2,10},{3,11},{4,20},{5,21},{6,22},{7,23},{8,0},{9,1},... | collective-permute-start | bytes 1572872 | tf_op jit(solution)/shard_map/ppermute | solution.py:610
  58.8 35.1 %collective-permute-start.10 = (bf16[2,512,128]{2,1,0:T(8,128)(2,1)S(1)}, bf16[2,512,128]{2,1,0:T(8,128)(2,1)S(1)}, u32[]{:S(2)}, u32[]{:S(2)}) collective-permute-start(bf16[2,512,128]{2,1,0:T(8,128)(2,1)S(1)} %get-tuple-element.237), channel_id=1, source_target_pairs={{0,1},{1,0},{2,3},{3,2},{4,6},{5,7},{6,4},{7,5},{8,9},{9,8},{10,11... | collective-permute-start | bytes 786440 | tf_op jit(solution)/shard_map/ppermute | solution.py:610
  61.6 32.3 %collective-permute-start.9 = (bf16[2,512,128]{2,1,0:T(8,128)(2,1)S(1)}, bf16[2,512,128]{2,1,0:T(8,128)(2,1)S(1)}, u32[]{:S(2)}, u32[]{:S(2)}) collective-permute-start(bf16[2,512,128]{2,1,0:T(8,128)(2,1)S(1)} %get-tuple-element.236), channel_id=1, source_target_pairs={{0,1},{1,0},{2,3},{3,2},{4,6},{5,7},{6,4},{7,5},{8,9},{9,8},{10,11... | collective-permute-start | bytes 786440 | tf_op jit(solution)/shard_map/ppermute | solution.py:610
  61.8 7.6 %collective-permute-start.11 = (bf16[4,64,512]{2,1,0:T(8,128)(2,1)S(1)}, bf16[4,64,512]{2,1,0:T(8,128)(2,1)S(1)}, u32[]{:S(2)}, u32[]{:S(2)}) collective-permute-start(bf16[4,64,512]{2,1,0:T(8,128)(2,1)S(1)} %add_convert_fusion.4), channel_id=1, source_target_pairs={{0,16},{1,17},{2,18},{3,19},{4,12},{5,13},{6,14},{7,15},{8,24},{9,... | collective-permute-start | bytes 786440 | tf_op jit(solution)/shard_map/ppermute | solution.py:610
  63.2 11.0 %collective-permute-start.14 = (bf16[4,64,512]{2,1,0:T(8,128)(2,1)S(1)}, bf16[4,64,512]{2,1,0:T(8,128)(2,1)S(1)}, u32[]{:S(2)}, u32[]{:S(2)}) collective-permute-start(bf16[4,64,512]{2,1,0:T(8,128)(2,1)S(1)} %add_convert_fusion.3.refs_19_), channel_id=1, source_target_pairs={{0,16},{1,17},{2,18},{3,19},{4,12},{5,13},{6,14},{7,15},{8,24},{9,... | collective-permute-start | bytes 786440 | tf_op jit(solution)/shard_map/ppermute | solution.py:610
  69.4 8.3 %collective-permute-start.13 = (bf16[2,64,512]{2,1,0:T(8,128)(2,1)S(1)}, bf16[2,64,512]{2,1,0:T(8,128)(2,1)S(1)}, u32[]{:S(2)}, u32[]{:S(2)}) collective-permute-start(bf16[2,64,512]{2,1,0:T(8,128)(2,1)S(1)} %add_convert_fusion.16), channel_id=1, source_target_pairs={{0,1},{1,0},{2,3},{3,2},{4,6},{5,7},{6,4},{7,5},{8,9},{9,8},{10,11... | collective-permute-start | bytes 393224 | tf_op jit(solution)/shard_map/ppermute | solution.py:610
  74.2 3.5 %collective-permute-start.15 = (bf16[32,512]{1,0:T(8,128)(2,1)S(1)}, bf16[32,512]{1,0:T(8,128)(2,1)S(1)}, u32[]{:S(2)}, u32[]{:S(2)}) collective-permute-start(bf16[32,512]{1,0:T(8,128)(2,1)S(1)} %pad_maximum_fusion.18), channel_id=1, source_target_pairs={{0,4},{4,0},{8,12},{12,8},{16,20},{20,16},{24,28},{28,24},{1,5},{5... | collective-permute-start | bytes 98312 | tf_op jit(solution)/shard_map/ppermute | solution.py:592
  74.5 7.0 %collective-permute-start.17 = (bf16[2,64,512]{2,1,0:T(8,128)(2,1)S(1)}, bf16[2,64,512]{2,1,0:T(8,128)(2,1)S(1)}, u32[]{:S(2)}, u32[]{:S(2)}) collective-permute-start(bf16[2,64,512]{2,1,0:T(8,128)(2,1)S(1)} %add_convert_fusion.15), channel_id=1, source_target_pairs={{0,1},{1,0},{2,3},{3,2},{4,6},{5,7},{6,4},{7,5},{8,9},{9,8},{10,11... | collective-permute-start | bytes 393224 | tf_op jit(solution)/shard_map/ppermute | solution.py:610
  77.7 4.0 %collective-permute-start.12 = (bf16[16,64,512]{2,1,0:T(8,128)(2,1)S(1)}, bf16[16,64,512]{2,1,0:T(8,128)(2,1)S(1)}, u32[]{:S(2)}, u32[]{:S(2)}) collective-permute-start(bf16[16,64,512]{2,1,0:T(8,128)(2,1)S(1)} %get-tuple-element.242), channel_id=1, source_target_pairs={{0,4},{4,0},{8,12},{12,8},{16,20},{20,16},{24,28},{28,24},{1,5},{5... | collective-permute-start | bytes 3145736 | tf_op jit(solution)/shard_map/ppermute | solution.py:592
  77.9 6.3 %collective-permute-start.19 = (bf16[2,64,512]{2,1,0:T(8,128)(2,1)S(1)}, bf16[2,64,512]{2,1,0:T(8,128)(2,1)S(1)}, u32[]{:S(2)}, u32[]{:S(2)}) collective-permute-start(bf16[2,64,512]{2,1,0:T(8,128)(2,1)S(1)} %pad_maximum_fusion.16), channel_id=1, source_target_pairs={{0,2},{1,3},{2,0},{3,1},{4,5},{5,4},{6,7},{7,6},{8,10},{9,11},{10,... | collective-permute-start | bytes 393224 | tf_op jit(solution)/shard_map/ppermute | solution.py:610
  81.9 8.4 %collective-permute-start.16 = (bf16[544,512]{1,0:T(8,128)(2,1)S(1)}, bf16[544,512]{1,0:T(8,128)(2,1)S(1)}, u32[]{:S(2)}, u32[]{:S(2)}) collective-permute-start(bf16[544,512]{1,0:T(8,128)(2,1)S(1)} %pad_maximum_fusion.3), channel_id=1, source_target_pairs={{0,8},{1,9},{2,10},{3,11},{4,20},{5,21},{6,22},{7,23},{8,0},{9,1},... | collective-permute-start | bytes 1671176 | tf_op jit(solution)/shard_map/ppermute | solution.py:610
  82.0 4.6 %collective-permute-start.18 = (bf16[2,64,512]{2,1,0:T(8,128)(2,1)S(1)}, bf16[2,64,512]{2,1,0:T(8,128)(2,1)S(1)}, u32[]{:S(2)}, u32[]{:S(2)}) collective-permute-start(bf16[2,64,512]{2,1,0:T(8,128)(2,1)S(1)} %pad_maximum_fusion.15), channel_id=1, source_target_pairs={{0,2},{1,3},{2,0},{3,1},{4,5},{5,4},{6,7},{7,6},{8,10},{9,11},{10,... | collective-permute-start | bytes 393224 | tf_op jit(solution)/shard_map/ppermute | solution.py:610
  90.5 5.9 %collective-permute-start.20 = (bf16[288,512]{1,0:T(8,128)(2,1)S(1)}, bf16[288,512]{1,0:T(8,128)(2,1)S(1)}, u32[]{:S(2)}, u32[]{:S(2)}) collective-permute-start(bf16[288,512]{1,0:T(8,128)(2,1)S(1)} %pad_maximum_fusion.9), channel_id=1, source_target_pairs={{0,16},{1,17},{2,18},{3,19},{4,12},{5,13},{6,14},{7,15},{8,24},{9,... | collective-permute-start | bytes 884744 | tf_op jit(solution)/shard_map/ppermute | solution.py:610
  91.5 15.2 %collective-permute-start.26 = (bf16[2,64,512]{2,1,0:T(8,128)(2,1)S(1)}, bf16[2,64,512]{2,1,0:T(8,128)(2,1)S(1)}, u32[]{:S(2)}, u32[]{:S(2)}) collective-permute-start(bf16[2,64,512]{2,1,0:T(8,128)(2,1)S(1)} %add_convert_fusion.9), channel_id=1, source_target_pairs={{0,1},{1,0},{2,3},{3,2},{4,6},{5,7},{6,4},{7,5},{8,9},{9,8},{10,11... | collective-permute-start | bytes 393224 | tf_op jit(solution)/shard_map/ppermute | solution.py:610
  93.0 12.0 %collective-permute-start.24 = (bf16[2,64,512]{2,1,0:T(8,128)(2,1)S(1)}, bf16[2,64,512]{2,1,0:T(8,128)(2,1)S(1)}, u32[]{:S(2)}, u32[]{:S(2)}) collective-permute-start(bf16[2,64,512]{2,1,0:T(8,128)(2,1)S(1)} %add_convert_fusion.10), channel_id=1, source_target_pairs={{0,1},{1,0},{2,3},{3,2},{4,6},{5,7},{6,4},{7,5},{8,9},{9,8},{10,11... | collective-permute-start | bytes 393224 | tf_op jit(solution)/shard_map/ppermute | solution.py:610
  96.6 8.3 %collective-permute-start.22 = (bf16[160,512]{1,0:T(8,128)(2,1)S(1)}, bf16[160,512]{1,0:T(8,128)(2,1)S(1)}, u32[]{:S(2)}, u32[]{:S(2)}) collective-permute-start(bf16[160,512]{1,0:T(8,128)(2,1)S(1)} %pad_maximum_fusion.13), channel_id=1, source_target_pairs={{0,1},{1,0},{2,3},{3,2},{4,6},{5,7},{6,4},{7,5},{8,9},{9,8},{10,11... | collective-permute-start | bytes 491528 | tf_op jit(solution)/shard_map/ppermute | solution.py:610
  98.5 16.3 %collective-permute-start.21 = (bf16[2,512,128]{2,1,0:T(8,128)(2,1)S(1)}, bf16[2,512,128]{2,1,0:T(8,128)(2,1)S(1)}, u32[]{:S(2)}, u32[]{:S(2)}) collective-permute-start(bf16[2,512,128]{2,1,0:T(8,128)(2,1)S(1)} %get-tuple-element.263), channel_id=1, source_target_pairs={{0,1},{1,0},{2,3},{3,2},{4,6},{5,7},{6,4},{7,5},{8,9},{9,8},{10,11... | collective-permute-start | bytes 786440 | tf_op jit(solution)/shard_map/ppermute | solution.py:610
  105.1 5.6 %collective-permute-start.25 = (bf16[4,64,512]{2,1,0:T(8,128)(2,1)S(1)}, bf16[4,64,512]{2,1,0:T(8,128)(2,1)S(1)}, u32[]{:S(2)}, u32[]{:S(2)}) collective-permute-start(bf16[4,64,512]{2,1,0:T(8,128)(2,1)S(1)} %pad_maximum_fusion.10), channel_id=1, source_target_pairs={{0,16},{1,17},{2,18},{3,19},{4,12},{5,13},{6,14},{7,15},{8,24},{9,... | collective-permute-start | bytes 786440 | tf_op jit(solution)/shard_map/ppermute | solution.py:610
  105.9 8.8 %collective-permute-start.23 = (bf16[160,512]{1,0:T(8,128)(2,1)S(1)}, bf16[160,512]{1,0:T(8,128)(2,1)S(1)}, u32[]{:S(2)}, u32[]{:S(2)}) collective-permute-start(bf16[160,512]{1,0:T(8,128)(2,1)S(1)} %pad_maximum_fusion.14), channel_id=1, source_target_pairs={{0,2},{1,3},{2,0},{3,1},{4,5},{5,4},{6,7},{7,6},{8,10},{9,11},{10,... | collective-permute-start | bytes 491528 | tf_op jit(solution)/shard_map/ppermute | solution.py:610
  106.7 11.6 %collective-permute-start.30 = (bf16[4,64,512]{2,1,0:T(8,128)(2,1)S(1)}, bf16[4,64,512]{2,1,0:T(8,128)(2,1)S(1)}, u32[]{:S(2)}, u32[]{:S(2)}) collective-permute-start(bf16[4,64,512]{2,1,0:T(8,128)(2,1)S(1)} %pad_maximum_fusion.11), channel_id=1, source_target_pairs={{0,16},{1,17},{2,18},{3,19},{4,12},{5,13},{6,14},{7,15},{8,24},{9,... | collective-permute-start | bytes 786440 | tf_op jit(solution)/shard_map/ppermute | solution.py:610
  110.7 10.5 %collective-permute-start.29 = (bf16[8,64,512]{2,1,0:T(8,128)(2,1)S(1)}, bf16[8,64,512]{2,1,0:T(8,128)(2,1)S(1)}, u32[]{:S(2)}, u32[]{:S(2)}) collective-permute-start(bf16[8,64,512]{2,1,0:T(8,128)(2,1)S(1)} %pad_maximum_fusion.4), channel_id=1, source_target_pairs={{0,8},{1,9},{2,10},{3,11},{4,20},{5,21},{6,22},{7,23},{8,0},{9,1},... | collective-permute-start | bytes 1572872 | tf_op jit(solution)/shard_map/ppermute | solution.py:610
  114.7 6.8 %collective-permute-start.28 = (bf16[2,64,512]{2,1,0:T(8,128)(2,1)S(1)}, bf16[2,64,512]{2,1,0:T(8,128)(2,1)S(1)}, u32[]{:S(2)}, u32[]{:S(2)}) collective-permute-start(bf16[2,64,512]{2,1,0:T(8,128)(2,1)S(1)} %fusion.1), channel_id=1, source_target_pairs={{0,1},{1,0},{2,3},{3,2},{4,6},{5,7},{6,4},{7,5},{8,9},{9,8},{10,11... | collective-permute-start | bytes 393224 | tf_op jit(solution)/shard_map/ppermute | solution.py:610
  114.9 15.1 %collective-permute-start.27 = (bf16[3,512,128]{2,1,0:T(8,128)(2,1)S(1)}, bf16[3,512,128]{2,1,0:T(8,128)(2,1)S(1)}, u32[]{:S(2)}, u32[]{:S(2)}) collective-permute-start(bf16[3,512,128]{2,1,0:T(8,128)(2,1)S(1)} %pad_maximum_fusion.8), channel_id=1, source_target_pairs={{0,2},{1,3},{2,0},{3,1},{4,5},{5,4},{6,7},{7,6},{8,10},{9,11},{10,... | collective-permute-start | bytes 1179656 | tf_op jit(solution)/shard_map/ppermute | solution.py:610
  118.4 13.0 %collective-permute-start.33 = (bf16[8,64,512]{2,1,0:T(8,128)(2,1)S(1)}, bf16[8,64,512]{2,1,0:T(8,128)(2,1)S(1)}, u32[]{:S(2)}, u32[]{:S(2)}) collective-permute-start(bf16[8,64,512]{2,1,0:T(8,128)(2,1)S(1)} %pad_maximum_fusion.5), channel_id=1, source_target_pairs={{0,8},{1,9},{2,10},{3,11},{4,20},{5,21},{6,22},{7,23},{8,0},{9,1},... | collective-permute-start | bytes 1572872 | tf_op jit(solution)/shard_map/ppermute | solution.py:610
  121.5 8.5 %collective-permute-start.31 = (bf16[4,64,512]{2,1,0:T(8,128)(2,1)S(1)}, bf16[4,64,512]{2,1,0:T(8,128)(2,1)S(1)}, u32[]{:S(2)}, u32[]{:S(2)}) collective-permute-start(bf16[4,64,512]{2,1,0:T(8,128)(2,1)S(1)} %pad_maximum_fusion.12), channel_id=1, source_target_pairs={{0,16},{1,17},{2,18},{3,19},{4,12},{5,13},{6,14},{7,15},{8,24},{9,... | collective-permute-start | bytes 786440 | tf_op jit(solution)/shard_map/ppermute | solution.py:610
  122.6 11.1 %collective-permute-start.35 = (bf16[16,64,512]{2,1,0:T(8,128)(2,1)S(1)}, bf16[16,64,512]{2,1,0:T(8,128)(2,1)S(1)}, u32[]{:S(2)}, u32[]{:S(2)}) collective-permute-start(bf16[16,64,512]{2,1,0:T(8,128)(2,1)S(1)} %pad_maximum_fusion.own_ref), channel_id=1, source_target_pairs={{0,4},{4,0},{8,12},{12,8},{16,20},{20,16},{24,28},{28,24},{1,5},{5... | collective-permute-start | bytes 3145736 | tf_op jit(solution)/shard_map/ppermute | solution.py:592
  131.4 4.9 %collective-permute-start.34 = (bf16[16,64,512]{2,1,0:T(8,128)(2,1)S(1)}, bf16[16,64,512]{2,1,0:T(8,128)(2,1)S(1)}, u32[]{:S(2)}, u32[]{:S(2)}) collective-permute-start(bf16[16,64,512]{2,1,0:T(8,128)(2,1)S(1)} %pad_maximum_fusion.1.own_ref), channel_id=1, source_target_pairs={{0,4},{4,0},{8,12},{12,8},{16,20},{20,16},{24,28},{28,24},{1,5},{5... | collective-permute-start | bytes 3145736 | tf_op jit(solution)/shard_map/ppermute | solution.py:592
  133.1 8.3 %collective-permute-start.32 = (bf16[8,64,512]{2,1,0:T(8,128)(2,1)S(1)}, bf16[8,64,512]{2,1,0:T(8,128)(2,1)S(1)}, u32[]{:S(2)}, u32[]{:S(2)}) collective-permute-start(bf16[8,64,512]{2,1,0:T(8,128)(2,1)S(1)} %pad_maximum_fusion.6), channel_id=1, source_target_pairs={{0,8},{1,9},{2,10},{3,11},{4,20},{5,21},{6,22},{7,23},{8,0},{9,1},... | collective-permute-start | bytes 1572872 | tf_op jit(solution)/shard_map/ppermute | solution.py:610
  141.6 4.1 %collective-permute-start.36 = (bf16[16,64,512]{2,1,0:T(8,128)(2,1)S(1)}, bf16[16,64,512]{2,1,0:T(8,128)(2,1)S(1)}, u32[]{:S(2)}, u32[]{:S(2)}) collective-permute-start(bf16[16,64,512]{2,1,0:T(8,128)(2,1)S(1)} %pad_maximum_fusion.2.half_ref), channel_id=1, source_target_pairs={{0,4},{4,0},{8,12},{12,8},{16,20},{20,16},{24,28},{28,24},{1,5},{5... | collective-permute-start | bytes 3145736 | tf_op jit(solution)/shard_map/ppermute | solution.py:592
